TPU v7x, 32 devices: a whole 2x2x4 slice. The times are simulated.
32 devices in a mesh: lat: 4 (over y, x), lon: 8 (over z, core).
Axes of the slice: x: 2, y: 2, z: 4, core: 2. Of those that a mesh axis runs over, the one named last changes fastest.
Arguments:
- nodes: bfloat16 [64, 512, 512], P('lat', 'lon'), may hold values from -6 to 6
- cotangent: bfloat16 [64, 512, 512], P('lat', 'lon'), may hold values from -6 to 6
- w_send: bfloat16 [512, 512], replicated, may hold values from -0.25 to 0.25
- w_recv: bfloat16 [512, 512], replicated, may hold values from -0.25 to 0.25
- edge_bias: float32 [512], replicated, may hold values from -4 to 4
- w_self: bfloat16 [512, 512], replicated, may hold values from -0.25 to 0.25
- w_agg: bfloat16 [512, 512], replicated, may hold values from -0.25 to 0.25
- node_bias: float32 [512], replicated, may hold values from -3 to 3
- w_out: bfloat16 [512, 512], replicated, may hold values from -0.25 to 0.25
- gain: float32 [512], replicated, may hold values from 0.5 to 1.5
- coarse_slots: int32 [4, 8, 16], P('lat', 'lon'), may hold values from 0 to 1023, as said below
- long_senders: int32 [4, 8, 8, 8], P('lat', 'lon'), may hold values from 0 to 15
- long_receivers: int32 [4, 8, 8, 8], P('lat', 'lon'), may hold values from 0 to 15
Outputs:
- new_nodes: bfloat16 [64, 512, 512], P('lat', 'lon')
- grad_nodes: bfloat16 [64, 512, 512], P('lat', 'lon')
- grad_send: float32 [512, 512], replicated
- grad_recv: float32 [512, 512], replicated
- grad_edge_bias: float32 [512], replicated
- grad_self: float32 [512, 512], replicated
- grad_agg: float32 [512, 512], replicated
- grad_node_bias: float32 [512], replicated
- grad_out: float32 [512, 512], replicated
- grad_gain: float32 [512], replicated
Inputs may be any that keep to these rules, and one draw needn't show every extreme that they name: `coarse_slots`: the 16 entries of one patch are distinct positions r * 64 + c of that patch.
All inputs are finite; a program needn't handle non-finite values.
Results may differ from a plain program's by a relative error of at most 0.008.
Values may be sent and summed in bfloat16 or wider, within the bound.
No kernel may reach another device: no remote copies, remote signals or barrier semaphores. Data moves between devices by JAX's collectives and lax.ppermute only.
A program may use at most 128 MiB of HBM per device.

v0:
```python
import jax
import jax.numpy as jnp
from jax import lax
from jax.sharding import PartitionSpec as P

OFFSETS = ((1, 0), (-1, 0), (0, 1), (0, -1), (1, -1), (-1, 1))
epsilon = 1e-05


def extended(cells, sides, width):
    for axis, dim in sides:
        count = lax.axis_size(axis)
        head = lax.slice_in_dim(cells, 0, width, axis=dim)
        tail = lax.slice_in_dim(cells, cells.shape[dim] - width, cells.shape[dim], axis=dim)
        cells = jnp.concatenate(
            [
                lax.ppermute(tail, axis, [(i, (i + 1) % count) for i in range(count)]),
                cells,
                lax.ppermute(head, axis, [((i + 1) % count, i) for i in range(count)]),
            ],
            axis=dim,
        )
    return cells


def silu_slope(values):
    sigmoid = jax.nn.sigmoid(values)
    return sigmoid * (1.0 + values * (1.0 - sigmoid))


def matmul(left, right):
    return jnp.dot(left, right, preferred_element_type=jnp.float32)


def on_device(
    nodes,
    cotangent,
    w_send,
    w_recv,
    edge_bias,
    w_self,
    w_agg,
    node_bias,
    w_out,
    gain,
    coarse_slots,
    long_senders,
    long_receivers,
):
    patch_rows, patch_cols, depth = nodes.shape
    patch_size = patch_rows * patch_cols
    lat_count = lax.axis_size("lat")
    lon_count = lax.axis_size("lon")
    grid_rows = patch_rows * lat_count
    grad_scale = float(patch_size * lat_count * lon_count) ** (-0.5)
    highest = lax.Precision.HIGHEST
    flat_nodes = nodes.reshape(patch_size, depth)
    send_flat = matmul(flat_nodes, w_send).astype(jnp.bfloat16)
    recv_flat = matmul(flat_nodes, w_recv)
    send_proj = send_flat.reshape(patch_rows, patch_cols, depth)
    recv_proj = recv_flat.reshape(patch_rows, patch_cols, depth)
    padded = extended(send_proj, (("lat", 0), ("lon", 1)), 1)
    grid_row = lax.axis_index("lat") * patch_rows + jnp.arange(patch_rows)

    def row_valid(lat_step):
        inside = (grid_row + lat_step >= 0) & (grid_row + lat_step < grid_rows)
        return inside.astype(jnp.float32)[:, None, None]

    def sender_of(lat_step, lon_step):
        window = padded[
            1 + lat_step : 1 + lat_step + patch_rows, 1 + lon_step : 1 + lon_step + patch_cols
        ]
        return window.astype(jnp.float32)

    fine_sum = jnp.zeros((patch_rows, patch_cols, depth), jnp.float32)
    for lat_step, lon_step in OFFSETS:
        fine_sum = fine_sum + row_valid(lat_step) * jax.nn.silu(
            sender_of(lat_step, lon_step) + recv_proj + edge_bias
        )
    coarse_pos = coarse_slots.reshape(-1)
    coarse_count = coarse_pos.shape[0]
    senders = long_senders.reshape(lon_count, -1)
    receivers = long_receivers.reshape(lon_count, -1)
    coarse_send = jnp.take(send_flat, coarse_pos, axis=0)
    coarse_recv = jnp.take(recv_flat, coarse_pos, axis=0)
    blocks = lax.all_gather(coarse_send, "lon", axis=0, tiled=True).reshape(
        lon_count, coarse_count, depth
    )
    edge_send = jnp.take_along_axis(blocks, senders[:, :, None], axis=1).astype(jnp.float32)
    edge_recv = jnp.take(coarse_recv, receivers, axis=0)
    pre_long = edge_send + edge_recv + edge_bias
    slot_ids = jnp.arange(coarse_count)
    recv_hot = (receivers[:, :, None] == slot_ids).astype(jnp.float32)
    send_hot = (senders[:, :, None] == slot_ids).astype(jnp.float32)
    coarse_sum = jnp.einsum("seb,sed->bd", recv_hot, jax.nn.silu(pre_long), precision=highest)
    total = fine_sum.reshape(patch_size, depth).at[coarse_pos].add(coarse_sum)
    gathered = total.astype(jnp.bfloat16)
    pre_node = matmul(flat_nodes, w_self) + matmul(gathered, w_agg) + node_bias
    hidden = jax.nn.silu(pre_node).astype(jnp.bfloat16)
    output = matmul(hidden, w_out)
    row_mean = jnp.mean(output, axis=-1, keepdims=True)
    centred = output - row_mean
    inv_std = lax.rsqrt(jnp.mean(centred * centred, axis=-1, keepdims=True) + epsilon)
    normed = centred * inv_std
    new_flat = (flat_nodes.astype(jnp.float32) + gain * normed).astype(jnp.bfloat16)
    cot_flat = cotangent.reshape(patch_size, depth).astype(jnp.float32)
    gain_grad = jnp.sum(cot_flat * normed, axis=0)
    d_norm = cot_flat * gain
    d_output = (
        inv_std
        * (
            d_norm
            - jnp.mean(d_norm, axis=-1, keepdims=True)
            - normed * jnp.mean(d_norm * normed, axis=-1, keepdims=True)
        )
    ).astype(jnp.bfloat16)
    out_grad = matmul(hidden.T, d_output)
    d_pre = matmul(d_output, w_out.T) * silu_slope(pre_node)
    node_bias_grad = jnp.sum(d_pre, axis=0)
    d_pre_b = d_pre.astype(jnp.bfloat16)
    self_grad = matmul(flat_nodes.T, d_pre_b)
    agg_grad = matmul(gathered.T, d_pre_b)
    d_sum_b = lax.optimization_barrier(matmul(d_pre_b, w_agg.T).astype(jnp.bfloat16))
    dsum_flat = d_sum_b.astype(jnp.float32)
    d_sum = dsum_flat.reshape(patch_rows, patch_cols, depth)
    beside_all = extended(
        jnp.stack([d_sum, recv_proj]).astype(jnp.bfloat16), (("lat", 1), ("lon", 2)), 1
    ).astype(jnp.float32)
    dsum_around = beside_all[0]
    recv_around = beside_all[1]
    own_send = send_proj.astype(jnp.float32)
    d_recv = jnp.zeros((patch_rows, patch_cols, depth), jnp.float32)
    d_send = jnp.zeros((patch_rows, patch_cols, depth), jnp.float32)
    edge_bias_grad = jnp.zeros((depth,), jnp.float32)
    for lat_step, lon_step in OFFSETS:
        slope_in = (
            row_valid(lat_step)
            * d_sum
            * silu_slope(sender_of(lat_step, lon_step) + recv_proj + edge_bias)
        )
        d_recv = d_recv + slope_in
        edge_bias_grad = edge_bias_grad + jnp.sum(slope_in, axis=(0, 1))
        far_dsum = dsum_around[
            1 - lat_step : 1 - lat_step + patch_rows, 1 - lon_step : 1 - lon_step + patch_cols
        ]
        far_recv = recv_around[
            1 - lat_step : 1 - lat_step + patch_rows, 1 - lon_step : 1 - lon_step + patch_cols
        ]
        d_send = d_send + row_valid(-lat_step) * far_dsum * silu_slope(
            own_send + far_recv + edge_bias
        )
    coarse_dsum = jnp.take(dsum_flat, coarse_pos, axis=0)
    slope_long = jnp.take(coarse_dsum, receivers, axis=0) * silu_slope(pre_long)
    edge_bias_grad = edge_bias_grad + jnp.sum(slope_long, axis=(0, 1))
    recv_long = jnp.einsum("seb,sed->bd", recv_hot, slope_long, precision=highest)
    block_grads = jnp.einsum("seb,sed->sbd", send_hot, slope_long, precision=highest)
    flat_grads = block_grads.reshape(lon_count * coarse_count, depth)
    send_long = lax.psum_scatter(
        flat_grads.astype(jnp.bfloat16), "lon", scatter_dimension=0, tiled=True
    ).astype(jnp.float32)
    d_recv_b = d_recv.reshape(patch_size, depth).at[coarse_pos].add(recv_long).astype(jnp.bfloat16)
    d_send_b = d_send.reshape(patch_size, depth).at[coarse_pos].add(send_long).astype(jnp.bfloat16)
    recv_grad = matmul(flat_nodes.T, d_recv_b)
    send_grad = matmul(flat_nodes.T, d_send_b)
    grad_flat = (
        cot_flat
        + matmul(d_pre_b, w_self.T)
        + matmul(d_recv_b, w_recv.T)
        + matmul(d_send_b, w_send.T)
    ).astype(jnp.bfloat16)
    summed = lax.psum(
        (
            send_grad,
            recv_grad,
            edge_bias_grad,
            self_grad,
            agg_grad,
            node_bias_grad,
            out_grad,
            gain_grad,
        ),
        ("lat", "lon"),
    )
    return (
        new_flat.reshape(patch_rows, patch_cols, depth),
        grad_flat.reshape(patch_rows, patch_cols, depth),
        grad_scale * summed[0],
        grad_scale * summed[1],
        grad_scale * summed[2],
        grad_scale * summed[3],
        grad_scale * summed[4],
        grad_scale * summed[5],
        grad_scale * summed[6],
        grad_scale * summed[7],
    )


def solution(mesh):
    placed = (
        P("lat", "lon", None),
        P("lat", "lon", None),
        P(),
        P(),
        P(),
        P(),
        P(),
        P(),
        P(),
        P(),
        P("lat", "lon", None),
        P("lat", "lon", None, None),
        P("lat", "lon", None, None),
    )
    return jax.shard_map(
        on_device,
        mesh=mesh,
        in_specs=placed,
        out_specs=(
            P("lat", "lon", None),
            P("lat", "lon", None),
            P(),
            P(),
            P(),
            P(),
            P(),
            P(),
            P(),
            P(),
        ),
        check_vma=False,
    )
```

profile of v0, /device:TPU:0, one launch (start us, length us, event | category | flops | bytes accessed | tf_op | source)
XLA Modules:
  0.0 314.1 jit_solution(11482342519500545111)
XLA Ops:
  7.3 2.2 convolution_convert_fusion.1
  9.5 0.7 slice_bitcast_fusion.2
  10.2 3.9 %collective-permute-start = (bf16[1,64,512]{2,1,0:T(8,128)(2,1)}, bf16[1,64,512]{2,1,0:T(8,128)(2,1)S(1)}, u32[]{:S(2)}, u32[]{:S(2)}) collective-permute-start(bf16[1,64,512]{2,1,0:T(8,128)(2,1)} %get-tuple-element.75), channel_id=1, source_target_pairs={{8,0},{16,8},{24,16},{0,24},{9,1},{17,9},{25,17},{1,25},{10,2},{18... | collective-permute-start | bytes 196616 | tf_op jit(solution)/shard_map/ppermute | solution.py:19
  14.2 2.0 fusion.62
  16.2 2.4 fusion.61
  18.7 0.6 gather_fusion
  19.3 2.2 gather_fusion.2
  21.6 14.2 %all_gather.3 = bf16[128,512]{1,0:T(8,128)(2,1)S(1)} all-gather(bf16[16,512]{1,0:T(8,128)(2,1)S(1)} %broadcast_select_fusion.2), channel_id=1, replica_groups=mesh['lat'=4,'lon'=8] {'lon'}, dimensions={0}, use_global_device_ids=true | all-gather | bytes 147456 | tf_op jit(solution)/shard_map/all_gather | solution.py:86
  36.0 1.5 fusion.23
  37.5 0.7 gather_fusion.3
  38.2 1.6 gather_fusion.1
  39.8 1.0 fusion.41
  41.0 0.8 pad_maximum_fusion.9
  42.2 3.2 %collective-permute-start.2 = (bf16[18,1,512]{2,1,0:T(2,128)(2,1)S(1)}, bf16[18,1,512]{2,1,0:T(2,128)(2,1)}, u32[]{:S(2)}, u32[]{:S(2)}) collective-permute-start(bf16[18,1,512]{2,1,0:T(2,128)(2,1)S(1)} %get-tuple-element.73), channel_id=1, source_target_pairs={{1,0},{2,1},{3,2},{4,3},{5,4},{6,5},{7,6},{0,7},{9,8},{10,9},{11,1... | collective-permute-start | bytes 55304 | tf_op jit(solution)/shard_map/ppermute | solution.py:19
  45.5 1.7 collective-permute-done.3
  47.2 1.7 maximum_maximum_fusion
  49.0 6.6 %multiply_add_fusion = f32[16,64,512]{2,1,0:T(8,128)} fusion(f32[16,64,512]{2,1,0:T(8,128)S(1)} %bitcast.139, f32[16]{0:T(128)S(1)} %get-tuple-element.83, f32[16]{0:T(128)S(1)} %get-tuple-element.84, f32[512]{0:T(512)S(1)} %copy-done.29, f32[16]{0:T(128)S(1)} %and_convert_fusion.2, bf16[18,65,512]{2,1,0:T(8,128)(2,1)S(1)} %get-tuple-element.71, ...), kind=kLoop, calls=%fused_computation.69 | loop fusion | flops 28835840 | bytes 9570496 | tf_op jit(solution)/shard_map/add | solution.py:77
  55.6 3.6 %scatter_fusion = f32[1024,512]{1,0:T(8,128)} fusion(f32[1024,512]{1,0:T(8,128)} %bitcast.144, s32[16]{0:T(128)S(1)} %copy-done.42, f32[16,512]{1,0:T(8,128)S(1)} %convolution_bitcast_fusion.4), kind=kCustom, calls=%fused_computation.6 | custom fusion | flops 8192 | bytes 98368 | tf_op jit(solution)/shard_map/scatter-add | solution.py:96
  59.1 3.3 %multiply_convert_fusion = (bf16[1024,512]{1,0:T(8,128)(2,1)S(1)}, f32[1024,512]{1,0:T(8,128)S(1)}) fusion(f32[512]{0:T(512)S(1)} %copy-done.45, f32[1024,512]{1,0:T(8,128)} %fusion.62, bf16[512,512]{1,0:T(8,128)(2,1)S(1)} %copy-done, f32[1024,512]{1,0:T(8,128)} %scatter_fusion), kind=kOutput, calls=%fused_computation.66 | convolution fusion | flops 541065216 | bytes 7866368 | tf_op jit(solution)/shard_map/dot_general | solution.py:32
  62.5 0.8 fusion.60
  64.1 1.0 fusion.27
  65.1 2.1 fusion.21
  67.2 1.8 fusion.59
  69.0 0.7 convolution_convert_fusion
  69.8 0.9 copy-done.3
  70.6 1.7 convolution_bitcast_fusion
  72.4 1.7 fusion.33
  74.1 1.6 convert_element_type.147
  75.7 2.2 gather_fusion.4
  78.0 0.7 gather_fusion.5
  79.1 1.1 pad_maximum_fusion.4
  80.2 3.0 collective-permute-start.5
  83.2 7.7 %fusion.51 = (f32[512]{0:T(512)S(1)}, f32[16,64,512]{2,1,0:T(8,128)S(1)}, f32[512]{0:T(512)S(1)}, f32[16,64,512]{2,1,0:T(8,128)S(1)}, f32[512]{0:T(512)S(1)}, /*...) fusion(f32[512]{0:T(512)S(1)} %copy-done.29, ...), kind=kLoop, calls=%fused_computation.166 | loop fusion | flops 40891392 | bytes 21117120 | tf_op jit(solution)/shard_map/reduce_sum | solution.py:142
  91.0 3.0 add_add_fusion
  93.9 3.5 %scatter_fusion.1 = f32[1024,512]{1,0:T(8,128)} fusion(f32[1024,512]{1,0:T(8,128)} %bitcast.138, s32[16]{0:T(128)S(1)} %copy-done.43, f32[16,512]{1,0:T(8,128)S(1)} %convolution_bitcast_fusion.3), kind=kCustom, calls=%fused_computation.7 | custom fusion | flops 8192 | bytes 98368 | tf_op jit(solution)/shard_map/scatter-add | solution.py:161
  97.5 3.7 %convolution_bitcast_fusion.1 = f32[512,512]{0,1:T(8,128)} fusion(bf16[1024,512]{1,0:T(8,128)(2,1)} %bitcast.133, f32[1024,512]{1,0:T(8,128)} %scatter_fusion.1), kind=kOutput, calls=%fused_computation.86 | convolution fusion | flops 537395200 | bytes 4194304 | tf_op jit(solution)/shard_map/dot_general | solution.py:32
  101.2 1.7 fusion.64
  103.1 3.3 %collective-permute-start.7 = (bf16[2,18,1,512]{3,2,1,0:T(2,128)(2,1)S(1)}, bf16[2,18,1,512]{3,2,1,0:T(2,128)(2,1)S(1)}, u32[]{:S(2)}, u32[]{:S(2)}) collective-permute-start(bf16[2,18,1,512]{3,2,1,0:T(2,128)(2,1)S(1)} %get-tuple-element.63), channel_id=1, source_target_pairs={{1,0},{2,1},{3,2},{4,3},{5,4},{6,5},{7,6},{0,7},{9,8},{10,9},{11,1... | collective-permute-start | bytes 110600 | tf_op jit(solution)/shard_map/ppermute | solution.py:19
  106.3 1.0 convolution_convert_fusion.2
  107.5 0.9 collective-permute-done.7
  108.3 3.6 %collective-permute-done.6 = bf16[2,18,1,512]{3,2,1,0:T(2,128)(2,1)S(1)} collective-permute-done((bf16[2,18,1,512]{3,2,1,0:T(2,128)(2,1)S(1)}, bf16[2,18,1,512]{3,2,1,0:T(2,128)(2,1)S(1)}, u32[]{:S(2)}, u32[]{:S(2)}) %collective-permute-start.6) | collective-permute-done | bytes 36896 | tf_op jit(solution)/shard_map/ppermute | solution.py:17
  111.9 2.4 maximum_convert_fusion
  114.4 0.6 slice_bitcast_fusion
  115.0 7.3 %fusion.7 = f32[16,64,512]{2,1,0:T(8,128)} fusion(f32[18,66,512]{2,1,0:T(8,128)S(1)} %get-tuple-element.51, f32[18,66,512]{2,1,0:T(8,128)S(1)} %get-tuple-element.50, f32[16]{0:T(128)S(1)} %copy-done.34, f32[16]{0:T(128)S(1)} %copy-done.36, f32[512]{0:T(512)S(1)} %copy-done.29, f32[16]{0:T(128)S(1)} %copy-done.38, ...), kind=kLoop, calls=%fused_computation.26 | loop fusion | flops 37748736 | bytes 28313792 | tf_op jit(solution)/shard_map/add | solution.py:149
  122.3 16.9 %reduce-scatter.2.cloned.1.call-done = bf16[16,512]{1,0:T(8,128)(2,1)} async-done(((bf16[128,512]{1,0:T(8,128)(2,1)}), bf16[16,512]{1,0:T(8,128)(2,1)}) %reduce-scatter.2.cloned.1.call-update) | async-done | bytes 16400 | tf_op jit(solution)/shard_map/reduce_scatter | solution.py:158
  139.1 3.7 %scatter_custom_fusion.2 = f32[1024,512]{1,0:T(8,128)} fusion(f32[1024,512]{1,0:T(8,128)} %bitcast.140, s32[16]{0:T(128)S(1)} %copy-done.43, bf16[16,512]{1,0:T(8,128)(2,1)} %reduce-scatter.2.cloned.1.call-done), kind=kCustom, calls=%fused_computation.129 | custom fusion | flops 16384 | bytes 2113536 | tf_op jit(solution)/shard_map/scatter-add | solution.py:162
  142.9 3.3 %convolution_bitcast_fusion.2 = f32[512,512]{0,1:T(8,128)} fusion(bf16[1024,512]{1,0:T(8,128)(2,1)S(1)} %bitcast.137, f32[1024,512]{1,0:T(8,128)} %scatter_custom_fusion.2), kind=kOutput, calls=%fused_computation.87 | convolution fusion | flops 537395200 | bytes 4194304 | tf_op jit(solution)/shard_map/dot_general | solution.py:32
  146.2 0.6 copy-done.44
  146.9 38.5 %all-reduce = (f32[512]{0:T(512)S(1)}, f32[512]{0:T(512)S(1)}, f32[512]{0:T(512)S(1)}) all-reduce(f32[512]{0:T(512)S(1)} %add_add_fusion.8, f32[512]{0:T(512)S(1)} %copy-done.44, f32[512]{0:T(512)S(1)} %get-tuple-element.22), channel_id=1, replica_groups=mesh['lat'=4,'lon'=8] {'lat','lon'}, use_global_device_ids=true, to_apply=%region_17.20 | all-reduce | flops 1536 | bytes 12288 | tf_op jit(solution)/shard_map/psum | solution.py:171
  185.4 0.6 broadcast_multiply_fusion.10
  186.0 0.6 broadcast_multiply_fusion.9
  186.6 0.6 broadcast_multiply_fusion.8
  187.2 0.7 fusion.63
  187.9 2.5 fusion.31
  190.5 1.9 fusion.26
  192.4 103.9 %all-reduce.4.cloned.1.call-done = (f32[512,512]{0,1:T(8,128)}, f32[512,512]{0,1:T(8,128)}, f32[512,512]{0,1:T(8,128)}, f32[512,512]{0,1:T(8,128)}, f32[512,512]{0,1:T(8,128)}) async-done(((f32[512,512]{0,1:T(8,128)}, f32[512,512]{0,1:T(8,128)}, f32[512,512]{0,1:T(8,128)}, f32[512,512]{0,1:T(8,128)}, f32[512,512]{0,1:T(8,128)}), (f32[512,512]{0,1:T(8,128)}, f32[512,512]{0,1:T(8,128)}, f32[512,512]{0,1:T(8,128)}, ...) | async-done | bytes 5242896 | tf_op jit(solution)/shard_map/psum | solution.py:171
  296.3 1.3 broadcast_multiply_fusion.4
  297.6 1.3 copy.28
  298.9 1.4 broadcast_multiply_fusion.3
  300.4 1.3 copy.29
  301.8 1.3 copy.30
  303.1 1.4 broadcast_multiply_fusion.1
  304.5 1.3 copy.31
  305.9 1.3 copy.32
  (135 shorter events, 3.3 us)
Async XLA Ops:
  7.2 52.0 %copy-start = (bf16[512,512]{1,0:T(8,128)(2,1)S(1)}, bf16[512,512]{1,0:T(8,128)(2,1)}, u32[]{:S(2)}) copy-start(bf16[512,512]{1,0:T(8,128)(2,1)} %param.23) | copy-start | bytes 1572868
  7.2 7.0 %copy-start.2 = (bf16[16,64,512]{2,1,0:T(8,128)(2,1)S(1)}, bf16[16,64,512]{2,1,0:T(8,128)(2,1)}, u32[]{:S(2)}) copy-start(bf16[16,64,512]{2,1,0:T(8,128)(2,1)} %param.17) | copy-start | bytes 3145732
  7.2 6.9 %copy-start.46 = (s32[1,1,16]{2,1,0:T(1,128)S(1)}, s32[1,1,16]{2,1,0:T(1,128)}, u32[]{:S(2)}) copy-start(s32[1,1,16]{2,1,0:T(1,128)} %param.27) | copy-start | bytes 196
  7.2 6.9 %copy-start.31 = (s32[1,1,8,8]{3,2,1,0:T(8,128)S(1)}, s32[1,1,8,8]{3,2,1,0:T(8,128)}, u32[]{:S(2)}) copy-start(s32[1,1,8,8]{3,2,1,0:T(8,128)} %param.29) | copy-start | bytes 772
  7.2 6.9 %copy-start.30 = (s32[1,1,8,8]{3,2,1,0:T(8,128)S(1)}, s32[1,1,8,8]{3,2,1,0:T(8,128)}, u32[]{:S(2)}) copy-start(s32[1,1,8,8]{3,2,1,0:T(8,128)} %param.28) | copy-start | bytes 772
  7.2 7.0 %copy-start.17 = (bf16[512,512]{1,0:T(8,128)(2,1)S(1)}, bf16[512,512]{1,0:T(8,128)(2,1)}, u32[]{:S(2)}) copy-start(bf16[512,512]{1,0:T(8,128)(2,1)} %param.22) | copy-start | bytes 1572868
  7.2 131.9 %reduce-scatter.2.cloned.1.call-start = ((), (), s32[]{:S(2)}) async-start(), calls=%async_computation.1 | async-start | bytes 147456 | tf_op jit(solution)/shard_map/reduce_scatter | solution.py:158
  9.5 6.7 %copy-start.18 = (bf16[512,512]{1,0:T(8,128)(2,1)S(1)}, bf16[512,512]{1,0:T(8,128)(2,1)}, u32[]{:S(2)}) copy-start(bf16[512,512]{1,0:T(8,128)(2,1)} %param.20) | copy-start | bytes 1572868
  10.2 30.9 %collective-permute-start = (bf16[1,64,512]{2,1,0:T(8,128)(2,1)}, bf16[1,64,512]{2,1,0:T(8,128)(2,1)S(1)}, u32[]{:S(2)}, u32[]{:S(2)}) collective-permute-start(bf16[1,64,512]{2,1,0:T(8,128)(2,1)} %get-tuple-element.75), channel_id=1, source_target_pairs={{8,0},{16,8},{24,16},{0,24},{9,1},{17,9},{25,17},{1,25},{10,2},{18... | collective-permute-start | bytes 196616 | tf_op jit(solution)/shard_map/ppermute | solution.py:19
  14.1 27.0 %collective-permute-start.1 = (bf16[1,64,512]{2,1,0:T(8,128)(2,1)}, bf16[1,64,512]{2,1,0:T(8,128)(2,1)}, u32[]{:S(2)}, u32[]{:S(2)}) collective-permute-start(bf16[1,64,512]{2,1,0:T(8,128)(2,1)} %get-tuple-element.74), channel_id=1, source_target_pairs={{0,8},{8,16},{16,24},{24,0},{1,9},{9,17},{17,25},{25,1},{2,10},{10... | collective-permute-start | bytes 196616 | tf_op jit(solution)/shard_map/ppermute | solution.py:17
  14.1 4.6 %copy-start.41 = (s32[16]{0:T(128)}, s32[16]{0:T(128)S(1)}, u32[]{:S(2)}) copy-start(s32[16]{0:T(128)S(1)} %fusion.50) | copy-start | bytes 196
  14.1 7.4 %copy-start.39 = (pred[16]{0:T(512)(128)(4,1)}, pred[16]{0:T(512)(128)(4,1)S(1)}, u32[]{:S(2)}) copy-start(pred[16]{0:T(512)(128)(4,1)S(1)} %compare_and_fusion.2) | copy-start | bytes 52
  16.2 19.8 %copy-start.32 = (f32[512]{0:T(512)S(1)}, f32[512]{0:T(512)}, u32[]{:S(2)}) copy-start(f32[512]{0:T(512)} %param.26) | copy-start | bytes 6148
  18.6 21.2 %copy-start.29 = (f32[512]{0:T(512)S(1)}, f32[512]{0:T(512)}, u32[]{:S(2)}) copy-start(f32[512]{0:T(512)} %param.21) | copy-start | bytes 6148
  41.0 7.9 %copy-start.33 = (f32[16]{0:T(128)}, f32[16]{0:T(128)S(1)}, u32[]{:S(2)}) copy-start(f32[16]{0:T(128)S(1)} %get-tuple-element.83) | copy-start | bytes 196
  41.0 7.9 %copy-start.35 = (f32[16]{0:T(128)}, f32[16]{0:T(128)S(1)}, u32[]{:S(2)}) copy-start(f32[16]{0:T(128)S(1)} %get-tuple-element.84) | copy-start | bytes 196
  41.8 5.4 %collective-permute-start.3 = (bf16[18,1,512]{2,1,0:T(2,128)(2,1)S(1)}, bf16[18,1,512]{2,1,0:T(2,128)(2,1)S(1)}, u32[]{:S(2)}, u32[]{:S(2)}) collective-permute-start(bf16[18,1,512]{2,1,0:T(2,128)(2,1)S(1)} %get-tuple-element.72), channel_id=1, source_target_pairs={{0,1},{1,2},{2,3},{3,4},{4,5},{5,6},{6,7},{7,0},{8,9},{9,10},{10,1... | collective-permute-start | bytes 55304 | tf_op jit(solution)/shard_map/ppermute | solution.py:17
  42.2 5.0 %collective-permute-start.2 = (bf16[18,1,512]{2,1,0:T(2,128)(2,1)S(1)}, bf16[18,1,512]{2,1,0:T(2,128)(2,1)}, u32[]{:S(2)}, u32[]{:S(2)}) collective-permute-start(bf16[18,1,512]{2,1,0:T(2,128)(2,1)S(1)} %get-tuple-element.73), channel_id=1, source_target_pairs={{1,0},{2,1},{3,2},{4,3},{5,4},{6,5},{7,6},{0,7},{9,8},{10,9},{11,1... | collective-permute-start | bytes 55304 | tf_op jit(solution)/shard_map/ppermute | solution.py:19
  45.4 10.1 %copy-start.37 = (f32[16]{0:T(128)}, f32[16]{0:T(128)S(1)}, u32[]{:S(2)}) copy-start(f32[16]{0:T(128)S(1)} %and_convert_fusion.2) | copy-start | bytes 196
  45.5 3.5 %copy-start.9 = (f32[1024,512]{1,0:T(8,128)S(1)}, f32[1024,512]{1,0:T(8,128)}, u32[]{:S(2)}) copy-start(f32[1024,512]{1,0:T(8,128)} %get-tuple-element.82) | copy-start | bytes 6291460
  48.9 6.6 %copy-start.5 = (bf16[18,65,512]{2,1,0:T(8,128)(2,1)}, bf16[18,65,512]{2,1,0:T(8,128)(2,1)S(1)}, u32[]{:S(2)}) copy-start(bf16[18,65,512]{2,1,0:T(8,128)(2,1)S(1)} %get-tuple-element.70) | copy-start | bytes 3594244
  48.9 6.6 %copy-start.7 = (bf16[18,65,512]{2,1,0:T(8,128)(2,1)}, bf16[18,65,512]{2,1,0:T(8,128)(2,1)S(1)}, u32[]{:S(2)}) copy-start(bf16[18,65,512]{2,1,0:T(8,128)(2,1)S(1)} %get-tuple-element.71) | copy-start | bytes 3594244
  49.0 6.6 %copy-start.42 = (s32[16]{0:T(128)S(1)}, s32[16]{0:T(128)}, u32[]{:S(2)}) copy-start(s32[16]{0:T(128)} %copy-done.41) | copy-start | bytes 196
  49.0 10.2 %copy-start.45 = (f32[512]{0:T(512)S(1)}, f32[512]{0:T(512)}, u32[]{:S(2)}) copy-start(f32[512]{0:T(512)} %param.24) | copy-start | bytes 6148
  59.1 3.4 %copy-start.28 = (bf16[512,512]{1,0:T(8,128)(2,1)S(1)}, bf16[512,512]{1,0:T(8,128)(2,1)}, u32[]{:S(2)}) copy-start(bf16[512,512]{1,0:T(8,128)(2,1)} %param.25) | copy-start | bytes 1572868
  62.5 1.3 copy-start.22
  62.5 1.6 copy-start.11
  67.2 1.9 copy-start.24
  69.0 3.3 %copy-start.15 = (bf16[1024,512]{1,0:T(8,128)(2,1)}, bf16[1024,512]{1,0:T(8,128)(2,1)S(1)}, u32[]{:S(2)}) copy-start(bf16[1024,512]{1,0:T(8,128)(2,1)S(1)} %get-tuple-element.67) | copy-start | bytes 3145732
  69.0 1.6 copy-start.3
  70.6 1.7 copy-start.14
  74.1 3.8 %copy-start.40 = (pred[16]{0:T(512)(128)(4,1)S(1)}, pred[16]{0:T(512)(128)(4,1)}, u32[]{:S(2)}) copy-start(pred[16]{0:T(512)(128)(4,1)} %copy-done.39) | copy-start | bytes 52
  74.1 4.5 %copy-start.26 = (bf16[64,512]{1,0:T(8,128)(2,1)S(1)}, bf16[64,512]{1,0:T(8,128)(2,1)}, u32[]{:S(2)}) copy-start(bf16[64,512]{1,0:T(8,128)(2,1)} %gather_fusion.1) | copy-start | bytes 196612
  77.9 5.2 %copy-start.34 = (f32[16]{0:T(128)S(1)}, f32[16]{0:T(128)}, u32[]{:S(2)}) copy-start(f32[16]{0:T(128)} %copy-done.33) | copy-start | bytes 196
  77.9 5.2 %copy-start.36 = (f32[16]{0:T(128)S(1)}, f32[16]{0:T(128)}, u32[]{:S(2)}) copy-start(f32[16]{0:T(128)} %copy-done.35) | copy-start | bytes 196
  77.9 5.2 %copy-start.38 = (f32[16]{0:T(128)S(1)}, f32[16]{0:T(128)}, u32[]{:S(2)}) copy-start(f32[16]{0:T(128)} %copy-done.37) | copy-start | bytes 196
  78.6 4.6 %copy-start.6 = (bf16[18,65,512]{2,1,0:T(8,128)(2,1)S(1)}, bf16[18,65,512]{2,1,0:T(8,128)(2,1)}, u32[]{:S(2)}) copy-start(bf16[18,65,512]{2,1,0:T(8,128)(2,1)} %copy-done.5) | copy-start | bytes 3594244
  78.6 4.6 %copy-start.8 = (bf16[18,65,512]{2,1,0:T(8,128)(2,1)S(1)}, bf16[18,65,512]{2,1,0:T(8,128)(2,1)}, u32[]{:S(2)}) copy-start(bf16[18,65,512]{2,1,0:T(8,128)(2,1)} %copy-done.7) | copy-start | bytes 3594244
  80.2 22.7 %collective-permute-start.5 = (bf16[2,1,64,512]{3,2,1,0:T(8,128)(2,1)S(1)}, bf16[2,1,64,512]{3,2,1,0:T(8,128)(2,1)S(1)}, u32[]{:S(2)}, u32[]{:S(2)}) collective-permute-start(bf16[2,1,64,512]{3,2,1,0:T(8,128)(2,1)S(1)} %get-tuple-element.69), channel_id=1, source_target_pairs={{8,0},{16,8},{24,16},{0,24},{9,1},{17,9},{25,17},{1,25},{10,2},{18... | collective-permute-start | bytes 393224 | tf_op jit(solution)/shard_map/ppermute | solution.py:19
  83.2 19.7 %collective-permute-start.4 = (bf16[2,1,64,512]{3,2,1,0:T(8,128)(2,1)S(1)}, bf16[2,1,64,512]{3,2,1,0:T(8,128)(2,1)S(1)}, u32[]{:S(2)}, u32[]{:S(2)}) collective-permute-start(bf16[2,1,64,512]{3,2,1,0:T(8,128)(2,1)S(1)} %get-tuple-element.68), channel_id=1, source_target_pairs={{0,8},{8,16},{16,24},{24,0},{1,9},{9,17},{17,25},{25,1},{2,10},{10... | collective-permute-start | bytes 393224 | tf_op jit(solution)/shard_map/ppermute | solution.py:17
  91.0 3.0 copy-start.43
  97.4 3.7 %copy-start.23 = (bf16[1024,512]{1,0:T(8,128)(2,1)S(1)}, bf16[1024,512]{1,0:T(8,128)(2,1)}, u32[]{:S(2)}) copy-start(bf16[1024,512]{1,0:T(8,128)(2,1)} %copy-done.22) | copy-start | bytes 3145732
  97.4 3.7 %copy-start.25 = (bf16[1024,512]{1,0:T(8,128)(2,1)S(1)}, bf16[1024,512]{1,0:T(8,128)(2,1)}, u32[]{:S(2)}) copy-start(bf16[1024,512]{1,0:T(8,128)(2,1)} %copy-done.24) | copy-start | bytes 3145732
  101.2 1.8 copy-start.13
  103.1 5.3 %collective-permute-start.7 = (bf16[2,18,1,512]{3,2,1,0:T(2,128)(2,1)S(1)}, bf16[2,18,1,512]{3,2,1,0:T(2,128)(2,1)S(1)}, u32[]{:S(2)}, u32[]{:S(2)}) collective-permute-start(bf16[2,18,1,512]{3,2,1,0:T(2,128)(2,1)S(1)} %get-tuple-element.63), channel_id=1, source_target_pairs={{1,0},{2,1},{3,2},{4,3},{5,4},{6,5},{7,6},{0,7},{9,8},{10,9},{11,1... | collective-permute-start | bytes 110600 | tf_op jit(solution)/shard_map/ppermute | solution.py:19
  106.3 5.6 %collective-permute-start.6 = (bf16[2,18,1,512]{3,2,1,0:T(2,128)(2,1)S(1)}, bf16[2,18,1,512]{3,2,1,0:T(2,128)(2,1)S(1)}, u32[]{:S(2)}, u32[]{:S(2)}) collective-permute-start(bf16[2,18,1,512]{3,2,1,0:T(2,128)(2,1)S(1)} %get-tuple-element.62), channel_id=1, source_target_pairs={{0,1},{1,2},{2,3},{3,4},{4,5},{5,6},{6,7},{7,0},{8,9},{9,10},{10,1... | collective-permute-start | bytes 110600 | tf_op jit(solution)/shard_map/ppermute | solution.py:17
  107.4 188.9 %all-reduce.4.cloned.1.call-start = ((), (), s32[]{:S(2)}) async-start(), calls=%async_computation.2 | async-start | bytes 10485760 | tf_op jit(solution)/shard_map/psum | solution.py:171
  122.3 20.6 %copy-start.4 = (bf16[16,64,512]{2,1,0:T(8,128)(2,1)S(1)}, bf16[16,64,512]{2,1,0:T(8,128)(2,1)}, u32[]{:S(2)}) copy-start(bf16[16,64,512]{2,1,0:T(8,128)(2,1)} %param.17) | copy-start | bytes 3145732
  146.2 0.7 copy-start.44
  146.2 41.0 %copy-start.16 = (bf16[1024,512]{1,0:T(8,128)(2,1)S(1)}, bf16[1024,512]{1,0:T(8,128)(2,1)}, u32[]{:S(2)}) copy-start(bf16[1024,512]{1,0:T(8,128)(2,1)} %copy-done.15) | copy-start | bytes 3145732
  146.2 41.7 %copy-start.19 = (bf16[512,512]{1,0:T(8,128)(2,1)S(1)}, bf16[512,512]{1,0:T(8,128)(2,1)}, u32[]{:S(2)}) copy-start(bf16[512,512]{1,0:T(8,128)(2,1)} %param.20) | copy-start | bytes 1572868
  187.9 2.5 copy-start.10
  187.9 2.5 copy-start.12
  187.9 2.6 copy-start.27
  298.9 2.7 copy-start.21
  303.1 2.7 copy-start.20
  305.8 1.4 copy-start.1
Sparse Core Ops, SparseCore 0:
  107.5 31.5 reduce-scatter.1
  147.8 148.3 all-reduce.3
where the time goes:
time: 315 us; the launch traced here: 314 us
  waiting for transfers between devices  127 us (40%)
  other arithmetic  55.7 us (18%)
  blocking collectives  52.8 us (17%)
  matrix products  32.2 us (10%)
  local copies, waits for them, and re-layouts  18 us (6%)
  between operations  14.7 us (5%)
  starting transfers between devices  13.8 us (4%)
    psum x1, waiting for transfers between devices, on_device(): lax.psum((send_grad, recv_grad, edge_bias_grad, self_grad, agg_grad, node...  104 us
    psum x1, blocking collectives, on_device(): lax.psum((send_grad, recv_grad, edge_bias_grad, self_grad, agg_grad, node...  38.5 us
    dot_general x15, matrix products, matmul(): return jnp.dot(left, right, preferred_element_type=jnp.float32)  30.6 us
    reduce_scatter x1, waiting for transfers between devices, on_device(): lax.psum_scatter(flat_grads.astype(jnp.bfloat16), 'lon', scatter_dimensio...  16.9 us
    all_gather x1, blocking collectives, on_device(): lax.all_gather(coarse_send, 'lon', axis=0, tiled=True)  14.2 us
    ppermute x4, starting transfers between devices, extended(): lax.ppermute(head, axis, [((i + 1) % count, i) for i in range(count)])  13.3 us
    unnamed x99, local copies, waits for them, and re-layouts  8.66 us
    reduce_sum x1, other arithmetic, on_device(): edge_bias_grad = edge_bias_grad + jnp.sum(slope_in, axis=(0, 1))  7.72 us
  transfers between devices with their start and end apart: 10, of which 5 were waited for; matrix products, arithmetic and copies ran while one was open for 16% of the time, Pallas kernels for 0%

commit v1 on v0

--- a/solution.py
+++ b/solution.py
@@ -30,6 +30,38 @@
 
 def matmul(left, right):
     return jnp.dot(left, right, preferred_element_type=jnp.float32)
+
+
+def exchanged(values, axis, bit):
+    count = lax.axis_size(axis)
+    return lax.ppermute(values, axis, [(i, i ^ bit) for i in range(count)])
+
+
+def scatter_sum(values, axis, place, steps):
+    parts = values.reshape(len(steps) + 1, -1, values.shape[-1])
+    total = parts[place].astype(jnp.float32)
+    for rank, step in enumerate(steps):
+        total = total + exchanged(parts[place ^ (rank + 1)], axis, step).astype(jnp.float32)
+    return total.astype(jnp.bfloat16)
+
+
+def gather_all(values, axis, place, steps):
+    parts = jnp.stack([values] + [exchanged(values, axis, step) for step in steps])
+    return parts[place ^ jnp.arange(len(steps) + 1)].reshape(-1, values.shape[-1])
+
+
+def sum_everywhere(values):
+    lat_steps = range(1, lax.axis_size("lat"))
+    chip_steps = range(2, lax.axis_size("lon"), 2)
+    lat_place = lax.axis_index("lat")
+    core_place = lax.axis_index("lon") % 2
+    chip_place = lax.axis_index("lon") // 2
+    values = scatter_sum(values, "lon", core_place, (1,))
+    values = scatter_sum(values, "lat", lat_place, lat_steps)
+    values = scatter_sum(values, "lon", chip_place, chip_steps)
+    values = gather_all(values, "lon", chip_place, chip_steps)
+    values = gather_all(values, "lat", lat_place, lat_steps)
+    return gather_all(values, "lon", core_place, (1,))
 
 
 def on_device(
@@ -168,30 +200,25 @@
         + matmul(d_recv_b, w_recv.T)
         + matmul(d_send_b, w_send.T)
     ).astype(jnp.bfloat16)
-    summed = lax.psum(
-        (
-            send_grad,
-            recv_grad,
-            edge_bias_grad,
-            self_grad,
-            agg_grad,
-            node_bias_grad,
-            out_grad,
-            gain_grad,
-        ),
-        ("lat", "lon"),
-    )
+    vectors = jnp.stack([edge_bias_grad, node_bias_grad, gain_grad])
+    stacked = jnp.concatenate([send_grad, recv_grad, self_grad, agg_grad, out_grad, vectors])
+    multiple = 8 * lat_count * lon_count
+    padding = -stacked.shape[0] % multiple
+    stacked = jnp.pad(stacked.astype(jnp.bfloat16), ((0, padding), (0, 0)))
+    summed = grad_scale * sum_everywhere(stacked).astype(jnp.float32)
+    matrices = summed[: 5 * depth].reshape(5, depth, depth)
+    rows = summed[5 * depth :]
     return (
         new_flat.reshape(patch_rows, patch_cols, depth),
         grad_flat.reshape(patch_rows, patch_cols, depth),
-        grad_scale * summed[0],
-        grad_scale * summed[1],
-        grad_scale * summed[2],
-        grad_scale * summed[3],
-        grad_scale * summed[4],
-        grad_scale * summed[5],
-        grad_scale * summed[6],
-        grad_scale * summed[7],
+        matrices[0],
+        matrices[1],
+        rows[0],
+        matrices[2],
+        matrices[3],
+        rows[1],
+        matrices[4],
+        rows[2],
     )
 
 

time: 315 us -> 243 us (0.77)
  waiting for transfers between devices: 127 us -> 59.7 us
  blocking collectives: 52.8 us -> 14.9 us
  local copies, waits for them, and re-layouts: 18 us -> 35.4 us
  starting transfers between devices: 13.8 us -> 29.2 us
  other arithmetic: 55.7 us -> 59.2 us
    psum x1 -> x0, waiting for transfers between devices: 104 us -> none  [on_device(): lax.psum((send_grad, recv_grad, edge_bias_grad, self_grad, agg_grad, node...]
    ppermute x0 -> x14, waiting for transfers between devices: none -> 43.7 us  [exchanged(): return lax.ppermute(values, axis, [(i, i ^ bit) for i in range(count)])]
    psum x1 -> x0, blocking collectives: 38.5 us -> none  [on_device(): lax.psum((send_grad, recv_grad, edge_bias_grad, self_grad, agg_grad, node...]
    ppermute x0 -> x14, starting transfers between devices: none -> 15.2 us  [exchanged(): return lax.ppermute(values, axis, [(i, i ^ bit) for i in range(count)])]
    concatenate x0 -> x1, local copies, waits for them, and re-layouts: none -> 11.2 us  [on_device(): jnp.concatenate([send_grad, recv_grad, self_grad, agg_grad, out_grad, vec...]
    gather x0 -> x3, local copies, waits for them, and re-layouts: none -> 6.47 us  [gather_all(): parts[place ^ jnp.arange(len(steps) + 1)].reshape(-1, values.shape[-1])]
    reduce_scatter x1, waiting for transfers between devices: 16.9 us -> 11.7 us  [on_device(): lax.psum_scatter(flat_grads.astype(jnp.bfloat16), 'lon', scatter_dimensio...]
    unnamed x99 -> x76, local copies, waits for them, and re-layouts: 8.66 us -> 3.82 us
  transfers between devices with their start and end apart: 10 -> 23, of which waited for: 5 -> 14; matrix products, arithmetic and copies ran while one was open for 16% -> 21% of each run, Pallas kernels for 0% -> 0%
where the time goes in v1:
time: 243 us; the launch traced here: 242 us
  waiting for transfers between devices  59.7 us (25%)
  other arithmetic  59.2 us (24%)
  local copies, waits for them, and re-layouts  35.4 us (15%)
  starting transfers between devices  29.2 us (12%)
  matrix products  29.1 us (12%)
  blocking collectives  14.9 us (6%)
  between operations  14.7 us (6%)
    ppermute x14, waiting for transfers between devices, exchanged(): return lax.ppermute(values, axis, [(i, i ^ bit) for i in range(count)])  43.7 us
    dot_general x15, matrix products, matmul(): return jnp.dot(left, right, preferred_element_type=jnp.float32)  27.6 us
    ppermute x14, starting transfers between devices, exchanged(): return lax.ppermute(values, axis, [(i, i ^ bit) for i in range(count)])  15.2 us
    all_gather x1, blocking collectives, on_device(): lax.all_gather(coarse_send, 'lon', axis=0, tiled=True)  14.9 us
    reduce_scatter x1, waiting for transfers between devices, on_device(): lax.psum_scatter(flat_grads.astype(jnp.bfloat16), 'lon', scatter_dimensio...  11.7 us
    concatenate x1, local copies, waits for them, and re-layouts, on_device(): jnp.concatenate([send_grad, recv_grad, self_grad, agg_grad, out_grad, vec...  11.2 us
    ppermute x4, starting transfers between devices, extended(): lax.ppermute(head, axis, [((i + 1) % count, i) for i in range(count)])  9.98 us
    reduce_sum x1, other arithmetic, on_device(): edge_bias_grad = edge_bias_grad + jnp.sum(slope_in, axis=(0, 1))  8.13 us
  transfers between devices with their start and end apart: 23, of which 14 were waited for; matrix products, arithmetic and copies ran while one was open for 21% of the time, Pallas kernels for 0%

profile of v1, /device:TPU:0, one launch (start us, length us, event | category | flops | bytes accessed | tf_op | source)
XLA Modules:
  0.0 242.2 jit_solution(11802568244986913863)
XLA Ops:
  7.3 2.2 convolution_convert_fusion.1
  10.2 2.9 %collective-permute-start.1 = (bf16[1,64,512]{2,1,0:T(8,128)(2,1)}, bf16[1,64,512]{2,1,0:T(8,128)(2,1)S(1)}, u32[]{:S(2)}, u32[]{:S(2)}) collective-permute-start(bf16[1,64,512]{2,1,0:T(8,128)(2,1)} %get-tuple-element.67), channel_id=1, source_target_pairs={{0,8},{8,16},{16,24},{24,0},{1,9},{9,17},{17,25},{25,1},{2,10},{10... | collective-permute-start | bytes 196616 | tf_op jit(solution)/shard_map/ppermute | solution.py:17
  14.6 1.5 fusion.24
  16.8 14.9 %all_gather.3 = bf16[128,512]{1,0:T(8,128)(2,1)S(1)} all-gather(bf16[16,512]{1,0:T(8,128)(2,1)S(1)} %broadcast_select_fusion.2), channel_id=1, replica_groups=mesh['lat'=4,'lon'=8] {'lon'}, dimensions={0}, use_global_device_ids=true | all-gather | bytes 147456 | tf_op jit(solution)/shard_map/all_gather | solution.py:118
  31.6 2.0 fusion.76
  33.7 2.4 fusion.75
  36.1 2.2 gather_fusion.5
  41.9 3.2 %collective-permute-start.2 = (bf16[18,1,512]{2,1,0:T(2,128)(2,1)}, bf16[18,1,512]{2,1,0:T(2,128)(2,1)}, u32[]{:S(2)}, u32[]{:S(2)}) collective-permute-start(bf16[18,1,512]{2,1,0:T(2,128)(2,1)} %get-tuple-element.66), channel_id=1, source_target_pairs={{1,0},{2,1},{3,2},{4,3},{5,4},{6,5},{7,6},{0,7},{9,8},{10,9},{11,1... | collective-permute-start | bytes 55304 | tf_op jit(solution)/shard_map/ppermute | solution.py:19
  45.7 1.5 collective-permute-done.3
  47.2 1.6 maximum_maximum_fusion
  48.9 6.4 %multiply_add_fusion = f32[16,64,512]{2,1,0:T(8,128)} fusion(f32[16,64,512]{2,1,0:T(8,128)S(1)} %bitcast.189, f32[16]{0:T(128)S(1)} %get-tuple-element.81, f32[16]{0:T(128)} %get-tuple-element.82, f32[512]{0:T(512)S(1)} %copy-done.23, f32[16]{0:T(128)S(1)} %copy-done.30, bf16[18,65,512]{2,1,0:T(8,128)(2,1)S(1)} %get-tuple-element.64, ...), kind=kLoop, calls=%fused_computation.76 | loop fusion | flops 28835840 | bytes 9570496 | tf_op jit(solution)/shard_map/add | solution.py:109
  55.2 3.6 %scatter_fusion = f32[1024,512]{1,0:T(8,128)} fusion(f32[1024,512]{1,0:T(8,128)} %bitcast.196, s32[16]{0:T(128)S(1)} %copy-done.35, f32[16,512]{1,0:T(8,128)S(1)} %convolution_bitcast_fusion.1), kind=kCustom, calls=%fused_computation.9 | custom fusion | flops 8192 | bytes 98368 | tf_op jit(solution)/shard_map/scatter-add | solution.py:128
  58.8 3.3 %multiply_convert_fusion = (bf16[1024,512]{1,0:T(8,128)(2,1)S(1)}, f32[1024,512]{1,0:T(8,128)S(1)}) fusion(f32[512]{0:T(512)} %param.24, f32[1024,512]{1,0:T(8,128)} %fusion.76, bf16[512,512]{1,0:T(8,128)(2,1)S(1)} %copy-done, f32[1024,512]{1,0:T(8,128)} %scatter_fusion), kind=kOutput, calls=%fused_computation.73 | convolution fusion | flops 541065216 | bytes 7866368 | tf_op jit(solution)/shard_map/dot_general | solution.py:32
  64.4 2.1 fusion.22
  66.5 1.5 convolution_convert_fusion.2
  68.0 1.3 fusion.73
  69.6 1.5 convolution_convert_fusion.3
  71.1 1.6 fusion.31
  73.5 1.6 convert_element_type.202
  76.8 2.3 collective-permute-start.5
  79.1 2.2 gather_fusion.7
  82.5 8.1 %fusion.63 = (f32[512]{0:T(512)S(1)}, f32[16,64,512]{2,1,0:T(8,128)S(1)}, f32[512]{0:T(512)S(1)}, f32[16,64,512]{2,1,0:T(8,128)S(1)}, f32[512]{0:T(512)S(1)}, /*...) fusion(f32[512]{0:T(512)S(1)} %copy-done.23, ...), kind=kLoop, calls=%fused_computation.195 | loop fusion | flops 40891392 | bytes 21117120 | tf_op jit(solution)/shard_map/reduce_sum | solution.py:174
  90.7 3.0 %add_add_fusion = f32[16,64,512]{2,1,0:T(8,128)} fusion(f32[16,64,512]{2,1,0:T(8,128)S(1)} %get-tuple-element.45, f32[16,64,512]{2,1,0:T(8,128)S(1)} %get-tuple-element.49, f32[16,64,512]{2,1,0:T(8,128)S(1)} %get-tuple-element.51, f32[16,64,512]{2,1,0:T(8,128)S(1)} %get-tuple-element.47, f32[16,64,512]{2,1,0:T(8,128)S(1)} %get-tuple-element.43, ...), kind=kLoop, calls=%fused_computation.64 | loop fusion | flops 2621440 | bytes 14680064 | tf_op jit(solution)/shard_map/add | solution.py:173
  93.7 3.6 %scatter_fusion.1 = f32[1024,512]{1,0:T(8,128)} fusion(f32[1024,512]{1,0:T(8,128)} %bitcast.188, s32[16]{0:T(128)S(1)} %copy-done.36, f32[16,512]{1,0:T(8,128)S(1)} %convolution_bitcast_fusion), kind=kCustom, calls=%fused_computation.10 | custom fusion | flops 8192 | bytes 98368 | tf_op jit(solution)/shard_map/scatter-add | solution.py:193
  97.2 3.1 %fusion.30 = bf16[512,512]{1,0:T(8,128)(2,1)} fusion(bf16[1024,512]{1,0:T(8,128)(2,1)S(1)} %bitcast.181, f32[1024,512]{1,0:T(8,128)} %scatter_fusion.1), kind=kOutput, calls=%fused_computation.102 | convolution fusion | flops 537657344 | bytes 3670016 | tf_op jit(solution)/shard_map/dot_general | solution.py:32
  100.4 1.0 convolution_convert_fusion.7
  101.5 1.2 pad_maximum_fusion.11
  102.8 3.5 %collective-permute-start.7 = (bf16[2,18,1,512]{3,2,1,0:T(2,128)(2,1)S(1)}, bf16[2,18,1,512]{3,2,1,0:T(2,128)(2,1)S(1)}, u32[]{:S(2)}, u32[]{:S(2)}) collective-permute-start(bf16[2,18,1,512]{3,2,1,0:T(2,128)(2,1)S(1)} %get-tuple-element.53), channel_id=1, source_target_pairs={{1,0},{2,1},{3,2},{4,3},{5,4},{6,5},{7,6},{0,7},{9,8},{10,9},{11,1... | collective-permute-start | bytes 110600 | tf_op jit(solution)/shard_map/ppermute | solution.py:19
  106.3 2.8 %collective-permute-done.6 = bf16[2,18,1,512]{3,2,1,0:T(2,128)(2,1)S(1)} collective-permute-done((bf16[2,18,1,512]{3,2,1,0:T(2,128)(2,1)S(1)}, bf16[2,18,1,512]{3,2,1,0:T(2,128)(2,1)S(1)}, u32[]{:S(2)}, u32[]{:S(2)}) %collective-permute-start.6) | collective-permute-done | bytes 36896 | tf_op jit(solution)/shard_map/ppermute | solution.py:17
  109.1 2.7 %maximum_convert_fusion = f32[2,18,66,512]{3,2,1,0:T(8,128)S(1)} fusion(bf16[2,18,1,512]{3,2,1,0:T(2,128)(2,1)S(1)} %collective-permute-done.7, bf16[2,1,64,512]{3,2,1,0:T(8,128)(2,1)S(1)} %collective-permute-done.5, bf16[1,16,64,512]{3,2,1,0:T(8,128)(2,1)} %bitcast.192, bf16[1,16,64,512]{3,2,1,0:T(8,128)(2,1)} %bitcast.185, ...), kind=kLoop, calls=%fused_computation.24 | loop fusion | flops 14598144 | bytes 7299072 | tf_op jit(solution)/shard_map/convert_element_type | solution.py:160
  112.4 7.3 %fusion.8 = f32[16,64,512]{2,1,0:T(8,128)} fusion(f32[18,66,512]{2,1,0:T(8,128)S(1)} %get-tuple-element.41, f32[18,66,512]{2,1,0:T(8,128)S(1)} %get-tuple-element.40, f32[16]{0:T(128)S(1)} %copy-done.28, f32[16]{0:T(128)S(1)} %copy-done.29, f32[512]{0:T(512)S(1)} %copy-done.23, f32[16]{0:T(128)S(1)} %copy-done.31, ...), kind=kLoop, calls=%fused_computation.33 | loop fusion | flops 37748736 | bytes 28313792 | tf_op jit(solution)/shard_map/add | solution.py:181
  119.7 11.7 %reduce-scatter.2.cloned.1.call-done = bf16[16,512]{1,0:T(8,128)(2,1)} async-done(((bf16[128,512]{1,0:T(8,128)(2,1)}), bf16[16,512]{1,0:T(8,128)(2,1)}) %reduce-scatter.2.cloned.1.call-update) | async-done | bytes 16400 | tf_op jit(solution)/shard_map/reduce_scatter | solution.py:190
  131.4 3.8 %scatter_custom_fusion.2 = f32[1024,512]{1,0:T(8,128)} fusion(f32[1024,512]{1,0:T(8,128)} %bitcast.190, s32[16]{0:T(128)S(1)} %copy-done.36, bf16[16,512]{1,0:T(8,128)(2,1)} %reduce-scatter.2.cloned.1.call-done), kind=kCustom, calls=%fused_computation.152 | custom fusion | flops 16384 | bytes 2113536 | tf_op jit(solution)/shard_map/scatter-add | solution.py:194
  135.2 2.4 %fusion.29 = bf16[512,512]{1,0:T(8,128)(2,1)S(1)} fusion(bf16[1024,512]{1,0:T(8,128)(2,1)S(1)} %bitcast.182, f32[1024,512]{1,0:T(8,128)} %scatter_custom_fusion.2), kind=kOutput, calls=%fused_computation.101 | convolution fusion | flops 537657344 | bytes 3670016 | tf_op jit(solution)/shard_map/dot_general | solution.py:32
  137.6 11.2 %concatenate.35 = bf16[2563,512]{1,0:T(8,128)(2,1)} concatenate(bf16[512,512]{1,0:T(8,128)(2,1)S(1)} %fusion.29, bf16[512,512]{1,0:T(8,128)(2,1)S(1)} %copy-done.20, bf16[512,512]{1,0:T(8,128)(2,1)} %fusion.31, bf16[512,512]{1,0:T(8,128)(2,1)S(1)} %copy-done.19, bf16[512,512]{1,0:T(8,128)(2,1)} %convolution_convert_fusion.2, bf16[1,512]{1,0:T(2,128)(2,1)S(1)} %reshape.367, ...), dimensions={0} | concatenate | bytes 5249024 | tf_op jit(solution)/shard_map/concatenate | solution.py:204
  148.8 1.9 pad.4
  150.8 1.6 copy-done.12
  152.6 3.3 %collective-permute-done.8 = bf16[1408,512]{1,0:T(8,128)(2,1)} collective-permute-done((bf16[1408,512]{1,0:T(8,128)(2,1)S(1)}, bf16[1408,512]{1,0:T(8,128)(2,1)}, u32[]{:S(2)}, u32[]{:S(2)}) %collective-permute-start.8) | collective-permute-done | bytes 1441824 | tf_op jit(solution)/shard_map/ppermute | solution.py:37
  155.9 2.2 fusion
  158.2 1.6 collective-permute-start.9
  159.7 1.5 collective-permute-start.11
  161.7 7.9 %collective-permute-done.9 = bf16[352,512]{1,0:T(8,128)(2,1)} collective-permute-done((bf16[352,512]{1,0:T(8,128)(2,1)S(1)}, bf16[352,512]{1,0:T(8,128)(2,1)}, u32[]{:S(2)}, u32[]{:S(2)}) %collective-permute-start.9) | collective-permute-done | bytes 360480 | tf_op jit(solution)/shard_map/ppermute | solution.py:37
  169.6 8.0 %collective-permute-done.11 = bf16[352,512]{1,0:T(8,128)(2,1)} collective-permute-done((bf16[352,512]{1,0:T(8,128)(2,1)S(1)}, bf16[352,512]{1,0:T(8,128)(2,1)}, u32[]{:S(2)}, u32[]{:S(2)}) %collective-permute-start.11) | collective-permute-done | bytes 360480 | tf_op jit(solution)/shard_map/ppermute | solution.py:37
  177.6 1.4 collective-permute-done.10
  178.9 1.4 fusion.34
  181.2 2.7 %collective-permute-start.13 = (bf16[88,512]{1,0:T(8,128)(2,1)S(1)}, bf16[88,512]{1,0:T(8,128)(2,1)S(1)}, u32[]{:S(2)}, u32[]{:S(2)}) collective-permute-start(bf16[88,512]{1,0:T(8,128)(2,1)S(1)} %get-tuple-element.71), channel_id=1, source_target_pairs={{0,4},{1,5},{2,6},{3,7},{4,0},{5,1},{6,2},{7,3},{8,12},{9,13},{10,... | collective-permute-start | bytes 270344 | tf_op jit(solution)/shard_map/ppermute | solution.py:37
  183.9 1.7 collective-permute-done.12
  185.6 1.2 collective-permute-done.14
  186.8 3.9 %collective-permute-done.13 = bf16[88,512]{1,0:T(8,128)(2,1)S(1)} collective-permute-done((bf16[88,512]{1,0:T(8,128)(2,1)S(1)}, bf16[88,512]{1,0:T(8,128)(2,1)S(1)}, u32[]{:S(2)}, u32[]{:S(2)}) %collective-permute-start.13) | collective-permute-done | bytes 90144 | tf_op jit(solution)/shard_map/ppermute | solution.py:37
  190.8 1.8 collective-permute-start.17
  192.6 2.7 %collective-permute-start.15 = (bf16[88,512]{1,0:T(8,128)(2,1)S(1)}, bf16[88,512]{1,0:T(8,128)(2,1)S(1)}, u32[]{:S(2)}, u32[]{:S(2)}) collective-permute-start(bf16[88,512]{1,0:T(8,128)(2,1)S(1)} %fusion.44), channel_id=1, source_target_pairs={{0,2},{1,3},{2,0},{3,1},{4,6},{5,7},{6,4},{7,5},{8,10},{9,11},{10,... | collective-permute-start | bytes 270344 | tf_op jit(solution)/shard_map/ppermute | solution.py:37
  195.3 2.1 collective-permute-done.17
  197.3 1.9 collective-permute-done.16
  199.8 1.5 collective-permute-start.20
  201.3 1.4 collective-permute-start.19
  203.4 8.7 %collective-permute-done.20 = bf16[352,512]{1,0:T(8,128)(2,1)S(1)} collective-permute-done((bf16[352,512]{1,0:T(8,128)(2,1)S(1)}, bf16[352,512]{1,0:T(8,128)(2,1)S(1)}, u32[]{:S(2)}, u32[]{:S(2)}) %collective-permute-start.20) | collective-permute-done | bytes 360480 | tf_op jit(solution)/shard_map/ppermute | solution.py:37
  212.2 3.7 %collective-permute-done.19 = bf16[352,512]{1,0:T(8,128)(2,1)S(1)} collective-permute-done((bf16[352,512]{1,0:T(8,128)(2,1)S(1)}, bf16[352,512]{1,0:T(8,128)(2,1)S(1)}, u32[]{:S(2)}, u32[]{:S(2)}) %collective-permute-start.19) | collective-permute-done | bytes 360480 | tf_op jit(solution)/shard_map/ppermute | solution.py:37
  216.0 1.8 gather_fusion.2
  217.8 2.1 fusion.77
  222.0 1.8 fusion.27
  223.8 1.8 pad_maximum_fusion
  225.6 4.1 %gather_fusion.3 = bf16[2,1408,512]{2,1,0:T(8,128)(2,1)} fusion(bf16[2,1408,512]{2,1,0:T(8,128)(2,1)} %pad_maximum_fusion, s32[1024]{0:T(1024)S(1)} %pad_clamp_fusion), kind=kCustom, calls=%fused_computation.7 | custom fusion | bytes 5767176 | tf_op jit(solution)/shard_map/gather | solution.py:50
  229.7 2.6 %convert_multiply_fusion = f32[2,1408,512]{2,1,0:T(8,128)S(1)} fusion(bf16[2,1408,512]{2,1,0:T(8,128)(2,1)} %gather_fusion.3), kind=kLoop, calls=%fused_computation.12 | loop fusion | flops 2883584 | bytes 8650752 | tf_op jit(solution)/shard_map/mul | solution.py:208
  233.0 2.4 fusion.72
  (154 shorter events, 19.8 us)
Async XLA Ops:
  7.2 51.6 %copy-start = (bf16[512,512]{1,0:T(8,128)(2,1)S(1)}, bf16[512,512]{1,0:T(8,128)(2,1)}, u32[]{:S(2)}) copy-start(bf16[512,512]{1,0:T(8,128)(2,1)} %param.23) | copy-start | bytes 1572868
  7.2 6.9 %copy-start.37 = (s32[1,1,16]{2,1,0:T(1,128)S(1)}, s32[1,1,16]{2,1,0:T(1,128)}, u32[]{:S(2)}) copy-start(s32[1,1,16]{2,1,0:T(1,128)} %param.27) | copy-start | bytes 196
  7.2 6.9 %copy-start.24 = (s32[1,1,8,8]{3,2,1,0:T(8,128)S(1)}, s32[1,1,8,8]{3,2,1,0:T(8,128)}, u32[]{:S(2)}) copy-start(s32[1,1,8,8]{3,2,1,0:T(8,128)} %param.28) | copy-start | bytes 772
  7.2 6.9 %copy-start.25 = (s32[1,1,8,8]{3,2,1,0:T(8,128)S(1)}, s32[1,1,8,8]{3,2,1,0:T(8,128)}, u32[]{:S(2)}) copy-start(s32[1,1,8,8]{3,2,1,0:T(8,128)} %param.29) | copy-start | bytes 772
  7.2 7.4 %copy-start.26 = (f32[512]{0:T(512)S(1)}, f32[512]{0:T(512)}, u32[]{:S(2)}) copy-start(f32[512]{0:T(512)} %param.26) | copy-start | bytes 6148
  7.2 124.1 %reduce-scatter.2.cloned.1.call-start = ((), (), s32[]{:S(2)}) async-start(), calls=%async_computation.1 | async-start | bytes 147456 | tf_op jit(solution)/shard_map/reduce_scatter | solution.py:190
  7.3 24.4 %copy-start.2 = (bf16[16,64,512]{2,1,0:T(8,128)(2,1)S(1)}, bf16[16,64,512]{2,1,0:T(8,128)(2,1)}, u32[]{:S(2)}) copy-start(bf16[16,64,512]{2,1,0:T(8,128)(2,1)} %param.17) | copy-start | bytes 3145732
  7.3 24.4 %copy-start.16 = (bf16[512,512]{1,0:T(8,128)(2,1)S(1)}, bf16[512,512]{1,0:T(8,128)(2,1)}, u32[]{:S(2)}) copy-start(bf16[512,512]{1,0:T(8,128)(2,1)} %param.22) | copy-start | bytes 1572868
  10.2 30.7 %collective-permute-start.1 = (bf16[1,64,512]{2,1,0:T(8,128)(2,1)}, bf16[1,64,512]{2,1,0:T(8,128)(2,1)S(1)}, u32[]{:S(2)}, u32[]{:S(2)}) collective-permute-start(bf16[1,64,512]{2,1,0:T(8,128)(2,1)} %get-tuple-element.67), channel_id=1, source_target_pairs={{0,8},{8,16},{16,24},{24,0},{1,9},{9,17},{17,25},{25,1},{2,10},{10... | collective-permute-start | bytes 196616 | tf_op jit(solution)/shard_map/ppermute | solution.py:17
  13.1 27.8 %collective-permute-start = (bf16[1,64,512]{2,1,0:T(8,128)(2,1)}, bf16[1,64,512]{2,1,0:T(8,128)(2,1)S(1)}, u32[]{:S(2)}, u32[]{:S(2)}) collective-permute-start(bf16[1,64,512]{2,1,0:T(8,128)(2,1)} %get-tuple-element.68), channel_id=1, source_target_pairs={{8,0},{16,8},{24,16},{0,24},{9,1},{17,9},{25,17},{1,25},{10,2},{18... | collective-permute-start | bytes 196616 | tf_op jit(solution)/shard_map/ppermute | solution.py:19
  14.1 0.5 copy-start.34
  14.1 24.2 %copy-start.32 = (pred[16]{0:T(512)(128)(4,1)}, pred[16]{0:T(512)(128)(4,1)S(1)}, u32[]{:S(2)}) copy-start(pred[16]{0:T(512)(128)(4,1)S(1)} %compare_and_fusion.2) | copy-start | bytes 52
  16.7 17.0 %copy-start.17 = (bf16[512,512]{1,0:T(8,128)(2,1)S(1)}, bf16[512,512]{1,0:T(8,128)(2,1)}, u32[]{:S(2)}) copy-start(bf16[512,512]{1,0:T(8,128)(2,1)} %param.20) | copy-start | bytes 1572868
  36.0 3.9 %copy-start.23 = (f32[512]{0:T(512)S(1)}, f32[512]{0:T(512)}, u32[]{:S(2)}) copy-start(f32[512]{0:T(512)} %param.21) | copy-start | bytes 6148
  40.9 8.0 %copy-start.27 = (f32[16]{0:T(128)}, f32[16]{0:T(128)S(1)}, u32[]{:S(2)}) copy-start(f32[16]{0:T(128)S(1)} %get-tuple-element.81) | copy-start | bytes 196
  41.6 5.6 %collective-permute-start.3 = (bf16[18,1,512]{2,1,0:T(2,128)(2,1)}, bf16[18,1,512]{2,1,0:T(2,128)(2,1)}, u32[]{:S(2)}, u32[]{:S(2)}) collective-permute-start(bf16[18,1,512]{2,1,0:T(2,128)(2,1)} %get-tuple-element.65), channel_id=1, source_target_pairs={{0,1},{1,2},{2,3},{3,4},{4,5},{5,6},{6,7},{7,0},{8,9},{9,10},{10,1... | collective-permute-start | bytes 55304 | tf_op jit(solution)/shard_map/ppermute | solution.py:17
  41.9 5.3 %collective-permute-start.2 = (bf16[18,1,512]{2,1,0:T(2,128)(2,1)}, bf16[18,1,512]{2,1,0:T(2,128)(2,1)}, u32[]{:S(2)}, u32[]{:S(2)}) collective-permute-start(bf16[18,1,512]{2,1,0:T(2,128)(2,1)} %get-tuple-element.66), channel_id=1, source_target_pairs={{1,0},{2,1},{3,2},{4,3},{5,4},{6,5},{7,6},{0,7},{9,8},{10,9},{11,1... | collective-permute-start | bytes 55304 | tf_op jit(solution)/shard_map/ppermute | solution.py:19
  45.7 3.1 %copy-start.30 = (f32[16]{0:T(128)S(1)}, f32[16]{0:T(128)}, u32[]{:S(2)}) copy-start(f32[16]{0:T(128)} %and_convert_fusion.2) | copy-start | bytes 196
  45.7 3.1 %copy-start.7 = (f32[1024,512]{1,0:T(8,128)S(1)}, f32[1024,512]{1,0:T(8,128)}, u32[]{:S(2)}) copy-start(f32[1024,512]{1,0:T(8,128)} %get-tuple-element.78) | copy-start | bytes 6291460
  48.8 6.4 %copy-start.4 = (bf16[18,65,512]{2,1,0:T(8,128)(2,1)}, bf16[18,65,512]{2,1,0:T(8,128)(2,1)S(1)}, u32[]{:S(2)}) copy-start(bf16[18,65,512]{2,1,0:T(8,128)(2,1)S(1)} %get-tuple-element.63) | copy-start | bytes 3594244
  48.8 6.4 %copy-start.5 = (bf16[18,65,512]{2,1,0:T(8,128)(2,1)}, bf16[18,65,512]{2,1,0:T(8,128)(2,1)S(1)}, u32[]{:S(2)}) copy-start(bf16[18,65,512]{2,1,0:T(8,128)(2,1)S(1)} %get-tuple-element.64) | copy-start | bytes 3594244
  48.8 6.4 %copy-start.35 = (s32[16]{0:T(128)S(1)}, s32[16]{0:T(128)}, u32[]{:S(2)}) copy-start(s32[16]{0:T(128)} %copy-done.34) | copy-start | bytes 196
  58.8 3.3 %copy-start.22 = (bf16[512,512]{1,0:T(8,128)(2,1)S(1)}, bf16[512,512]{1,0:T(8,128)(2,1)}, u32[]{:S(2)}) copy-start(bf16[512,512]{1,0:T(8,128)(2,1)} %param.25) | copy-start | bytes 1572868
  62.2 1.2 copy-start.9
  68.0 1.6 copy-start.13
  69.3 3.4 %copy-start.15 = (bf16[1024,512]{1,0:T(8,128)(2,1)}, bf16[1024,512]{1,0:T(8,128)(2,1)S(1)}, u32[]{:S(2)}) copy-start(bf16[1024,512]{1,0:T(8,128)(2,1)S(1)} %get-tuple-element.57) | copy-start | bytes 3145732
  73.4 2.8 %copy-start.3 = (bf16[1024,512]{1,0:T(8,128)(2,1)}, bf16[1024,512]{1,0:T(8,128)(2,1)S(1)}, u32[]{:S(2)}) copy-start(bf16[1024,512]{1,0:T(8,128)(2,1)S(1)} %convolution_convert_fusion) | copy-start | bytes 3145732
  73.5 2.0 copy-start.11
  75.1 6.2 %copy-start.33 = (pred[16]{0:T(512)(128)(4,1)S(1)}, pred[16]{0:T(512)(128)(4,1)}, u32[]{:S(2)}) copy-start(pred[16]{0:T(512)(128)(4,1)} %copy-done.32) | copy-start | bytes 52
  75.5 7.0 %copy-start.28 = (f32[16]{0:T(128)S(1)}, f32[16]{0:T(128)}, u32[]{:S(2)}) copy-start(f32[16]{0:T(128)} %copy-done.27) | copy-start | bytes 196
  75.5 7.0 %copy-start.29 = (f32[16]{0:T(128)S(1)}, f32[16]{0:T(128)}, u32[]{:S(2)}) copy-start(f32[16]{0:T(128)} %get-tuple-element.82) | copy-start | bytes 196
  76.2 25.3 %collective-permute-start.4 = (bf16[2,1,64,512]{3,2,1,0:T(8,128)(2,1)}, bf16[2,1,64,512]{3,2,1,0:T(8,128)(2,1)S(1)}, u32[]{:S(2)}, u32[]{:S(2)}) collective-permute-start(bf16[2,1,64,512]{3,2,1,0:T(8,128)(2,1)} %get-tuple-element.58), channel_id=1, source_target_pairs={{0,8},{8,16},{16,24},{24,0},{1,9},{9,17},{17,25},{25,1},{2,10},{10... | collective-permute-start | bytes 393224 | tf_op jit(solution)/shard_map/ppermute | solution.py:17
  76.8 24.6 %collective-permute-start.5 = (bf16[2,1,64,512]{3,2,1,0:T(8,128)(2,1)}, bf16[2,1,64,512]{3,2,1,0:T(8,128)(2,1)S(1)}, u32[]{:S(2)}, u32[]{:S(2)}) collective-permute-start(bf16[2,1,64,512]{3,2,1,0:T(8,128)(2,1)} %get-tuple-element.59), channel_id=1, source_target_pairs={{8,0},{16,8},{24,16},{0,24},{9,1},{17,9},{25,17},{1,25},{10,2},{18... | collective-permute-start | bytes 393224 | tf_op jit(solution)/shard_map/ppermute | solution.py:19
  90.6 3.0 %copy-start.36 = (s32[16]{0:T(128)S(1)}, s32[16]{0:T(128)}, u32[]{:S(2)}) copy-start(s32[16]{0:T(128)} %copy-done.34) | copy-start | bytes 196
  102.7 6.4 %collective-permute-start.6 = (bf16[2,18,1,512]{3,2,1,0:T(2,128)(2,1)S(1)}, bf16[2,18,1,512]{3,2,1,0:T(2,128)(2,1)S(1)}, u32[]{:S(2)}, u32[]{:S(2)}) collective-permute-start(bf16[2,18,1,512]{3,2,1,0:T(2,128)(2,1)S(1)} %get-tuple-element.52), channel_id=1, source_target_pairs={{0,1},{1,2},{2,3},{3,4},{4,5},{5,6},{6,7},{7,0},{8,9},{9,10},{10,1... | collective-permute-start | bytes 110600 | tf_op jit(solution)/shard_map/ppermute | solution.py:17
  102.8 6.3 %collective-permute-start.7 = (bf16[2,18,1,512]{3,2,1,0:T(2,128)(2,1)S(1)}, bf16[2,18,1,512]{3,2,1,0:T(2,128)(2,1)S(1)}, u32[]{:S(2)}, u32[]{:S(2)}) collective-permute-start(bf16[2,18,1,512]{3,2,1,0:T(2,128)(2,1)S(1)} %get-tuple-element.53), channel_id=1, source_target_pairs={{1,0},{2,1},{3,2},{4,3},{5,4},{6,5},{7,6},{0,7},{9,8},{10,9},{11,1... | collective-permute-start | bytes 110600 | tf_op jit(solution)/shard_map/ppermute | solution.py:19
  111.8 0.7 copy-start.31
  135.2 2.4 %copy-start.19 = (bf16[512,512]{1,0:T(8,128)(2,1)S(1)}, bf16[512,512]{1,0:T(8,128)(2,1)}, u32[]{:S(2)}) copy-start(bf16[512,512]{1,0:T(8,128)(2,1)} %convolution_convert_fusion.3) | copy-start | bytes 1572868
  135.2 2.5 %copy-start.20 = (bf16[512,512]{1,0:T(8,128)(2,1)S(1)}, bf16[512,512]{1,0:T(8,128)(2,1)}, u32[]{:S(2)}) copy-start(bf16[512,512]{1,0:T(8,128)(2,1)} %fusion.30) | copy-start | bytes 1572868
  150.8 1.6 copy-start.12
  152.5 3.4 %collective-permute-start.8 = (bf16[1408,512]{1,0:T(8,128)(2,1)S(1)}, bf16[1408,512]{1,0:T(8,128)(2,1)}, u32[]{:S(2)}, u32[]{:S(2)}) collective-permute-start(bf16[1408,512]{1,0:T(8,128)(2,1)S(1)} %dynamic-slice_bitcast_fusion), channel_id=1, source_target_pairs={{0,1},{1,0},{2,3},{3,2},{4,5},{5,4},{6,7},{7,6},{8,9},{9,8},{10,11... | collective-permute-start | bytes 4325384 | tf_op jit(solution)/shard_map/ppermute | solution.py:37
  158.2 11.4 %collective-permute-start.9 = (bf16[352,512]{1,0:T(8,128)(2,1)S(1)}, bf16[352,512]{1,0:T(8,128)(2,1)}, u32[]{:S(2)}, u32[]{:S(2)}) collective-permute-start(bf16[352,512]{1,0:T(8,128)(2,1)S(1)} %get-tuple-element.60), channel_id=1, source_target_pairs={{0,8},{8,0},{16,24},{24,16},{1,9},{9,1},{17,25},{25,17},{2,10},{10... | collective-permute-start | bytes 1081352 | tf_op jit(solution)/shard_map/ppermute | solution.py:37
  159.7 17.8 %collective-permute-start.11 = (bf16[352,512]{1,0:T(8,128)(2,1)S(1)}, bf16[352,512]{1,0:T(8,128)(2,1)}, u32[]{:S(2)}, u32[]{:S(2)}) collective-permute-start(bf16[352,512]{1,0:T(8,128)(2,1)S(1)} %get-tuple-element.61), channel_id=1, source_target_pairs={{0,24},{8,16},{16,8},{24,0},{1,25},{9,17},{17,9},{25,1},{2,26},{10... | collective-permute-start | bytes 1081352 | tf_op jit(solution)/shard_map/ppermute | solution.py:37
  161.2 17.7 %collective-permute-start.10 = (bf16[352,512]{1,0:T(8,128)(2,1)S(1)}, bf16[352,512]{1,0:T(8,128)(2,1)}, u32[]{:S(2)}, u32[]{:S(2)}) collective-permute-start(bf16[352,512]{1,0:T(8,128)(2,1)S(1)} %get-tuple-element.62), channel_id=1, source_target_pairs={{0,16},{8,24},{16,0},{24,8},{1,17},{9,25},{17,1},{25,9},{2,18},{10... | collective-permute-start | bytes 1081352 | tf_op jit(solution)/shard_map/ppermute | solution.py:37
  180.3 5.3 %collective-permute-start.12 = (bf16[88,512]{1,0:T(8,128)(2,1)S(1)}, bf16[88,512]{1,0:T(8,128)(2,1)S(1)}, u32[]{:S(2)}, u32[]{:S(2)}) collective-permute-start(bf16[88,512]{1,0:T(8,128)(2,1)S(1)} %get-tuple-element.69), channel_id=1, source_target_pairs={{0,2},{1,3},{2,0},{3,1},{4,6},{5,7},{6,4},{7,5},{8,10},{9,11},{10,... | collective-permute-start | bytes 270344 | tf_op jit(solution)/shard_map/ppermute | solution.py:37
  180.4 6.4 %collective-permute-start.14 = (bf16[88,512]{1,0:T(8,128)(2,1)S(1)}, bf16[88,512]{1,0:T(8,128)(2,1)S(1)}, u32[]{:S(2)}, u32[]{:S(2)}) collective-permute-start(bf16[88,512]{1,0:T(8,128)(2,1)S(1)} %get-tuple-element.70), channel_id=1, source_target_pairs={{0,6},{1,7},{2,4},{3,5},{4,2},{5,3},{6,0},{7,1},{8,14},{9,15},{10,... | collective-permute-start | bytes 270344 | tf_op jit(solution)/shard_map/ppermute | solution.py:37
  181.2 9.6 %collective-permute-start.13 = (bf16[88,512]{1,0:T(8,128)(2,1)S(1)}, bf16[88,512]{1,0:T(8,128)(2,1)S(1)}, u32[]{:S(2)}, u32[]{:S(2)}) collective-permute-start(bf16[88,512]{1,0:T(8,128)(2,1)S(1)} %get-tuple-element.71), channel_id=1, source_target_pairs={{0,4},{1,5},{2,6},{3,7},{4,0},{5,1},{6,2},{7,3},{8,12},{9,13},{10,... | collective-permute-start | bytes 270344 | tf_op jit(solution)/shard_map/ppermute | solution.py:37
  190.8 6.5 %collective-permute-start.17 = (bf16[88,512]{1,0:T(8,128)(2,1)S(1)}, bf16[88,512]{1,0:T(8,128)(2,1)S(1)}, u32[]{:S(2)}, u32[]{:S(2)}) collective-permute-start(bf16[88,512]{1,0:T(8,128)(2,1)S(1)} %fusion.44), channel_id=1, source_target_pairs={{0,6},{1,7},{2,4},{3,5},{4,2},{5,3},{6,0},{7,1},{8,14},{9,15},{10,... | collective-permute-start | bytes 270344 | tf_op jit(solution)/shard_map/ppermute | solution.py:37
  192.6 6.6 %collective-permute-start.16 = (bf16[88,512]{1,0:T(8,128)(2,1)S(1)}, bf16[88,512]{1,0:T(8,128)(2,1)S(1)}, u32[]{:S(2)}, u32[]{:S(2)}) collective-permute-start(bf16[88,512]{1,0:T(8,128)(2,1)S(1)} %fusion.44), channel_id=1, source_target_pairs={{0,4},{1,5},{2,6},{3,7},{4,0},{5,1},{6,2},{7,3},{8,12},{9,13},{10,... | collective-permute-start | bytes 270344 | tf_op jit(solution)/shard_map/ppermute | solution.py:37
  192.6 6.6 %collective-permute-start.15 = (bf16[88,512]{1,0:T(8,128)(2,1)S(1)}, bf16[88,512]{1,0:T(8,128)(2,1)S(1)}, u32[]{:S(2)}, u32[]{:S(2)}) collective-permute-start(bf16[88,512]{1,0:T(8,128)(2,1)S(1)} %fusion.44), channel_id=1, source_target_pairs={{0,2},{1,3},{2,0},{3,1},{4,6},{5,7},{6,4},{7,5},{8,10},{9,11},{10,... | collective-permute-start | bytes 270344 | tf_op jit(solution)/shard_map/ppermute | solution.py:37
  199.8 12.3 %collective-permute-start.20 = (bf16[352,512]{1,0:T(8,128)(2,1)S(1)}, bf16[352,512]{1,0:T(8,128)(2,1)S(1)}, u32[]{:S(2)}, u32[]{:S(2)}) collective-permute-start(bf16[352,512]{1,0:T(8,128)(2,1)S(1)} %bitcast.204), channel_id=1, source_target_pairs={{0,24},{8,16},{16,8},{24,0},{1,25},{9,17},{17,9},{25,1},{2,26},{10... | collective-permute-start | bytes 1081352 | tf_op jit(solution)/shard_map/ppermute | solution.py:37
  201.3 14.5 %collective-permute-start.19 = (bf16[352,512]{1,0:T(8,128)(2,1)S(1)}, bf16[352,512]{1,0:T(8,128)(2,1)S(1)}, u32[]{:S(2)}, u32[]{:S(2)}) collective-permute-start(bf16[352,512]{1,0:T(8,128)(2,1)S(1)} %bitcast.205), channel_id=1, source_target_pairs={{0,16},{8,24},{16,0},{24,8},{1,17},{9,25},{17,1},{25,9},{2,18},{10... | collective-permute-start | bytes 1081352 | tf_op jit(solution)/shard_map/ppermute | solution.py:37
  202.7 13.1 %collective-permute-start.18 = (bf16[352,512]{1,0:T(8,128)(2,1)S(1)}, bf16[352,512]{1,0:T(8,128)(2,1)S(1)}, u32[]{:S(2)}, u32[]{:S(2)}) collective-permute-start(bf16[352,512]{1,0:T(8,128)(2,1)S(1)} %bitcast.206), channel_id=1, source_target_pairs={{0,8},{8,0},{16,24},{24,16},{1,9},{9,1},{17,25},{25,17},{2,10},{10... | collective-permute-start | bytes 1081352 | tf_op jit(solution)/shard_map/ppermute | solution.py:37
  217.8 2.1 copy-start.6
  217.8 2.2 copy-start.18
  217.8 6.0 %collective-permute-start.21 = (bf16[1408,512]{1,0:T(8,128)(2,1)}, bf16[1408,512]{1,0:T(8,128)(2,1)S(1)}, u32[]{:S(2)}, u32[]{:S(2)}) collective-permute-start(bf16[1408,512]{1,0:T(8,128)(2,1)} %bitcast.199), channel_id=1, source_target_pairs={{0,1},{1,0},{2,3},{3,2},{4,5},{5,4},{6,7},{7,6},{8,9},{9,8},{10,11... | collective-permute-start | bytes 4325384 | tf_op jit(solution)/shard_map/ppermute | solution.py:37
  220.0 1.6 copy-start.8
  220.0 1.8 copy-start.10
  220.0 2.0 copy-start.21
  222.0 1.8 copy-start.14
  233.0 2.4 %copy-start.1 = (bf16[512,512]{1,0:T(8,128)(2,1)S(1)}, bf16[512,512]{1,0:T(8,128)(2,1)}, u32[]{:S(2)}) copy-start(bf16[512,512]{1,0:T(8,128)(2,1)} %param.23) | copy-start | bytes 1572868
Sparse Core Ops, SparseCore 0:
  101.6 29.7 reduce-scatter.1

commit v2 on v0

v2 whole, which is shorter than its diff:
```python
import functools

import jax
import jax.numpy as jnp
from jax import lax
from jax.experimental import pallas as pl
from jax.experimental.pallas import tpu as pltpu
from jax.sharding import PartitionSpec as P

epsilon = 1e-05
EXACT = lax.Precision.HIGHEST
ABSENT = -1000.0
VMEM_BYTES = 60 * 1024 * 1024


def dot(left, right):
    return jnp.dot(left, right, preferred_element_type=jnp.float32)


def dot_nt(left, right):
    return lax.dot_general(left, right, (((1,), (1,)), ((), ())), preferred_element_type=jnp.float32)


def dot_tn(left, right):
    return lax.dot_general(left, right, (((0,), (0,)), ((), ())), preferred_element_type=jnp.float32)


def dot_exact(left, right):
    return jnp.dot(left, right, preferred_element_type=jnp.float32, precision=EXACT)


def to_bf16(values):
    return values.astype(jnp.bfloat16)


def to_f32(values):
    return values.astype(jnp.float32)


def half_sum_and_slope(half):
    curve = jnp.tanh(half)
    part = half * curve
    return half + part, (1.0 + curve) * (1.0 + half - part)


def eight_rows(values):
    return jnp.sum(values.reshape(-1, 8, values.shape[-1]), axis=0)


def aligned(start, multiple):
    return pl.multiple_of(start, multiple)


def project_kernel(nodes, w_send, w_recv, w_self, edge_bias, node_bias, send, recv_half, own):
    block = nodes[...]
    send[...] = to_bf16(dot(block, w_send[...]))
    recv_half[...] = 0.5 * (dot(block, w_recv[...]) + edge_bias[...])
    own[...] = dot(block, w_self[...]) + node_bias[...]


def project(nodes, w_send, w_recv, w_self, edge_bias, node_bias):
    rows, depth = nodes.shape
    step = 256
    whole = pl.BlockSpec((depth, depth), lambda i: (0, 0))
    vector = pl.BlockSpec((1, depth), lambda i: (0, 0))
    block = pl.BlockSpec((step, depth), lambda i: (i, 0))
    return pl.pallas_call(
        project_kernel,
        grid=(rows // step,),
        in_specs=[block, whole, whole, whole, vector, vector],
        out_specs=[block, block, block],
        out_shape=[
            jax.ShapeDtypeStruct((rows, depth), jnp.bfloat16),
            jax.ShapeDtypeStruct((rows, depth), jnp.float32),
            jax.ShapeDtypeStruct((rows, depth), jnp.float32),
        ],
        cost_estimate=pl.CostEstimate(
            flops=6 * rows * depth * depth, bytes_accessed=8_000_000, transcendentals=0
        ),
        name="project",
    )(nodes, w_send, w_recv, w_self, edge_bias, node_bias)


def update_kernel(
    dims,
    slots,
    facts,
    nodes,
    cotangent,
    send,
    recv_half,
    own,
    above,
    below,
    corner_above,
    corner_below,
    gathered,
    w_send,
    w_recv,
    w_agg,
    w_out,
    edge_bias,
    gain,
    send_col,
    send_row,
    recv_col,
    recv_row,
    new_nodes,
    d_pre_b,
    d_recv_b,
    d_send,
    d_up,
    d_down,
    d_corner_up,
    d_corner_down,
    d_gathered,
    grads_mine,
    grads_other,
    mid,
    right,
    left,
    slopes,
    slope_sum,
    total,
    work,
    agg_b,
    hidden_b,
    d_out_b,
    d_half,
    d_recv,
    far,
    far_d,
    near_nodes,
    near_d,
    sums,
    coarse,
    coarse_d,
):
    patch_rows, cols, lon_count, coarse_count, lat_count = dims
    rows = patch_rows * cols
    depth = nodes.shape[-1]
    pack = coarse_count + 2 * patch_rows
    top_valid, bottom_valid, right_at, left_at, core, lat = (facts[i] for i in range(6))
    tile = 16

    upper, lower = pl.ds(0, cols), pl.ds(cols, cols)
    corner_up, corner_down = pl.ds(2 * cols, 16), pl.ds(2 * cols + 16, 16)
    near_nodes[upper, :] = above[...]
    near_nodes[lower, :] = below[...]
    near_nodes[corner_up, :] = corner_above[...]
    near_nodes[corner_down, :] = corner_below[...]
    near_half = 0.5 * to_f32(to_bf16(dot(near_nodes[...], w_send[...])))
    far[...] = 0.5 * to_f32(to_bf16(dot(gathered[...], w_send[...])))
    sums[...] = jnp.zeros_like(sums)
    first = lax.broadcasted_iota(jnp.int32, (cols, 1), 0) == 0
    last = lax.broadcasted_iota(jnp.int32, (cols, 1), 0) == cols - 1
    top = jnp.where(top_valid == 1, near_half[:cols], ABSENT)
    bottom = jnp.where(bottom_valid == 1, near_half[cols : 2 * cols], ABSENT)
    top_corner = jnp.where(top_valid == 1, near_half[2 * cols : 2 * cols + 1], ABSENT)
    bottom_corner = jnp.where(
        bottom_valid == 1, near_half[2 * cols + 31 : 2 * cols + 32], ABSENT
    )
    mid[pl.ds(0, cols), :] = top
    mid[pl.ds(rows + cols, cols), :] = bottom
    right[pl.ds(0, cols), :] = jnp.where(last, top_corner, pltpu.roll(top, cols - 1, 0))
    left[pl.ds(rows + cols, cols), :] = jnp.where(first, bottom_corner, pltpu.roll(bottom, 1, 0))

    right_edge = far[pl.ds(aligned(right_at + coarse_count, 16), patch_rows), :]
    left_edge = far[pl.ds(aligned(left_at + coarse_count + patch_rows, 16), patch_rows), :]
    for row in range(patch_rows):
        here, there = pl.ds(row * cols, cols), pl.ds((row + 1) * cols, cols)
        for lane in range(0, depth, 128):
            lanes = pl.ds(lane, 128)
            block = 0.5 * to_f32(send[here, lanes])
            mid[there, lanes] = block
            edge = right_edge[row : row + 1, lane : lane + 128]
            right[there, lanes] = jnp.where(last, edge, pltpu.roll(block, cols - 1, 0))
            edge = left_edge[row : row + 1, lane : lane + 128]
            left[there, lanes] = jnp.where(first, edge, pltpu.roll(block, 1, 0))

    senders = ((mid, 2), (mid, 0), (right, 1), (left, 1), (left, 2), (right, 0))

    def edges(step, carry):
        base = aligned(step * tile, tile)
        here = pl.ds(base, tile)
        recv = recv_half[here, :]
        summed = jnp.zeros((tile, depth), jnp.float32)
        slope_total = jnp.zeros((tile, depth), jnp.float32)
        for which, (source, shift) in enumerate(senders):
            half = source[pl.ds(aligned(base + shift * cols, tile), tile), :] + recv
            value, slope = half_sum_and_slope(half)
            summed = summed + value
            slope_total = slope_total + slope
            slopes[which, pl.ds(aligned(base + cols, tile), tile), :] = to_bf16(slope)
        total[here, :] = summed
        slope_sum[here, :] = slope_total
        return carry

    lax.fori_loop(0, rows // tile, edges, 0)

    edge_count = send_col.shape[0]
    for source in range(lon_count):
        coarse[pl.ds(source * coarse_count, coarse_count), :] = far[
            pl.ds(source * pack, coarse_count), :
        ]
    coarse_ids = lon_count * coarse_count
    send_hot = to_f32(
        send_col[...] == lax.broadcasted_iota(jnp.int32, (edge_count, coarse_ids), 1)
    )
    send_hot_t = to_f32(
        send_row[...] == lax.broadcasted_iota(jnp.int32, (coarse_ids, edge_count), 0)
    )
    recv_hot = to_f32(
        recv_col[...] == lax.broadcasted_iota(jnp.int32, (edge_count, coarse_count), 1)
    )
    recv_hot_t = to_f32(
        recv_row[...] == lax.broadcasted_iota(jnp.int32, (coarse_count, edge_count), 0)
    )
    coarse_recv = 0.5 * (dot(gathered[pl.ds(0, coarse_count), :], w_recv[...]) + edge_bias[...])
    long_half = dot_exact(send_hot, coarse[...]) + dot_exact(recv_hot, coarse_recv)
    long_value, long_slope = half_sum_and_slope(long_half)
    coarse_d[...] = dot_exact(recv_hot_t, long_value)
    for k in range(coarse_count):
        spot = pl.ds(slots[k], 1)
        total[spot, :] = total[spot, :] + coarse_d[pl.ds(k, 1), :]

    step_rows = 256
    blocks = [pl.ds(start, step_rows) for start in range(0, rows, step_rows)]
    for block in blocks:
        agg_b[block, :] = to_bf16(total[block, :])
        work[block, :] = 0.5 * (own[block, :] + dot(agg_b[block, :], w_agg[...]))

    def activate(step, carry):
        here = pl.ds(aligned(step * tile, tile), tile)
        half = work[here, :]
        hidden_b[here, :] = to_bf16(half + half * jnp.tanh(half))
        return carry

    lax.fori_loop(0, rows // tile, activate, 0)
    for block in blocks:
        total[block, :] = dot(hidden_b[block, :], w_out[...])

    wide = 32

    def normalise(step, carry):
        here = pl.ds(aligned(step * wide, wide), wide)
        output = total[here, :]
        cot = to_f32(cotangent[here, :])
        d_norm = cot * gain[...]
        d_mean = jnp.mean(d_norm, axis=-1, keepdims=True)
        centred = output - jnp.mean(output, axis=-1, keepdims=True)
        inv_std = lax.rsqrt(jnp.mean(centred * centred, axis=-1, keepdims=True) + epsilon)
        normed = centred * inv_std
        new_nodes[here, :] = to_bf16(to_f32(nodes[here, :]) + gain[...] * normed)
        sums[2] += eight_rows(cot * normed)
        d_dot = jnp.mean(d_norm * normed, axis=-1, keepdims=True)
        d_out_b[here, :] = to_bf16(inv_std * (d_norm - d_mean - normed * d_dot))
        return carry

    lax.fori_loop(0, rows // wide, normalise, 0, unroll=2)

    for block in blocks:
        total[block, :] = dot_nt(d_out_b[block, :], w_out[...])

    def deactivate(step, carry):
        here = pl.ds(aligned(step * tile, tile), tile)
        slope = half_sum_and_slope(work[here, :])[1]
        d_pre = total[here, :] * (0.5 * slope)
        sums[1] += eight_rows(d_pre)
        d_pre_b[here, :] = to_bf16(d_pre)
        return carry

    lax.fori_loop(0, rows // tile, deactivate, 0)
    share = depth // (2 * lat_count)

    def put(which, half_at, values):
        block = to_bf16(values)
        for grads, core_at in ((grads_mine, half_at), (grads_other, 1 - half_at)):

            @pl.when(core == core_at)
            def _():
                for place in range(lat_count):
                    grads[lat ^ place, pl.ds(which * share, share), :] = block[
                        place * share : (place + 1) * share
                    ]

    for half_at in range(2):
        columns = pl.ds(half_at * (depth // 2), depth // 2)
        put(2, half_at, dot_tn(nodes[:, columns], d_pre_b[...]))
        put(3, half_at, dot_tn(agg_b[:, columns], d_pre_b[...]))
        put(4, half_at, dot_tn(hidden_b[:, columns], d_out_b[...]))
    d_half[pl.ds(0, cols), :] = jnp.zeros((cols, depth), jnp.float32)
    d_half[pl.ds(rows + cols, cols), :] = jnp.zeros((cols, depth), jnp.float32)
    for which in (0, 4):
        slopes[which, pl.ds(0, cols), :] = jnp.zeros((cols, depth), jnp.bfloat16)
    for which in (1, 5):
        slopes[which, pl.ds(rows + cols, cols), :] = jnp.zeros((cols, depth), jnp.bfloat16)
    for start in range(0, rows, step_rows):
        d_sum = dot_nt(d_pre_b[pl.ds(start, step_rows), :], w_agg[...])
        d_half[pl.ds(start + cols, step_rows), :] = 0.5 * to_f32(to_bf16(d_sum))

    def slope_times(which, place, lanes):
        return to_f32(slopes[which, place, lanes]) * d_half[place, lanes]

    def receive(step, carry):
        base = aligned(step * tile, tile)
        here = pl.ds(base, tile)
        value = d_half[pl.ds(aligned(base + cols, tile), tile), :] * slope_sum[here, :]
        d_recv[here, :] = value
        sums[0] += eight_rows(value)
        return carry

    lax.fori_loop(0, rows // tile, receive, 0)
    far_d[...] = jnp.zeros_like(far_d)

    edge_place = lax.broadcasted_iota(jnp.int32, (patch_rows, 1), 0)
    for lane in range(0, depth, 128):
        lanes = pl.ds(lane, 128)
        right_edge = jnp.zeros((patch_rows, 128), jnp.float32)
        left_edge = jnp.zeros((patch_rows, 128), jnp.float32)
        for row in range(patch_rows):
            above_row, out = pl.ds(row * cols, cols), pl.ds(row * cols, cols)
            here, below_row = pl.ds((row + 1) * cols, cols), pl.ds((row + 2) * cols, cols)
            to_mid = slope_times(0, above_row, lanes) + slope_times(1, below_row, lanes)
            to_right = slope_times(2, here, lanes) + slope_times(5, below_row, lanes)
            to_left = slope_times(3, here, lanes) + slope_times(4, above_row, lanes)
            d_send[out, lanes] = (
                to_mid
                + jnp.where(first, 0.0, pltpu.roll(to_right, 1, 0))
                + jnp.where(last, 0.0, pltpu.roll(to_left, cols - 1, 0))
            )
            right_edge = jnp.where(edge_place == row, to_right[cols - 1 : cols], right_edge)
            left_edge = jnp.where(edge_place == row, to_left[0:1], left_edge)
        far_d[pl.ds(aligned(right_at + coarse_count, 16), patch_rows), lanes] = right_edge
        far_d[pl.ds(aligned(left_at + coarse_count + patch_rows, 16), patch_rows), lanes] = left_edge
    row_first, row_last = pl.ds(cols, cols), pl.ds(rows, cols)
    for lane in range(0, depth, 128):
        lanes = pl.ds(lane, 128)
        to_right = slope_times(5, row_first, lanes)
        to_left = slope_times(4, row_last, lanes)
        up = slope_times(1, row_first, lanes) + jnp.where(first, 0.0, pltpu.roll(to_right, 1, 0))
        down = slope_times(0, row_last, lanes) + jnp.where(
            last, 0.0, pltpu.roll(to_left, cols - 1, 0)
        )
        sixteen = lax.broadcasted_iota(jnp.int32, (16, 1), 0)
        near_d[upper, lanes] = to_bf16(up)
        near_d[lower, lanes] = to_bf16(down)
        near_d[corner_up, lanes] = to_bf16(
            jnp.where(sixteen == 0, to_right[cols - 1 : cols], 0.0)
        )
        near_d[corner_down, lanes] = to_bf16(jnp.where(sixteen == 15, to_left[0:1], 0.0))
    d_up[...] = near_d[upper, :]
    d_down[...] = near_d[lower, :]
    d_corner_up[...] = near_d[corner_up, :]
    d_corner_down[...] = near_d[corner_down, :]

    for k in range(coarse_count):
        coarse_d[pl.ds(k, 1), :] = d_half[pl.ds(slots[k] + cols, 1), :]
    long_d = dot_exact(recv_hot, coarse_d[...]) * long_slope
    sums[0] += eight_rows(long_d)
    coarse_d[...] = dot_exact(recv_hot_t, long_d)
    for k in range(coarse_count):
        spot = pl.ds(slots[k], 1)
        d_recv[spot, :] = d_recv[spot, :] + coarse_d[pl.ds(k, 1), :]
    coarse[...] = dot_exact(send_hot_t, long_d)
    for source in range(lon_count):
        far_d[pl.ds(source * pack, coarse_count), :] = coarse[
            pl.ds(source * coarse_count, coarse_count), :
        ]
    d_gathered[...] = to_bf16(far_d[...])
    for block in blocks:
        d_recv_b[block, :] = to_bf16(d_recv[block, :])
        agg_b[block, :] = to_bf16(d_send[block, :])
    for half_at in range(2):
        columns = pl.ds(half_at * (depth // 2), depth // 2)
        put(0, half_at, dot_tn(nodes[:, columns], agg_b[...])
            + dot_tn(near_nodes[:, columns], near_d[...])
            + dot_tn(gathered[:, columns], d_gathered[...]))
        put(1, half_at, dot_tn(nodes[:, columns], d_recv_b[...]))
    place = lax.broadcasted_iota(jnp.int32, (16, depth), 0)
    vectors = jnp.zeros((16, depth), jnp.float32)
    for which in range(3):
        vectors = jnp.where(place == which, jnp.sum(sums[which], axis=0, keepdims=True), vectors)
    for spot in range(lat_count):
        grads_mine[spot, pl.ds(5 * share, 16), :] = to_bf16(vectors)
        grads_other[spot, pl.ds(5 * share, 16), :] = to_bf16(vectors)


def update(dims, ints, arrays):
    patch_rows, cols, lon_count, coarse_count, lat_count = dims
    rows, depth = arrays[0].shape
    share = depth // (2 * lat_count)
    far_rows = lon_count * (coarse_count + 2 * patch_rows)
    long_rows = rows + 2 * cols
    shape = jax.ShapeDtypeStruct
    scratch = lambda *size, kind=jnp.float32: pltpu.VMEM(size, kind)
    smem, vmem = pl.BlockSpec(memory_space=pltpu.SMEM), pl.BlockSpec(memory_space=pltpu.VMEM)
    return pl.pallas_call(
        functools.partial(update_kernel, dims),
        in_specs=[smem] * 2 + [vmem] * len(arrays),
        out_specs=[vmem] * 11,
        out_shape=[
            shape((rows, depth), jnp.bfloat16),
            shape((rows, depth), jnp.bfloat16),
            shape((rows, depth), jnp.bfloat16),
            shape((rows, depth), jnp.float32),
            shape((cols, depth), jnp.bfloat16),
            shape((cols, depth), jnp.bfloat16),
            shape((16, depth), jnp.bfloat16),
            shape((16, depth), jnp.bfloat16),
            shape((far_rows, depth), jnp.bfloat16),
            shape((lat_count, 5 * share + 16, depth), jnp.bfloat16),
            shape((lat_count, 5 * share + 16, depth), jnp.bfloat16),
        ],
        scratch_shapes=[
            scratch(long_rows, depth),
            scratch(long_rows, depth),
            scratch(long_rows, depth),
            scratch(6, long_rows, depth, kind=jnp.bfloat16),
            scratch(rows, depth),
            scratch(rows, depth),
            scratch(rows, depth),
            scratch(rows, depth, kind=jnp.bfloat16),
            scratch(rows, depth, kind=jnp.bfloat16),
            scratch(rows, depth, kind=jnp.bfloat16),
            scratch(long_rows, depth),
            scratch(rows, depth),
            scratch(far_rows, depth),
            scratch(far_rows, depth),
            scratch(2 * cols + 32, depth, kind=jnp.bfloat16),
            scratch(2 * cols + 32, depth, kind=jnp.bfloat16),
            scratch(3, 8, depth),
            scratch(lon_count * coarse_count, depth),
            scratch(coarse_count, depth),
        ],
        compiler_params=pltpu.CompilerParams(vmem_limit_bytes=VMEM_BYTES),
        cost_estimate=pl.CostEstimate(
            flops=20 * rows * depth * depth, bytes_accessed=20_000_000, transcendentals=0
        ),
        name="update",
    )(*ints, *arrays)


def finish_kernel(
    dims,
    slots,
    cotangent,
    d_pre_b,
    d_recv_b,
    d_send,
    from_below,
    from_above,
    corner_below,
    corner_above,
    back,
    w_self,
    w_recv,
    w_send,
    grad_nodes,
    total,
):
    patch_rows, cols, _, coarse_count, _ = dims
    rows = patch_rows * cols
    step_rows = 256
    for start in range(0, rows, step_rows):
        block = pl.ds(start, step_rows)
        total[block, :] = d_send[block, :]
    for start, part in (
        (rows - cols, from_below),
        (0, from_above),
        (rows - cols, corner_below),
        (cols - 16, corner_above),
    ):
        block = pl.ds(start, part.shape[0])
        total[block, :] = total[block, :] + to_f32(part[...])
    returned = to_f32(back[...])
    for row in range(patch_rows):
        for spot, at in ((row * cols, 0), (row * cols + cols - 1, patch_rows)):
            one = coarse_count + at + row
            total[pl.ds(spot, 1), :] = total[pl.ds(spot, 1), :] + returned[one : one + 1]
    for k in range(coarse_count):
        spot = pl.ds(slots[k], 1)
        total[spot, :] = total[spot, :] + returned[k : k + 1]
    for start in range(0, rows, step_rows):
        block = pl.ds(start, step_rows)
        grad_nodes[block, :] = to_bf16(
            to_f32(cotangent[block, :])
            + dot_nt(d_pre_b[block, :], w_self[...])
            + dot_nt(d_recv_b[block, :], w_recv[...])
            + dot_nt(to_bf16(total[block, :]), w_send[...])
        )


def finish(dims, slots, arrays):
    rows, depth = arrays[0].shape
    smem, vmem = pl.BlockSpec(memory_space=pltpu.SMEM), pl.BlockSpec(memory_space=pltpu.VMEM)
    return pl.pallas_call(
        functools.partial(finish_kernel, dims),
        in_specs=[smem] + [vmem] * len(arrays),
        out_specs=vmem,
        out_shape=jax.ShapeDtypeStruct((rows, depth), jnp.bfloat16),
        scratch_shapes=[pltpu.VMEM((rows, depth), jnp.float32)],
        compiler_params=pltpu.CompilerParams(vmem_limit_bytes=VMEM_BYTES),
        cost_estimate=pl.CostEstimate(
            flops=6 * rows * depth * depth, bytes_accessed=8_000_000, transcendentals=0
        ),
        name="finish",
    )(slots, *arrays)


def swapped(values, axis, bit):
    count = lax.axis_size(axis)
    return lax.ppermute(values, axis, [(i, i ^ bit) for i in range(count)])


def summed_shares(mine, other):
    lat_count, _, depth = mine.shape
    chip_count = lax.axis_size("lon") // 2
    chip = lax.axis_index("lon") // 2
    share = depth // (2 * lat_count)
    own = to_bf16(to_f32(mine) + to_f32(swapped(other, "lon", 1)))
    total = to_f32(own[0])
    for step in range(1, lat_count):
        total = total + to_f32(swapped(own[step], "lat", step))
    total = to_bf16(total)
    vectors = total[5 * share :]
    parts = total[: 5 * share].reshape(5, chip_count, share // chip_count, depth)

    def part_of(place):
        part = lax.dynamic_index_in_dim(parts, place, axis=1, keepdims=False)
        return jnp.concatenate([part.reshape(-1, depth), vectors])

    total = to_f32(part_of(chip))
    for step in range(1, chip_count):
        total = total + to_f32(swapped(part_of(chip ^ step), "lon", 2 * step))
    part = to_bf16(total[:-16])
    parts = jnp.stack([part] + [swapped(part, "lon", 2 * k) for k in range(1, chip_count)])
    parts = parts[chip ^ jnp.arange(chip_count)].reshape(chip_count, 5, -1, depth)
    ready = jnp.transpose(parts, (1, 0, 2, 3)).reshape(5 * share, depth)
    shares = [ready] + [swapped(ready, "lat", step) for step in range(1, lat_count)]
    return shares + [swapped(part, "lon", 1) for part in shares], total[-16:]


def unpack_kernel(lat_count, scale, facts, vectors, *refs):
    shares, outs = refs[: 2 * lat_count], refs[2 * lat_count :]
    depth = vectors.shape[-1]
    share = depth // (2 * lat_count)
    core, lat = facts[4], facts[5]
    for flip in range(2):
        for step in range(lat_count):
            start = (core ^ flip) * (depth // 2) + (lat ^ step) * share
            place = pl.ds(aligned(start, share), share)
            for which in range(5):
                block = shares[flip * lat_count + step][pl.ds(which * share, share), :]
                outs[which][place, :] = scale * to_f32(block)
    for which in range(3):
        outs[5 + which][...] = scale * vectors[pl.ds(which, 1), :]


def unpack(lat_count, scale, facts, vectors, shares):
    depth = vectors.shape[-1]
    smem, vmem = pl.BlockSpec(memory_space=pltpu.SMEM), pl.BlockSpec(memory_space=pltpu.VMEM)
    shape = jax.ShapeDtypeStruct
    return pl.pallas_call(
        functools.partial(unpack_kernel, lat_count, scale),
        in_specs=[smem] + [vmem] * (1 + len(shares)),
        out_specs=[vmem] * 8,
        out_shape=[shape((depth, depth), jnp.float32)] * 5 + [shape((1, depth), jnp.float32)] * 3,
        compiler_params=pltpu.CompilerParams(vmem_limit_bytes=VMEM_BYTES),
        name="unpack",
    )(facts, vectors, *shares)


def on_device(
    nodes,
    cotangent,
    w_send,
    w_recv,
    edge_bias,
    w_self,
    w_agg,
    node_bias,
    w_out,
    gain,
    coarse_slots,
    long_senders,
    long_receivers,
):
    patch_rows, cols, depth = nodes.shape
    rows = patch_rows * cols
    lat_count, lon_count = lax.axis_size("lat"), lax.axis_size("lon")
    chip_count = lon_count // 2
    lat, lon = lax.axis_index("lat"), lax.axis_index("lon")
    scale = float(rows * lat_count * lon_count) ** (-0.5)
    slots = coarse_slots.reshape(-1)
    coarse_count = slots.shape[0]
    dims = (patch_rows, cols, lon_count, coarse_count, lat_count)
    flat = nodes.reshape(rows, depth)
    cot = cotangent.reshape(rows, depth)

    down = [(i, i + 1) for i in range(lat_count - 1)]
    up = [(i + 1, i) for i in range(lat_count - 1)]

    def number(lat_place, lon_place):
        return lat_place * lon_count + lon_place % lon_count

    lats, lons = range(lat_count), range(lon_count)
    down_left = [(number(i, j), number(i + 1, j - 1)) for i in lats[:-1] for j in lons]
    up_right = [(number(i, j), number(i - 1, j + 1)) for i in lats[1:] for j in lons]
    above = lax.ppermute(flat[-cols:], "lat", down)
    below = lax.ppermute(flat[:cols], "lat", up)
    corner_above = lax.ppermute(flat[-cols : 16 - cols], ("lat", "lon"), down_left)
    corner_below = lax.ppermute(flat[cols - 16 : cols], ("lat", "lon"), up_right)
    packed = jnp.concatenate([flat[slots], nodes[:, 0], nodes[:, -1]])
    chips = [packed] + [swapped(packed, "lon", 2 * k) for k in range(1, chip_count)]
    chips = jnp.concatenate(chips)
    gathered = jnp.concatenate([chips, swapped(chips, "lon", 1)])

    def place_of(other):
        apart = other ^ lon
        return (apart % 2) * chip_count + apart // 2

    pack = packed.shape[0]
    facts = jnp.stack(
        [
            (lat > 0).astype(jnp.int32),
            (lat < lat_count - 1).astype(jnp.int32),
            place_of((lon + 1) % lon_count) * pack,
            place_of((lon + lon_count - 1) % lon_count) * pack,
            lon % 2,
            lat,
        ]
    ).astype(jnp.int32)
    sources = place_of(jnp.arange(lon_count))[:, None]
    sender_ids = (long_senders.reshape(lon_count, -1) + sources * coarse_count).reshape(-1)
    receiver_ids = long_receivers.reshape(-1)

    send, recv_half, own = project(
        flat, w_send, w_recv, w_self, edge_bias[None], node_bias[None]
    )
    (
        new_nodes,
        d_pre_b,
        d_recv_b,
        d_send,
        d_up,
        d_down,
        d_corner_up,
        d_corner_down,
        d_gathered,
        grads_mine,
        grads_other,
    ) = update(
        dims,
        (slots, facts),
        (
            flat,
            cot,
            send,
            recv_half,
            own,
            above,
            below,
            corner_above,
            corner_below,
            gathered,
            w_send,
            w_recv,
            w_agg,
            w_out,
            edge_bias[None],
            gain[None],
            sender_ids[:, None],
            sender_ids[None],
            receiver_ids[:, None],
            receiver_ids[None],
        ),
    )
    shares, vectors = summed_shares(grads_mine, grads_other)

    from_below = lax.ppermute(d_up, "lat", up)
    from_above = lax.ppermute(d_down, "lat", down)
    at_corner_below = lax.ppermute(d_corner_up, ("lat", "lon"), up_right)
    at_corner_above = lax.ppermute(d_corner_down, ("lat", "lon"), down_left)
    half = chip_count * pack
    chips = to_bf16(to_f32(d_gathered[:half]) + to_f32(swapped(d_gathered[half:], "lon", 1)))
    back = to_f32(chips[:pack])
    for k in range(1, chip_count):
        back = back + to_f32(swapped(chips[k * pack : (k + 1) * pack], "lon", 2 * k))
    grad_nodes = finish(
        dims,
        slots,
        (
            cot,
            d_pre_b,
            d_recv_b,
            d_send,
            from_below,
            from_above,
            at_corner_below,
            at_corner_above,
            back,
            w_self,
            w_recv,
            w_send,
        ),
    )
    outs = unpack(lat_count, scale, facts, vectors, shares)
    return (
        new_nodes.reshape(patch_rows, cols, depth),
        grad_nodes.reshape(patch_rows, cols, depth),
        outs[0],
        outs[1],
        outs[5][0],
        outs[2],
        outs[3],
        outs[6][0],
        outs[4],
        outs[7][0],
    )


def solution(mesh):
    patches = P("lat", "lon", None)
    edges = P("lat", "lon", None, None)
    return jax.shard_map(
        on_device,
        mesh=mesh,
        in_specs=(patches, patches) + (P(),) * 8 + (patches, edges, edges),
        out_specs=(patches, patches) + (P(),) * 8,
        check_vma=False,
    )
```

time: 315 us -> 146 us (0.46)
  waiting for transfers between devices: 127 us -> 28.4 us
  blocking collectives: 52.8 us -> 0 us
  other arithmetic: 55.7 us -> 4.63 us
  Pallas kernels: 0 us -> 48 us
  starting transfers between devices: 13.8 us -> 49.8 us
  matrix products: 32.2 us -> 0 us
  between operations: 14.7 us -> 1.26 us
  local copies, waits for them, and re-layouts: 18 us -> 13 us
    psum x1 -> x0, waiting for transfers between devices: 104 us -> none  [on_device(): lax.psum((send_grad, recv_grad, edge_bias_grad, self_grad, agg_grad, node...]
    pallas_call x0 -> x4, Pallas kernels: none -> 48 us  [the longest x1 32.3 us: update(): pl.pallas_call(functools.partial(update_kernel, dims), in_specs=[smem] *...]
    psum x1 -> x0, blocking collectives: 38.5 us -> none  [on_device(): lax.psum((send_grad, recv_grad, edge_bias_grad, self_grad, agg_grad, node...]
    ppermute x8 -> x33, starting transfers between devices: 13.7 us -> 49.8 us  [the longest x25 30.6 us: swapped(): return lax.ppermute(values, axis, [(i, i ^ bit) for i in range(count)])]
    dot_general x18 -> x0, matrix products: 32.2 us -> none  [the longest x15 30.6 us: matmul(): return jnp.dot(left, right, preferred_element_type=jnp.float32)]
    ppermute x8 -> x33, waiting for transfers between devices: 6.17 us -> 28.4 us  [the longest x25 28.3 us: swapped(): return lax.ppermute(values, axis, [(i, i ^ bit) for i in range(count)])]
    reduce_scatter x1 -> x0, waiting for transfers between devices: 16.9 us -> none  [on_device(): lax.psum_scatter(flat_grads.astype(jnp.bfloat16), 'lon', scatter_dimensio...]
    add x4, other arithmetic: 16.9 us -> 1.32 us  [the longest x1 0.72 us: on_device(): back = back + to_f32(swapped(chips[k * pack:(k + 1) * pack], 'lon', 2 * k))]
  transfers between devices with their start and end apart: 10 -> 33, of which waited for: 5 -> 11; matrix products, arithmetic and copies ran while one was open for 16% -> 6% of each run, Pallas kernels for 0% -> 8%
where the time goes in v2:
time: 146 us; the launch traced here: 145 us
  starting transfers between devices  49.8 us (34%)
  Pallas kernels  48 us (33%)
  waiting for transfers between devices  28.4 us (19%)
  local copies, waits for them, and re-layouts  13 us (9%)
  other arithmetic  4.63 us (3%)
    pallas_call x1, Pallas kernels, update(): pl.pallas_call(functools.partial(update_kernel, dims), in_specs=[smem] *...  32.3 us
    ppermute x25, starting transfers between devices, swapped(): return lax.ppermute(values, axis, [(i, i ^ bit) for i in range(count)])  30.6 us
    ppermute x25, waiting for transfers between devices, swapped(): return lax.ppermute(values, axis, [(i, i ^ bit) for i in range(count)])  28.3 us
    pallas_call x1, Pallas kernels, finish(): pl.pallas_call(functools.partial(finish_kernel, dims), in_specs=[smem] +...  5.91 us
    pallas_call x1, Pallas kernels, project(): pl.pallas_call(project_kernel, grid=(rows // step,), in_specs=[block, who...  5.44 us
    ppermute x1, starting transfers between devices, on_device(): lax.ppermute(flat[-cols:16 - cols], ('lat', 'lon'), down_left)  5.24 us
    pallas_call x1, Pallas kernels, unpack(): pl.pallas_call(functools.partial(unpack_kernel, lat_count, scale), in_spe...  4.41 us
    ppermute x1, starting transfers between devices, on_device(): above = lax.ppermute(flat[-cols:], 'lat', down)  4.03 us
  transfers between devices with their start and end apart: 33, of which 11 were waited for; matrix products, arithmetic and copies ran while one was open for 6% of the time, Pallas kernels for 8%

profile of v2, /device:TPU:0, one launch (start us, length us, event | category | flops | bytes accessed | tf_op | source)
XLA Modules:
  0.0 145.1 jit_solution(12596738265885808275)
XLA Ops:
  0.7 0.7 fusion.5
  1.3 1.0 fusion.8
  2.4 2.0 %gather_fusion = bf16[16,512]{1,0:T(8,128)(2,1)S(1)} fusion(bf16[1024,512]{1,0:T(8,128)(2,1)} %bitcast.80, s32[1024]{0:T(1024)S(1)} %pad_clamp_fusion.1), kind=kCustom, calls=%fused_computation | custom fusion | bytes 32832 | tf_op jit(solution)/shard_map/gather | solution.py:614
  4.4 3.1 %collective-permute-start.4 = (bf16[48,512]{1,0:T(8,128)(2,1)S(1)}, bf16[48,512]{1,0:T(8,128)(2,1)S(1)}, u32[]{:S(2)}, u32[]{:S(2)}) collective-permute-start(bf16[48,512]{1,0:T(8,128)(2,1)S(1)} %pad_maximum_fusion.5), channel_id=1, source_target_pairs={{0,2},{1,3},{2,0},{3,1},{4,6},{5,7},{6,4},{7,5},{8,10},{9,11},{10,... | collective-permute-start | bytes 147464 | tf_op jit(solution)/shard_map/ppermute | solution.py:513
  7.5 2.6 %collective-permute-start.5 = (bf16[48,512]{1,0:T(8,128)(2,1)S(1)}, bf16[48,512]{1,0:T(8,128)(2,1)S(1)}, u32[]{:S(2)}, u32[]{:S(2)}) collective-permute-start(bf16[48,512]{1,0:T(8,128)(2,1)S(1)} %pad_maximum_fusion.5), channel_id=1, source_target_pairs={{0,4},{1,5},{2,6},{3,7},{4,0},{5,1},{6,2},{7,3},{8,12},{9,13},{10,... | collective-permute-start | bytes 147464 | tf_op jit(solution)/shard_map/ppermute | solution.py:513
  10.1 0.7 fusion.9
  10.8 5.2 %collective-permute-start.2 = (bf16[16,512]{1,0:T(8,128)(2,1)S(1)}, bf16[16,512]{1,0:T(8,128)(2,1)S(1)}, u32[]{:S(2)}, u32[]{:S(2)}) collective-permute-start(bf16[16,512]{1,0:T(8,128)(2,1)S(1)} %get-tuple-element.64), channel_id=1, source_target_pairs={{0,15},{1,8},{2,9},{3,10},{4,11},{5,12},{6,13},{7,14},{8,23},{9,16... | collective-permute-start | bytes 49160 | tf_op jit(solution)/shard_map/ppermute | solution.py:612
  16.0 1.3 collective-permute-start.3
  17.3 0.9 slice_bitcast_fusion.4
  18.3 4.0 %collective-permute-start = (bf16[64,512]{1,0:T(8,128)(2,1)S(1)}, bf16[64,512]{1,0:T(8,128)(2,1)S(1)}, u32[]{:S(2)}, u32[]{:S(2)}) collective-permute-start(bf16[64,512]{1,0:T(8,128)(2,1)S(1)} %get-tuple-element.66), channel_id=1, source_target_pairs={{0,8},{8,16},{16,24},{1,9},{9,17},{17,25},{2,10},{10,18},{18,26},{... | collective-permute-start | bytes 196616 | tf_op jit(solution)/shard_map/ppermute | solution.py:610
  22.3 1.3 collective-permute-start.1
  24.2 0.7 broadcast_in_dim_reshape.10.recv_col
  24.9 0.6 broadcast_in_dim_reshape.9.recv_row
  25.5 0.7 copy.31.send_col
  26.2 0.5 add.163.send_row
  26.8 0.7 stack.50.facts
  27.5 5.4 %project.1 = (bf16[1024,512]{1,0:T(8,128)(2,1)}, f32[1024,512]{1,0:T(8,128)}, f32[1024,512]{1,0:T(8,128)}) custom-call(bf16[1024,512]{1,0:T(8,128)(2,1)} %bitcast.82, bf16[512,512]{1,0:T(8,128)(2,1)} %w_send.5, bf16[512,512]{1,0:T(8,128)(2,1)} %w_recv.5, bf16[512,512]{1,0:T(8,128)(2,1)} %w_self.3, f32[1,512]{1,0:T(1,128)} %bitcast.90, f32[1,512]{1,0:T(1,128)} %bitcast.89), custom_call_target="tpu_custom_call" | custom-call | flops 1610612736 | bytes 8000000 | tf_op jit(solution)/shard_map/project/pallas_call | solution.py:67
  33.0 0.7 copy-done.14
  33.7 32.3 %update.1 = (bf16[1024,512]{1,0:T(8,128)(2,1)}, bf16[1024,512]{1,0:T(8,128)(2,1)}, bf16[1024,512]{1,0:T(8,128)(2,1)}, f32[1024,512]{1,0:T(8,128)}, bf16[64,512]{...) custom-call(s32[16]{0:T(128)} %bitcast.87, ...), custom_call_target="tpu_custom_call" | custom-call | flops 5368709120 | bytes 20000000 | tf_op jit(solution)/shard_map/update/pallas_call | solution.py:398
  66.0 0.6 collective-permute-start.16
  66.5 3.0 %collective-permute-done.16 = bf16[4,336,512]{2,1,0:T(8,128)(2,1)S(1)} collective-permute-done((bf16[4,336,512]{2,1,0:T(8,128)(2,1)}, bf16[4,336,512]{2,1,0:T(8,128)(2,1)S(1)}, u32[]{:S(2)}, u32[]{:S(2)}) %collective-permute-start.16) | collective-permute-done | bytes 1376288 | tf_op jit(solution)/shard_map/ppermute | solution.py:513
  69.5 1.7 %add_convert_fusion = bf16[4,336,512]{2,1,0:T(8,128)(2,1)S(1)} fusion(bf16[4,336,512]{2,1,0:T(8,128)(2,1)S(1)} %collective-permute-done.16, bf16[4,336,512]{2,1,0:T(8,128)(2,1)} %get-tuple-element.44), kind=kLoop, calls=%fused_computation.2 | loop fusion | flops 2752512 | bytes 4128768 | tf_op jit(solution)/shard_map/convert_element_type | solution.py:33
  71.2 0.8 slice_bitcast_fusion.2
  72.0 2.7 %collective-permute-start.17 = (bf16[336,512]{1,0:T(8,128)(2,1)}, bf16[336,512]{1,0:T(8,128)(2,1)S(1)}, u32[]{:S(2)}, u32[]{:S(2)}) collective-permute-start(bf16[336,512]{1,0:T(8,128)(2,1)} %get-tuple-element.58), channel_id=1, source_target_pairs={{0,8},{8,0},{16,24},{24,16},{1,9},{9,1},{17,25},{25,17},{2,10},{10... | collective-permute-start | bytes 1032200 | tf_op jit(solution)/shard_map/ppermute | solution.py:513
  74.7 0.9 collective-permute-start.18
  75.6 1.5 %collective-permute-start.19 = (bf16[336,512]{1,0:T(8,128)(2,1)S(1)}, bf16[336,512]{1,0:T(8,128)(2,1)S(1)}, u32[]{:S(2)}, u32[]{:S(2)}) collective-permute-start(bf16[336,512]{1,0:T(8,128)(2,1)S(1)} %get-tuple-element.59), channel_id=1, source_target_pairs={{0,24},{8,16},{16,8},{24,0},{1,25},{9,17},{17,9},{25,1},{2,26},{10... | collective-permute-start | bytes 1032200 | tf_op jit(solution)/shard_map/ppermute | solution.py:513
  77.1 0.6 pad_clamp_fusion
  77.8 1.5 %collective-permute-start.8 = (bf16[64,512]{1,0:T(8,128)(2,1)}, bf16[64,512]{1,0:T(8,128)(2,1)S(1)}, u32[]{:S(2)}, u32[]{:S(2)}) collective-permute-start(bf16[64,512]{1,0:T(8,128)(2,1)} %get-tuple-element.39), channel_id=1, source_target_pairs={{8,0},{16,8},{24,16},{9,1},{17,9},{25,17},{10,2},{18,10},{26,18},{... | collective-permute-start | bytes 196616 | tf_op jit(solution)/shard_map/ppermute | solution.py:681
  79.3 4.6 %collective-permute-done.17 = bf16[336,512]{1,0:T(8,128)(2,1)S(1)} collective-permute-done((bf16[336,512]{1,0:T(8,128)(2,1)}, bf16[336,512]{1,0:T(8,128)(2,1)S(1)}, u32[]{:S(2)}, u32[]{:S(2)}) %collective-permute-start.17) | collective-permute-done | bytes 344096 | tf_op jit(solution)/shard_map/ppermute | solution.py:513
  83.8 1.3 collective-permute-start.10
  85.1 5.8 %collective-permute-done.18 = bf16[336,512]{1,0:T(8,128)(2,1)S(1)} collective-permute-done((bf16[336,512]{1,0:T(8,128)(2,1)S(1)}, bf16[336,512]{1,0:T(8,128)(2,1)S(1)}, u32[]{:S(2)}, u32[]{:S(2)}) %collective-permute-start.18) | collective-permute-done | bytes 344096 | tf_op jit(solution)/shard_map/ppermute | solution.py:513
  90.9 2.6 %collective-permute-done.19 = bf16[336,512]{1,0:T(8,128)(2,1)S(1)} collective-permute-done((bf16[336,512]{1,0:T(8,128)(2,1)S(1)}, bf16[336,512]{1,0:T(8,128)(2,1)S(1)}, u32[]{:S(2)}, u32[]{:S(2)}) %collective-permute-start.19) | collective-permute-done | bytes 344096 | tf_op jit(solution)/shard_map/ppermute | solution.py:513
  93.5 0.2 fusion.2
  93.8 0.4 collective-permute-start.20
  94.3 4.4 %collective-permute-start.21 = (bf16[96,512]{1,0:T(8,128)(2,1)S(1)}, bf16[96,512]{1,0:T(8,128)(2,1)S(1)}, u32[]{:S(2)}, u32[]{:S(2)}) collective-permute-start(bf16[96,512]{1,0:T(8,128)(2,1)S(1)} %get-tuple-element.81), channel_id=1, source_target_pairs={{0,4},{1,5},{2,6},{3,7},{4,0},{5,1},{6,2},{7,3},{8,12},{9,13},{10,... | collective-permute-start | bytes 294920 | tf_op jit(solution)/shard_map/ppermute | solution.py:513
  98.7 0.7 collective-permute-done.20
  99.4 4.6 %collective-permute-done.21 = bf16[96,512]{1,0:T(8,128)(2,1)S(1)} collective-permute-done((bf16[96,512]{1,0:T(8,128)(2,1)S(1)}, bf16[96,512]{1,0:T(8,128)(2,1)S(1)}, u32[]{:S(2)}, u32[]{:S(2)}) %collective-permute-start.21) | collective-permute-done | bytes 98336 | tf_op jit(solution)/shard_map/ppermute | solution.py:513
  104.0 1.2 collective-permute-done.22
  105.3 1.5 %collective-permute-start.23 = (bf16[80,512]{1,0:T(8,128)(2,1)S(1)}, bf16[80,512]{1,0:T(8,128)(2,1)S(1)}, u32[]{:S(2)}, u32[]{:S(2)}) collective-permute-start(bf16[80,512]{1,0:T(8,128)(2,1)S(1)} %slice.118), channel_id=1, source_target_pairs={{0,2},{1,3},{2,0},{3,1},{4,6},{5,7},{6,4},{7,5},{8,10},{9,11},{10,... | collective-permute-start | bytes 245768 | tf_op jit(solution)/shard_map/ppermute | solution.py:513
  106.8 1.4 collective-permute-start.24
  108.2 1.5 %collective-permute-start.25 = (bf16[80,512]{1,0:T(8,128)(2,1)S(1)}, bf16[80,512]{1,0:T(8,128)(2,1)S(1)}, u32[]{:S(2)}, u32[]{:S(2)}) collective-permute-start(bf16[80,512]{1,0:T(8,128)(2,1)S(1)} %slice.118), channel_id=1, source_target_pairs={{0,6},{1,7},{2,4},{3,5},{4,2},{5,3},{6,0},{7,1},{8,14},{9,15},{10,... | collective-permute-start | bytes 245768 | tf_op jit(solution)/shard_map/ppermute | solution.py:513
  109.8 1.7 %collective-permute-start.11 = (bf16[16,512]{1,0:T(8,128)(2,1)S(1)}, bf16[16,512]{1,0:T(8,128)(2,1)S(1)}, u32[]{:S(2)}, u32[]{:S(2)}) collective-permute-start(bf16[16,512]{1,0:T(8,128)(2,1)S(1)} %copy-done.20), channel_id=1, source_target_pairs={{0,15},{1,8},{2,9},{3,10},{4,11},{5,12},{6,13},{7,14},{8,23},{9,16... | collective-permute-start | bytes 49160 | tf_op jit(solution)/shard_map/ppermute | solution.py:684
  111.5 3.0 %collective-permute-done.24 = bf16[80,512]{1,0:T(8,128)(2,1)S(1)} collective-permute-done((bf16[80,512]{1,0:T(8,128)(2,1)S(1)}, bf16[80,512]{1,0:T(8,128)(2,1)S(1)}, u32[]{:S(2)}, u32[]{:S(2)}) %collective-permute-start.24) | collective-permute-done | bytes 81952 | tf_op jit(solution)/shard_map/ppermute | solution.py:513
  114.6 0.7 gather_fusion.1
  115.3 1.2 collective-permute-start.26
  116.5 1.0 collective-permute-start.27
  117.5 1.4 collective-permute-start.28
  118.9 1.5 %collective-permute-start.13 = (bf16[48,512]{1,0:T(8,128)(2,1)S(1)}, bf16[48,512]{1,0:T(8,128)(2,1)S(1)}, u32[]{:S(2)}, u32[]{:S(2)}) collective-permute-start(bf16[48,512]{1,0:T(8,128)(2,1)S(1)} %get-tuple-element.71), channel_id=1, source_target_pairs={{0,2},{1,3},{2,0},{3,1},{4,6},{5,7},{6,4},{7,5},{8,10},{9,11},{10,... | collective-permute-start | bytes 147464 | tf_op jit(solution)/shard_map/ppermute | solution.py:513
  120.4 1.8 %collective-permute-start.14 = (bf16[48,512]{1,0:T(8,128)(2,1)S(1)}, bf16[48,512]{1,0:T(8,128)(2,1)S(1)}, u32[]{:S(2)}, u32[]{:S(2)}) collective-permute-start(bf16[48,512]{1,0:T(8,128)(2,1)S(1)} %get-tuple-element.73), channel_id=1, source_target_pairs={{0,4},{1,5},{2,6},{3,7},{4,0},{5,1},{6,2},{7,3},{8,12},{9,13},{10,... | collective-permute-start | bytes 147464 | tf_op jit(solution)/shard_map/ppermute | solution.py:513
  122.2 1.1 collective-permute-done.13
  123.3 2.4 %collective-permute-start.15 = (bf16[48,512]{1,0:T(8,128)(2,1)S(1)}, bf16[48,512]{1,0:T(8,128)(2,1)S(1)}, u32[]{:S(2)}, u32[]{:S(2)}) collective-permute-start(bf16[48,512]{1,0:T(8,128)(2,1)S(1)} %get-tuple-element.72), channel_id=1, source_target_pairs={{0,6},{1,7},{2,4},{3,5},{4,2},{5,3},{6,0},{7,1},{8,14},{9,15},{10,... | collective-permute-start | bytes 147464 | tf_op jit(solution)/shard_map/ppermute | solution.py:513
  125.7 0.6 collective-permute-done.14
  126.4 2.9 %collective-permute-start.9 = (bf16[64,512]{1,0:T(8,128)(2,1)S(1)}, bf16[64,512]{1,0:T(8,128)(2,1)S(1)}, u32[]{:S(2)}, u32[]{:S(2)}) collective-permute-start(bf16[64,512]{1,0:T(8,128)(2,1)S(1)} %copy-done.15), channel_id=1, source_target_pairs={{0,8},{8,16},{16,24},{1,9},{9,17},{17,25},{2,10},{10,18},{18,26},{... | collective-permute-start | bytes 196616 | tf_op jit(solution)/shard_map/ppermute | solution.py:682
  129.3 0.5 collective-permute-start.30
  129.9 1.1 collective-permute-done.28.refs_3_
  131.1 0.7 convert_add_fusion.2.back
  131.8 0.6 copy-done.10
  132.4 5.9 %finish.1 = bf16[1024,512]{1,0:T(8,128)(2,1)} custom-call(s32[16]{0:T(128)} %bitcast.88, bf16[1024,512]{1,0:T(8,128)(2,1)} %bitcast.74, bf16[1024,512]{1,0:T(8,128)(2,1)} %get-tuple-element.36.d_pre_b, bf16[1024,512]{1,0:T(8,128)(2,1)} %get-tuple-element.37.d_recv_b, f32[1024,512]{1,0:T(8,128)} %get-tuple-element.38.d_send, bf16[64,512]{1,0:T(8,128)(2,1)} %copy-done.9, ...), custom_call_target="tpu_custom_call" | custom-call | flops 1610612736 | bytes 8000000 | tf_op jit(solution)/shard_map/finish/pallas_call | solution.py:497
  138.3 0.6 slice.105.vectors
  139.0 0.7 copy-done.5
  139.7 0.1 copy-done.6
  139.8 0.1 copy-done.7
  140.0 0.7 copy-done.8
  140.7 4.4 %unpack.1 = (f32[512,512]{1,0:T(8,128)}, f32[512,512]{1,0:T(8,128)}, f32[512,512]{1,0:T(8,128)}, f32[512,512]{1,0:T(8,128)}, f32[512,512]{1,0:T(8,128)}, /*index...) custom-call(s32[6]{0:T(128)} %stack.50.facts, f32[16,512]{1,0:T(8,128)} %slice.105.vectors, ...), custom_call_target="tpu_custom_call" | custom-call | tf_op jit(solution)/shard_map/unpack/pallas_call | solution.py:564
  (96 shorter events, 1.3 us)
Async XLA Ops:
  0.6 23.4 %copy-start.13 = (s32[1,1,8,8]{3,2,1,0:T(8,128)S(1)}, s32[1,1,8,8]{3,2,1,0:T(8,128)}, u32[]{:S(2)}) copy-start(s32[1,1,8,8]{3,2,1,0:T(8,128)} %param.24) | copy-start | bytes 772
  0.7 23.6 %copy-start.12 = (s32[1,1,8,8]{3,2,1,0:T(8,128)S(1)}, s32[1,1,8,8]{3,2,1,0:T(8,128)}, u32[]{:S(2)}) copy-start(s32[1,1,8,8]{3,2,1,0:T(8,128)} %param.25) | copy-start | bytes 772
  4.4 13.9 %collective-permute-start.4 = (bf16[48,512]{1,0:T(8,128)(2,1)S(1)}, bf16[48,512]{1,0:T(8,128)(2,1)S(1)}, u32[]{:S(2)}, u32[]{:S(2)}) collective-permute-start(bf16[48,512]{1,0:T(8,128)(2,1)S(1)} %pad_maximum_fusion.5), channel_id=1, source_target_pairs={{0,2},{1,3},{2,0},{3,1},{4,6},{5,7},{6,4},{7,5},{8,10},{9,11},{10,... | collective-permute-start | bytes 147464 | tf_op jit(solution)/shard_map/ppermute | solution.py:513
  7.5 14.9 %collective-permute-start.5 = (bf16[48,512]{1,0:T(8,128)(2,1)S(1)}, bf16[48,512]{1,0:T(8,128)(2,1)S(1)}, u32[]{:S(2)}, u32[]{:S(2)}) collective-permute-start(bf16[48,512]{1,0:T(8,128)(2,1)S(1)} %pad_maximum_fusion.5), channel_id=1, source_target_pairs={{0,4},{1,5},{2,6},{3,7},{4,0},{5,1},{6,2},{7,3},{8,12},{9,13},{10,... | collective-permute-start | bytes 147464 | tf_op jit(solution)/shard_map/ppermute | solution.py:513
  10.1 13.6 %collective-permute-start.6 = (bf16[48,512]{1,0:T(8,128)(2,1)S(1)}, bf16[48,512]{1,0:T(8,128)(2,1)S(1)}, u32[]{:S(2)}, u32[]{:S(2)}) collective-permute-start(bf16[48,512]{1,0:T(8,128)(2,1)S(1)} %pad_maximum_fusion.5), channel_id=1, source_target_pairs={{0,6},{1,7},{2,4},{3,5},{4,2},{5,3},{6,0},{7,1},{8,14},{9,15},{10,... | collective-permute-start | bytes 147464 | tf_op jit(solution)/shard_map/ppermute | solution.py:513
  10.8 22.1 %collective-permute-start.2 = (bf16[16,512]{1,0:T(8,128)(2,1)S(1)}, bf16[16,512]{1,0:T(8,128)(2,1)S(1)}, u32[]{:S(2)}, u32[]{:S(2)}) collective-permute-start(bf16[16,512]{1,0:T(8,128)(2,1)S(1)} %get-tuple-element.64), channel_id=1, source_target_pairs={{0,15},{1,8},{2,9},{3,10},{4,11},{5,12},{6,13},{7,14},{8,23},{9,16... | collective-permute-start | bytes 49160 | tf_op jit(solution)/shard_map/ppermute | solution.py:612
  16.0 16.9 %collective-permute-start.3 = (bf16[16,512]{1,0:T(8,128)(2,1)S(1)}, bf16[16,512]{1,0:T(8,128)(2,1)S(1)}, u32[]{:S(2)}, u32[]{:S(2)}) collective-permute-start(bf16[16,512]{1,0:T(8,128)(2,1)S(1)} %get-tuple-element.63), channel_id=1, source_target_pairs={{8,1},{9,2},{10,3},{11,4},{12,5},{13,6},{14,7},{15,0},{16,9},{17,1... | collective-permute-start | bytes 49160 | tf_op jit(solution)/shard_map/ppermute | solution.py:613
  18.3 14.7 %collective-permute-start = (bf16[64,512]{1,0:T(8,128)(2,1)S(1)}, bf16[64,512]{1,0:T(8,128)(2,1)S(1)}, u32[]{:S(2)}, u32[]{:S(2)}) collective-permute-start(bf16[64,512]{1,0:T(8,128)(2,1)S(1)} %get-tuple-element.66), channel_id=1, source_target_pairs={{0,8},{8,16},{16,24},{1,9},{9,17},{17,25},{2,10},{10,18},{18,26},{... | collective-permute-start | bytes 196616 | tf_op jit(solution)/shard_map/ppermute | solution.py:610
  22.3 10.7 %collective-permute-start.1 = (bf16[64,512]{1,0:T(8,128)(2,1)S(1)}, bf16[64,512]{1,0:T(8,128)(2,1)S(1)}, u32[]{:S(2)}, u32[]{:S(2)}) collective-permute-start(bf16[64,512]{1,0:T(8,128)(2,1)S(1)} %get-tuple-element.65), channel_id=1, source_target_pairs={{8,0},{16,8},{24,16},{9,1},{17,9},{25,17},{10,2},{18,10},{26,18},{... | collective-permute-start | bytes 196616 | tf_op jit(solution)/shard_map/ppermute | solution.py:611
  23.7 9.2 %collective-permute-start.7 = (bf16[192,512]{1,0:T(8,128)(2,1)S(1)}, bf16[192,512]{1,0:T(8,128)(2,1)S(1)}, u32[]{:S(2)}, u32[]{:S(2)}) collective-permute-start(bf16[192,512]{1,0:T(8,128)(2,1)S(1)} %get-tuple-element.74), channel_id=1, source_target_pairs={{0,1},{1,0},{2,3},{3,2},{4,5},{5,4},{6,7},{7,6},{8,9},{9,8},{10,11... | collective-permute-start | bytes 589832 | tf_op jit(solution)/shard_map/ppermute | solution.py:513
  32.9 0.7 copy-start.14
  32.9 0.7 copy-start.18
  33.0 0.7 copy-start.19
  33.0 0.7 copy-start.16
  33.0 0.7 copy-start.17
  66.0 3.5 %collective-permute-start.16 = (bf16[4,336,512]{2,1,0:T(8,128)(2,1)}, bf16[4,336,512]{2,1,0:T(8,128)(2,1)S(1)}, u32[]{:S(2)}, u32[]{:S(2)}) collective-permute-start(bf16[4,336,512]{2,1,0:T(8,128)(2,1)} %get-tuple-element.45), channel_id=1, source_target_pairs={{0,1},{1,0},{2,3},{3,2},{4,5},{5,4},{6,7},{7,6},{8,9},{9,8},{10,11... | collective-permute-start | bytes 4128776 | tf_op jit(solution)/shard_map/ppermute | solution.py:513
  71.2 6.5 %copy-start.1 = (bf16[384,512]{1,0:T(8,128)(2,1)S(1)}, bf16[384,512]{1,0:T(8,128)(2,1)}, u32[]{:S(2)}) copy-start(bf16[384,512]{1,0:T(8,128)(2,1)} %get-tuple-element.43) | copy-start | bytes 1179652
  72.0 11.8 %collective-permute-start.17 = (bf16[336,512]{1,0:T(8,128)(2,1)}, bf16[336,512]{1,0:T(8,128)(2,1)S(1)}, u32[]{:S(2)}, u32[]{:S(2)}) collective-permute-start(bf16[336,512]{1,0:T(8,128)(2,1)} %get-tuple-element.58), channel_id=1, source_target_pairs={{0,8},{8,0},{16,24},{24,16},{1,9},{9,1},{17,25},{25,17},{2,10},{10... | collective-permute-start | bytes 1032200 | tf_op jit(solution)/shard_map/ppermute | solution.py:513
  74.7 16.2 %collective-permute-start.18 = (bf16[336,512]{1,0:T(8,128)(2,1)S(1)}, bf16[336,512]{1,0:T(8,128)(2,1)S(1)}, u32[]{:S(2)}, u32[]{:S(2)}) collective-permute-start(bf16[336,512]{1,0:T(8,128)(2,1)S(1)} %get-tuple-element.60), channel_id=1, source_target_pairs={{0,16},{8,24},{16,0},{24,8},{1,17},{9,25},{17,1},{25,9},{2,18},{10... | collective-permute-start | bytes 1032200 | tf_op jit(solution)/shard_map/ppermute | solution.py:513
  75.6 17.9 %collective-permute-start.19 = (bf16[336,512]{1,0:T(8,128)(2,1)S(1)}, bf16[336,512]{1,0:T(8,128)(2,1)S(1)}, u32[]{:S(2)}, u32[]{:S(2)}) collective-permute-start(bf16[336,512]{1,0:T(8,128)(2,1)S(1)} %get-tuple-element.59), channel_id=1, source_target_pairs={{0,24},{8,16},{16,8},{24,0},{1,25},{9,17},{17,9},{25,1},{2,26},{10... | collective-permute-start | bytes 1032200 | tf_op jit(solution)/shard_map/ppermute | solution.py:513
  77.7 20.9 %collective-permute-start.12 = (bf16[192,512]{1,0:T(8,128)(2,1)S(1)}, bf16[192,512]{1,0:T(8,128)(2,1)S(1)}, u32[]{:S(2)}, u32[]{:S(2)}) collective-permute-start(bf16[192,512]{1,0:T(8,128)(2,1)S(1)} %slice.76), channel_id=1, source_target_pairs={{0,1},{1,0},{2,3},{3,2},{4,5},{5,4},{6,7},{7,6},{8,9},{9,8},{10,11... | collective-permute-start | bytes 589832 | tf_op jit(solution)/shard_map/ppermute | solution.py:513
  77.8 42.6 %collective-permute-start.8 = (bf16[64,512]{1,0:T(8,128)(2,1)}, bf16[64,512]{1,0:T(8,128)(2,1)S(1)}, u32[]{:S(2)}, u32[]{:S(2)}) collective-permute-start(bf16[64,512]{1,0:T(8,128)(2,1)} %get-tuple-element.39), channel_id=1, source_target_pairs={{8,0},{16,8},{24,16},{9,1},{17,9},{25,17},{10,2},{18,10},{26,18},{... | collective-permute-start | bytes 196616 | tf_op jit(solution)/shard_map/ppermute | solution.py:681
  83.8 33.7 %collective-permute-start.10 = (bf16[16,512]{1,0:T(8,128)(2,1)}, bf16[16,512]{1,0:T(8,128)(2,1)}, u32[]{:S(2)}, u32[]{:S(2)}) collective-permute-start(bf16[16,512]{1,0:T(8,128)(2,1)} %get-tuple-element.41), channel_id=1, source_target_pairs={{8,1},{9,2},{10,3},{11,4},{12,5},{13,6},{14,7},{15,0},{16,9},{17,1... | collective-permute-start | bytes 49160 | tf_op jit(solution)/shard_map/ppermute | solution.py:683
  93.7 16.0 %copy-start.20 = (bf16[16,512]{1,0:T(8,128)(2,1)S(1)}, bf16[16,512]{1,0:T(8,128)(2,1)}, u32[]{:S(2)}) copy-start(bf16[16,512]{1,0:T(8,128)(2,1)} %get-tuple-element.42) | copy-start | bytes 49156
  93.8 5.6 %collective-permute-start.20 = (bf16[96,512]{1,0:T(8,128)(2,1)S(1)}, bf16[96,512]{1,0:T(8,128)(2,1)S(1)}, u32[]{:S(2)}, u32[]{:S(2)}) collective-permute-start(bf16[96,512]{1,0:T(8,128)(2,1)S(1)} %get-tuple-element.80), channel_id=1, source_target_pairs={{0,2},{1,3},{2,0},{3,1},{4,6},{5,7},{6,4},{7,5},{8,10},{9,11},{10,... | collective-permute-start | bytes 294920 | tf_op jit(solution)/shard_map/ppermute | solution.py:513
  94.3 9.7 %collective-permute-start.21 = (bf16[96,512]{1,0:T(8,128)(2,1)S(1)}, bf16[96,512]{1,0:T(8,128)(2,1)S(1)}, u32[]{:S(2)}, u32[]{:S(2)}) collective-permute-start(bf16[96,512]{1,0:T(8,128)(2,1)S(1)} %get-tuple-element.81), channel_id=1, source_target_pairs={{0,4},{1,5},{2,6},{3,7},{4,0},{5,1},{6,2},{7,3},{8,12},{9,13},{10,... | collective-permute-start | bytes 294920 | tf_op jit(solution)/shard_map/ppermute | solution.py:513
  98.6 6.5 %collective-permute-start.22 = (bf16[96,512]{1,0:T(8,128)(2,1)S(1)}, bf16[96,512]{1,0:T(8,128)(2,1)S(1)}, u32[]{:S(2)}, u32[]{:S(2)}) collective-permute-start(bf16[96,512]{1,0:T(8,128)(2,1)S(1)} %get-tuple-element.82), channel_id=1, source_target_pairs={{0,6},{1,7},{2,4},{3,5},{4,2},{5,3},{6,0},{7,1},{8,14},{9,15},{10,... | collective-permute-start | bytes 294920 | tf_op jit(solution)/shard_map/ppermute | solution.py:513
  105.2 21.1 %copy-start.15 = (bf16[64,512]{1,0:T(8,128)(2,1)S(1)}, bf16[64,512]{1,0:T(8,128)(2,1)}, u32[]{:S(2)}) copy-start(bf16[64,512]{1,0:T(8,128)(2,1)} %get-tuple-element.40) | copy-start | bytes 196612
  105.3 4.5 %collective-permute-start.23 = (bf16[80,512]{1,0:T(8,128)(2,1)S(1)}, bf16[80,512]{1,0:T(8,128)(2,1)S(1)}, u32[]{:S(2)}, u32[]{:S(2)}) collective-permute-start(bf16[80,512]{1,0:T(8,128)(2,1)S(1)} %slice.118), channel_id=1, source_target_pairs={{0,2},{1,3},{2,0},{3,1},{4,6},{5,7},{6,4},{7,5},{8,10},{9,11},{10,... | collective-permute-start | bytes 245768 | tf_op jit(solution)/shard_map/ppermute | solution.py:513
  106.8 7.7 %collective-permute-start.24 = (bf16[80,512]{1,0:T(8,128)(2,1)S(1)}, bf16[80,512]{1,0:T(8,128)(2,1)S(1)}, u32[]{:S(2)}, u32[]{:S(2)}) collective-permute-start(bf16[80,512]{1,0:T(8,128)(2,1)S(1)} %slice.118), channel_id=1, source_target_pairs={{0,4},{1,5},{2,6},{3,7},{4,0},{5,1},{6,2},{7,3},{8,12},{9,13},{10,... | collective-permute-start | bytes 245768 | tf_op jit(solution)/shard_map/ppermute | solution.py:513
  108.2 6.3 %collective-permute-start.25 = (bf16[80,512]{1,0:T(8,128)(2,1)S(1)}, bf16[80,512]{1,0:T(8,128)(2,1)S(1)}, u32[]{:S(2)}, u32[]{:S(2)}) collective-permute-start(bf16[80,512]{1,0:T(8,128)(2,1)S(1)} %slice.118), channel_id=1, source_target_pairs={{0,6},{1,7},{2,4},{3,5},{4,2},{5,3},{6,0},{7,1},{8,14},{9,15},{10,... | collective-permute-start | bytes 245768 | tf_op jit(solution)/shard_map/ppermute | solution.py:513
  109.8 9.1 %collective-permute-start.11 = (bf16[16,512]{1,0:T(8,128)(2,1)S(1)}, bf16[16,512]{1,0:T(8,128)(2,1)S(1)}, u32[]{:S(2)}, u32[]{:S(2)}) collective-permute-start(bf16[16,512]{1,0:T(8,128)(2,1)S(1)} %copy-done.20), channel_id=1, source_target_pairs={{0,15},{1,8},{2,9},{3,10},{4,11},{5,12},{6,13},{7,14},{8,23},{9,16... | collective-permute-start | bytes 49160 | tf_op jit(solution)/shard_map/ppermute | solution.py:684
  115.3 23.0 %copy-start = (bf16[4,5,16,512]{3,2,0,1:T(8,128)(2,1)}, bf16[4,5,16,512]{3,2,0,1:T(8,128)(2,1)S(1)}, u32[]{:S(2)}) copy-start(bf16[4,5,16,512]{3,2,0,1:T(8,128)(2,1)S(1)} %copy.33) | copy-start | bytes 983044
  115.3 14.0 %collective-permute-start.26 = (bf16[320,512]{1,0:T(8,128)(2,1)S(1)}, bf16[320,512]{1,0:T(8,128)(2,1)S(1)}, u32[]{:S(2)}, u32[]{:S(2)}) collective-permute-start(bf16[320,512]{1,0:T(8,128)(2,1)S(1)} %bitcast.68), channel_id=1, source_target_pairs={{0,8},{8,0},{16,24},{24,16},{1,9},{9,1},{17,25},{25,17},{2,10},{10... | collective-permute-start | bytes 983048 | tf_op jit(solution)/shard_map/ppermute | solution.py:513
  116.5 13.3 %collective-permute-start.27 = (bf16[320,512]{1,0:T(8,128)(2,1)S(1)}, bf16[320,512]{1,0:T(8,128)(2,1)S(1)}, u32[]{:S(2)}, u32[]{:S(2)}) collective-permute-start(bf16[320,512]{1,0:T(8,128)(2,1)S(1)} %bitcast.69), channel_id=1, source_target_pairs={{0,16},{8,24},{16,0},{24,8},{1,17},{9,25},{17,1},{25,9},{2,18},{10... | collective-permute-start | bytes 983048 | tf_op jit(solution)/shard_map/ppermute | solution.py:513
  117.5 13.5 %collective-permute-start.28 = (bf16[320,512]{1,0:T(8,128)(2,1)S(1)}, bf16[320,512]{1,0:T(8,128)(2,1)S(1)}, u32[]{:S(2)}, u32[]{:S(2)}) collective-permute-start(bf16[320,512]{1,0:T(8,128)(2,1)S(1)} %bitcast.70), channel_id=1, source_target_pairs={{0,24},{8,16},{16,8},{24,0},{1,25},{9,17},{17,9},{25,1},{2,26},{10... | collective-permute-start | bytes 983048 | tf_op jit(solution)/shard_map/ppermute | solution.py:513
  118.9 12.9 %copy-start.11 = (bf16[16,512]{1,0:T(8,128)(2,1)}, bf16[16,512]{1,0:T(8,128)(2,1)S(1)}, u32[]{:S(2)}) copy-start(bf16[16,512]{1,0:T(8,128)(2,1)S(1)} %collective-permute-done.11.corner_above) | copy-start | bytes 49156
  118.9 4.4 %collective-permute-start.13 = (bf16[48,512]{1,0:T(8,128)(2,1)S(1)}, bf16[48,512]{1,0:T(8,128)(2,1)S(1)}, u32[]{:S(2)}, u32[]{:S(2)}) collective-permute-start(bf16[48,512]{1,0:T(8,128)(2,1)S(1)} %get-tuple-element.71), channel_id=1, source_target_pairs={{0,2},{1,3},{2,0},{3,1},{4,6},{5,7},{6,4},{7,5},{8,10},{9,11},{10,... | collective-permute-start | bytes 147464 | tf_op jit(solution)/shard_map/ppermute | solution.py:513
  120.4 11.4 %copy-start.9 = (bf16[64,512]{1,0:T(8,128)(2,1)}, bf16[64,512]{1,0:T(8,128)(2,1)S(1)}, u32[]{:S(2)}) copy-start(bf16[64,512]{1,0:T(8,128)(2,1)S(1)} %collective-permute-done.8.from_below) | copy-start | bytes 196612
  120.4 5.9 %collective-permute-start.14 = (bf16[48,512]{1,0:T(8,128)(2,1)S(1)}, bf16[48,512]{1,0:T(8,128)(2,1)S(1)}, u32[]{:S(2)}, u32[]{:S(2)}) collective-permute-start(bf16[48,512]{1,0:T(8,128)(2,1)S(1)} %get-tuple-element.73), channel_id=1, source_target_pairs={{0,4},{1,5},{2,6},{3,7},{4,0},{5,1},{6,2},{7,3},{8,12},{9,13},{10,... | collective-permute-start | bytes 147464 | tf_op jit(solution)/shard_map/ppermute | solution.py:513
  123.3 6.0 %collective-permute-start.15 = (bf16[48,512]{1,0:T(8,128)(2,1)S(1)}, bf16[48,512]{1,0:T(8,128)(2,1)S(1)}, u32[]{:S(2)}, u32[]{:S(2)}) collective-permute-start(bf16[48,512]{1,0:T(8,128)(2,1)S(1)} %get-tuple-element.72), channel_id=1, source_target_pairs={{0,6},{1,7},{2,4},{3,5},{4,2},{5,3},{6,0},{7,1},{8,14},{9,15},{10,... | collective-permute-start | bytes 147464 | tf_op jit(solution)/shard_map/ppermute | solution.py:513
  126.4 5.4 %collective-permute-start.9 = (bf16[64,512]{1,0:T(8,128)(2,1)S(1)}, bf16[64,512]{1,0:T(8,128)(2,1)S(1)}, u32[]{:S(2)}, u32[]{:S(2)}) collective-permute-start(bf16[64,512]{1,0:T(8,128)(2,1)S(1)} %copy-done.15), channel_id=1, source_target_pairs={{0,8},{8,16},{16,24},{1,9},{9,17},{17,25},{2,10},{10,18},{18,26},{... | collective-permute-start | bytes 196616 | tf_op jit(solution)/shard_map/ppermute | solution.py:682
  129.2 9.7 %collective-permute-start.29 = (bf16[320,512]{1,0:T(8,128)(2,1)S(1)}, bf16[320,512]{1,0:T(8,128)(2,1)S(1)}, u32[]{:S(2)}, u32[]{:S(2)}) collective-permute-start(bf16[320,512]{1,0:T(8,128)(2,1)S(1)} %bitcast.71), channel_id=1, source_target_pairs={{0,1},{1,0},{2,3},{3,2},{4,5},{5,4},{6,7},{7,6},{8,9},{9,8},{10,11... | collective-permute-start | bytes 983048 | tf_op jit(solution)/shard_map/ppermute | solution.py:513
  129.3 9.0 %copy-start.2 = (bf16[320,512]{1,0:T(8,128)(2,1)}, bf16[320,512]{1,0:T(8,128)(2,1)S(1)}, u32[]{:S(2)}) copy-start(bf16[320,512]{1,0:T(8,128)(2,1)S(1)} %collective-permute-done.26.refs_1_) | copy-start | bytes 983044
  129.3 9.6 %collective-permute-start.30 = (bf16[320,512]{1,0:T(8,128)(2,1)S(1)}, bf16[320,512]{1,0:T(8,128)(2,1)S(1)}, u32[]{:S(2)}, u32[]{:S(2)}) collective-permute-start(bf16[320,512]{1,0:T(8,128)(2,1)S(1)} %collective-permute-done.26.refs_1_), channel_id=1, source_target_pairs={{0,1},{1,0},{2,3},{3,2},{4,5},{5,4},{6,7},{7,6},{8,9},{9,8},{10,11... | collective-permute-start | bytes 983048 | tf_op jit(solution)/shard_map/ppermute | solution.py:513
  129.8 8.5 %copy-start.3 = (bf16[320,512]{1,0:T(8,128)(2,1)}, bf16[320,512]{1,0:T(8,128)(2,1)S(1)}, u32[]{:S(2)}) copy-start(bf16[320,512]{1,0:T(8,128)(2,1)S(1)} %collective-permute-done.27.refs_2_) | copy-start | bytes 983044
  129.8 9.2 %collective-permute-start.31 = (bf16[320,512]{1,0:T(8,128)(2,1)S(1)}, bf16[320,512]{1,0:T(8,128)(2,1)S(1)}, u32[]{:S(2)}, u32[]{:S(2)}) collective-permute-start(bf16[320,512]{1,0:T(8,128)(2,1)S(1)} %collective-permute-done.27.refs_2_), channel_id=1, source_target_pairs={{0,1},{1,0},{2,3},{3,2},{4,5},{5,4},{6,7},{7,6},{8,9},{9,8},{10,11... | collective-permute-start | bytes 983048 | tf_op jit(solution)/shard_map/ppermute | solution.py:513
  131.0 7.3 %copy-start.4 = (bf16[320,512]{1,0:T(8,128)(2,1)}, bf16[320,512]{1,0:T(8,128)(2,1)S(1)}, u32[]{:S(2)}) copy-start(bf16[320,512]{1,0:T(8,128)(2,1)S(1)} %collective-permute-done.28.refs_3_) | copy-start | bytes 983044
  131.0 7.9 %collective-permute-start.32 = (bf16[320,512]{1,0:T(8,128)(2,1)S(1)}, bf16[320,512]{1,0:T(8,128)(2,1)S(1)}, u32[]{:S(2)}, u32[]{:S(2)}) collective-permute-start(bf16[320,512]{1,0:T(8,128)(2,1)S(1)} %collective-permute-done.28.refs_3_), channel_id=1, source_target_pairs={{0,1},{1,0},{2,3},{3,2},{4,5},{5,4},{6,7},{7,6},{8,9},{9,8},{10,11... | collective-permute-start | bytes 983048 | tf_op jit(solution)/shard_map/ppermute | solution.py:513
  131.8 0.6 copy-start.10
  139.0 0.7 copy-start.5
  139.0 0.9 copy-start.6
  139.0 1.0 copy-start.7
  140.0 0.8 copy-start.8

commit v3 on v2

v3 whole, which is shorter than its diff:
```python
import functools

import jax
import jax.numpy as jnp
from jax import lax
from jax.experimental import pallas as pl
from jax.experimental.pallas import tpu as pltpu
from jax.sharding import PartitionSpec as P

epsilon = 1e-05
EXACT = lax.Precision.HIGHEST
ABSENT = -1000.0
VMEM_BYTES = 60 * 1024 * 1024


def dot(left, right):
    return jnp.dot(left, right, preferred_element_type=jnp.float32)


def dot_nt(left, right):
    return lax.dot_general(left, right, (((1,), (1,)), ((), ())), preferred_element_type=jnp.float32)


def dot_tn(left, right):
    return lax.dot_general(left, right, (((0,), (0,)), ((), ())), preferred_element_type=jnp.float32)


def dot_exact(left, right):
    return jnp.dot(left, right, preferred_element_type=jnp.float32, precision=EXACT)


def dot_exact_tn(left, right):
    return lax.dot_general(
        left, right, (((0,), (0,)), ((), ())), preferred_element_type=jnp.float32, precision=EXACT
    )


def to_bf16(values):
    return values.astype(jnp.bfloat16)


def to_f32(values):
    return values.astype(jnp.float32)


def half_sum_and_slope(half):
    curve = jnp.tanh(half)
    part = half * curve
    return half + part, (1.0 + curve) * (1.0 + half - part)


def eight_rows(values):
    return jnp.sum(values.reshape(-1, 8, values.shape[-1]), axis=0)


def aligned(start, multiple):
    return pl.multiple_of(start, multiple)


def pack_kernel(cols, slots, nodes, above, below, packed):
    rows = nodes.shape[0]
    count, patch_rows = slots.shape[0], rows // cols
    size = count + 2 * patch_rows
    place = lax.broadcasted_iota(jnp.int32, (size, 1), 0)
    wanted = jnp.where(
        place < count + patch_rows,
        (place - count) * cols,
        (place - count - patch_rows) * cols + cols - 1,
    )
    for k in range(count):
        wanted = jnp.where(place == k, slots[k], wanted)
    column = lax.broadcasted_iota(jnp.int32, (size, rows), 1)
    packed[pl.ds(0, size), :] = to_bf16(dot(to_bf16(to_f32(column == wanted)), nodes[...]))
    place = lax.broadcasted_iota(jnp.int32, (16, 1), 0)
    top = to_f32(above[pl.ds(0, 16), :])[0:1]
    bottom = to_f32(below[pl.ds(cols - 16, 16), :])[15:16]
    corners = jnp.where(place == 0, top, jnp.where(place == 1, bottom, 0.0))
    packed[pl.ds(size, 16), :] = to_bf16(corners)


def pack_nodes(cols, slots, nodes, above, below):
    rows, depth = nodes.shape
    count = slots.shape[0] + 2 * (rows // cols) + 16
    smem, vmem = pl.BlockSpec(memory_space=pltpu.SMEM), pl.BlockSpec(memory_space=pltpu.VMEM)
    return pl.pallas_call(
        functools.partial(pack_kernel, cols),
        in_specs=[smem, vmem, vmem, vmem],
        out_specs=vmem,
        out_shape=jax.ShapeDtypeStruct((count, depth), jnp.bfloat16),
        name="pack_nodes",
    )(slots, nodes, above, below)


def project_send_kernel(nodes, w_send, send):
    send[...] = to_bf16(dot(nodes[...], w_send[...]))


def project_own_kernel(nodes, w_recv, w_self, edge_bias, node_bias, recv_half, own):
    block = nodes[...]
    recv_half[...] = 0.5 * (dot(block, w_recv[...]) + edge_bias[...])
    own[...] = dot(block, w_self[...]) + node_bias[...]


def project(kernel, name, nodes, weights, vectors, kinds):
    rows, depth = nodes.shape
    step = 256
    whole = pl.BlockSpec((depth, depth), lambda i: (0, 0))
    vector = pl.BlockSpec((1, depth), lambda i: (0, 0))
    block = pl.BlockSpec((step, depth), lambda i: (i, 0))
    return pl.pallas_call(
        kernel,
        grid=(rows // step,),
        in_specs=[block] + [whole] * len(weights) + [vector] * len(vectors),
        out_specs=[block] * len(kinds),
        out_shape=[jax.ShapeDtypeStruct((rows, depth), kind) for kind in kinds],
        cost_estimate=pl.CostEstimate(
            flops=2 * len(weights) * rows * depth * depth,
            bytes_accessed=4_000_000 * len(weights),
            transcendentals=0,
        ),
        name=name,
    )(nodes, *weights, *vectors)


def update_kernel(
    dims,
    slots,
    long_senders,
    long_receivers,
    nodes,
    cotangent,
    send,
    recv_half,
    own,
    above,
    below,
    gathered,
    crossed,
    w_send,
    w_recv,
    w_agg,
    w_out,
    edge_bias,
    gain,
    new_nodes,
    d_pre_b,
    d_recv_b,
    d_send,
    d_up,
    d_down,
    d_gathered,
    d_crossed,
    *rest,
):
    patch_rows, cols, lon_count, coarse_count, lat_count = dims
    outs, rest = rest[: 2 * lat_count], rest[2 * lat_count :]
    (
        mid,
        right,
        left,
        slopes,
        slope_sum,
        total,
        work,
        agg_b,
        hidden_b,
        d_out_b,
        d_half,
        far,
        far_d,
        near_nodes,
        near_d,
        sums,
        coarse,
        coarse_d,
        send_hot,
        recv_hot,
        grads,
        out_sems,
    ) = rest
    rows = patch_rows * cols
    depth = nodes.shape[-1]
    pack = coarse_count + 2 * patch_rows + 16
    chip_count = lon_count // 2
    lat, lon = lax.axis_index("lat"), lax.axis_index("lon")
    core = lon % 2
    top_valid, bottom_valid = lat > 0, lat < lat_count - 1

    def place_of(other):
        apart = other ^ lon
        return (apart % 2) * chip_count + apart // 2

    right_at = place_of((lon + 1) % lon_count) * pack
    left_at = place_of((lon + lon_count - 1) % lon_count) * pack
    tile = 16

    upper, lower = pl.ds(0, cols), pl.ds(cols, cols)
    near_nodes[upper, :] = above[...]
    near_nodes[lower, :] = below[...]
    near_half = 0.5 * to_f32(to_bf16(dot(near_nodes[...], w_send[...])))
    half_far = chip_count * pack
    same, cross = pl.ds(0, half_far), pl.ds(half_far, half_far)
    far[same, :] = 0.5 * to_f32(to_bf16(dot(gathered[...], w_send[...])))
    far[cross, :] = 0.5 * to_f32(to_bf16(dot(crossed[...], w_send[...])))
    sums[...] = jnp.zeros_like(sums)
    first = lax.broadcasted_iota(jnp.int32, (cols, 1), 0) == 0
    last = lax.broadcasted_iota(jnp.int32, (cols, 1), 0) == cols - 1
    top = jnp.where(top_valid, near_half[:cols], ABSENT)
    bottom = jnp.where(bottom_valid, near_half[cols : 2 * cols], ABSENT)
    corner_at = pack - 16
    right_corners = far[pl.ds(aligned(right_at + corner_at, 16), 16), :]
    left_corners = far[pl.ds(aligned(left_at + corner_at, 16), 16), :]
    top_corner = jnp.where(top_valid, right_corners[0:1], ABSENT)
    bottom_corner = jnp.where(bottom_valid, left_corners[1:2], ABSENT)
    mid[pl.ds(0, cols), :] = top
    mid[pl.ds(rows + cols, cols), :] = bottom
    right[pl.ds(0, cols), :] = jnp.where(last, top_corner, pltpu.roll(top, cols - 1, 0))
    left[pl.ds(rows + cols, cols), :] = jnp.where(first, bottom_corner, pltpu.roll(bottom, 1, 0))

    right_edge = far[pl.ds(aligned(right_at + coarse_count, 16), patch_rows), :]
    left_edge = far[pl.ds(aligned(left_at + coarse_count + patch_rows, 16), patch_rows), :]
    for row in range(patch_rows):
        here, there = pl.ds(row * cols, cols), pl.ds((row + 1) * cols, cols)
        for lane in range(0, depth, 128):
            lanes = pl.ds(lane, 128)
            block = 0.5 * to_f32(send[here, lanes])
            mid[there, lanes] = block
            edge = right_edge[row : row + 1, lane : lane + 128]
            right[there, lanes] = jnp.where(last, edge, pltpu.roll(block, cols - 1, 0))
            edge = left_edge[row : row + 1, lane : lane + 128]
            left[there, lanes] = jnp.where(first, edge, pltpu.roll(block, 1, 0))

    senders = ((mid, 2), (mid, 0), (right, 1), (left, 1), (left, 2), (right, 0))

    def edges(step, carry):
        base = aligned(step * tile, tile)
        here = pl.ds(base, tile)
        recv = recv_half[here, :]
        summed = jnp.zeros((tile, depth), jnp.float32)
        slope_total = jnp.zeros((tile, depth), jnp.float32)
        for which, (source, shift) in enumerate(senders):
            half = source[pl.ds(aligned(base + shift * cols, tile), tile), :] + recv
            value, slope = half_sum_and_slope(half)
            summed = summed + value
            slope_total = slope_total + slope
            slopes[which, pl.ds(aligned(base + cols, tile), tile), :] = to_bf16(slope)
        total[here, :] = summed
        slope_sum[here, :] = slope_total
        return carry

    lax.fori_loop(0, rows // tile, edges, 0)

    per_source = long_senders.shape[1]
    coarse_lane = lax.broadcasted_iota(jnp.int32, (1, coarse.shape[0]), 1)
    slot_lane = lax.broadcasted_iota(jnp.int32, (1, coarse_count), 1)
    for source in range(lon_count):
        first_id = place_of(source) * coarse_count
        for edge in range(per_source):
            row = pl.ds(source * per_source + edge, 1)
            send_hot[row, :] = to_f32(coarse_lane == first_id + long_senders[source, edge])
            recv_hot[row, :] = to_f32(slot_lane == long_receivers[source, edge])
    for source in range(lon_count):
        coarse[pl.ds(source * coarse_count, coarse_count), :] = far[
            pl.ds(source * pack, coarse_count), :
        ]
    coarse_recv = 0.5 * (dot(gathered[pl.ds(0, coarse_count), :], w_recv[...]) + edge_bias[...])
    long_half = dot_exact(send_hot[...], coarse[...]) + dot_exact(
        recv_hot[...], coarse_recv
    )
    long_value, long_slope = half_sum_and_slope(long_half)
    coarse_d[...] = dot_exact_tn(recv_hot[...], long_value)
    for k in range(coarse_count):
        spot = pl.ds(slots[k], 1)
        total[spot, :] = total[spot, :] + coarse_d[pl.ds(k, 1), :]

    step_rows = 256
    blocks = [pl.ds(start, step_rows) for start in range(0, rows, step_rows)]
    for block in blocks:
        agg_b[block, :] = to_bf16(total[block, :])
        work[block, :] = 0.5 * (own[block, :] + dot(agg_b[block, :], w_agg[...]))

    def activate(step, carry):
        here = pl.ds(aligned(step * tile, tile), tile)
        half = work[here, :]
        hidden_b[here, :] = to_bf16(half + half * jnp.tanh(half))
        return carry

    lax.fori_loop(0, rows // tile, activate, 0)
    for block in blocks:
        total[block, :] = dot(hidden_b[block, :], w_out[...])

    wide = 32

    def normalise(step, carry):
        here = pl.ds(aligned(step * wide, wide), wide)
        output = total[here, :]
        cot = to_f32(cotangent[here, :])
        d_norm = cot * gain[...]
        d_mean = jnp.mean(d_norm, axis=-1, keepdims=True)
        centred = output - jnp.mean(output, axis=-1, keepdims=True)
        inv_std = lax.rsqrt(jnp.mean(centred * centred, axis=-1, keepdims=True) + epsilon)
        normed = centred * inv_std
        new_nodes[here, :] = to_bf16(to_f32(nodes[here, :]) + gain[...] * normed)
        sums[2] += eight_rows(cot * normed)
        d_dot = jnp.mean(d_norm * normed, axis=-1, keepdims=True)
        d_out_b[here, :] = to_bf16(inv_std * (d_norm - d_mean - normed * d_dot))
        return carry

    lax.fori_loop(0, rows // wide, normalise, 0, unroll=2)

    for block in blocks:
        total[block, :] = dot_nt(d_out_b[block, :], w_out[...])

    def deactivate(step, carry):
        here = pl.ds(aligned(step * tile, tile), tile)
        slope = half_sum_and_slope(work[here, :])[1]
        d_pre = total[here, :] * (0.5 * slope)
        sums[1] += eight_rows(d_pre)
        d_pre_b[here, :] = to_bf16(d_pre)
        return carry

    lax.fori_loop(0, rows // tile, deactivate, 0)
    share = depth // (2 * lat_count)

    def put(which, half_at, values):
        block = to_bf16(values)
        for place in range(lat_count):
            grads[half_at ^ core, lat ^ place, pl.ds(which * share, share), :] = block[
                place * share : (place + 1) * share
            ]

    for half_at in range(2):
        columns = pl.ds(half_at * (depth // 2), depth // 2)
        put(2, half_at, dot_tn(nodes[:, columns], d_pre_b[...]))
        put(3, half_at, dot_tn(agg_b[:, columns], d_pre_b[...]))
        put(4, half_at, dot_tn(hidden_b[:, columns], d_out_b[...]))
    d_half[pl.ds(0, cols), :] = jnp.zeros((cols, depth), jnp.float32)
    d_half[pl.ds(rows + cols, cols), :] = jnp.zeros((cols, depth), jnp.float32)
    for which in (0, 4):
        slopes[which, pl.ds(0, cols), :] = jnp.zeros((cols, depth), jnp.bfloat16)
    for which in (1, 5):
        slopes[which, pl.ds(rows + cols, cols), :] = jnp.zeros((cols, depth), jnp.bfloat16)
    for start in range(0, rows, step_rows):
        d_sum = dot_nt(d_pre_b[pl.ds(start, step_rows), :], w_agg[...])
        d_half[pl.ds(start + cols, step_rows), :] = 0.5 * to_f32(to_bf16(d_sum))

    def slope_times(which, place, lanes):
        return to_f32(slopes[which, place, lanes]) * d_half[place, lanes]

    def receive(step, carry):
        base = aligned(step * tile, tile)
        here = pl.ds(base, tile)
        value = d_half[pl.ds(aligned(base + cols, tile), tile), :] * slope_sum[here, :]
        total[here, :] = value
        sums[0] += eight_rows(value)
        return carry

    lax.fori_loop(0, rows // tile, receive, 0)
    far_d[...] = jnp.zeros_like(far_d)

    edge_place = lax.broadcasted_iota(jnp.int32, (patch_rows, 1), 0)
    for lane in range(0, depth, 128):
        lanes = pl.ds(lane, 128)
        right_edge = jnp.zeros((patch_rows, 128), jnp.float32)
        left_edge = jnp.zeros((patch_rows, 128), jnp.float32)
        for row in range(patch_rows):
            above_row, out = pl.ds(row * cols, cols), pl.ds(row * cols, cols)
            here, below_row = pl.ds((row + 1) * cols, cols), pl.ds((row + 2) * cols, cols)
            to_mid = slope_times(0, above_row, lanes) + slope_times(1, below_row, lanes)
            to_right = slope_times(2, here, lanes) + slope_times(5, below_row, lanes)
            to_left = slope_times(3, here, lanes) + slope_times(4, above_row, lanes)
            d_send[out, lanes] = (
                to_mid
                + jnp.where(first, 0.0, pltpu.roll(to_right, 1, 0))
                + jnp.where(last, 0.0, pltpu.roll(to_left, cols - 1, 0))
            )
            right_edge = jnp.where(edge_place == row, to_right[cols - 1 : cols], right_edge)
            left_edge = jnp.where(edge_place == row, to_left[0:1], left_edge)
        far_d[pl.ds(aligned(right_at + coarse_count, 16), patch_rows), lanes] = right_edge
        far_d[pl.ds(aligned(left_at + coarse_count + patch_rows, 16), patch_rows), lanes] = left_edge
    row_first, row_last = pl.ds(cols, cols), pl.ds(rows, cols)
    sixteen = lax.broadcasted_iota(jnp.int32, (16, 1), 0)
    for lane in range(0, depth, 128):
        lanes = pl.ds(lane, 128)
        to_right = slope_times(5, row_first, lanes)
        to_left = slope_times(4, row_last, lanes)
        up = slope_times(1, row_first, lanes) + jnp.where(first, 0.0, pltpu.roll(to_right, 1, 0))
        down = slope_times(0, row_last, lanes) + jnp.where(
            last, 0.0, pltpu.roll(to_left, cols - 1, 0)
        )
        near_d[upper, lanes] = to_bf16(up)
        near_d[lower, lanes] = to_bf16(down)
        corner = jnp.where(sixteen == 0, to_right[cols - 1 : cols], 0.0)
        far_d[pl.ds(aligned(right_at + corner_at, 16), 16), lanes] = corner
        corner = jnp.where(sixteen == 1, to_left[0:1], 0.0)
        far_d[pl.ds(aligned(left_at + corner_at, 16), 16), lanes] = corner
    d_up[...] = near_d[upper, :]
    d_down[...] = near_d[lower, :]

    for k in range(coarse_count):
        coarse_d[pl.ds(k, 1), :] = d_half[pl.ds(slots[k] + cols, 1), :]
    long_d = dot_exact(recv_hot[...], coarse_d[...]) * long_slope
    sums[0] += eight_rows(long_d)
    coarse_d[...] = dot_exact_tn(recv_hot[...], long_d)
    for k in range(coarse_count):
        spot = pl.ds(slots[k], 1)
        total[spot, :] = total[spot, :] + coarse_d[pl.ds(k, 1), :]
    coarse[...] = dot_exact_tn(send_hot[...], long_d)
    for source in range(lon_count):
        far_d[pl.ds(source * pack, coarse_count), :] = coarse[
            pl.ds(source * coarse_count, coarse_count), :
        ]
    d_gathered[...] = to_bf16(far_d[same, :])
    d_crossed[...] = to_bf16(far_d[cross, :])
    for block in blocks:
        d_recv_b[block, :] = to_bf16(total[block, :])
        agg_b[block, :] = to_bf16(d_send[block, :])
    for half_at in range(2):
        columns = pl.ds(half_at * (depth // 2), depth // 2)
        put(0, half_at, dot_tn(nodes[:, columns], agg_b[...])
            + dot_tn(near_nodes[:, columns], near_d[...])
            + dot_tn(gathered[:, columns], d_gathered[...])
            + dot_tn(crossed[:, columns], d_crossed[...]))
        put(1, half_at, dot_tn(nodes[:, columns], d_recv_b[...]))
    place = lax.broadcasted_iota(jnp.int32, (16, depth), 0)
    vectors = jnp.zeros((16, depth), jnp.float32)
    for which in range(3):
        vectors = jnp.where(place == which, jnp.sum(sums[which], axis=0, keepdims=True), vectors)
    for part in range(2):
        for spot in range(lat_count):
            grads[part, spot, pl.ds(5 * share, 16), :] = to_bf16(vectors)
    copies = [
        pltpu.make_async_copy(
            grads.at[part, spot], outs[part * lat_count + spot], out_sems.at[part, spot]
        )
        for part in range(2)
        for spot in range(lat_count)
    ]
    for copy in copies:
        copy.start()
    for copy in copies:
        copy.wait()


def update(dims, ints, arrays):
    patch_rows, cols, lon_count, coarse_count, lat_count = dims
    rows, depth = arrays[0].shape
    share = depth // (2 * lat_count)
    edge_count = ints[1].shape[0] * ints[1].shape[1]
    coarse_ids = lon_count * coarse_count
    far_rows = lon_count * (coarse_count + 2 * patch_rows + 16)
    near_rows = 2 * cols
    long_rows = rows + 2 * cols
    half = lambda *size: jax.ShapeDtypeStruct(size, jnp.bfloat16)
    full = lambda *size: jax.ShapeDtypeStruct(size, jnp.float32)
    vmem_full = lambda *size: pltpu.VMEM(size, jnp.float32)
    vmem_half = lambda *size: pltpu.VMEM(size, jnp.bfloat16)
    smem, vmem = pl.BlockSpec(memory_space=pltpu.SMEM), pl.BlockSpec(memory_space=pltpu.VMEM)
    return pl.pallas_call(
        functools.partial(update_kernel, dims),
        in_specs=[smem] * len(ints) + [vmem] * len(arrays),
        out_specs=[vmem] * 8 + [pl.BlockSpec(memory_space=pl.ANY)] * (2 * lat_count),
        out_shape=[half(rows, depth)] * 3
        + [full(rows, depth)]
        + [half(cols, depth)] * 2
        + [half(far_rows // 2, depth)] * 2
        + [half(5 * share + 16, depth)] * (2 * lat_count),
        scratch_shapes=[vmem_full(long_rows, depth)] * 3
        + [vmem_half(6, long_rows, depth)]
        + [vmem_full(rows, depth)] * 3
        + [vmem_half(rows, depth)] * 3
        + [vmem_full(long_rows, depth)]
        + [vmem_full(far_rows, depth)] * 2
        + [vmem_half(near_rows, depth)] * 2
        + [
            vmem_full(3, 8, depth),
            vmem_full(coarse_ids, depth),
            vmem_full(coarse_count, depth),
            vmem_full(edge_count, coarse_ids),
            vmem_full(edge_count, coarse_count),
            vmem_half(2, lat_count, 5 * share + 16, depth),
            pltpu.SemaphoreType.DMA((2, lat_count)),
        ],
        compiler_params=pltpu.CompilerParams(vmem_limit_bytes=VMEM_BYTES),
        cost_estimate=pl.CostEstimate(
            flops=20 * rows * depth * depth, bytes_accessed=20_000_000, transcendentals=0
        ),
        name="update",
    )(*ints, *arrays)


def finish_kernel(dims, slots, *refs):
    patch_rows, cols, _, coarse_count, lat_count = dims
    rows = patch_rows * cols
    (
        cotangent,
        d_pre_b,
        d_recv_b,
        d_send,
        from_below,
        from_above,
        back,
        w_self,
        w_recv,
        w_send,
        grad_nodes,
        total,
    ) = refs
    step_rows = 256
    for start in range(0, rows, step_rows):
        block = pl.ds(start, step_rows)
        total[block, :] = d_send[block, :]
    for start, part in ((rows - cols, from_below), (0, from_above)):
        total[pl.ds(start, cols), :] += to_f32(part[...])
    returned = back[...]
    for row in range(patch_rows):
        for spot, at in ((row * cols, 0), (row * cols + cols - 1, patch_rows)):
            one = coarse_count + at + row
            total[pl.ds(spot, 1), :] += returned[one : one + 1]
    for k in range(coarse_count):
        total[pl.ds(slots[k], 1), :] += returned[k : k + 1]
    for start in range(0, rows, step_rows):
        block = pl.ds(start, step_rows)
        grad_nodes[block, :] = to_bf16(
            to_f32(cotangent[block, :])
            + dot_nt(d_pre_b[block, :], w_self[...])
            + dot_nt(d_recv_b[block, :], w_recv[...])
            + dot_nt(to_bf16(total[block, :]), w_send[...])
        )


def finish(dims, slots, arrays):
    rows, depth = arrays[0].shape
    smem, vmem = pl.BlockSpec(memory_space=pltpu.SMEM), pl.BlockSpec(memory_space=pltpu.VMEM)
    return pl.pallas_call(
        functools.partial(finish_kernel, dims),
        in_specs=[smem] + [vmem] * len(arrays),
        out_specs=vmem,
        out_shape=jax.ShapeDtypeStruct((rows, depth), jnp.bfloat16),
        scratch_shapes=[pltpu.VMEM((rows, depth), jnp.float32)],
        compiler_params=pltpu.CompilerParams(vmem_limit_bytes=VMEM_BYTES),
        cost_estimate=pl.CostEstimate(
            flops=6 * rows * depth * depth, bytes_accessed=8_000_000, transcendentals=0
        ),
        name="finish",
    )(slots, *arrays)


def swapped(values, axis, bit):
    count = lax.axis_size(axis)
    return lax.ppermute(values, axis, [(i, i ^ bit) for i in range(count)])


def summed_part(mine, other, returning, borders):
    lat_count, depth = len(mine), mine[0].shape[-1]
    chip_count = lax.axis_size("lon") // 2
    chip = lax.axis_index("lon") // 2
    share = depth // (2 * lat_count)
    order = list(range(lat_count - 1, -1, -1))
    crossed = {step: swapped(other[step], "lon", 1) for step in order}
    received = []
    for step in order[:-1]:
        message = to_bf16(to_f32(mine[step]) + to_f32(crossed[step]))
        received.append(swapped(message, "lat", step))
    received, returned = lax.optimization_barrier((received, returning()))
    total = to_f32(mine[0]) + to_f32(crossed[0])
    for part in received:
        total = total + to_f32(part)
    total = to_bf16(total)
    vectors = total[5 * share :]
    parts = total[: 5 * share].reshape(5, chip_count, share // chip_count, depth)

    def message_for(step):
        part = lax.dynamic_index_in_dim(parts, chip ^ step, axis=1, keepdims=False)
        return jnp.concatenate([part.reshape(-1, depth), vectors])

    received = [swapped(message_for(step), "lon", 2 * step) for step in range(1, chip_count)]
    received[0], returned = lax.optimization_barrier((received[0], returned))
    received, bordered = lax.optimization_barrier((received, borders(returned)))
    total = to_f32(message_for(0))
    for part in received:
        total = total + to_f32(part)
    return total, returned, bordered


def gathered_shares(total, lat_count, meanwhile):
    depth = total.shape[-1]
    share = depth // (2 * lat_count)
    chip_count = lax.axis_size("lon") // 2
    chip = lax.axis_index("lon") // 2
    part = to_bf16(total[: 5 * share // chip_count])
    parts = jnp.stack([part] + [swapped(part, "lon", 2 * k) for k in range(1, chip_count)])
    parts = parts[chip ^ jnp.arange(chip_count)].reshape(chip_count, 5, -1, depth)
    ready = jnp.transpose(parts, (1, 0, 2, 3)).reshape(5 * share, depth)
    shares = tuple(swapped(ready, "lat", step) for step in range(1, lat_count))
    shares, meanwhile = lax.optimization_barrier((shares, meanwhile))
    shares = [ready, *shares]
    return shares + [swapped(part, "lon", 1) for part in shares], meanwhile


def unpack_kernel(lat_count, scale, total, *refs):
    shares, outs = refs[: 2 * lat_count], refs[2 * lat_count : 2 * lat_count + 8]
    staged, sems = refs[2 * lat_count + 8 :]
    depth = total.shape[-1]
    share = depth // (2 * lat_count)
    core, lat = lax.axis_index("lon") % 2, lax.axis_index("lat")
    copies = []
    for which in range(5):
        for flip in range(2):
            for step in range(lat_count):
                start = (core ^ flip) * (depth // 2) + (lat ^ step) * share
                block = shares[flip * lat_count + step][pl.ds(which * share, share), :]
                staged[which, pl.ds(aligned(start, share), share), :] = scale * to_f32(block)
        copies.append(pltpu.make_async_copy(staged.at[which], outs[which], sems.at[which]))
        copies[-1].start()
    vectors_at = 5 * share // (lax.axis_size("lon") // 2)
    for which in range(3):
        outs[5 + which][...] = scale * total[pl.ds(vectors_at + which, 1), :]
    for copy in copies:
        copy.wait()


def unpack(lat_count, scale, total, shares):
    depth = total.shape[-1]
    vmem = pl.BlockSpec(memory_space=pltpu.VMEM)
    shape = jax.ShapeDtypeStruct
    return pl.pallas_call(
        functools.partial(unpack_kernel, lat_count, scale),
        in_specs=[vmem] * (1 + len(shares)),
        out_specs=[pl.BlockSpec(memory_space=pl.ANY)] * 5 + [vmem] * 3,
        out_shape=[shape((depth, depth), jnp.float32)] * 5 + [shape((1, depth), jnp.float32)] * 3,
        scratch_shapes=[
            pltpu.VMEM((5, depth, depth), jnp.float32),
            pltpu.SemaphoreType.DMA((5,)),
        ],
        compiler_params=pltpu.CompilerParams(vmem_limit_bytes=VMEM_BYTES),
        name="unpack",
    )(total, *shares)


def on_device(
    nodes,
    cotangent,
    w_send,
    w_recv,
    edge_bias,
    w_self,
    w_agg,
    node_bias,
    w_out,
    gain,
    coarse_slots,
    long_senders,
    long_receivers,
):
    patch_rows, cols, depth = nodes.shape
    rows = patch_rows * cols
    lat_count, lon_count = lax.axis_size("lat"), lax.axis_size("lon")
    chip_count = lon_count // 2
    lon = lax.axis_index("lon")
    scale = float(rows * lat_count * lon_count) ** (-0.5)
    slots = coarse_slots.reshape(-1)
    coarse_count = slots.shape[0]
    dims = (patch_rows, cols, lon_count, coarse_count, lat_count)
    flat = nodes.reshape(rows, depth)
    cot = cotangent.reshape(rows, depth)

    down = [(i, i + 1) for i in range(lat_count - 1)]
    up = [(i + 1, i) for i in range(lat_count - 1)]
    above = lax.ppermute(flat[-cols:], "lat", down)
    below = lax.ppermute(flat[:cols], "lat", up)
    bias, offset = edge_bias[None], node_bias[None]
    (send,) = project(project_send_kernel, "project_send", flat, [w_send], [], [jnp.bfloat16])
    above, below, send = lax.optimization_barrier((above, below, send))
    packed = pack_nodes(cols, slots, flat, above, below)
    chips = [swapped(packed, "lon", 2 * k) for k in range(1, chip_count)]
    recv_half, own = project(
        project_own_kernel, "project_own", flat, [w_recv, w_self], [bias, offset], [jnp.float32] * 2
    )
    chips, recv_half, own = lax.optimization_barrier((chips, recv_half, own))
    gathered = jnp.concatenate([packed, *chips])
    crossed = swapped(gathered, "lon", 1)
    outs = update(
        dims,
        (slots, long_senders.reshape(lon_count, -1), long_receivers.reshape(lon_count, -1)),
        (
            flat,
            cot,
            send,
            recv_half,
            own,
            above,
            below,
            gathered,
            crossed,
            w_send,
            w_recv,
            w_agg,
            w_out,
            bias,
            gain[None],
        ),
    )
    new_nodes, d_pre_b, d_recv_b, d_send, d_up, d_down, d_gathered, d_crossed = outs[:8]
    mine, other = outs[8 : 8 + lat_count], outs[8 + lat_count :]

    def returning():
        chips = to_bf16(to_f32(d_gathered) + to_f32(swapped(d_crossed, "lon", 1)))
        parts = chips.reshape(chip_count, -1, depth)
        received = [swapped(parts[step], "lon", 2 * step) for step in range(1, chip_count)]
        return sum([to_f32(one) for one in received], to_f32(parts[0]))

    def borders(back):
        corners = to_bf16(back[-16:-14])
        ups = jnp.concatenate([to_bf16(to_f32(d_up[:1]) + to_f32(corners[:1])), d_up[1:]])
        downs = jnp.concatenate([d_down[:-1], to_bf16(to_f32(d_down[-1:]) + to_f32(corners[1:]))])
        return lax.ppermute(ups, "lat", up), lax.ppermute(downs, "lat", down)

    total, back, bordered = summed_part(mine, other, returning, borders)
    grad_nodes = finish(
        dims,
        slots,
        (
            cot,
            d_pre_b,
            d_recv_b,
            d_send,
            *bordered,
            back,
            w_self,
            w_recv,
            w_send,
        ),
    )
    shares, grad_nodes = gathered_shares(total, lat_count, grad_nodes)
    outs = unpack(lat_count, scale, total, shares)
    return (
        new_nodes.reshape(patch_rows, cols, depth),
        grad_nodes.reshape(patch_rows, cols, depth),
        outs[0],
        outs[1],
        outs[5][0],
        outs[2],
        outs[3],
        outs[6][0],
        outs[4],
        outs[7][0],
    )


def solution(mesh):
    patches = P("lat", "lon", None)
    edges = P("lat", "lon", None, None)
    return jax.shard_map(
        on_device,
        mesh=mesh,
        in_specs=(patches, patches) + (P(),) * 8 + (patches, edges, edges),
        out_specs=(patches, patches) + (P(),) * 8,
        check_vma=False,
    )
```

time: 146 us -> 132 us (0.904)
  starting transfers between devices: 49.8 us -> 39 us
  local copies, waits for them, and re-layouts: 13 us -> 3.98 us
  Pallas kernels: 48 us -> 53 us
  waiting for transfers between devices: 28.4 us -> 31.8 us
  other arithmetic: 4.63 us -> 2.71 us
    ppermute x6 -> x2, starting transfers between devices: 13.8 us -> 4.07 us  [borders(): return (lax.ppermute(ups, 'lat', up), lax.ppermute(downs, 'lat', down))]
    pallas_call x1 -> x3, Pallas kernels: 5.44 us -> 11.2 us  [the longest x2 8.98 us: project(): pl.pallas_call(kernel, grid=(rows // step,), in_specs=[block] + [whole] *...]
    ppermute x6 -> x2, waiting for transfers between devices: 0.02 us -> 4.79 us  [borders(): return (lax.ppermute(ups, 'lat', up), lax.ppermute(downs, 'lat', down))]
    slice x8 -> x5, local copies, waits for them, and re-layouts: 2.43 us -> 0.07 us  [the longest x1 0.02 us: summed_part(): parts = total[:5 * share].reshape(5, chip_count, share // chip_count, depth)]
    ppermute x25 -> x28, waiting for transfers between devices: 28.3 us -> 26.2 us  [swapped(): return lax.ppermute(values, axis, [(i, i ^ bit) for i in range(count)])]
    gather x2 -> x1, local copies, waits for them, and re-layouts: 2.64 us -> 0.57 us  [gathered_shares(): parts[chip ^ jnp.arange(chip_count)].reshape(chip_count, 5, -1, depth)]
    another operation x4 -> x1, local copies, waits for them, and re-layouts: 1.97 us -> 0.01 us  [gathered_shares(): jnp.stack([part] + [swapped(part, 'lon', 2 * k) for k in range(1, chip_co...]
    ppermute x25 -> x28, starting transfers between devices: 30.6 us -> 28.8 us  [swapped(): return lax.ppermute(values, axis, [(i, i ^ bit) for i in range(count)])]
  transfers between devices with their start and end apart: 33 -> 32, of which waited for: 11 -> 17; matrix products, arithmetic and copies ran while one was open for 6% -> 2% of each run, Pallas kernels for 8% -> 11%
where the time goes in v3:
time: 132 us
  Pallas kernels  53 us (40%)
  starting transfers between devices  39 us (30%)
  waiting for transfers between devices  31.8 us (24%)
  local copies, waits for them, and re-layouts  3.98 us (3%)
  other arithmetic  2.71 us (2%)
    pallas_call x1, Pallas kernels, update(): pl.pallas_call(functools.partial(update_kernel, dims), in_specs=[smem] *...  31.1 us
    ppermute x28, starting transfers between devices, swapped(): return lax.ppermute(values, axis, [(i, i ^ bit) for i in range(count)])  28.8 us
    ppermute x28, waiting for transfers between devices, swapped(): return lax.ppermute(values, axis, [(i, i ^ bit) for i in range(count)])  26.2 us
    pallas_call x2, Pallas kernels, project(): pl.pallas_call(kernel, grid=(rows // step,), in_specs=[block] + [whole] *...  8.98 us
    pallas_call x1, Pallas kernels, finish(): pl.pallas_call(functools.partial(finish_kernel, dims), in_specs=[smem] +...  5.87 us
    ppermute x1, starting transfers between devices, on_device(): above = lax.ppermute(flat[-cols:], 'lat', down)  4.85 us
    ppermute x2, waiting for transfers between devices, borders(): return (lax.ppermute(ups, 'lat', up), lax.ppermute(downs, 'lat', down))  4.79 us
    pallas_call x1, Pallas kernels, unpack(): pl.pallas_call(functools.partial(unpack_kernel, lat_count, scale), in_spe...  4.79 us
  transfers between devices with their start and end apart: 32, of which 17 were waited for; matrix products, arithmetic and copies ran while one was open for 2% of the time, Pallas kernels for 11%

profile of v3, /device:TPU:0, one launch (start us, length us, event | category | flops | bytes accessed | tf_op | source)
XLA Modules:
  0.0 131.6 jit_solution(8058953812615199182)
XLA Ops:
  0.6 0.9 slice_bitcast_fusion
  1.5 4.8 %collective-permute-start = (bf16[64,512]{1,0:T(8,128)(2,1)S(1)}, bf16[64,512]{1,0:T(8,128)(2,1)S(1)}, u32[]{:S(2)}, u32[]{:S(2)}) collective-permute-start(bf16[64,512]{1,0:T(8,128)(2,1)S(1)} %get-tuple-element.109), channel_id=1, source_target_pairs={{0,8},{8,16},{16,24},{1,9},{9,17},{17,25},{2,10},{10,18},{18,26},{... | collective-permute-start | bytes 196616 | tf_op jit(solution)/shard_map/ppermute | solution.py:670
  6.4 1.3 collective-permute-start.1
  7.7 4.1 %project_send.1.send = bf16[1024,512]{1,0:T(8,128)(2,1)} custom-call(bf16[1024,512]{1,0:T(8,128)(2,1)} %bitcast.34, bf16[512,512]{1,0:T(8,128)(2,1)} %refs_9_.1), custom_call_target="tpu_custom_call" | custom-call | flops 536870912 | bytes 4000000 | tf_op jit(solution)/shard_map/project_send/pallas_call | solution.py:110
  11.8 0.7 collective-permute-done.1.below
  12.5 0.6 copy-done.20
  13.2 2.2 %pack_nodes.1 = bf16[64,512]{1,0:T(8,128)(2,1)} custom-call(s32[16]{0:T(128)} %bitcast.56, bf16[1024,512]{1,0:T(8,128)(2,1)} %bitcast.35, bf16[64,512]{1,0:T(8,128)(2,1)} %copy-done.19, bf16[64,512]{1,0:T(8,128)(2,1)} %copy-done.20), custom_call_target="tpu_custom_call" | custom-call | tf_op jit(solution)/shard_map/pack_nodes/pallas_call | solution.py:85
  15.4 1.6 %collective-permute-start.2 = (bf16[64,512]{1,0:T(8,128)(2,1)}, bf16[64,512]{1,0:T(8,128)(2,1)S(1)}, u32[]{:S(2)}, u32[]{:S(2)}) collective-permute-start(bf16[64,512]{1,0:T(8,128)(2,1)} %pack_nodes.1), channel_id=1, source_target_pairs={{0,2},{1,3},{2,0},{3,1},{4,6},{5,7},{6,4},{7,5},{8,10},{9,11},{10,... | collective-permute-start | bytes 196616 | tf_op jit(solution)/shard_map/ppermute | solution.py:551
  16.9 2.6 %collective-permute-start.3 = (bf16[64,512]{1,0:T(8,128)(2,1)}, bf16[64,512]{1,0:T(8,128)(2,1)S(1)}, u32[]{:S(2)}, u32[]{:S(2)}) collective-permute-start(bf16[64,512]{1,0:T(8,128)(2,1)} %pack_nodes.1), channel_id=1, source_target_pairs={{0,4},{1,5},{2,6},{3,7},{4,0},{5,1},{6,2},{7,3},{8,12},{9,13},{10,... | collective-permute-start | bytes 196616 | tf_op jit(solution)/shard_map/ppermute | solution.py:551
  19.5 0.2 collective-permute-start.4
  19.7 4.9 %project_own.1 = (f32[1024,512]{1,0:T(8,128)}, f32[1024,512]{1,0:T(8,128)}) custom-call(bf16[1024,512]{1,0:T(8,128)(2,1)} %bitcast.36, bf16[512,512]{1,0:T(8,128)(2,1)} %refs_8_.1, bf16[512,512]{1,0:T(8,128)(2,1)} %refs_7_.1, f32[1,512]{1,0:T(1,128)} %bitcast.62, f32[1,512]{1,0:T(1,128)} %bitcast.61), custom_call_target="tpu_custom_call" | custom-call | flops 1073741824 | bytes 8000000 | tf_op jit(solution)/shard_map/project_own/pallas_call | solution.py:110
  24.6 1.2 collective-permute-done.4
  25.8 0.1 collective-permute-start.5
  25.9 1.5 %collective-permute-done.5.crossed = bf16[256,512]{1,0:T(8,128)(2,1)S(1)} collective-permute-done((bf16[256,512]{1,0:T(8,128)(2,1)S(1)}, bf16[256,512]{1,0:T(8,128)(2,1)S(1)}, u32[]{:S(2)}, u32[]{:S(2)}) %collective-permute-start.5) | collective-permute-done | bytes 262176 | tf_op jit(solution)/shard_map/ppermute | solution.py:551
  27.4 0.7 copy-done.21
  28.2 31.1 %update.1 = (bf16[1024,512]{1,0:T(8,128)(2,1)}, bf16[1024,512]{1,0:T(8,128)(2,1)}, bf16[1024,512]{1,0:T(8,128)(2,1)}, f32[1024,512]{1,0:T(8,128)}, bf16[64,512]{...) custom-call(s32[16]{0:T(128)} %bitcast.57, ...), custom_call_target="tpu_custom_call" | custom-call | flops 5368709120 | bytes 20000000 | tf_op jit(solution)/shard_map/update/pallas_call | solution.py:459
  59.3 0.2 collective-permute-start.13
  59.5 0.4 collective-permute-start.11
  59.9 0.1 collective-permute-start.9
  60.0 0.4 collective-permute-start.7
  60.4 0.7 collective-permute-done.13
  61.1 1.0 add_convert_fusion.4
  62.2 0.1 collective-permute-start.14
  62.3 3.0 %collective-permute-start.15 = (bf16[64,512]{1,0:T(8,128)(2,1)S(1)}, bf16[64,512]{1,0:T(8,128)(2,1)S(1)}, u32[]{:S(2)}, u32[]{:S(2)}) collective-permute-start(bf16[64,512]{1,0:T(8,128)(2,1)S(1)} %get-tuple-element.116), channel_id=1, source_target_pairs={{0,4},{1,5},{2,6},{3,7},{4,0},{5,1},{6,2},{7,3},{8,12},{9,13},{10,... | collective-permute-start | bytes 196616 | tf_op jit(solution)/shard_map/ppermute | solution.py:551
  65.3 1.1 add_convert_fusion.1
  66.3 2.5 %collective-permute-start.12 = (bf16[336,512]{1,0:T(8,128)(2,1)S(1)}, bf16[336,512]{1,0:T(8,128)(2,1)S(1)}, u32[]{:S(2)}, u32[]{:S(2)}) collective-permute-start(bf16[336,512]{1,0:T(8,128)(2,1)S(1)} %add_convert_fusion.1), channel_id=1, source_target_pairs={{0,8},{8,0},{16,24},{24,16},{1,9},{9,1},{17,25},{25,17},{2,10},{10... | collective-permute-start | bytes 1032200 | tf_op jit(solution)/shard_map/ppermute | solution.py:551
  68.8 0.1 add_convert_fusion.2
  68.9 1.1 collective-permute-start.10
  70.0 0.1 add_convert_fusion.3
  70.1 1.0 collective-permute-start.8
  71.1 1.4 %collective-permute-start.16 = (bf16[64,512]{1,0:T(8,128)(2,1)S(1)}, bf16[64,512]{1,0:T(8,128)(2,1)S(1)}, u32[]{:S(2)}, u32[]{:S(2)}) collective-permute-start(bf16[64,512]{1,0:T(8,128)(2,1)S(1)} %get-tuple-element.115), channel_id=1, source_target_pairs={{0,6},{1,7},{2,4},{3,5},{4,2},{5,3},{6,0},{7,1},{8,14},{9,15},{10,... | collective-permute-start | bytes 196616 | tf_op jit(solution)/shard_map/ppermute | solution.py:551
  72.5 4.9 %collective-permute-done.16 = bf16[64,512]{1,0:T(8,128)(2,1)S(1)} collective-permute-done((bf16[64,512]{1,0:T(8,128)(2,1)S(1)}, bf16[64,512]{1,0:T(8,128)(2,1)S(1)}, u32[]{:S(2)}, u32[]{:S(2)}) %collective-permute-start.16) | collective-permute-done | bytes 65568 | tf_op jit(solution)/shard_map/ppermute | solution.py:551
  77.4 0.3 collective-permute-done.12
  77.7 6.5 %collective-permute-done.10 = bf16[336,512]{1,0:T(8,128)(2,1)S(1)} collective-permute-done((bf16[336,512]{1,0:T(8,128)(2,1)S(1)}, bf16[336,512]{1,0:T(8,128)(2,1)S(1)}, u32[]{:S(2)}, u32[]{:S(2)}) %collective-permute-start.10) | collective-permute-done | bytes 344096 | tf_op jit(solution)/shard_map/ppermute | solution.py:551
  84.2 1.4 %collective-permute-done.8 = bf16[336,512]{1,0:T(8,128)(2,1)S(1)} collective-permute-done((bf16[336,512]{1,0:T(8,128)(2,1)S(1)}, bf16[336,512]{1,0:T(8,128)(2,1)S(1)}, u32[]{:S(2)}, u32[]{:S(2)}) %collective-permute-start.8) | collective-permute-done | bytes 344096 | tf_op jit(solution)/shard_map/ppermute | solution.py:551
  85.6 0.2 add_convert_fusion
  86.0 0.4 collective-permute-start.17
  86.4 1.7 %collective-permute-start.18 = (bf16[96,512]{1,0:T(8,128)(2,1)S(1)}, bf16[96,512]{1,0:T(8,128)(2,1)S(1)}, u32[]{:S(2)}, u32[]{:S(2)}) collective-permute-start(bf16[96,512]{1,0:T(8,128)(2,1)S(1)} %get-tuple-element.121), channel_id=1, source_target_pairs={{0,4},{1,5},{2,6},{3,7},{4,0},{5,1},{6,2},{7,3},{8,12},{9,13},{10,... | collective-permute-start | bytes 294920 | tf_op jit(solution)/shard_map/ppermute | solution.py:551
  88.1 2.4 %collective-permute-start.19 = (bf16[96,512]{1,0:T(8,128)(2,1)S(1)}, bf16[96,512]{1,0:T(8,128)(2,1)S(1)}, u32[]{:S(2)}, u32[]{:S(2)}) collective-permute-start(bf16[96,512]{1,0:T(8,128)(2,1)S(1)} %get-tuple-element.119), channel_id=1, source_target_pairs={{0,6},{1,7},{2,4},{3,5},{4,2},{5,3},{6,0},{7,1},{8,14},{9,15},{10,... | collective-permute-start | bytes 294920 | tf_op jit(solution)/shard_map/ppermute | solution.py:551
  90.5 0.3 collective-permute-done.17
  90.9 2.6 %collective-permute-start.21 = (bf16[64,512]{1,0:T(8,128)(2,1)S(1)}, bf16[64,512]{1,0:T(8,128)(2,1)S(1)}, u32[]{:S(2)}, u32[]{:S(2)}) collective-permute-start(bf16[64,512]{1,0:T(8,128)(2,1)S(1)} %pad_maximum_fusion.7), channel_id=1, source_target_pairs={{0,8},{8,16},{16,24},{1,9},{9,17},{17,25},{2,10},{10,18},{18,26},{... | collective-permute-start | bytes 196616 | tf_op jit(solution)/shard_map/ppermute | solution.py:717
  93.6 1.5 %collective-permute-start.20 = (bf16[64,512]{1,0:T(8,128)(2,1)S(1)}, bf16[64,512]{1,0:T(8,128)(2,1)S(1)}, u32[]{:S(2)}, u32[]{:S(2)}) collective-permute-start(bf16[64,512]{1,0:T(8,128)(2,1)S(1)} %pad_maximum_fusion.6), channel_id=1, source_target_pairs={{8,0},{16,8},{24,16},{9,1},{17,9},{25,17},{10,2},{18,10},{26,18},{... | collective-permute-start | bytes 196616 | tf_op jit(solution)/shard_map/ppermute | solution.py:717
  95.1 1.0 collective-permute-done.18
  96.1 4.8 %collective-permute-done.20.refs_4_ = bf16[64,512]{1,0:T(8,128)(2,1)S(1)} collective-permute-done((bf16[64,512]{1,0:T(8,128)(2,1)S(1)}, bf16[64,512]{1,0:T(8,128)(2,1)S(1)}, u32[]{:S(2)}, u32[]{:S(2)}) %collective-permute-start.20) | collective-permute-done | bytes 65568 | tf_op jit(solution)/shard_map/ppermute | solution.py:717
  100.9 0.1 collective-permute-start.22
  101.0 1.0 collective-permute-start.23
  102.0 3.4 %collective-permute-start.24 = (bf16[80,512]{1,0:T(8,128)(2,1)S(1)}, bf16[80,512]{1,0:T(8,128)(2,1)S(1)}, u32[]{:S(2)}, u32[]{:S(2)}) collective-permute-start(bf16[80,512]{1,0:T(8,128)(2,1)S(1)} %slice.104), channel_id=1, source_target_pairs={{0,6},{1,7},{2,4},{3,5},{4,2},{5,3},{6,0},{7,1},{8,14},{9,15},{10,... | collective-permute-start | bytes 245768 | tf_op jit(solution)/shard_map/ppermute | solution.py:551
  105.5 1.0 collective-permute-done.23
  106.4 2.4 %collective-permute-done.24 = bf16[80,512]{1,0:T(8,128)(2,1)S(1)} collective-permute-done((bf16[80,512]{1,0:T(8,128)(2,1)S(1)}, bf16[80,512]{1,0:T(8,128)(2,1)S(1)}, u32[]{:S(2)}, u32[]{:S(2)}) %collective-permute-start.24) | collective-permute-done | bytes 81952 | tf_op jit(solution)/shard_map/ppermute | solution.py:551
  108.8 0.6 gather_fusion
  109.5 3.0 %collective-permute-start.25 = (bf16[320,512]{1,0:T(8,128)(2,1)S(1)}, bf16[320,512]{1,0:T(8,128)(2,1)S(1)}, u32[]{:S(2)}, u32[]{:S(2)}) collective-permute-start(bf16[320,512]{1,0:T(8,128)(2,1)S(1)} %bitcast.40), channel_id=1, source_target_pairs={{0,8},{8,0},{16,24},{24,16},{1,9},{9,1},{17,25},{25,17},{2,10},{10... | collective-permute-start | bytes 983048 | tf_op jit(solution)/shard_map/ppermute | solution.py:551
  112.4 1.5 %collective-permute-start.27 = (bf16[320,512]{1,0:T(8,128)(2,1)S(1)}, bf16[320,512]{1,0:T(8,128)(2,1)S(1)}, u32[]{:S(2)}, u32[]{:S(2)}) collective-permute-start(bf16[320,512]{1,0:T(8,128)(2,1)S(1)} %bitcast.42), channel_id=1, source_target_pairs={{0,24},{8,16},{16,8},{24,0},{1,25},{9,17},{17,9},{25,1},{2,26},{10... | collective-permute-start | bytes 983048 | tf_op jit(solution)/shard_map/ppermute | solution.py:551
  114.0 5.9 %finish.1 = bf16[1024,512]{1,0:T(8,128)(2,1)} custom-call(s32[16]{0:T(128)} %bitcast.58, bf16[1024,512]{1,0:T(8,128)(2,1)} %bitcast.46, bf16[1024,512]{1,0:T(8,128)(2,1)} %get-tuple-element.91.refs_1_, bf16[1024,512]{1,0:T(8,128)(2,1)} %get-tuple-element.92.refs_2_, f32[1024,512]{1,0:T(8,128)} %get-tuple-element.93.refs_3_, bf16[64,512]{1,0:T(8,128)(2,1)} %copy-done.18, ...), custom_call_target="tpu_custom_call" | custom-call | flops 1610612736 | bytes 8000000 | tf_op jit(solution)/shard_map/finish/pallas_call | solution.py:535
  119.9 0.1 collective-permute-start.28
  120.0 3.1 %collective-permute-done.26.refs_2_ = bf16[320,512]{1,0:T(8,128)(2,1)S(1)} collective-permute-done((bf16[320,512]{1,0:T(8,128)(2,1)S(1)}, bf16[320,512]{1,0:T(8,128)(2,1)S(1)}, u32[]{:S(2)}, u32[]{:S(2)}) %collective-permute-start.26) | collective-permute-done | bytes 327712 | tf_op jit(solution)/shard_map/ppermute | solution.py:551
  123.0 0.1 collective-permute-start.29
  123.1 0.5 collective-permute-start.30
  123.6 0.1 collective-permute-start.31
  123.7 1.0 collective-permute-done.29.refs_5_
  124.7 0.5 collective-permute-done.30.refs_6_
  125.2 0.5 collective-permute-done.31.refs_7_
  125.7 0.2 copy-done.11
  125.9 0.7 copy-done.12
  126.7 4.8 %unpack.1 = (f32[512,512]{1,0:T(8,128)}, f32[512,512]{1,0:T(8,128)}, f32[512,512]{1,0:T(8,128)}, f32[512,512]{1,0:T(8,128)}, f32[512,512]{1,0:T(8,128)}, /*index...) custom-call(f32[96,512]{1,0:T(8,128)} %copy-done, bf16[320,512]{1,0:T(8,128)(2,1)} %bitcast.44, ...), custom_call_target="tpu_custom_call" | custom-call | tf_op jit(solution)/shard_map/unpack/pallas_call | solution.py:627
  (76 shorter events, 0.5 us)
Async XLA Ops:
  1.5 10.3 %collective-permute-start = (bf16[64,512]{1,0:T(8,128)(2,1)S(1)}, bf16[64,512]{1,0:T(8,128)(2,1)S(1)}, u32[]{:S(2)}, u32[]{:S(2)}) collective-permute-start(bf16[64,512]{1,0:T(8,128)(2,1)S(1)} %get-tuple-element.109), channel_id=1, source_target_pairs={{0,8},{8,16},{16,24},{1,9},{9,17},{17,25},{2,10},{10,18},{18,26},{... | collective-permute-start | bytes 196616 | tf_op jit(solution)/shard_map/ppermute | solution.py:670
  6.4 6.2 %collective-permute-start.1 = (bf16[64,512]{1,0:T(8,128)(2,1)S(1)}, bf16[64,512]{1,0:T(8,128)(2,1)S(1)}, u32[]{:S(2)}, u32[]{:S(2)}) collective-permute-start(bf16[64,512]{1,0:T(8,128)(2,1)S(1)} %get-tuple-element.108), channel_id=1, source_target_pairs={{8,0},{16,8},{24,16},{9,1},{17,9},{25,17},{10,2},{18,10},{26,18},{... | collective-permute-start | bytes 196616 | tf_op jit(solution)/shard_map/ppermute | solution.py:671
  11.8 0.7 copy-start.19
  12.5 0.6 copy-start.20
  15.4 10.4 %copy-start.14 = (bf16[64,512]{1,0:T(8,128)(2,1)S(1)}, bf16[64,512]{1,0:T(8,128)(2,1)}, u32[]{:S(2)}) copy-start(bf16[64,512]{1,0:T(8,128)(2,1)} %pack_nodes.1) | copy-start | bytes 196612
  15.4 9.3 %collective-permute-start.2 = (bf16[64,512]{1,0:T(8,128)(2,1)}, bf16[64,512]{1,0:T(8,128)(2,1)S(1)}, u32[]{:S(2)}, u32[]{:S(2)}) collective-permute-start(bf16[64,512]{1,0:T(8,128)(2,1)} %pack_nodes.1), channel_id=1, source_target_pairs={{0,2},{1,3},{2,0},{3,1},{4,6},{5,7},{6,4},{7,5},{8,10},{9,11},{10,... | collective-permute-start | bytes 196616 | tf_op jit(solution)/shard_map/ppermute | solution.py:551
  16.9 7.7 %collective-permute-start.3 = (bf16[64,512]{1,0:T(8,128)(2,1)}, bf16[64,512]{1,0:T(8,128)(2,1)S(1)}, u32[]{:S(2)}, u32[]{:S(2)}) collective-permute-start(bf16[64,512]{1,0:T(8,128)(2,1)} %pack_nodes.1), channel_id=1, source_target_pairs={{0,4},{1,5},{2,6},{3,7},{4,0},{5,1},{6,2},{7,3},{8,12},{9,13},{10,... | collective-permute-start | bytes 196616 | tf_op jit(solution)/shard_map/ppermute | solution.py:551
  19.5 6.3 %collective-permute-start.4 = (bf16[64,512]{1,0:T(8,128)(2,1)}, bf16[64,512]{1,0:T(8,128)(2,1)S(1)}, u32[]{:S(2)}, u32[]{:S(2)}) collective-permute-start(bf16[64,512]{1,0:T(8,128)(2,1)} %pack_nodes.1), channel_id=1, source_target_pairs={{0,6},{1,7},{2,4},{3,5},{4,2},{5,3},{6,0},{7,1},{8,14},{9,15},{10,... | collective-permute-start | bytes 196616 | tf_op jit(solution)/shard_map/ppermute | solution.py:551
  25.8 1.6 %copy-start.13 = (bf16[256,512]{1,0:T(8,128)(2,1)}, bf16[256,512]{1,0:T(8,128)(2,1)S(1)}, u32[]{:S(2)}) copy-start(bf16[256,512]{1,0:T(8,128)(2,1)S(1)} %pad_maximum_fusion.1.gathered) | copy-start | bytes 786436
  25.8 1.6 %collective-permute-start.5 = (bf16[256,512]{1,0:T(8,128)(2,1)S(1)}, bf16[256,512]{1,0:T(8,128)(2,1)S(1)}, u32[]{:S(2)}, u32[]{:S(2)}) collective-permute-start(bf16[256,512]{1,0:T(8,128)(2,1)S(1)} %pad_maximum_fusion.1.gathered), channel_id=1, source_target_pairs={{0,1},{1,0},{2,3},{3,2},{4,5},{5,4},{6,7},{7,6},{8,9},{9,8},{10,11... | collective-permute-start | bytes 786440 | tf_op jit(solution)/shard_map/ppermute | solution.py:551
  27.4 0.7 copy-start.21
  59.3 9.5 %copy-start.4 = (bf16[336,512]{1,0:T(8,128)(2,1)S(1)}, bf16[336,512]{1,0:T(8,128)(2,1)}, u32[]{:S(2)}) copy-start(bf16[336,512]{1,0:T(8,128)(2,1)} %get-tuple-element.74) | copy-start | bytes 1032196
  59.3 10.7 %copy-start.3 = (bf16[336,512]{1,0:T(8,128)(2,1)S(1)}, bf16[336,512]{1,0:T(8,128)(2,1)}, u32[]{:S(2)}) copy-start(bf16[336,512]{1,0:T(8,128)(2,1)} %get-tuple-element.72) | copy-start | bytes 1032196
  59.3 1.8 %collective-permute-start.13 = (bf16[256,512]{1,0:T(8,128)(2,1)}, bf16[256,512]{1,0:T(8,128)(2,1)S(1)}, u32[]{:S(2)}, u32[]{:S(2)}) collective-permute-start(bf16[256,512]{1,0:T(8,128)(2,1)} %get-tuple-element.79), channel_id=1, source_target_pairs={{0,1},{1,0},{2,3},{3,2},{4,5},{5,4},{6,7},{7,6},{8,9},{9,8},{10,11... | collective-permute-start | bytes 786440 | tf_op jit(solution)/shard_map/ppermute | solution.py:551
  59.5 5.7 %collective-permute-start.11 = (bf16[336,512]{1,0:T(8,128)(2,1)}, bf16[336,512]{1,0:T(8,128)(2,1)S(1)}, u32[]{:S(2)}, u32[]{:S(2)}) collective-permute-start(bf16[336,512]{1,0:T(8,128)(2,1)} %get-tuple-element.77), channel_id=1, source_target_pairs={{0,1},{1,0},{2,3},{3,2},{4,5},{5,4},{6,7},{7,6},{8,9},{9,8},{10,11... | collective-permute-start | bytes 1032200 | tf_op jit(solution)/shard_map/ppermute | solution.py:551
  59.9 8.9 %collective-permute-start.9 = (bf16[336,512]{1,0:T(8,128)(2,1)}, bf16[336,512]{1,0:T(8,128)(2,1)S(1)}, u32[]{:S(2)}, u32[]{:S(2)}) collective-permute-start(bf16[336,512]{1,0:T(8,128)(2,1)} %get-tuple-element.75), channel_id=1, source_target_pairs={{0,1},{1,0},{2,3},{3,2},{4,5},{5,4},{6,7},{7,6},{8,9},{9,8},{10,11... | collective-permute-start | bytes 1032200 | tf_op jit(solution)/shard_map/ppermute | solution.py:551
  60.0 10.0 %collective-permute-start.7 = (bf16[336,512]{1,0:T(8,128)(2,1)}, bf16[336,512]{1,0:T(8,128)(2,1)S(1)}, u32[]{:S(2)}, u32[]{:S(2)}) collective-permute-start(bf16[336,512]{1,0:T(8,128)(2,1)} %get-tuple-element.73), channel_id=1, source_target_pairs={{0,1},{1,0},{2,3},{3,2},{4,5},{5,4},{6,7},{7,6},{8,9},{9,8},{10,11... | collective-permute-start | bytes 1032200 | tf_op jit(solution)/shard_map/ppermute | solution.py:551
  62.2 23.5 %copy-start.5 = (bf16[336,512]{1,0:T(8,128)(2,1)S(1)}, bf16[336,512]{1,0:T(8,128)(2,1)}, u32[]{:S(2)}) copy-start(bf16[336,512]{1,0:T(8,128)(2,1)} %get-tuple-element.70) | copy-start | bytes 1032196
  62.2 8.9 %collective-permute-start.14 = (bf16[64,512]{1,0:T(8,128)(2,1)S(1)}, bf16[64,512]{1,0:T(8,128)(2,1)S(1)}, u32[]{:S(2)}, u32[]{:S(2)}) collective-permute-start(bf16[64,512]{1,0:T(8,128)(2,1)S(1)} %get-tuple-element.114), channel_id=1, source_target_pairs={{0,2},{1,3},{2,0},{3,1},{4,6},{5,7},{6,4},{7,5},{8,10},{9,11},{10,... | collective-permute-start | bytes 196616 | tf_op jit(solution)/shard_map/ppermute | solution.py:551
  62.3 8.8 %collective-permute-start.15 = (bf16[64,512]{1,0:T(8,128)(2,1)S(1)}, bf16[64,512]{1,0:T(8,128)(2,1)S(1)}, u32[]{:S(2)}, u32[]{:S(2)}) collective-permute-start(bf16[64,512]{1,0:T(8,128)(2,1)S(1)} %get-tuple-element.116), channel_id=1, source_target_pairs={{0,4},{1,5},{2,6},{3,7},{4,0},{5,1},{6,2},{7,3},{8,12},{9,13},{10,... | collective-permute-start | bytes 196616 | tf_op jit(solution)/shard_map/ppermute | solution.py:551
  66.3 11.4 %collective-permute-start.12 = (bf16[336,512]{1,0:T(8,128)(2,1)S(1)}, bf16[336,512]{1,0:T(8,128)(2,1)S(1)}, u32[]{:S(2)}, u32[]{:S(2)}) collective-permute-start(bf16[336,512]{1,0:T(8,128)(2,1)S(1)} %add_convert_fusion.1), channel_id=1, source_target_pairs={{0,8},{8,0},{16,24},{24,16},{1,9},{9,1},{17,25},{25,17},{2,10},{10... | collective-permute-start | bytes 1032200 | tf_op jit(solution)/shard_map/ppermute | solution.py:551
  68.9 15.3 %collective-permute-start.10 = (bf16[336,512]{1,0:T(8,128)(2,1)S(1)}, bf16[336,512]{1,0:T(8,128)(2,1)S(1)}, u32[]{:S(2)}, u32[]{:S(2)}) collective-permute-start(bf16[336,512]{1,0:T(8,128)(2,1)S(1)} %add_convert_fusion.2), channel_id=1, source_target_pairs={{0,16},{8,24},{16,0},{24,8},{1,17},{9,25},{17,1},{25,9},{2,18},{10... | collective-permute-start | bytes 1032200 | tf_op jit(solution)/shard_map/ppermute | solution.py:551
  70.1 15.5 %collective-permute-start.8 = (bf16[336,512]{1,0:T(8,128)(2,1)S(1)}, bf16[336,512]{1,0:T(8,128)(2,1)S(1)}, u32[]{:S(2)}, u32[]{:S(2)}) collective-permute-start(bf16[336,512]{1,0:T(8,128)(2,1)S(1)} %add_convert_fusion.3), channel_id=1, source_target_pairs={{0,24},{8,16},{16,8},{24,0},{1,25},{9,17},{17,9},{25,1},{2,26},{10... | collective-permute-start | bytes 1032200 | tf_op jit(solution)/shard_map/ppermute | solution.py:551
  71.1 14.5 %collective-permute-start.6 = (bf16[336,512]{1,0:T(8,128)(2,1)}, bf16[336,512]{1,0:T(8,128)(2,1)S(1)}, u32[]{:S(2)}, u32[]{:S(2)}) collective-permute-start(bf16[336,512]{1,0:T(8,128)(2,1)} %get-tuple-element.71), channel_id=1, source_target_pairs={{0,1},{1,0},{2,3},{3,2},{4,5},{5,4},{6,7},{7,6},{8,9},{9,8},{10,11... | collective-permute-start | bytes 1032200 | tf_op jit(solution)/shard_map/ppermute | solution.py:551
  71.1 6.3 %collective-permute-start.16 = (bf16[64,512]{1,0:T(8,128)(2,1)S(1)}, bf16[64,512]{1,0:T(8,128)(2,1)S(1)}, u32[]{:S(2)}, u32[]{:S(2)}) collective-permute-start(bf16[64,512]{1,0:T(8,128)(2,1)S(1)} %get-tuple-element.115), channel_id=1, source_target_pairs={{0,6},{1,7},{2,4},{3,5},{4,2},{5,3},{6,0},{7,1},{8,14},{9,15},{10,... | collective-permute-start | bytes 196616 | tf_op jit(solution)/shard_map/ppermute | solution.py:551
  72.5 13.9 %copy-start.16 = (bf16[64,512]{1,0:T(8,128)(2,1)S(1)}, bf16[64,512]{1,0:T(8,128)(2,1)}, u32[]{:S(2)}) copy-start(bf16[64,512]{1,0:T(8,128)(2,1)} %get-tuple-element.85) | copy-start | bytes 196612
  77.4 13.4 %copy-start.2 = (f32[64,512]{1,0:T(8,128)}, f32[64,512]{1,0:T(8,128)S(1)}, u32[]{:S(2)}) copy-start(f32[64,512]{1,0:T(8,128)S(1)} %convert_add_fusion.1.refs_6_) | copy-start | bytes 393220
  85.6 5.3 %copy-start.15 = (bf16[64,512]{1,0:T(8,128)(2,1)S(1)}, bf16[64,512]{1,0:T(8,128)(2,1)}, u32[]{:S(2)}) copy-start(bf16[64,512]{1,0:T(8,128)(2,1)} %get-tuple-element.87) | copy-start | bytes 196612
  86.0 4.9 %collective-permute-start.17 = (bf16[96,512]{1,0:T(8,128)(2,1)S(1)}, bf16[96,512]{1,0:T(8,128)(2,1)S(1)}, u32[]{:S(2)}, u32[]{:S(2)}) collective-permute-start(bf16[96,512]{1,0:T(8,128)(2,1)S(1)} %get-tuple-element.120), channel_id=1, source_target_pairs={{0,2},{1,3},{2,0},{3,1},{4,6},{5,7},{6,4},{7,5},{8,10},{9,11},{10,... | collective-permute-start | bytes 294920 | tf_op jit(solution)/shard_map/ppermute | solution.py:551
  86.4 9.6 %collective-permute-start.18 = (bf16[96,512]{1,0:T(8,128)(2,1)S(1)}, bf16[96,512]{1,0:T(8,128)(2,1)S(1)}, u32[]{:S(2)}, u32[]{:S(2)}) collective-permute-start(bf16[96,512]{1,0:T(8,128)(2,1)S(1)} %get-tuple-element.121), channel_id=1, source_target_pairs={{0,4},{1,5},{2,6},{3,7},{4,0},{5,1},{6,2},{7,3},{8,12},{9,13},{10,... | collective-permute-start | bytes 294920 | tf_op jit(solution)/shard_map/ppermute | solution.py:551
  88.1 8.0 %collective-permute-start.19 = (bf16[96,512]{1,0:T(8,128)(2,1)S(1)}, bf16[96,512]{1,0:T(8,128)(2,1)S(1)}, u32[]{:S(2)}, u32[]{:S(2)}) collective-permute-start(bf16[96,512]{1,0:T(8,128)(2,1)S(1)} %get-tuple-element.119), channel_id=1, source_target_pairs={{0,6},{1,7},{2,4},{3,5},{4,2},{5,3},{6,0},{7,1},{8,14},{9,15},{10,... | collective-permute-start | bytes 294920 | tf_op jit(solution)/shard_map/ppermute | solution.py:551
  90.9 5.1 %collective-permute-start.21 = (bf16[64,512]{1,0:T(8,128)(2,1)S(1)}, bf16[64,512]{1,0:T(8,128)(2,1)S(1)}, u32[]{:S(2)}, u32[]{:S(2)}) collective-permute-start(bf16[64,512]{1,0:T(8,128)(2,1)S(1)} %pad_maximum_fusion.7), channel_id=1, source_target_pairs={{0,8},{8,16},{16,24},{1,9},{9,17},{17,25},{2,10},{10,18},{18,26},{... | collective-permute-start | bytes 196616 | tf_op jit(solution)/shard_map/ppermute | solution.py:717
  93.6 7.3 %collective-permute-start.20 = (bf16[64,512]{1,0:T(8,128)(2,1)S(1)}, bf16[64,512]{1,0:T(8,128)(2,1)S(1)}, u32[]{:S(2)}, u32[]{:S(2)}) collective-permute-start(bf16[64,512]{1,0:T(8,128)(2,1)S(1)} %pad_maximum_fusion.6), channel_id=1, source_target_pairs={{8,0},{16,8},{24,16},{9,1},{17,9},{25,17},{10,2},{18,10},{26,18},{... | collective-permute-start | bytes 196616 | tf_op jit(solution)/shard_map/ppermute | solution.py:717
  96.1 17.9 %copy-start.17 = (bf16[64,512]{1,0:T(8,128)(2,1)}, bf16[64,512]{1,0:T(8,128)(2,1)S(1)}, u32[]{:S(2)}) copy-start(bf16[64,512]{1,0:T(8,128)(2,1)S(1)} %collective-permute-done.21.refs_5_) | copy-start | bytes 196612
  100.9 13.1 %copy-start.18 = (bf16[64,512]{1,0:T(8,128)(2,1)}, bf16[64,512]{1,0:T(8,128)(2,1)S(1)}, u32[]{:S(2)}) copy-start(bf16[64,512]{1,0:T(8,128)(2,1)S(1)} %collective-permute-done.20.refs_4_) | copy-start | bytes 196612
  100.9 19.0 %copy-start = (f32[96,512]{1,0:T(8,128)}, f32[96,512]{1,0:T(8,128)S(1)}, u32[]{:S(2)}) copy-start(f32[96,512]{1,0:T(8,128)S(1)} %convert_add_fusion.total) | copy-start | bytes 589828
  100.9 4.5 %collective-permute-start.22 = (bf16[80,512]{1,0:T(8,128)(2,1)S(1)}, bf16[80,512]{1,0:T(8,128)(2,1)S(1)}, u32[]{:S(2)}, u32[]{:S(2)}) collective-permute-start(bf16[80,512]{1,0:T(8,128)(2,1)S(1)} %slice.104), channel_id=1, source_target_pairs={{0,2},{1,3},{2,0},{3,1},{4,6},{5,7},{6,4},{7,5},{8,10},{9,11},{10,... | collective-permute-start | bytes 245768 | tf_op jit(solution)/shard_map/ppermute | solution.py:551
  101.0 5.4 %collective-permute-start.23 = (bf16[80,512]{1,0:T(8,128)(2,1)S(1)}, bf16[80,512]{1,0:T(8,128)(2,1)S(1)}, u32[]{:S(2)}, u32[]{:S(2)}) collective-permute-start(bf16[80,512]{1,0:T(8,128)(2,1)S(1)} %slice.104), channel_id=1, source_target_pairs={{0,4},{1,5},{2,6},{3,7},{4,0},{5,1},{6,2},{7,3},{8,12},{9,13},{10,... | collective-permute-start | bytes 245768 | tf_op jit(solution)/shard_map/ppermute | solution.py:551
  102.0 6.8 %collective-permute-start.24 = (bf16[80,512]{1,0:T(8,128)(2,1)S(1)}, bf16[80,512]{1,0:T(8,128)(2,1)S(1)}, u32[]{:S(2)}, u32[]{:S(2)}) collective-permute-start(bf16[80,512]{1,0:T(8,128)(2,1)S(1)} %slice.104), channel_id=1, source_target_pairs={{0,6},{1,7},{2,4},{3,5},{4,2},{5,3},{6,0},{7,1},{8,14},{9,15},{10,... | collective-permute-start | bytes 245768 | tf_op jit(solution)/shard_map/ppermute | solution.py:551
  109.5 10.4 %copy-start.1 = (bf16[4,5,16,512]{3,2,0,1:T(8,128)(2,1)}, bf16[4,5,16,512]{3,2,0,1:T(8,128)(2,1)S(1)}, u32[]{:S(2)}) copy-start(bf16[4,5,16,512]{3,2,0,1:T(8,128)(2,1)S(1)} %copy.23) | copy-start | bytes 983044
  109.5 10.5 %collective-permute-start.25 = (bf16[320,512]{1,0:T(8,128)(2,1)S(1)}, bf16[320,512]{1,0:T(8,128)(2,1)S(1)}, u32[]{:S(2)}, u32[]{:S(2)}) collective-permute-start(bf16[320,512]{1,0:T(8,128)(2,1)S(1)} %bitcast.40), channel_id=1, source_target_pairs={{0,8},{8,0},{16,24},{24,16},{1,9},{9,1},{17,25},{25,17},{2,10},{10... | collective-permute-start | bytes 983048 | tf_op jit(solution)/shard_map/ppermute | solution.py:551
  112.4 10.6 %collective-permute-start.26 = (bf16[320,512]{1,0:T(8,128)(2,1)S(1)}, bf16[320,512]{1,0:T(8,128)(2,1)S(1)}, u32[]{:S(2)}, u32[]{:S(2)}) collective-permute-start(bf16[320,512]{1,0:T(8,128)(2,1)S(1)} %bitcast.41), channel_id=1, source_target_pairs={{0,16},{8,24},{16,0},{24,8},{1,17},{9,25},{17,1},{25,9},{2,18},{10... | collective-permute-start | bytes 983048 | tf_op jit(solution)/shard_map/ppermute | solution.py:551
  112.4 10.6 %collective-permute-start.27 = (bf16[320,512]{1,0:T(8,128)(2,1)S(1)}, bf16[320,512]{1,0:T(8,128)(2,1)S(1)}, u32[]{:S(2)}, u32[]{:S(2)}) collective-permute-start(bf16[320,512]{1,0:T(8,128)(2,1)S(1)} %bitcast.42), channel_id=1, source_target_pairs={{0,24},{8,16},{16,8},{24,0},{1,25},{9,17},{17,9},{25,1},{2,26},{10... | collective-permute-start | bytes 983048 | tf_op jit(solution)/shard_map/ppermute | solution.py:551
  119.9 3.8 %collective-permute-start.28 = (bf16[320,512]{1,0:T(8,128)(2,1)S(1)}, bf16[320,512]{1,0:T(8,128)(2,1)S(1)}, u32[]{:S(2)}, u32[]{:S(2)}) collective-permute-start(bf16[320,512]{1,0:T(8,128)(2,1)S(1)} %bitcast.43), channel_id=1, source_target_pairs={{0,1},{1,0},{2,3},{3,2},{4,5},{5,4},{6,7},{7,6},{8,9},{9,8},{10,11... | collective-permute-start | bytes 983048 | tf_op jit(solution)/shard_map/ppermute | solution.py:551
  120.0 5.7 %copy-start.6 = (bf16[320,512]{1,0:T(8,128)(2,1)}, bf16[320,512]{1,0:T(8,128)(2,1)S(1)}, u32[]{:S(2)}) copy-start(bf16[320,512]{1,0:T(8,128)(2,1)S(1)} %collective-permute-done.25.refs_1_) | copy-start | bytes 983044
  123.0 2.6 %copy-start.7 = (bf16[320,512]{1,0:T(8,128)(2,1)}, bf16[320,512]{1,0:T(8,128)(2,1)S(1)}, u32[]{:S(2)}) copy-start(bf16[320,512]{1,0:T(8,128)(2,1)S(1)} %collective-permute-done.26.refs_2_) | copy-start | bytes 983044
  123.0 2.6 %copy-start.8 = (bf16[320,512]{1,0:T(8,128)(2,1)}, bf16[320,512]{1,0:T(8,128)(2,1)S(1)}, u32[]{:S(2)}) copy-start(bf16[320,512]{1,0:T(8,128)(2,1)S(1)} %collective-permute-done.27.refs_3_) | copy-start | bytes 983044
  123.0 1.7 %collective-permute-start.29 = (bf16[320,512]{1,0:T(8,128)(2,1)S(1)}, bf16[320,512]{1,0:T(8,128)(2,1)S(1)}, u32[]{:S(2)}, u32[]{:S(2)}) collective-permute-start(bf16[320,512]{1,0:T(8,128)(2,1)S(1)} %collective-permute-done.25.refs_1_), channel_id=1, source_target_pairs={{0,1},{1,0},{2,3},{3,2},{4,5},{5,4},{6,7},{7,6},{8,9},{9,8},{10,11... | collective-permute-start | bytes 983048 | tf_op jit(solution)/shard_map/ppermute | solution.py:551
  123.1 2.1 %collective-permute-start.30 = (bf16[320,512]{1,0:T(8,128)(2,1)S(1)}, bf16[320,512]{1,0:T(8,128)(2,1)S(1)}, u32[]{:S(2)}, u32[]{:S(2)}) collective-permute-start(bf16[320,512]{1,0:T(8,128)(2,1)S(1)} %collective-permute-done.26.refs_2_), channel_id=1, source_target_pairs={{0,1},{1,0},{2,3},{3,2},{4,5},{5,4},{6,7},{7,6},{8,9},{9,8},{10,11... | collective-permute-start | bytes 983048 | tf_op jit(solution)/shard_map/ppermute | solution.py:551
  123.6 2.1 %collective-permute-start.31 = (bf16[320,512]{1,0:T(8,128)(2,1)S(1)}, bf16[320,512]{1,0:T(8,128)(2,1)S(1)}, u32[]{:S(2)}, u32[]{:S(2)}) collective-permute-start(bf16[320,512]{1,0:T(8,128)(2,1)S(1)} %collective-permute-done.27.refs_3_), channel_id=1, source_target_pairs={{0,1},{1,0},{2,3},{3,2},{4,5},{5,4},{6,7},{7,6},{8,9},{9,8},{10,11... | collective-permute-start | bytes 983048 | tf_op jit(solution)/shard_map/ppermute | solution.py:551
  123.7 2.0 %copy-start.9 = (bf16[320,512]{1,0:T(8,128)(2,1)}, bf16[320,512]{1,0:T(8,128)(2,1)S(1)}, u32[]{:S(2)}) copy-start(bf16[320,512]{1,0:T(8,128)(2,1)S(1)} %collective-permute-done.28.refs_4_) | copy-start | bytes 983044
  124.7 1.0 copy-start.10
  125.2 0.7 copy-start.11
  125.9 0.7 copy-start.12

commit v4 on v3

--- a/solution.py
+++ b/solution.py
@@ -57,7 +57,7 @@
     return pl.multiple_of(start, multiple)
 
 
-def pack_kernel(cols, slots, nodes, above, below, packed):
+def pack_kernel(cols, slots, nodes, packed):
     rows = nodes.shape[0]
     count, patch_rows = slots.shape[0], rows // cols
     size = count + 2 * patch_rows
@@ -70,96 +70,47 @@
     for k in range(count):
         wanted = jnp.where(place == k, slots[k], wanted)
     column = lax.broadcasted_iota(jnp.int32, (size, rows), 1)
-    packed[pl.ds(0, size), :] = to_bf16(dot(to_bf16(to_f32(column == wanted)), nodes[...]))
-    place = lax.broadcasted_iota(jnp.int32, (16, 1), 0)
-    top = to_f32(above[pl.ds(0, 16), :])[0:1]
-    bottom = to_f32(below[pl.ds(cols - 16, 16), :])[15:16]
-    corners = jnp.where(place == 0, top, jnp.where(place == 1, bottom, 0.0))
-    packed[pl.ds(size, 16), :] = to_bf16(corners)
-
-
-def pack_nodes(cols, slots, nodes, above, below):
+    packed[...] = to_bf16(dot(to_bf16(to_f32(column == wanted)), nodes[...]))
+
+
+def pack_nodes(cols, slots, nodes):
     rows, depth = nodes.shape
-    count = slots.shape[0] + 2 * (rows // cols) + 16
+    count = slots.shape[0] + 2 * (rows // cols)
     smem, vmem = pl.BlockSpec(memory_space=pltpu.SMEM), pl.BlockSpec(memory_space=pltpu.VMEM)
     return pl.pallas_call(
         functools.partial(pack_kernel, cols),
-        in_specs=[smem, vmem, vmem, vmem],
+        in_specs=[smem, vmem],
         out_specs=vmem,
         out_shape=jax.ShapeDtypeStruct((count, depth), jnp.bfloat16),
         name="pack_nodes",
-    )(slots, nodes, above, below)
-
-
-def project_send_kernel(nodes, w_send, send):
-    send[...] = to_bf16(dot(nodes[...], w_send[...]))
-
-
-def project_own_kernel(nodes, w_recv, w_self, edge_bias, node_bias, recv_half, own):
-    block = nodes[...]
-    recv_half[...] = 0.5 * (dot(block, w_recv[...]) + edge_bias[...])
-    own[...] = dot(block, w_self[...]) + node_bias[...]
-
-
-def project(kernel, name, nodes, weights, vectors, kinds):
-    rows, depth = nodes.shape
-    step = 256
-    whole = pl.BlockSpec((depth, depth), lambda i: (0, 0))
-    vector = pl.BlockSpec((1, depth), lambda i: (0, 0))
-    block = pl.BlockSpec((step, depth), lambda i: (i, 0))
-    return pl.pallas_call(
-        kernel,
-        grid=(rows // step,),
-        in_specs=[block] + [whole] * len(weights) + [vector] * len(vectors),
-        out_specs=[block] * len(kinds),
-        out_shape=[jax.ShapeDtypeStruct((rows, depth), kind) for kind in kinds],
-        cost_estimate=pl.CostEstimate(
-            flops=2 * len(weights) * rows * depth * depth,
-            bytes_accessed=4_000_000 * len(weights),
-            transcendentals=0,
-        ),
-        name=name,
-    )(nodes, *weights, *vectors)
-
-
-def update_kernel(
-    dims,
-    slots,
-    long_senders,
-    long_receivers,
-    nodes,
-    cotangent,
-    send,
-    recv_half,
-    own,
-    above,
-    below,
-    gathered,
-    crossed,
-    w_send,
-    w_recv,
-    w_agg,
-    w_out,
-    edge_bias,
-    gain,
-    new_nodes,
-    d_pre_b,
-    d_recv_b,
-    d_send,
-    d_up,
-    d_down,
-    d_gathered,
-    d_crossed,
-    *rest,
-):
+    )(slots, nodes)
+
+
+def update_kernel(dims, slots, long_senders, long_receivers, edge_bias, node_bias, gain, *refs):
     patch_rows, cols, lon_count, coarse_count, lat_count = dims
-    outs, rest = rest[: 2 * lat_count], rest[2 * lat_count :]
+    refs = iter(refs)
+    take = lambda count: [next(refs) for _ in range(count)]
+    sources, results, outs = take(11), take(8), take(2 * lat_count)
+    (
+        near_nodes,
+        gathered,
+        crossed,
+        w_send,
+        nodes,
+        w_recv,
+        w_self,
+        w_agg,
+        w_out,
+        cotangent,
+    ) = held = take(10)
+    d_up, d_down, d_gathered, d_crossed, new_nodes, d_pre_b, d_recv_b = kept = take(7)
     (
         mid,
         right,
         left,
         slopes,
         slope_sum,
+        recv_half,
         total,
         work,
         agg_b,
@@ -167,8 +118,6 @@
         d_out_b,
         d_half,
         far,
-        far_d,
-        near_nodes,
         near_d,
         sums,
         coarse,
@@ -176,8 +125,11 @@
         send_hot,
         recv_hot,
         grads,
+        in_sems,
+        near_sems,
         out_sems,
-    ) = rest
+        grad_sems,
+    ) = take(24)
     rows = patch_rows * cols
     depth = nodes.shape[-1]
     pack = coarse_count + 2 * patch_rows + 16
@@ -195,8 +147,30 @@
     tile = 16
 
     upper, lower = pl.ds(0, cols), pl.ds(cols, cols)
-    near_nodes[upper, :] = above[...]
-    near_nodes[lower, :] = below[...]
+    arriving = [
+        pltpu.make_async_copy(source, near_nodes.at[place], near_sems.at[k])
+        for k, (source, place) in enumerate(zip(sources[:2], (upper, lower)))
+    ]
+    loads = {}
+    for k, (source, target) in enumerate(zip(sources[2:], held[1:])):
+        loads[k] = pltpu.make_async_copy(source, target, in_sems.at[k])
+    for copy in (loads[3], loads[2], loads[4], *arriving, loads[0], loads[1]):
+        copy.start()
+    for k in range(5, 9):
+        loads[k].start()
+    leaving = []
+
+    def leave(source, target, sem):
+        leaving.append(pltpu.make_async_copy(source, target, sem))
+        leaving[-1].start()
+
+    for k in (3, 2):
+        loads[k].wait()
+    mid[pl.ds(cols, rows), :] = 0.5 * to_f32(to_bf16(dot(nodes[...], w_send[...])))
+    loads[4].wait()
+    recv_half[...] = 0.5 * (dot(nodes[...], w_recv[...]) + edge_bias[...])
+    for copy in (*arriving, loads[0], loads[1]):
+        copy.wait()
     near_half = 0.5 * to_f32(to_bf16(dot(near_nodes[...], w_send[...])))
     half_far = chip_count * pack
     same, cross = pl.ds(0, half_far), pl.ds(half_far, half_far)
@@ -211,7 +185,7 @@
     right_corners = far[pl.ds(aligned(right_at + corner_at, 16), 16), :]
     left_corners = far[pl.ds(aligned(left_at + corner_at, 16), 16), :]
     top_corner = jnp.where(top_valid, right_corners[0:1], ABSENT)
-    bottom_corner = jnp.where(bottom_valid, left_corners[1:2], ABSENT)
+    bottom_corner = jnp.where(bottom_valid, left_corners[15:16], ABSENT)
     mid[pl.ds(0, cols), :] = top
     mid[pl.ds(rows + cols, cols), :] = bottom
     right[pl.ds(0, cols), :] = jnp.where(last, top_corner, pltpu.roll(top, cols - 1, 0))
@@ -220,11 +194,10 @@
     right_edge = far[pl.ds(aligned(right_at + coarse_count, 16), patch_rows), :]
     left_edge = far[pl.ds(aligned(left_at + coarse_count + patch_rows, 16), patch_rows), :]
     for row in range(patch_rows):
-        here, there = pl.ds(row * cols, cols), pl.ds((row + 1) * cols, cols)
+        there = pl.ds((row + 1) * cols, cols)
         for lane in range(0, depth, 128):
             lanes = pl.ds(lane, 128)
-            block = 0.5 * to_f32(send[here, lanes])
-            mid[there, lanes] = block
+            block = mid[there, lanes]
             edge = right_edge[row : row + 1, lane : lane + 128]
             right[there, lanes] = jnp.where(last, edge, pltpu.roll(block, cols - 1, 0))
             edge = left_edge[row : row + 1, lane : lane + 128]
@@ -275,9 +248,15 @@
 
     step_rows = 256
     blocks = [pl.ds(start, step_rows) for start in range(0, rows, step_rows)]
+    loads[5].wait()
+    loads[6].wait()
     for block in blocks:
         agg_b[block, :] = to_bf16(total[block, :])
-        work[block, :] = 0.5 * (own[block, :] + dot(agg_b[block, :], w_agg[...]))
+        work[block, :] = 0.5 * (
+            dot(nodes[block, :], w_self[...])
+            + dot(agg_b[block, :], w_agg[...])
+            + node_bias[...]
+        )
 
     def activate(step, carry):
         here = pl.ds(aligned(step * tile, tile), tile)
@@ -286,12 +265,14 @@
         return carry
 
     lax.fori_loop(0, rows // tile, activate, 0)
+    loads[7].wait()
     for block in blocks:
         total[block, :] = dot(hidden_b[block, :], w_out[...])
 
-    wide = 32
-
-    def normalise(step, carry):
+    wide = 64
+    loads[8].wait()
+
+    def normalise(step, gain_sum):
         here = pl.ds(aligned(step * wide, wide), wide)
         output = total[here, :]
         cot = to_f32(cotangent[here, :])
@@ -301,12 +282,13 @@
         inv_std = lax.rsqrt(jnp.mean(centred * centred, axis=-1, keepdims=True) + epsilon)
         normed = centred * inv_std
         new_nodes[here, :] = to_bf16(to_f32(nodes[here, :]) + gain[...] * normed)
-        sums[2] += eight_rows(cot * normed)
         d_dot = jnp.mean(d_norm * normed, axis=-1, keepdims=True)
         d_out_b[here, :] = to_bf16(inv_std * (d_norm - d_mean - normed * d_dot))
-        return carry
-
-    lax.fori_loop(0, rows // wide, normalise, 0, unroll=2)
+        return gain_sum + eight_rows(cot * normed)
+
+    nothing = jnp.zeros((8, depth), jnp.float32)
+    sums[2] = lax.fori_loop(0, rows // wide, normalise, nothing, unroll=4)
+    leave(new_nodes, results[0], out_sems.at[0])
 
     for block in blocks:
         total[block, :] = dot_nt(d_out_b[block, :], w_out[...])
@@ -320,6 +302,7 @@
         return carry
 
     lax.fori_loop(0, rows // tile, deactivate, 0)
+    leave(d_pre_b, results[1], out_sems.at[1])
     share = depth // (2 * lat_count)
 
     def put(which, half_at, values):
@@ -334,6 +317,14 @@
         put(2, half_at, dot_tn(nodes[:, columns], d_pre_b[...]))
         put(3, half_at, dot_tn(agg_b[:, columns], d_pre_b[...]))
         put(4, half_at, dot_tn(hidden_b[:, columns], d_out_b[...]))
+    for part in range(2):
+        for spot in range(lat_count):
+            place = pl.ds(2 * share, 3 * share)
+            leave(
+                grads.at[part, spot, place],
+                outs[part * lat_count + spot].at[place],
+                grad_sems.at[part, spot, 0],
+            )
     d_half[pl.ds(0, cols), :] = jnp.zeros((cols, depth), jnp.float32)
     d_half[pl.ds(rows + cols, cols), :] = jnp.zeros((cols, depth), jnp.float32)
     for which in (0, 4):
@@ -356,7 +347,7 @@
         return carry
 
     lax.fori_loop(0, rows // tile, receive, 0)
-    far_d[...] = jnp.zeros_like(far_d)
+    far[...] = jnp.zeros_like(far)
 
     edge_place = lax.broadcasted_iota(jnp.int32, (patch_rows, 1), 0)
     for lane in range(0, depth, 128):
@@ -369,15 +360,15 @@
             to_mid = slope_times(0, above_row, lanes) + slope_times(1, below_row, lanes)
             to_right = slope_times(2, here, lanes) + slope_times(5, below_row, lanes)
             to_left = slope_times(3, here, lanes) + slope_times(4, above_row, lanes)
-            d_send[out, lanes] = (
+            work[out, lanes] = (
                 to_mid
                 + jnp.where(first, 0.0, pltpu.roll(to_right, 1, 0))
                 + jnp.where(last, 0.0, pltpu.roll(to_left, cols - 1, 0))
             )
             right_edge = jnp.where(edge_place == row, to_right[cols - 1 : cols], right_edge)
             left_edge = jnp.where(edge_place == row, to_left[0:1], left_edge)
-        far_d[pl.ds(aligned(right_at + coarse_count, 16), patch_rows), lanes] = right_edge
-        far_d[pl.ds(aligned(left_at + coarse_count + patch_rows, 16), patch_rows), lanes] = left_edge
+        far[pl.ds(aligned(right_at + coarse_count, 16), patch_rows), lanes] = right_edge
+        far[pl.ds(aligned(left_at + coarse_count + patch_rows, 16), patch_rows), lanes] = left_edge
     row_first, row_last = pl.ds(cols, cols), pl.ds(rows, cols)
     sixteen = lax.broadcasted_iota(jnp.int32, (16, 1), 0)
     for lane in range(0, depth, 128):
@@ -391,11 +382,13 @@
         near_d[upper, lanes] = to_bf16(up)
         near_d[lower, lanes] = to_bf16(down)
         corner = jnp.where(sixteen == 0, to_right[cols - 1 : cols], 0.0)
-        far_d[pl.ds(aligned(right_at + corner_at, 16), 16), lanes] = corner
-        corner = jnp.where(sixteen == 1, to_left[0:1], 0.0)
-        far_d[pl.ds(aligned(left_at + corner_at, 16), 16), lanes] = corner
+        far[pl.ds(aligned(right_at + corner_at, 16), 16), lanes] = corner
+        corner = jnp.where(sixteen == 15, to_left[0:1], 0.0)
+        far[pl.ds(aligned(left_at + corner_at, 16), 16), lanes] = corner
     d_up[...] = near_d[upper, :]
     d_down[...] = near_d[lower, :]
+    leave(d_up, results[4], out_sems.at[4])
+    leave(d_down, results[5], out_sems.at[5])
 
     for k in range(coarse_count):
         coarse_d[pl.ds(k, 1), :] = d_half[pl.ds(slots[k] + cols, 1), :]
@@ -407,14 +400,18 @@
         total[spot, :] = total[spot, :] + coarse_d[pl.ds(k, 1), :]
     coarse[...] = dot_exact_tn(send_hot[...], long_d)
     for source in range(lon_count):
-        far_d[pl.ds(source * pack, coarse_count), :] = coarse[
+        far[pl.ds(source * pack, coarse_count), :] = coarse[
             pl.ds(source * coarse_count, coarse_count), :
         ]
-    d_gathered[...] = to_bf16(far_d[same, :])
-    d_crossed[...] = to_bf16(far_d[cross, :])
+    d_gathered[...] = to_bf16(far[same, :])
+    d_crossed[...] = to_bf16(far[cross, :])
+    leave(d_gathered, results[6], out_sems.at[6])
+    leave(d_crossed, results[7], out_sems.at[7])
     for block in blocks:
         d_recv_b[block, :] = to_bf16(total[block, :])
-        agg_b[block, :] = to_bf16(d_send[block, :])
+        agg_b[block, :] = to_bf16(work[block, :])
+    leave(d_recv_b, results[2], out_sems.at[2])
+    leave(agg_b, results[3], out_sems.at[3])
     for half_at in range(2):
         columns = pl.ds(half_at * (depth // 2), depth // 2)
         put(0, half_at, dot_tn(nodes[:, columns], agg_b[...])
@@ -429,64 +426,73 @@
     for part in range(2):
         for spot in range(lat_count):
             grads[part, spot, pl.ds(5 * share, 16), :] = to_bf16(vectors)
-    copies = [
-        pltpu.make_async_copy(
-            grads.at[part, spot], outs[part * lat_count + spot], out_sems.at[part, spot]
-        )
-        for part in range(2)
-        for spot in range(lat_count)
-    ]
-    for copy in copies:
-        copy.start()
-    for copy in copies:
+    for part in range(2):
+        for spot in range(lat_count):
+            for k, place in ((1, pl.ds(0, 2 * share)), (2, pl.ds(5 * share, 16))):
+                leave(
+                    grads.at[part, spot, place],
+                    outs[part * lat_count + spot].at[place],
+                    grad_sems.at[part, spot, k],
+                )
+    for copy in leaving:
         copy.wait()
 
 
-def update(dims, ints, arrays):
+def update(dims, ints, vectors, arrays):
     patch_rows, cols, lon_count, coarse_count, lat_count = dims
-    rows, depth = arrays[0].shape
+    rows, depth = patch_rows * cols, vectors[0].shape[-1]
     share = depth // (2 * lat_count)
     edge_count = ints[1].shape[0] * ints[1].shape[1]
     coarse_ids = lon_count * coarse_count
     far_rows = lon_count * (coarse_count + 2 * patch_rows + 16)
     near_rows = 2 * cols
     long_rows = rows + 2 * cols
-    half = lambda *size: jax.ShapeDtypeStruct(size, jnp.bfloat16)
-    full = lambda *size: jax.ShapeDtypeStruct(size, jnp.float32)
-    vmem_full = lambda *size: pltpu.VMEM(size, jnp.float32)
-    vmem_half = lambda *size: pltpu.VMEM(size, jnp.bfloat16)
+    out = lambda *size: jax.ShapeDtypeStruct(size, jnp.bfloat16)
+    full = lambda *size: pltpu.VMEM(size, jnp.float32)
+    half = lambda *size: pltpu.VMEM(size, jnp.bfloat16)
     smem, vmem = pl.BlockSpec(memory_space=pltpu.SMEM), pl.BlockSpec(memory_space=pltpu.VMEM)
+    anywhere = pl.BlockSpec(memory_space=pl.ANY)
+    weight = half(depth, depth)
     return pl.pallas_call(
         functools.partial(update_kernel, dims),
-        in_specs=[smem] * len(ints) + [vmem] * len(arrays),
-        out_specs=[vmem] * 8 + [pl.BlockSpec(memory_space=pl.ANY)] * (2 * lat_count),
-        out_shape=[half(rows, depth)] * 3
-        + [full(rows, depth)]
+        in_specs=[smem] * len(ints) + [vmem] * len(vectors) + [anywhere] * len(arrays),
+        out_specs=[anywhere] * (8 + 2 * lat_count),
+        out_shape=[out(rows, depth)] * 4
+        + [out(cols, depth)] * 2
+        + [out(far_rows // 2, depth)] * 2
+        + [out(5 * share + 16, depth)] * (2 * lat_count),
+        scratch_shapes=[half(near_rows, depth)]
+        + [half(far_rows // 2, depth)] * 2
+        + [weight, half(rows, depth)]
+        + [weight] * 4
+        + [half(rows, depth)]
         + [half(cols, depth)] * 2
         + [half(far_rows // 2, depth)] * 2
-        + [half(5 * share + 16, depth)] * (2 * lat_count),
-        scratch_shapes=[vmem_full(long_rows, depth)] * 3
-        + [vmem_half(6, long_rows, depth)]
-        + [vmem_full(rows, depth)] * 3
-        + [vmem_half(rows, depth)] * 3
-        + [vmem_full(long_rows, depth)]
-        + [vmem_full(far_rows, depth)] * 2
-        + [vmem_half(near_rows, depth)] * 2
+        + [half(rows, depth)] * 3
+        + [full(long_rows, depth)] * 3
+        + [half(6, long_rows, depth)]
+        + [full(rows, depth)] * 4
+        + [half(rows, depth)] * 3
+        + [full(long_rows, depth), full(far_rows, depth)]
+        + [half(near_rows, depth)]
         + [
-            vmem_full(3, 8, depth),
-            vmem_full(coarse_ids, depth),
-            vmem_full(coarse_count, depth),
-            vmem_full(edge_count, coarse_ids),
-            vmem_full(edge_count, coarse_count),
-            vmem_half(2, lat_count, 5 * share + 16, depth),
-            pltpu.SemaphoreType.DMA((2, lat_count)),
+            full(3, 8, depth),
+            full(coarse_ids, depth),
+            full(coarse_count, depth),
+            full(edge_count, coarse_ids),
+            full(edge_count, coarse_count),
+            half(2, lat_count, 5 * share + 16, depth),
+            pltpu.SemaphoreType.DMA((9,)),
+            pltpu.SemaphoreType.DMA((2,)),
+            pltpu.SemaphoreType.DMA((8,)),
+            pltpu.SemaphoreType.DMA((2, lat_count, 3)),
         ],
         compiler_params=pltpu.CompilerParams(vmem_limit_bytes=VMEM_BYTES),
         cost_estimate=pl.CostEstimate(
-            flops=20 * rows * depth * depth, bytes_accessed=20_000_000, transcendentals=0
+            flops=26 * rows * depth * depth, bytes_accessed=20_000_000, transcendentals=0
         ),
         name="update",
-    )(*ints, *arrays)
+    )(*ints, *vectors, *arrays)
 
 
 def finish_kernel(dims, slots, *refs):
@@ -509,7 +515,7 @@
     step_rows = 256
     for start in range(0, rows, step_rows):
         block = pl.ds(start, step_rows)
-        total[block, :] = d_send[block, :]
+        total[block, :] = to_f32(d_send[block, :])
     for start, part in ((rows - cols, from_below), (0, from_above)):
         total[pl.ds(start, cols), :] += to_f32(part[...])
     returned = back[...]
@@ -595,47 +601,50 @@
     shares = tuple(swapped(ready, "lat", step) for step in range(1, lat_count))
     shares, meanwhile = lax.optimization_barrier((shares, meanwhile))
     shares = [ready, *shares]
-    return shares + [swapped(part, "lon", 1) for part in shares], meanwhile
-
-
-def unpack_kernel(lat_count, scale, total, *refs):
-    shares, outs = refs[: 2 * lat_count], refs[2 * lat_count : 2 * lat_count + 8]
-    staged, sems = refs[2 * lat_count + 8 :]
-    depth = total.shape[-1]
+    return shares, [swapped(part, "lon", 1) for part in shares], meanwhile
+
+
+def unpack_kernel(flip, scale, *refs):
+    count = len(refs)
+    lat_count = lax.axis_size("lat")
+    shares = refs[:lat_count]
+    staged, sems = refs[count - 2 :]
+    outs = refs[count - 7 : count - 2]
+    depth = outs[0].shape[-1]
     share = depth // (2 * lat_count)
     core, lat = lax.axis_index("lon") % 2, lax.axis_index("lat")
+    place = pl.ds(aligned((core ^ flip) * (depth // 2), depth // 2), depth // 2)
     copies = []
     for which in range(5):
-        for flip in range(2):
-            for step in range(lat_count):
-                start = (core ^ flip) * (depth // 2) + (lat ^ step) * share
-                block = shares[flip * lat_count + step][pl.ds(which * share, share), :]
-                staged[which, pl.ds(aligned(start, share), share), :] = scale * to_f32(block)
-        copies.append(pltpu.make_async_copy(staged.at[which], outs[which], sems.at[which]))
+        for step in range(lat_count):
+            block = shares[step][pl.ds(which * share, share), :]
+            start = aligned((lat ^ step) * share, share)
+            staged[which, pl.ds(start, share), :] = scale * to_f32(block)
+        copies.append(
+            pltpu.make_async_copy(staged.at[which], outs[which].at[place], sems.at[which])
+        )
         copies[-1].start()
-    vectors_at = 5 * share // (lax.axis_size("lon") // 2)
-    for which in range(3):
-        outs[5 + which][...] = scale * total[pl.ds(vectors_at + which, 1), :]
     for copy in copies:
         copy.wait()
 
 
-def unpack(lat_count, scale, total, shares):
-    depth = total.shape[-1]
-    vmem = pl.BlockSpec(memory_space=pltpu.VMEM)
-    shape = jax.ShapeDtypeStruct
+def unpack(flip, scale, shares, begun=()):
+    depth = shares[0].shape[-1]
+    vmem, anywhere = pl.BlockSpec(memory_space=pltpu.VMEM), pl.BlockSpec(memory_space=pl.ANY)
     return pl.pallas_call(
-        functools.partial(unpack_kernel, lat_count, scale),
-        in_specs=[vmem] * (1 + len(shares)),
-        out_specs=[pl.BlockSpec(memory_space=pl.ANY)] * 5 + [vmem] * 3,
-        out_shape=[shape((depth, depth), jnp.float32)] * 5 + [shape((1, depth), jnp.float32)] * 3,
+        functools.partial(unpack_kernel, flip, scale),
+        in_specs=[vmem] * len(shares) + [anywhere] * len(begun),
+        out_specs=[anywhere] * 5,
+        out_shape=[jax.ShapeDtypeStruct((depth, depth), jnp.float32)] * 5,
         scratch_shapes=[
-            pltpu.VMEM((5, depth, depth), jnp.float32),
+            pltpu.VMEM((5, depth // 2, depth), jnp.float32),
             pltpu.SemaphoreType.DMA((5,)),
         ],
+        input_output_aliases={len(shares) + k: k for k in range(len(begun))},
         compiler_params=pltpu.CompilerParams(vmem_limit_bytes=VMEM_BYTES),
-        name="unpack",
-    )(total, *shares)
+        cost_estimate=pl.CostEstimate(flops=0, bytes_accessed=8_000_000, transcendentals=0),
+        name=f"unpack_{flip}",
+    )(*shares, *begun)
 
 
 def on_device(
@@ -667,38 +676,31 @@
 
     down = [(i, i + 1) for i in range(lat_count - 1)]
     up = [(i + 1, i) for i in range(lat_count - 1)]
+
     above = lax.ppermute(flat[-cols:], "lat", down)
     below = lax.ppermute(flat[:cols], "lat", up)
-    bias, offset = edge_bias[None], node_bias[None]
-    (send,) = project(project_send_kernel, "project_send", flat, [w_send], [], [jnp.bfloat16])
-    above, below, send = lax.optimization_barrier((above, below, send))
-    packed = pack_nodes(cols, slots, flat, above, below)
+    packed = pack_nodes(cols, slots, flat)
+    filler = jnp.zeros((14, depth), jnp.bfloat16)
+    packed = jnp.concatenate([packed, above[:1], filler, below[-1:]])
     chips = [swapped(packed, "lon", 2 * k) for k in range(1, chip_count)]
-    recv_half, own = project(
-        project_own_kernel, "project_own", flat, [w_recv, w_self], [bias, offset], [jnp.float32] * 2
-    )
-    chips, recv_half, own = lax.optimization_barrier((chips, recv_half, own))
     gathered = jnp.concatenate([packed, *chips])
     crossed = swapped(gathered, "lon", 1)
     outs = update(
         dims,
         (slots, long_senders.reshape(lon_count, -1), long_receivers.reshape(lon_count, -1)),
+        (edge_bias[None], node_bias[None], gain[None]),
         (
-            flat,
-            cot,
-            send,
-            recv_half,
-            own,
             above,
             below,
             gathered,
             crossed,
             w_send,
+            flat,
             w_recv,
+            w_self,
             w_agg,
             w_out,
-            bias,
-            gain[None],
+            cot,
         ),
     )
     new_nodes, d_pre_b, d_recv_b, d_send, d_up, d_down, d_gathered, d_crossed = outs[:8]
@@ -711,9 +713,9 @@
         return sum([to_f32(one) for one in received], to_f32(parts[0]))
 
     def borders(back):
-        corners = to_bf16(back[-16:-14])
+        corners = to_bf16(back[-16:])
         ups = jnp.concatenate([to_bf16(to_f32(d_up[:1]) + to_f32(corners[:1])), d_up[1:]])
-        downs = jnp.concatenate([d_down[:-1], to_bf16(to_f32(d_down[-1:]) + to_f32(corners[1:]))])
+        downs = jnp.concatenate([d_down[:-1], to_bf16(to_f32(d_down[-1:]) + to_f32(corners[-1:]))])
         return lax.ppermute(ups, "lat", up), lax.ppermute(downs, "lat", down)
 
     total, back, bordered = summed_part(mine, other, returning, borders)
@@ -732,19 +734,21 @@
             w_send,
         ),
     )
-    shares, grad_nodes = gathered_shares(total, lat_count, grad_nodes)
-    outs = unpack(lat_count, scale, total, shares)
+    shares, crossed_shares, grad_nodes = gathered_shares(total, lat_count, grad_nodes)
+    outs = unpack(0, scale, shares)
+    outs = unpack(1, scale, crossed_shares, outs)
+    vectors = scale * total[-16:]
     return (
         new_nodes.reshape(patch_rows, cols, depth),
         grad_nodes.reshape(patch_rows, cols, depth),
         outs[0],
         outs[1],
-        outs[5][0],
+        vectors[0],
         outs[2],
         outs[3],
-        outs[6][0],
+        vectors[1],
         outs[4],
-        outs[7][0],
+        vectors[2],
     )
 
 

time: 132 us -> 124 us (0.939)
  Pallas kernels: 53 us -> 39.5 us
  waiting for transfers between devices: 31.8 us -> 34.2 us
  local copies, waits for them, and re-layouts: 3.98 us -> 5.45 us
    pallas_call x3 -> x2, Pallas kernels: 13.8 us -> 5.68 us  [unpack(): pl.pallas_call(functools.partial(unpack_kernel, flip, scale), in_specs=[v...]
    ppermute x28, waiting for transfers between devices: 26.2 us -> 32.3 us  [swapped(): return lax.ppermute(values, axis, [(i, i ^ bit) for i in range(count)])]
    pallas_call x1, Pallas kernels: 31.1 us -> 26.1 us  [update(): pl.pallas_call(functools.partial(update_kernel, dims), in_specs=[smem] *...]
    ppermute x2, waiting for transfers between devices: 4.79 us -> 1.85 us  [borders(): return (lax.ppermute(ups, 'lat', up), lax.ppermute(downs, 'lat', down))]
    ppermute x2, starting transfers between devices: 4.07 us -> 5.84 us  [borders(): return (lax.ppermute(ups, 'lat', up), lax.ppermute(downs, 'lat', down))]
  transfers between devices with their start and end apart: 32 -> 32, of which waited for: 17 -> 16; matrix products, arithmetic and copies ran while one was open for 2% -> 2% of each run, Pallas kernels for 11% -> 9%
where the time goes in v4:
time: 124 us; the launch traced here: 123 us
  starting transfers between devices  40.2 us (32%)
  Pallas kernels  39.5 us (32%)
  waiting for transfers between devices  34.2 us (28%)
  local copies, waits for them, and re-layouts  5.45 us (4%)
  other arithmetic  2.6 us (2%)
  between operations  1.32 us (1%)
    ppermute x28, waiting for transfers between devices, swapped(): return lax.ppermute(values, axis, [(i, i ^ bit) for i in range(count)])  32.3 us
    ppermute x28, starting transfers between devices, swapped(): return lax.ppermute(values, axis, [(i, i ^ bit) for i in range(count)])  27.6 us
    pallas_call x1, Pallas kernels, update(): pl.pallas_call(functools.partial(update_kernel, dims), in_specs=[smem] *...  26.1 us
    ppermute x2, starting transfers between devices, borders(): return (lax.ppermute(ups, 'lat', up), lax.ppermute(downs, 'lat', down))  5.84 us
    pallas_call x2, Pallas kernels, unpack(): pl.pallas_call(functools.partial(unpack_kernel, flip, scale), in_specs=[v...  5.68 us
    pallas_call x1, Pallas kernels, finish(): pl.pallas_call(functools.partial(finish_kernel, dims), in_specs=[smem] +...  5.6 us
    ppermute x1, starting transfers between devices, on_device(): above = lax.ppermute(flat[-cols:], 'lat', down)  5.47 us
    unnamed x44, local copies, waits for them, and re-layouts  3.09 us
  transfers between devices with their start and end apart: 32, of which 16 were waited for; matrix products, arithmetic and copies ran while one was open for 2% of the time, Pallas kernels for 9%

profile of v4, /device:TPU:0, one launch (start us, length us, event | category | flops | bytes accessed | tf_op | source)
XLA Modules:
  0.0 123.3 jit_solution(4258734026474710189)
XLA Ops:
  0.6 0.9 slice_bitcast_fusion
  1.5 1.3 %collective-permute-start.1 = (bf16[64,512]{1,0:T(8,128)(2,1)S(1)}, bf16[64,512]{1,0:T(8,128)(2,1)S(1)}, u32[]{:S(2)}, u32[]{:S(2)}) collective-permute-start(bf16[64,512]{1,0:T(8,128)(2,1)S(1)} %get-tuple-element.92), channel_id=1, source_target_pairs={{8,0},{16,8},{24,16},{9,1},{17,9},{25,17},{10,2},{18,10},{26,18},{... | collective-permute-start | bytes 196616 | tf_op jit(solution)/shard_map/ppermute | solution.py:681
  2.8 5.5 %collective-permute-start = (bf16[64,512]{1,0:T(8,128)(2,1)S(1)}, bf16[64,512]{1,0:T(8,128)(2,1)S(1)}, u32[]{:S(2)}, u32[]{:S(2)}) collective-permute-start(bf16[64,512]{1,0:T(8,128)(2,1)S(1)} %get-tuple-element.93), channel_id=1, source_target_pairs={{0,8},{8,16},{16,24},{1,9},{9,17},{17,25},{2,10},{10,18},{18,26},{... | collective-permute-start | bytes 196616 | tf_op jit(solution)/shard_map/ppermute | solution.py:680
  8.3 2.1 %pack_nodes.1 = bf16[48,512]{1,0:T(8,128)(2,1)} custom-call(s32[16]{0:T(128)} %bitcast.54, bf16[1024,512]{1,0:T(8,128)(2,1)} %bitcast.34), custom_call_target="tpu_custom_call" | custom-call | tf_op jit(solution)/shard_map/pack_nodes/pallas_call | solution.py:80
  10.5 0.9 pad_maximum_fusion.5
  11.4 4.2 %collective-permute-start.4 = (bf16[64,512]{1,0:T(8,128)(2,1)S(1)}, bf16[64,512]{1,0:T(8,128)(2,1)S(1)}, u32[]{:S(2)}, u32[]{:S(2)}) collective-permute-start(bf16[64,512]{1,0:T(8,128)(2,1)S(1)} %pad_maximum_fusion.5), channel_id=1, source_target_pairs={{0,6},{1,7},{2,4},{3,5},{4,2},{5,3},{6,0},{7,1},{8,14},{9,15},{10,... | collective-permute-start | bytes 196616 | tf_op jit(solution)/shard_map/ppermute | solution.py:557
  15.6 0.6 collective-permute-start.2
  16.3 2.4 %collective-permute-done.4 = bf16[64,512]{1,0:T(8,128)(2,1)S(1)} collective-permute-done((bf16[64,512]{1,0:T(8,128)(2,1)S(1)}, bf16[64,512]{1,0:T(8,128)(2,1)S(1)}, u32[]{:S(2)}, u32[]{:S(2)}) %collective-permute-start.4) | collective-permute-done | bytes 65568 | tf_op jit(solution)/shard_map/ppermute | solution.py:557
  18.6 2.3 %collective-permute-done.3 = bf16[64,512]{1,0:T(8,128)(2,1)S(1)} collective-permute-done((bf16[64,512]{1,0:T(8,128)(2,1)S(1)}, bf16[64,512]{1,0:T(8,128)(2,1)S(1)}, u32[]{:S(2)}, u32[]{:S(2)}) %collective-permute-start.3) | collective-permute-done | bytes 65568 | tf_op jit(solution)/shard_map/ppermute | solution.py:557
  20.9 0.2 concatenate.26.refs_2_
  21.0 0.1 collective-permute-start.5
  21.1 1.5 %collective-permute-done.5.refs_3_ = bf16[256,512]{1,0:T(8,128)(2,1)S(1)} collective-permute-done((bf16[256,512]{1,0:T(8,128)(2,1)S(1)}, bf16[256,512]{1,0:T(8,128)(2,1)S(1)}, u32[]{:S(2)}, u32[]{:S(2)}) %collective-permute-start.5) | collective-permute-done | bytes 262176 | tf_op jit(solution)/shard_map/ppermute | solution.py:557
  22.7 0.7 copy-done.21
  23.4 26.1 %update.1 = (bf16[1024,512]{1,0:T(8,128)(2,1)}, bf16[1024,512]{1,0:T(8,128)(2,1)}, bf16[1024,512]{1,0:T(8,128)(2,1)}, bf16[1024,512]{1,0:T(8,128)(2,1)}, bf16[64...) custom-call(s32[16]{0:T(128)} %bitcast.55, ...), custom_call_target="tpu_custom_call" | custom-call | flops 6979321856 | bytes 20000000 | tf_op jit(solution)/shard_map/update/pallas_call | solution.py:456
  49.5 0.2 collective-permute-start.13
  49.7 0.4 collective-permute-start.7
  50.1 0.1 collective-permute-start.9
  50.2 0.4 collective-permute-start.11
  50.6 0.7 collective-permute-done.13
  51.3 1.0 add_convert_fusion.4
  52.3 0.9 collective-permute-start.14
  53.3 2.5 %collective-permute-start.16 = (bf16[64,512]{1,0:T(8,128)(2,1)S(1)}, bf16[64,512]{1,0:T(8,128)(2,1)S(1)}, u32[]{:S(2)}, u32[]{:S(2)}) collective-permute-start(bf16[64,512]{1,0:T(8,128)(2,1)S(1)} %get-tuple-element.99), channel_id=1, source_target_pairs={{0,6},{1,7},{2,4},{3,5},{4,2},{5,3},{6,0},{7,1},{8,14},{9,15},{10,... | collective-permute-start | bytes 196616 | tf_op jit(solution)/shard_map/ppermute | solution.py:557
  55.8 0.1 add_convert_fusion.3
  55.9 3.1 %collective-permute-start.8 = (bf16[336,512]{1,0:T(8,128)(2,1)S(1)}, bf16[336,512]{1,0:T(8,128)(2,1)S(1)}, u32[]{:S(2)}, u32[]{:S(2)}) collective-permute-start(bf16[336,512]{1,0:T(8,128)(2,1)S(1)} %add_convert_fusion.3), channel_id=1, source_target_pairs={{0,24},{8,16},{16,8},{24,0},{1,25},{9,17},{17,9},{25,1},{2,26},{10... | collective-permute-start | bytes 1032200 | tf_op jit(solution)/shard_map/ppermute | solution.py:557
  59.0 0.1 add_convert_fusion.2
  59.1 1.8 %collective-permute-start.10 = (bf16[336,512]{1,0:T(8,128)(2,1)S(1)}, bf16[336,512]{1,0:T(8,128)(2,1)S(1)}, u32[]{:S(2)}, u32[]{:S(2)}) collective-permute-start(bf16[336,512]{1,0:T(8,128)(2,1)S(1)} %add_convert_fusion.2), channel_id=1, source_target_pairs={{0,16},{8,24},{16,0},{24,8},{1,17},{9,25},{17,1},{25,9},{2,18},{10... | collective-permute-start | bytes 1032200 | tf_op jit(solution)/shard_map/ppermute | solution.py:557
  60.9 0.1 add_convert_fusion.1
  61.0 1.5 %collective-permute-start.12 = (bf16[336,512]{1,0:T(8,128)(2,1)S(1)}, bf16[336,512]{1,0:T(8,128)(2,1)S(1)}, u32[]{:S(2)}, u32[]{:S(2)}) collective-permute-start(bf16[336,512]{1,0:T(8,128)(2,1)S(1)} %add_convert_fusion.1), channel_id=1, source_target_pairs={{0,8},{8,0},{16,24},{24,16},{1,9},{9,1},{17,25},{25,17},{2,10},{10... | collective-permute-start | bytes 1032200 | tf_op jit(solution)/shard_map/ppermute | solution.py:557
  62.5 0.1 collective-permute-start.15
  62.6 5.6 %collective-permute-done.15 = bf16[64,512]{1,0:T(8,128)(2,1)S(1)} collective-permute-done((bf16[64,512]{1,0:T(8,128)(2,1)S(1)}, bf16[64,512]{1,0:T(8,128)(2,1)S(1)}, u32[]{:S(2)}, u32[]{:S(2)}) %collective-permute-start.15) | collective-permute-done | bytes 65568 | tf_op jit(solution)/shard_map/ppermute | solution.py:557
  68.3 6.9 %collective-permute-done.10 = bf16[336,512]{1,0:T(8,128)(2,1)S(1)} collective-permute-done((bf16[336,512]{1,0:T(8,128)(2,1)S(1)}, bf16[336,512]{1,0:T(8,128)(2,1)S(1)}, u32[]{:S(2)}, u32[]{:S(2)}) %collective-permute-start.10) | collective-permute-done | bytes 344096 | tf_op jit(solution)/shard_map/ppermute | solution.py:557
  75.2 1.1 collective-permute-done.12
  76.3 0.2 add_convert_fusion
  76.6 0.1 collective-permute-start.17
  76.7 0.7 copy-done.16
  77.4 0.9 collective-permute-start.19
  78.4 1.9 %collective-permute-start.18 = (bf16[96,512]{1,0:T(8,128)(2,1)S(1)}, bf16[96,512]{1,0:T(8,128)(2,1)S(1)}, u32[]{:S(2)}, u32[]{:S(2)}) collective-permute-start(bf16[96,512]{1,0:T(8,128)(2,1)S(1)} %get-tuple-element.108), channel_id=1, source_target_pairs={{0,4},{1,5},{2,6},{3,7},{4,0},{5,1},{6,2},{7,3},{8,12},{9,13},{10,... | collective-permute-start | bytes 294920 | tf_op jit(solution)/shard_map/ppermute | solution.py:557
  80.3 2.5 %collective-permute-done.17 = bf16[96,512]{1,0:T(8,128)(2,1)S(1)} collective-permute-done((bf16[96,512]{1,0:T(8,128)(2,1)S(1)}, bf16[96,512]{1,0:T(8,128)(2,1)S(1)}, u32[]{:S(2)}, u32[]{:S(2)}) %collective-permute-start.17) | collective-permute-done | bytes 98336 | tf_op jit(solution)/shard_map/ppermute | solution.py:557
  82.8 1.3 %collective-permute-start.20 = (bf16[64,512]{1,0:T(8,128)(2,1)S(1)}, bf16[64,512]{1,0:T(8,128)(2,1)S(1)}, u32[]{:S(2)}, u32[]{:S(2)}) collective-permute-start(bf16[64,512]{1,0:T(8,128)(2,1)S(1)} %pad_maximum_fusion.6), channel_id=1, source_target_pairs={{8,0},{16,8},{24,16},{9,1},{17,9},{25,17},{10,2},{18,10},{26,18},{... | collective-permute-start | bytes 196616 | tf_op jit(solution)/shard_map/ppermute | solution.py:719
  84.1 4.5 %collective-permute-start.21 = (bf16[64,512]{1,0:T(8,128)(2,1)S(1)}, bf16[64,512]{1,0:T(8,128)(2,1)S(1)}, u32[]{:S(2)}, u32[]{:S(2)}) collective-permute-start(bf16[64,512]{1,0:T(8,128)(2,1)S(1)} %pad_maximum_fusion.7), channel_id=1, source_target_pairs={{0,8},{8,16},{16,24},{1,9},{9,17},{17,25},{2,10},{10,18},{18,26},{... | collective-permute-start | bytes 196616 | tf_op jit(solution)/shard_map/ppermute | solution.py:719
  88.7 0.6 collective-permute-done.20.refs_4_
  89.4 1.2 collective-permute-done.21.refs_5_
  90.6 0.6 copy-done.18
  91.2 0.1 collective-permute-start.22
  91.3 0.7 collective-permute-start.23
  92.0 3.6 %collective-permute-start.24 = (bf16[80,512]{1,0:T(8,128)(2,1)S(1)}, bf16[80,512]{1,0:T(8,128)(2,1)S(1)}, u32[]{:S(2)}, u32[]{:S(2)}) collective-permute-start(bf16[80,512]{1,0:T(8,128)(2,1)S(1)} %slice.135), channel_id=1, source_target_pairs={{0,6},{1,7},{2,4},{3,5},{4,2},{5,3},{6,0},{7,1},{8,14},{9,15},{10,... | collective-permute-start | bytes 245768 | tf_op jit(solution)/shard_map/ppermute | solution.py:557
  95.7 0.1 collective-permute-done.22
  95.8 1.0 collective-permute-done.23
  96.7 2.4 %collective-permute-done.24 = bf16[80,512]{1,0:T(8,128)(2,1)S(1)} collective-permute-done((bf16[80,512]{1,0:T(8,128)(2,1)S(1)}, bf16[80,512]{1,0:T(8,128)(2,1)S(1)}, u32[]{:S(2)}, u32[]{:S(2)}) %collective-permute-start.24) | collective-permute-done | bytes 81952 | tf_op jit(solution)/shard_map/ppermute | solution.py:557
  99.1 0.6 gather_fusion
  99.7 2.2 %collective-permute-start.27 = (bf16[320,512]{1,0:T(8,128)(2,1)S(1)}, bf16[320,512]{1,0:T(8,128)(2,1)S(1)}, u32[]{:S(2)}, u32[]{:S(2)}) collective-permute-start(bf16[320,512]{1,0:T(8,128)(2,1)S(1)} %bitcast.36), channel_id=1, source_target_pairs={{0,24},{8,16},{16,8},{24,0},{1,25},{9,17},{17,9},{25,1},{2,26},{10... | collective-permute-start | bytes 983048 | tf_op jit(solution)/shard_map/ppermute | solution.py:557
  101.9 1.7 %collective-permute-start.26 = (bf16[320,512]{1,0:T(8,128)(2,1)S(1)}, bf16[320,512]{1,0:T(8,128)(2,1)S(1)}, u32[]{:S(2)}, u32[]{:S(2)}) collective-permute-start(bf16[320,512]{1,0:T(8,128)(2,1)S(1)} %bitcast.37), channel_id=1, source_target_pairs={{0,16},{8,24},{16,0},{24,8},{1,17},{9,25},{17,1},{25,9},{2,18},{10... | collective-permute-start | bytes 983048 | tf_op jit(solution)/shard_map/ppermute | solution.py:557
  103.6 5.6 %finish.1 = bf16[1024,512]{1,0:T(8,128)(2,1)} custom-call(s32[16]{0:T(128)} %bitcast.56, bf16[1024,512]{1,0:T(8,128)(2,1)} %bitcast.44, bf16[1024,512]{1,0:T(8,128)(2,1)} %get-tuple-element.73.refs_1_, bf16[1024,512]{1,0:T(8,128)(2,1)} %get-tuple-element.74.refs_2_, bf16[1024,512]{1,0:T(8,128)(2,1)} %get-tuple-element.75.refs_3_, ...), custom_call_target="tpu_custom_call" | custom-call | flops 1610612736 | bytes 8000000 | tf_op jit(solution)/shard_map/finish/pallas_call | solution.py:541
  109.3 1.2 collective-permute-done.27.refs_3_
  110.4 3.4 %collective-permute-done.26.refs_2_ = bf16[320,512]{1,0:T(8,128)(2,1)S(1)} collective-permute-done((bf16[320,512]{1,0:T(8,128)(2,1)S(1)}, bf16[320,512]{1,0:T(8,128)(2,1)S(1)}, u32[]{:S(2)}, u32[]{:S(2)}) %collective-permute-start.26) | collective-permute-done | bytes 327712 | tf_op jit(solution)/shard_map/ppermute | solution.py:557
  113.8 1.5 %collective-permute-done.25.refs_1_ = bf16[320,512]{1,0:T(8,128)(2,1)S(1)} collective-permute-done((bf16[320,512]{1,0:T(8,128)(2,1)S(1)}, bf16[320,512]{1,0:T(8,128)(2,1)S(1)}, u32[]{:S(2)}, u32[]{:S(2)}) %collective-permute-start.25) | collective-permute-done | bytes 327712 | tf_op jit(solution)/shard_map/ppermute | solution.py:557
  115.3 0.5 collective-permute-start.30
  115.8 0.6 fusion.6
  116.4 2.8 %unpack_0.1 = (f32[512,512]{1,0:T(8,128)}, f32[512,512]{1,0:T(8,128)}, f32[512,512]{1,0:T(8,128)}, f32[512,512]{1,0:T(8,128)}, f32[512,512]{1,0:T(8,128)}) custom-call(bf16[320,512]{1,0:T(8,128)(2,1)} %bitcast.40, bf16[320,512]{1,0:T(8,128)(2,1)} %copy-done.13, bf16[320,512]{1,0:T(8,128)(2,1)} %copy-done.12, bf16[320,512]{1,0:T(8,128)(2,1)} %copy-done.11), custom_call_target="tpu_custom_call" | custom-call | bytes 8000000 | tf_op jit(solution)/shard_map/unpack_0/pallas_call | solution.py:634
  119.3 0.7 copy-done.7
  120.0 0.1 copy-done.8
  120.1 0.2 copy-done.9
  120.2 0.1 copy-done.10
  120.3 2.8 %unpack_1.1 = (f32[512,512]{1,0:T(8,128)}, f32[512,512]{1,0:T(8,128)}, f32[512,512]{1,0:T(8,128)}, f32[512,512]{1,0:T(8,128)}, f32[512,512]{1,0:T(8,128)}) custom-call(bf16[320,512]{1,0:T(8,128)(2,1)} %copy-done.7, bf16[320,512]{1,0:T(8,128)(2,1)} %copy-done.8, ...), custom_call_target="tpu_custom_call", output_to_operand_aliasing={{0}: (4, {}), {1}: (5, {}), {2}: (6, {}), {3}: (7, {}), {4}... | custom-call | bytes 8000000 | tf_op jit(solution)/shard_map/unpack_1/pallas_call | solution.py:634
  (81 shorter events, 0.5 us)
Async XLA Ops:
  1.5 8.9 %collective-permute-start.1 = (bf16[64,512]{1,0:T(8,128)(2,1)S(1)}, bf16[64,512]{1,0:T(8,128)(2,1)S(1)}, u32[]{:S(2)}, u32[]{:S(2)}) collective-permute-start(bf16[64,512]{1,0:T(8,128)(2,1)S(1)} %get-tuple-element.92), channel_id=1, source_target_pairs={{8,0},{16,8},{24,16},{9,1},{17,9},{25,17},{10,2},{18,10},{26,18},{... | collective-permute-start | bytes 196616 | tf_op jit(solution)/shard_map/ppermute | solution.py:681
  2.8 7.6 %collective-permute-start = (bf16[64,512]{1,0:T(8,128)(2,1)S(1)}, bf16[64,512]{1,0:T(8,128)(2,1)S(1)}, u32[]{:S(2)}, u32[]{:S(2)}) collective-permute-start(bf16[64,512]{1,0:T(8,128)(2,1)S(1)} %get-tuple-element.93), channel_id=1, source_target_pairs={{0,8},{8,16},{16,24},{1,9},{9,17},{17,25},{2,10},{10,18},{18,26},{... | collective-permute-start | bytes 196616 | tf_op jit(solution)/shard_map/ppermute | solution.py:680
  10.5 0.9 copy-start.19
  10.5 0.9 copy-start.20
  10.5 10.4 %copy-start.2 = (bf16[48,512]{1,0:T(8,128)(2,1)S(1)}, bf16[48,512]{1,0:T(8,128)(2,1)}, u32[]{:S(2)}) copy-start(bf16[48,512]{1,0:T(8,128)(2,1)} %pack_nodes.1) | copy-start | bytes 147460
  11.4 7.2 %collective-permute-start.4 = (bf16[64,512]{1,0:T(8,128)(2,1)S(1)}, bf16[64,512]{1,0:T(8,128)(2,1)S(1)}, u32[]{:S(2)}, u32[]{:S(2)}) collective-permute-start(bf16[64,512]{1,0:T(8,128)(2,1)S(1)} %pad_maximum_fusion.5), channel_id=1, source_target_pairs={{0,6},{1,7},{2,4},{3,5},{4,2},{5,3},{6,0},{7,1},{8,14},{9,15},{10,... | collective-permute-start | bytes 196616 | tf_op jit(solution)/shard_map/ppermute | solution.py:557
  15.6 5.2 %collective-permute-start.3 = (bf16[64,512]{1,0:T(8,128)(2,1)S(1)}, bf16[64,512]{1,0:T(8,128)(2,1)S(1)}, u32[]{:S(2)}, u32[]{:S(2)}) collective-permute-start(bf16[64,512]{1,0:T(8,128)(2,1)S(1)} %pad_maximum_fusion.5), channel_id=1, source_target_pairs={{0,4},{1,5},{2,6},{3,7},{4,0},{5,1},{6,2},{7,3},{8,12},{9,13},{10,... | collective-permute-start | bytes 196616 | tf_op jit(solution)/shard_map/ppermute | solution.py:557
  15.6 5.2 %collective-permute-start.2 = (bf16[64,512]{1,0:T(8,128)(2,1)S(1)}, bf16[64,512]{1,0:T(8,128)(2,1)S(1)}, u32[]{:S(2)}, u32[]{:S(2)}) collective-permute-start(bf16[64,512]{1,0:T(8,128)(2,1)S(1)} %pad_maximum_fusion.5), channel_id=1, source_target_pairs={{0,2},{1,3},{2,0},{3,1},{4,6},{5,7},{6,4},{7,5},{8,10},{9,11},{10,... | collective-permute-start | bytes 196616 | tf_op jit(solution)/shard_map/ppermute | solution.py:557
  21.0 1.6 %copy-start.14 = (bf16[256,512]{1,0:T(8,128)(2,1)}, bf16[256,512]{1,0:T(8,128)(2,1)S(1)}, u32[]{:S(2)}) copy-start(bf16[256,512]{1,0:T(8,128)(2,1)S(1)} %concatenate.26.refs_2_) | copy-start | bytes 786436
  21.0 1.6 %collective-permute-start.5 = (bf16[256,512]{1,0:T(8,128)(2,1)S(1)}, bf16[256,512]{1,0:T(8,128)(2,1)S(1)}, u32[]{:S(2)}, u32[]{:S(2)}) collective-permute-start(bf16[256,512]{1,0:T(8,128)(2,1)S(1)} %concatenate.26.refs_2_), channel_id=1, source_target_pairs={{0,1},{1,0},{2,3},{3,2},{4,5},{5,4},{6,7},{7,6},{8,9},{9,8},{10,11... | collective-permute-start | bytes 786440 | tf_op jit(solution)/shard_map/ppermute | solution.py:557
  22.6 0.7 copy-start.21
  49.5 1.8 %collective-permute-start.13 = (bf16[256,512]{1,0:T(8,128)(2,1)}, bf16[256,512]{1,0:T(8,128)(2,1)S(1)}, u32[]{:S(2)}, u32[]{:S(2)}) collective-permute-start(bf16[256,512]{1,0:T(8,128)(2,1)} %get-tuple-element.61), channel_id=1, source_target_pairs={{0,1},{1,0},{2,3},{3,2},{4,5},{5,4},{6,7},{7,6},{8,9},{9,8},{10,11... | collective-permute-start | bytes 786440 | tf_op jit(solution)/shard_map/ppermute | solution.py:557
  49.7 6.1 %collective-permute-start.7 = (bf16[336,512]{1,0:T(8,128)(2,1)}, bf16[336,512]{1,0:T(8,128)(2,1)S(1)}, u32[]{:S(2)}, u32[]{:S(2)}) collective-permute-start(bf16[336,512]{1,0:T(8,128)(2,1)} %get-tuple-element.55), channel_id=1, source_target_pairs={{0,1},{1,0},{2,3},{3,2},{4,5},{5,4},{6,7},{7,6},{8,9},{9,8},{10,11... | collective-permute-start | bytes 1032200 | tf_op jit(solution)/shard_map/ppermute | solution.py:557
  50.1 8.9 %collective-permute-start.9 = (bf16[336,512]{1,0:T(8,128)(2,1)}, bf16[336,512]{1,0:T(8,128)(2,1)S(1)}, u32[]{:S(2)}, u32[]{:S(2)}) collective-permute-start(bf16[336,512]{1,0:T(8,128)(2,1)} %get-tuple-element.57), channel_id=1, source_target_pairs={{0,1},{1,0},{2,3},{3,2},{4,5},{5,4},{6,7},{7,6},{8,9},{9,8},{10,11... | collective-permute-start | bytes 1032200 | tf_op jit(solution)/shard_map/ppermute | solution.py:557
  50.2 10.7 %collective-permute-start.11 = (bf16[336,512]{1,0:T(8,128)(2,1)}, bf16[336,512]{1,0:T(8,128)(2,1)S(1)}, u32[]{:S(2)}, u32[]{:S(2)}) collective-permute-start(bf16[336,512]{1,0:T(8,128)(2,1)} %get-tuple-element.59), channel_id=1, source_target_pairs={{0,1},{1,0},{2,3},{3,2},{4,5},{5,4},{6,7},{7,6},{8,9},{9,8},{10,11... | collective-permute-start | bytes 1032200 | tf_op jit(solution)/shard_map/ppermute | solution.py:557
  52.3 3.5 %copy-start.5 = (bf16[336,512]{1,0:T(8,128)(2,1)S(1)}, bf16[336,512]{1,0:T(8,128)(2,1)}, u32[]{:S(2)}) copy-start(bf16[336,512]{1,0:T(8,128)(2,1)} %get-tuple-element.54) | copy-start | bytes 1032196
  52.3 10.1 %collective-permute-start.14 = (bf16[64,512]{1,0:T(8,128)(2,1)S(1)}, bf16[64,512]{1,0:T(8,128)(2,1)S(1)}, u32[]{:S(2)}, u32[]{:S(2)}) collective-permute-start(bf16[64,512]{1,0:T(8,128)(2,1)S(1)} %get-tuple-element.98), channel_id=1, source_target_pairs={{0,2},{1,3},{2,0},{3,1},{4,6},{5,7},{6,4},{7,5},{8,10},{9,11},{10,... | collective-permute-start | bytes 196616 | tf_op jit(solution)/shard_map/ppermute | solution.py:557
  53.3 9.2 %collective-permute-start.16 = (bf16[64,512]{1,0:T(8,128)(2,1)S(1)}, bf16[64,512]{1,0:T(8,128)(2,1)S(1)}, u32[]{:S(2)}, u32[]{:S(2)}) collective-permute-start(bf16[64,512]{1,0:T(8,128)(2,1)S(1)} %get-tuple-element.99), channel_id=1, source_target_pairs={{0,6},{1,7},{2,4},{3,5},{4,2},{5,3},{6,0},{7,1},{8,14},{9,15},{10,... | collective-permute-start | bytes 196616 | tf_op jit(solution)/shard_map/ppermute | solution.py:557
  55.8 3.2 %copy-start.4 = (bf16[336,512]{1,0:T(8,128)(2,1)S(1)}, bf16[336,512]{1,0:T(8,128)(2,1)}, u32[]{:S(2)}) copy-start(bf16[336,512]{1,0:T(8,128)(2,1)} %get-tuple-element.56) | copy-start | bytes 1032196
  55.9 12.4 %collective-permute-start.8 = (bf16[336,512]{1,0:T(8,128)(2,1)S(1)}, bf16[336,512]{1,0:T(8,128)(2,1)S(1)}, u32[]{:S(2)}, u32[]{:S(2)}) collective-permute-start(bf16[336,512]{1,0:T(8,128)(2,1)S(1)} %add_convert_fusion.3), channel_id=1, source_target_pairs={{0,24},{8,16},{16,8},{24,0},{1,25},{9,17},{17,9},{25,1},{2,26},{10... | collective-permute-start | bytes 1032200 | tf_op jit(solution)/shard_map/ppermute | solution.py:557
  59.0 1.9 %copy-start.3 = (bf16[336,512]{1,0:T(8,128)(2,1)S(1)}, bf16[336,512]{1,0:T(8,128)(2,1)}, u32[]{:S(2)}) copy-start(bf16[336,512]{1,0:T(8,128)(2,1)} %get-tuple-element.58) | copy-start | bytes 1032196
  59.1 16.1 %collective-permute-start.10 = (bf16[336,512]{1,0:T(8,128)(2,1)S(1)}, bf16[336,512]{1,0:T(8,128)(2,1)S(1)}, u32[]{:S(2)}, u32[]{:S(2)}) collective-permute-start(bf16[336,512]{1,0:T(8,128)(2,1)S(1)} %add_convert_fusion.2), channel_id=1, source_target_pairs={{0,16},{8,24},{16,0},{24,8},{1,17},{9,25},{17,1},{25,9},{2,18},{10... | collective-permute-start | bytes 1032200 | tf_op jit(solution)/shard_map/ppermute | solution.py:557
  60.9 15.3 %copy-start.6 = (bf16[336,512]{1,0:T(8,128)(2,1)S(1)}, bf16[336,512]{1,0:T(8,128)(2,1)}, u32[]{:S(2)}) copy-start(bf16[336,512]{1,0:T(8,128)(2,1)} %get-tuple-element.52) | copy-start | bytes 1032196
  61.0 15.3 %collective-permute-start.12 = (bf16[336,512]{1,0:T(8,128)(2,1)S(1)}, bf16[336,512]{1,0:T(8,128)(2,1)S(1)}, u32[]{:S(2)}, u32[]{:S(2)}) collective-permute-start(bf16[336,512]{1,0:T(8,128)(2,1)S(1)} %add_convert_fusion.1), channel_id=1, source_target_pairs={{0,8},{8,0},{16,24},{24,16},{1,9},{9,1},{17,25},{25,17},{2,10},{10... | collective-permute-start | bytes 1032200 | tf_op jit(solution)/shard_map/ppermute | solution.py:557
  62.5 13.8 %collective-permute-start.6 = (bf16[336,512]{1,0:T(8,128)(2,1)}, bf16[336,512]{1,0:T(8,128)(2,1)S(1)}, u32[]{:S(2)}, u32[]{:S(2)}) collective-permute-start(bf16[336,512]{1,0:T(8,128)(2,1)} %get-tuple-element.53), channel_id=1, source_target_pairs={{0,1},{1,0},{2,3},{3,2},{4,5},{5,4},{6,7},{7,6},{8,9},{9,8},{10,11... | collective-permute-start | bytes 1032200 | tf_op jit(solution)/shard_map/ppermute | solution.py:557
  62.5 5.7 %collective-permute-start.15 = (bf16[64,512]{1,0:T(8,128)(2,1)S(1)}, bf16[64,512]{1,0:T(8,128)(2,1)S(1)}, u32[]{:S(2)}, u32[]{:S(2)}) collective-permute-start(bf16[64,512]{1,0:T(8,128)(2,1)S(1)} %get-tuple-element.100), channel_id=1, source_target_pairs={{0,4},{1,5},{2,6},{3,7},{4,0},{5,1},{6,2},{7,3},{8,12},{9,13},{10,... | collective-permute-start | bytes 196616 | tf_op jit(solution)/shard_map/ppermute | solution.py:557
  68.2 14.5 %copy-start.1 = (f32[64,512]{1,0:T(8,128)}, f32[64,512]{1,0:T(8,128)S(1)}, u32[]{:S(2)}) copy-start(f32[64,512]{1,0:T(8,128)S(1)} %convert_add_fusion.1.refs_6_) | copy-start | bytes 393220
  76.6 0.8 copy-start.16
  76.6 6.1 %collective-permute-start.17 = (bf16[96,512]{1,0:T(8,128)(2,1)S(1)}, bf16[96,512]{1,0:T(8,128)(2,1)S(1)}, u32[]{:S(2)}, u32[]{:S(2)}) collective-permute-start(bf16[96,512]{1,0:T(8,128)(2,1)S(1)} %get-tuple-element.107), channel_id=1, source_target_pairs={{0,2},{1,3},{2,0},{3,1},{4,6},{5,7},{6,4},{7,5},{8,10},{9,11},{10,... | collective-permute-start | bytes 294920 | tf_op jit(solution)/shard_map/ppermute | solution.py:557
  77.4 11.3 %collective-permute-start.19 = (bf16[96,512]{1,0:T(8,128)(2,1)S(1)}, bf16[96,512]{1,0:T(8,128)(2,1)S(1)}, u32[]{:S(2)}, u32[]{:S(2)}) collective-permute-start(bf16[96,512]{1,0:T(8,128)(2,1)S(1)} %get-tuple-element.106), channel_id=1, source_target_pairs={{0,6},{1,7},{2,4},{3,5},{4,2},{5,3},{6,0},{7,1},{8,14},{9,15},{10,... | collective-permute-start | bytes 294920 | tf_op jit(solution)/shard_map/ppermute | solution.py:557
  78.4 4.4 %copy-start.15 = (bf16[64,512]{1,0:T(8,128)(2,1)S(1)}, bf16[64,512]{1,0:T(8,128)(2,1)}, u32[]{:S(2)}) copy-start(bf16[64,512]{1,0:T(8,128)(2,1)} %get-tuple-element.69) | copy-start | bytes 196612
  78.4 10.3 %collective-permute-start.18 = (bf16[96,512]{1,0:T(8,128)(2,1)S(1)}, bf16[96,512]{1,0:T(8,128)(2,1)S(1)}, u32[]{:S(2)}, u32[]{:S(2)}) collective-permute-start(bf16[96,512]{1,0:T(8,128)(2,1)S(1)} %get-tuple-element.108), channel_id=1, source_target_pairs={{0,4},{1,5},{2,6},{3,7},{4,0},{5,1},{6,2},{7,3},{8,12},{9,13},{10,... | collective-permute-start | bytes 294920 | tf_op jit(solution)/shard_map/ppermute | solution.py:557
  82.8 6.5 %collective-permute-start.20 = (bf16[64,512]{1,0:T(8,128)(2,1)S(1)}, bf16[64,512]{1,0:T(8,128)(2,1)S(1)}, u32[]{:S(2)}, u32[]{:S(2)}) collective-permute-start(bf16[64,512]{1,0:T(8,128)(2,1)S(1)} %pad_maximum_fusion.6), channel_id=1, source_target_pairs={{8,0},{16,8},{24,16},{9,1},{17,9},{25,17},{10,2},{18,10},{26,18},{... | collective-permute-start | bytes 196616 | tf_op jit(solution)/shard_map/ppermute | solution.py:719
  84.1 6.4 %collective-permute-start.21 = (bf16[64,512]{1,0:T(8,128)(2,1)S(1)}, bf16[64,512]{1,0:T(8,128)(2,1)S(1)}, u32[]{:S(2)}, u32[]{:S(2)}) collective-permute-start(bf16[64,512]{1,0:T(8,128)(2,1)S(1)} %pad_maximum_fusion.7), channel_id=1, source_target_pairs={{0,8},{8,16},{16,24},{1,9},{9,17},{17,25},{2,10},{10,18},{18,26},{... | collective-permute-start | bytes 196616 | tf_op jit(solution)/shard_map/ppermute | solution.py:719
  89.4 1.3 %copy-start.17 = (bf16[64,512]{1,0:T(8,128)(2,1)}, bf16[64,512]{1,0:T(8,128)(2,1)S(1)}, u32[]{:S(2)}) copy-start(bf16[64,512]{1,0:T(8,128)(2,1)S(1)} %collective-permute-done.20.refs_4_) | copy-start | bytes 196612
  90.6 0.6 copy-start.18
  91.2 4.5 %collective-permute-start.22 = (bf16[80,512]{1,0:T(8,128)(2,1)S(1)}, bf16[80,512]{1,0:T(8,128)(2,1)S(1)}, u32[]{:S(2)}, u32[]{:S(2)}) collective-permute-start(bf16[80,512]{1,0:T(8,128)(2,1)S(1)} %slice.135), channel_id=1, source_target_pairs={{0,2},{1,3},{2,0},{3,1},{4,6},{5,7},{6,4},{7,5},{8,10},{9,11},{10,... | collective-permute-start | bytes 245768 | tf_op jit(solution)/shard_map/ppermute | solution.py:557
  91.3 5.4 %collective-permute-start.23 = (bf16[80,512]{1,0:T(8,128)(2,1)S(1)}, bf16[80,512]{1,0:T(8,128)(2,1)S(1)}, u32[]{:S(2)}, u32[]{:S(2)}) collective-permute-start(bf16[80,512]{1,0:T(8,128)(2,1)S(1)} %slice.135), channel_id=1, source_target_pairs={{0,4},{1,5},{2,6},{3,7},{4,0},{5,1},{6,2},{7,3},{8,12},{9,13},{10,... | collective-permute-start | bytes 245768 | tf_op jit(solution)/shard_map/ppermute | solution.py:557
  92.0 7.0 %collective-permute-start.24 = (bf16[80,512]{1,0:T(8,128)(2,1)S(1)}, bf16[80,512]{1,0:T(8,128)(2,1)S(1)}, u32[]{:S(2)}, u32[]{:S(2)}) collective-permute-start(bf16[80,512]{1,0:T(8,128)(2,1)S(1)} %slice.135), channel_id=1, source_target_pairs={{0,6},{1,7},{2,4},{3,5},{4,2},{5,3},{6,0},{7,1},{8,14},{9,15},{10,... | collective-permute-start | bytes 245768 | tf_op jit(solution)/shard_map/ppermute | solution.py:557
  99.7 9.5 %copy-start = (bf16[5,4,16,512]{3,2,1,0:T(8,128)(2,1)}, bf16[5,4,16,512]{3,2,1,0:T(8,128)(2,1)S(1)}, u32[]{:S(2)}) copy-start(bf16[5,4,16,512]{3,2,1,0:T(8,128)(2,1)S(1)} %copy.28) | copy-start | bytes 983044
  99.7 10.7 %collective-permute-start.27 = (bf16[320,512]{1,0:T(8,128)(2,1)S(1)}, bf16[320,512]{1,0:T(8,128)(2,1)S(1)}, u32[]{:S(2)}, u32[]{:S(2)}) collective-permute-start(bf16[320,512]{1,0:T(8,128)(2,1)S(1)} %bitcast.36), channel_id=1, source_target_pairs={{0,24},{8,16},{16,8},{24,0},{1,25},{9,17},{17,9},{25,1},{2,26},{10... | collective-permute-start | bytes 983048 | tf_op jit(solution)/shard_map/ppermute | solution.py:557
  101.9 11.9 %collective-permute-start.26 = (bf16[320,512]{1,0:T(8,128)(2,1)S(1)}, bf16[320,512]{1,0:T(8,128)(2,1)S(1)}, u32[]{:S(2)}, u32[]{:S(2)}) collective-permute-start(bf16[320,512]{1,0:T(8,128)(2,1)S(1)} %bitcast.37), channel_id=1, source_target_pairs={{0,16},{8,24},{16,0},{24,8},{1,17},{9,25},{17,1},{25,9},{2,18},{10... | collective-permute-start | bytes 983048 | tf_op jit(solution)/shard_map/ppermute | solution.py:557
  103.6 11.6 %collective-permute-start.25 = (bf16[320,512]{1,0:T(8,128)(2,1)S(1)}, bf16[320,512]{1,0:T(8,128)(2,1)S(1)}, u32[]{:S(2)}, u32[]{:S(2)}) collective-permute-start(bf16[320,512]{1,0:T(8,128)(2,1)S(1)} %bitcast.38), channel_id=1, source_target_pairs={{0,8},{8,0},{16,24},{24,16},{1,9},{9,1},{17,25},{25,17},{2,10},{10... | collective-permute-start | bytes 983048 | tf_op jit(solution)/shard_map/ppermute | solution.py:557
  109.2 10.0 %collective-permute-start.28 = (bf16[320,512]{1,0:T(8,128)(2,1)S(1)}, bf16[320,512]{1,0:T(8,128)(2,1)S(1)}, u32[]{:S(2)}, u32[]{:S(2)}) collective-permute-start(bf16[320,512]{1,0:T(8,128)(2,1)S(1)} %bitcast.39), channel_id=1, source_target_pairs={{0,1},{1,0},{2,3},{3,2},{4,5},{5,4},{6,7},{7,6},{8,9},{9,8},{10,11... | collective-permute-start | bytes 983048 | tf_op jit(solution)/shard_map/ppermute | solution.py:557
  110.4 6.0 %copy-start.11 = (bf16[320,512]{1,0:T(8,128)(2,1)}, bf16[320,512]{1,0:T(8,128)(2,1)S(1)}, u32[]{:S(2)}) copy-start(bf16[320,512]{1,0:T(8,128)(2,1)S(1)} %collective-permute-done.27.refs_3_) | copy-start | bytes 983044
  113.8 2.6 %copy-start.12 = (bf16[320,512]{1,0:T(8,128)(2,1)}, bf16[320,512]{1,0:T(8,128)(2,1)S(1)}, u32[]{:S(2)}) copy-start(bf16[320,512]{1,0:T(8,128)(2,1)S(1)} %collective-permute-done.26.refs_2_) | copy-start | bytes 983044
  115.3 1.1 copy-start.13
  115.3 4.0 %collective-permute-start.29 = (bf16[320,512]{1,0:T(8,128)(2,1)S(1)}, bf16[320,512]{1,0:T(8,128)(2,1)S(1)}, u32[]{:S(2)}, u32[]{:S(2)}) collective-permute-start(bf16[320,512]{1,0:T(8,128)(2,1)S(1)} %collective-permute-done.25.refs_1_), channel_id=1, source_target_pairs={{0,1},{1,0},{2,3},{3,2},{4,5},{5,4},{6,7},{7,6},{8,9},{9,8},{10,11... | collective-permute-start | bytes 983048 | tf_op jit(solution)/shard_map/ppermute | solution.py:557
  115.3 4.0 %collective-permute-start.30 = (bf16[320,512]{1,0:T(8,128)(2,1)S(1)}, bf16[320,512]{1,0:T(8,128)(2,1)S(1)}, u32[]{:S(2)}, u32[]{:S(2)}) collective-permute-start(bf16[320,512]{1,0:T(8,128)(2,1)S(1)} %collective-permute-done.26.refs_2_), channel_id=1, source_target_pairs={{0,1},{1,0},{2,3},{3,2},{4,5},{5,4},{6,7},{7,6},{8,9},{9,8},{10,11... | collective-permute-start | bytes 983048 | tf_op jit(solution)/shard_map/ppermute | solution.py:557
  115.8 3.5 %collective-permute-start.31 = (bf16[320,512]{1,0:T(8,128)(2,1)S(1)}, bf16[320,512]{1,0:T(8,128)(2,1)S(1)}, u32[]{:S(2)}, u32[]{:S(2)}) collective-permute-start(bf16[320,512]{1,0:T(8,128)(2,1)S(1)} %collective-permute-done.27.refs_3_), channel_id=1, source_target_pairs={{0,1},{1,0},{2,3},{3,2},{4,5},{5,4},{6,7},{7,6},{8,9},{9,8},{10,11... | collective-permute-start | bytes 983048 | tf_op jit(solution)/shard_map/ppermute | solution.py:557
  119.2 0.7 copy-start.7
  119.3 0.8 copy-start.8
  119.3 1.0 copy-start.9
  119.3 1.0 copy-start.10

commit v5 on v4

--- a/solution.py
+++ b/solution.py
@@ -10,7 +10,7 @@
 epsilon = 1e-05
 EXACT = lax.Precision.HIGHEST
 ABSENT = -1000.0
-VMEM_BYTES = 60 * 1024 * 1024
+MIB = 1024 * 1024
 
 
 def dot(left, right):
@@ -264,7 +264,7 @@
         hidden_b[here, :] = to_bf16(half + half * jnp.tanh(half))
         return carry
 
-    lax.fori_loop(0, rows // tile, activate, 0)
+    lax.fori_loop(0, rows // tile, activate, 0, unroll=4)
     loads[7].wait()
     for block in blocks:
         total[block, :] = dot(hidden_b[block, :], w_out[...])
@@ -293,15 +293,14 @@
     for block in blocks:
         total[block, :] = dot_nt(d_out_b[block, :], w_out[...])
 
-    def deactivate(step, carry):
+    def deactivate(step, bias_sum):
         here = pl.ds(aligned(step * tile, tile), tile)
         slope = half_sum_and_slope(work[here, :])[1]
         d_pre = total[here, :] * (0.5 * slope)
-        sums[1] += eight_rows(d_pre)
         d_pre_b[here, :] = to_bf16(d_pre)
-        return carry
-
-    lax.fori_loop(0, rows // tile, deactivate, 0)
+        return bias_sum + eight_rows(d_pre)
+
+    sums[1] = lax.fori_loop(0, rows // tile, deactivate, nothing, unroll=4)
     leave(d_pre_b, results[1], out_sems.at[1])
     share = depth // (2 * lat_count)
 
@@ -338,15 +337,14 @@
     def slope_times(which, place, lanes):
         return to_f32(slopes[which, place, lanes]) * d_half[place, lanes]
 
-    def receive(step, carry):
+    def receive(step, bias_sum):
         base = aligned(step * tile, tile)
         here = pl.ds(base, tile)
         value = d_half[pl.ds(aligned(base + cols, tile), tile), :] * slope_sum[here, :]
         total[here, :] = value
-        sums[0] += eight_rows(value)
-        return carry
-
-    lax.fori_loop(0, rows // tile, receive, 0)
+        return bias_sum + eight_rows(value)
+
+    sums[0] = lax.fori_loop(0, rows // tile, receive, nothing, unroll=4)
     far[...] = jnp.zeros_like(far)
 
     edge_place = lax.broadcasted_iota(jnp.int32, (patch_rows, 1), 0)
@@ -487,7 +485,7 @@
             pltpu.SemaphoreType.DMA((8,)),
             pltpu.SemaphoreType.DMA((2, lat_count, 3)),
         ],
-        compiler_params=pltpu.CompilerParams(vmem_limit_bytes=VMEM_BYTES),
+        compiler_params=pltpu.CompilerParams(vmem_limit_bytes=63 * MIB),
         cost_estimate=pl.CostEstimate(
             flops=26 * rows * depth * depth, bytes_accessed=20_000_000, transcendentals=0
         ),
@@ -495,7 +493,7 @@
     )(*ints, *vectors, *arrays)
 
 
-def finish_kernel(dims, slots, *refs):
+def finish_kernel(dims, scale, slots, *refs):
     patch_rows, cols, _, coarse_count, lat_count = dims
     rows = patch_rows * cols
     (
@@ -509,7 +507,9 @@
         w_self,
         w_recv,
         w_send,
+        summed,
         grad_nodes,
+        *vectors,
         total,
     ) = refs
     step_rows = 256
@@ -518,6 +518,8 @@
         total[block, :] = to_f32(d_send[block, :])
     for start, part in ((rows - cols, from_below), (0, from_above)):
         total[pl.ds(start, cols), :] += to_f32(part[...])
+    for which, vector in enumerate(vectors):
+        vector[...] = scale * summed[pl.ds(summed.shape[0] - 8 + which, 1), :]
     returned = back[...]
     for row in range(patch_rows):
         for spot, at in ((row * cols, 0), (row * cols + cols - 1, patch_rows)):
@@ -535,16 +537,17 @@
         )
 
 
-def finish(dims, slots, arrays):
+def finish(dims, scale, slots, arrays):
     rows, depth = arrays[0].shape
     smem, vmem = pl.BlockSpec(memory_space=pltpu.SMEM), pl.BlockSpec(memory_space=pltpu.VMEM)
     return pl.pallas_call(
-        functools.partial(finish_kernel, dims),
+        functools.partial(finish_kernel, dims, scale),
         in_specs=[smem] + [vmem] * len(arrays),
-        out_specs=vmem,
-        out_shape=jax.ShapeDtypeStruct((rows, depth), jnp.bfloat16),
+        out_specs=[vmem] * 4,
+        out_shape=[jax.ShapeDtypeStruct((rows, depth), jnp.bfloat16)]
+        + [jax.ShapeDtypeStruct((1, depth), jnp.float32)] * 3,
         scratch_shapes=[pltpu.VMEM((rows, depth), jnp.float32)],
-        compiler_params=pltpu.CompilerParams(vmem_limit_bytes=VMEM_BYTES),
+        compiler_params=pltpu.CompilerParams(vmem_limit_bytes=63 * MIB),
         cost_estimate=pl.CostEstimate(
             flops=6 * rows * depth * depth, bytes_accessed=8_000_000, transcendentals=0
         ),
@@ -557,23 +560,22 @@
     return lax.ppermute(values, axis, [(i, i ^ bit) for i in range(count)])
 
 
-def summed_part(mine, other, returning, borders):
+def summed_part(mine, other, d_crossed, returning, borders):
     lat_count, depth = len(mine), mine[0].shape[-1]
     chip_count = lax.axis_size("lon") // 2
     chip = lax.axis_index("lon") // 2
     share = depth // (2 * lat_count)
     order = list(range(lat_count - 1, -1, -1))
     crossed = {step: swapped(other[step], "lon", 1) for step in order}
-    received = []
-    for step in order[:-1]:
-        message = to_bf16(to_f32(mine[step]) + to_f32(crossed[step]))
-        received.append(swapped(message, "lat", step))
-    received, returned = lax.optimization_barrier((received, returning()))
+    messages = [to_bf16(to_f32(mine[step]) + to_f32(crossed[step])) for step in order[:-1]]
+    messages[0], d_crossed = lax.optimization_barrier((messages[0], d_crossed))
+    received = [swapped(part, "lat", step) for part, step in zip(messages, order)]
+    received, returned = lax.optimization_barrier((received, returning(d_crossed)))
     total = to_f32(mine[0]) + to_f32(crossed[0])
     for part in received:
         total = total + to_f32(part)
     total = to_bf16(total)
-    vectors = total[5 * share :]
+    vectors = total[5 * share : 5 * share + 8]
     parts = total[: 5 * share].reshape(5, chip_count, share // chip_count, depth)
 
     def message_for(step):
@@ -589,7 +591,7 @@
     return total, returned, bordered
 
 
-def gathered_shares(total, lat_count, meanwhile):
+def gathered_share(total, lat_count):
     depth = total.shape[-1]
     share = depth // (2 * lat_count)
     chip_count = lax.axis_size("lon") // 2
@@ -597,53 +599,57 @@
     part = to_bf16(total[: 5 * share // chip_count])
     parts = jnp.stack([part] + [swapped(part, "lon", 2 * k) for k in range(1, chip_count)])
     parts = parts[chip ^ jnp.arange(chip_count)].reshape(chip_count, 5, -1, depth)
-    ready = jnp.transpose(parts, (1, 0, 2, 3)).reshape(5 * share, depth)
-    shares = tuple(swapped(ready, "lat", step) for step in range(1, lat_count))
-    shares, meanwhile = lax.optimization_barrier((shares, meanwhile))
-    shares = [ready, *shares]
-    return shares, [swapped(part, "lon", 1) for part in shares], meanwhile
-
-
-def unpack_kernel(flip, scale, *refs):
+    return jnp.transpose(parts, (1, 0, 2, 3)).reshape(5 * share, depth)
+
+
+def unpack_kernel(pieces, scale, *refs):
     count = len(refs)
-    lat_count = lax.axis_size("lat")
-    shares = refs[:lat_count]
-    staged, sems = refs[count - 2 :]
-    outs = refs[count - 7 : count - 2]
+    held, staged, load_sems, sems = refs[count - 4 :]
+    outs = refs[count - 9 : count - 4]
     depth = outs[0].shape[-1]
-    share = depth // (2 * lat_count)
+    share = depth // (2 * lax.axis_size("lat"))
     core, lat = lax.axis_index("lon") % 2, lax.axis_index("lat")
-    place = pl.ds(aligned((core ^ flip) * (depth // 2), depth // 2), depth // 2)
+    loads = [
+        pltpu.make_async_copy(refs[k], held.at[k], load_sems.at[k]) for k in range(len(pieces))
+    ]
+    for load in loads:
+        load.start()
     copies = []
-    for which in range(5):
-        for step in range(lat_count):
-            block = shares[step][pl.ds(which * share, share), :]
-            start = aligned((lat ^ step) * share, share)
-            staged[which, pl.ds(start, share), :] = scale * to_f32(block)
-        copies.append(
-            pltpu.make_async_copy(staged.at[which], outs[which].at[place], sems.at[which])
-        )
-        copies[-1].start()
+    for k, (flip, step) in enumerate(pieces):
+        loads[k].wait()
+        start = (core ^ flip) * (depth // 2) + (lat ^ step) * share
+        place = pl.ds(aligned(start, share), share)
+        for which in range(5):
+            staged[k, which] = scale * to_f32(held[k, pl.ds(which * share, share), :])
+            copies.append(
+                pltpu.make_async_copy(
+                    staged.at[k, which], outs[which].at[place], sems.at[k, which]
+                )
+            )
+            copies[-1].start()
     for copy in copies:
         copy.wait()
 
 
-def unpack(flip, scale, shares, begun=()):
+def unpack(pieces, scale, shares, begun=()):
     depth = shares[0].shape[-1]
-    vmem, anywhere = pl.BlockSpec(memory_space=pltpu.VMEM), pl.BlockSpec(memory_space=pl.ANY)
+    rows = shares[0].shape[0]
+    anywhere = pl.BlockSpec(memory_space=pl.ANY)
     return pl.pallas_call(
-        functools.partial(unpack_kernel, flip, scale),
-        in_specs=[vmem] * len(shares) + [anywhere] * len(begun),
+        functools.partial(unpack_kernel, pieces, scale),
+        in_specs=[anywhere] * (len(shares) + len(begun)),
         out_specs=[anywhere] * 5,
         out_shape=[jax.ShapeDtypeStruct((depth, depth), jnp.float32)] * 5,
         scratch_shapes=[
-            pltpu.VMEM((5, depth // 2, depth), jnp.float32),
-            pltpu.SemaphoreType.DMA((5,)),
+            pltpu.VMEM((len(shares), rows, depth), jnp.bfloat16),
+            pltpu.VMEM((len(shares), 5, rows // 5, depth), jnp.float32),
+            pltpu.SemaphoreType.DMA((len(shares),)),
+            pltpu.SemaphoreType.DMA((len(shares), 5)),
         ],
         input_output_aliases={len(shares) + k: k for k in range(len(begun))},
-        compiler_params=pltpu.CompilerParams(vmem_limit_bytes=VMEM_BYTES),
+        compiler_params=pltpu.CompilerParams(vmem_limit_bytes=10 * MIB),
         cost_estimate=pl.CostEstimate(flops=0, bytes_accessed=8_000_000, transcendentals=0),
-        name=f"unpack_{flip}",
+        name=f"unpack_{len(pieces)}",
     )(*shares, *begun)
 
 
@@ -706,7 +712,7 @@
     new_nodes, d_pre_b, d_recv_b, d_send, d_up, d_down, d_gathered, d_crossed = outs[:8]
     mine, other = outs[8 : 8 + lat_count], outs[8 + lat_count :]
 
-    def returning():
+    def returning(d_crossed):
         chips = to_bf16(to_f32(d_gathered) + to_f32(swapped(d_crossed, "lon", 1)))
         parts = chips.reshape(chip_count, -1, depth)
         received = [swapped(parts[step], "lon", 2 * step) for step in range(1, chip_count)]
@@ -718,9 +724,10 @@
         downs = jnp.concatenate([d_down[:-1], to_bf16(to_f32(d_down[-1:]) + to_f32(corners[-1:]))])
         return lax.ppermute(ups, "lat", up), lax.ppermute(downs, "lat", down)
 
-    total, back, bordered = summed_part(mine, other, returning, borders)
-    grad_nodes = finish(
+    total, back, bordered = summed_part(mine, other, d_crossed, returning, borders)
+    grad_nodes, *vectors = finish(
         dims,
+        scale,
         slots,
         (
             cot,
@@ -732,23 +739,29 @@
             w_self,
             w_recv,
             w_send,
+            total,
         ),
     )
-    shares, crossed_shares, grad_nodes = gathered_shares(total, lat_count, grad_nodes)
-    outs = unpack(0, scale, shares)
-    outs = unpack(1, scale, crossed_shares, outs)
-    vectors = scale * total[-16:]
+
+    ready = gathered_share(total, lat_count)
+    shares = [swapped(ready, "lat", step) for step in range(1, lat_count)]
+    outs = unpack([(0, 0)], scale, [ready])
+    shares, grad_nodes, outs = lax.optimization_barrier((shares, grad_nodes, outs))
+    crossed = [swapped(part, "lon", 1) for part in (ready, *shares)]
+    pieces = [(1, 0)] + [(flip, step) for step in range(1, lat_count) for flip in range(2)]
+    parts = [crossed[step] if flip else shares[step - 1] for flip, step in pieces]
+    outs = unpack(pieces, scale, parts, outs)
     return (
         new_nodes.reshape(patch_rows, cols, depth),
         grad_nodes.reshape(patch_rows, cols, depth),
         outs[0],
         outs[1],
-        vectors[0],
+        vectors[0][0],
         outs[2],
         outs[3],
-        vectors[1],
+        vectors[1][0],
         outs[4],
-        vectors[2],
+        vectors[2][0],
     )
 
 

time: 124 us -> 118 us (0.952)
  waiting for transfers between devices: 34.2 us -> 31.1 us
  Pallas kernels: 39.5 us -> 36.8 us
  local copies, waits for them, and re-layouts: 5.45 us -> 3.36 us
  starting transfers between devices: 40.2 us -> 42.1 us
    ppermute x28, waiting for transfers between devices: 32.3 us -> 30.1 us  [swapped(): return lax.ppermute(values, axis, [(i, i ^ bit) for i in range(count)])]
    ppermute x28, starting transfers between devices: 27.6 us -> 29.5 us  [swapped(): return lax.ppermute(values, axis, [(i, i ^ bit) for i in range(count)])]
    unnamed x44 -> x34, local copies, waits for them, and re-layouts: 3.09 us -> 1.59 us
    pallas_call x1, Pallas kernels: 26.1 us -> 24.6 us  [update(): pl.pallas_call(functools.partial(update_kernel, dims), in_specs=[smem] *...]
    pallas_call x3, Pallas kernels: 11.3 us -> 9.99 us  [the longest x1 5.63 us: finish(): pl.pallas_call(functools.partial(finish_kernel, dims, scale), in_specs=[s...]
  transfers between devices with their start and end apart: 32 -> 32, of which waited for: 16 -> 17; matrix products, arithmetic and copies ran while one was open for 2% -> 1% of each run, Pallas kernels for 9% -> 7%
where the time goes in v5:
time: 118 us; the launch traced here: 117 us
  starting transfers between devices  42.1 us (36%)
  Pallas kernels  36.8 us (31%)
  waiting for transfers between devices  31.1 us (26%)
  local copies, waits for them, and re-layouts  3.36 us (3%)
  other arithmetic  2.71 us (2%)
  between operations  1.2 us (1%)
    ppermute x28, waiting for transfers between devices, swapped(): return lax.ppermute(values, axis, [(i, i ^ bit) for i in range(count)])  30.1 us
    ppermute x28, starting transfers between devices, swapped(): return lax.ppermute(values, axis, [(i, i ^ bit) for i in range(count)])  29.5 us
    pallas_call x1, Pallas kernels, update(): pl.pallas_call(functools.partial(update_kernel, dims), in_specs=[smem] *...  24.6 us
    ppermute x2, starting transfers between devices, borders(): return (lax.ppermute(ups, 'lat', up), lax.ppermute(downs, 'lat', down))  5.84 us
    pallas_call x1, Pallas kernels, finish(): pl.pallas_call(functools.partial(finish_kernel, dims, scale), in_specs=[s...  5.63 us
    ppermute x1, starting transfers between devices, on_device(): above = lax.ppermute(flat[-cols:], 'lat', down)  5.47 us
    pallas_call x2, Pallas kernels, unpack(): pl.pallas_call(functools.partial(unpack_kernel, pieces, scale), in_specs=...  4.36 us
  transfers between devices with their start and end apart: 32, of which 17 were waited for; matrix products, arithmetic and copies ran while one was open for 1% of the time, Pallas kernels for 7%

profile of v5, /device:TPU:0, one launch (start us, length us, event | category | flops | bytes accessed | tf_op | source)
XLA Modules:
  0.0 117.3 jit_solution(3028117724584158513)
XLA Ops:
  0.6 0.9 slice_bitcast_fusion
  1.5 1.3 %collective-permute-start.1 = (bf16[64,512]{1,0:T(8,128)(2,1)S(1)}, bf16[64,512]{1,0:T(8,128)(2,1)S(1)}, u32[]{:S(2)}, u32[]{:S(2)}) collective-permute-start(bf16[64,512]{1,0:T(8,128)(2,1)S(1)} %get-tuple-element.114), channel_id=1, source_target_pairs={{8,0},{16,8},{24,16},{9,1},{17,9},{25,17},{10,2},{18,10},{26,18},{... | collective-permute-start | bytes 196616 | tf_op jit(solution)/shard_map/ppermute | solution.py:687
  2.8 5.5 %collective-permute-start = (bf16[64,512]{1,0:T(8,128)(2,1)S(1)}, bf16[64,512]{1,0:T(8,128)(2,1)S(1)}, u32[]{:S(2)}, u32[]{:S(2)}) collective-permute-start(bf16[64,512]{1,0:T(8,128)(2,1)S(1)} %get-tuple-element.115), channel_id=1, source_target_pairs={{0,8},{8,16},{16,24},{1,9},{9,17},{17,25},{2,10},{10,18},{18,26},{... | collective-permute-start | bytes 196616 | tf_op jit(solution)/shard_map/ppermute | solution.py:686
  8.3 2.1 %pack_nodes.1 = bf16[48,512]{1,0:T(8,128)(2,1)} custom-call(s32[16]{0:T(128)} %bitcast.53, bf16[1024,512]{1,0:T(8,128)(2,1)} %bitcast.39), custom_call_target="tpu_custom_call" | custom-call | tf_op jit(solution)/shard_map/pack_nodes/pallas_call | solution.py:80
  10.5 0.9 pad_maximum_fusion.5
  11.4 4.2 %collective-permute-start.4 = (bf16[64,512]{1,0:T(8,128)(2,1)S(1)}, bf16[64,512]{1,0:T(8,128)(2,1)S(1)}, u32[]{:S(2)}, u32[]{:S(2)}) collective-permute-start(bf16[64,512]{1,0:T(8,128)(2,1)S(1)} %pad_maximum_fusion.5), channel_id=1, source_target_pairs={{0,6},{1,7},{2,4},{3,5},{4,2},{5,3},{6,0},{7,1},{8,14},{9,15},{10,... | collective-permute-start | bytes 196616 | tf_op jit(solution)/shard_map/ppermute | solution.py:560
  15.6 0.6 collective-permute-start.2
  16.3 2.4 %collective-permute-done.4 = bf16[64,512]{1,0:T(8,128)(2,1)S(1)} collective-permute-done((bf16[64,512]{1,0:T(8,128)(2,1)S(1)}, bf16[64,512]{1,0:T(8,128)(2,1)S(1)}, u32[]{:S(2)}, u32[]{:S(2)}) %collective-permute-start.4) | collective-permute-done | bytes 65568 | tf_op jit(solution)/shard_map/ppermute | solution.py:560
  18.6 2.3 %collective-permute-done.3 = bf16[64,512]{1,0:T(8,128)(2,1)S(1)} collective-permute-done((bf16[64,512]{1,0:T(8,128)(2,1)S(1)}, bf16[64,512]{1,0:T(8,128)(2,1)S(1)}, u32[]{:S(2)}, u32[]{:S(2)}) %collective-permute-start.3) | collective-permute-done | bytes 65568 | tf_op jit(solution)/shard_map/ppermute | solution.py:560
  20.9 0.2 concatenate.26.refs_2_
  21.0 0.1 collective-permute-start.5
  21.1 1.5 %collective-permute-done.5.refs_3_ = bf16[256,512]{1,0:T(8,128)(2,1)S(1)} collective-permute-done((bf16[256,512]{1,0:T(8,128)(2,1)S(1)}, bf16[256,512]{1,0:T(8,128)(2,1)S(1)}, u32[]{:S(2)}, u32[]{:S(2)}) %collective-permute-start.5) | collective-permute-done | bytes 262176 | tf_op jit(solution)/shard_map/ppermute | solution.py:560
  22.7 0.7 copy-done.16
  23.4 24.6 %update.1 = (bf16[1024,512]{1,0:T(8,128)(2,1)}, bf16[1024,512]{1,0:T(8,128)(2,1)}, bf16[1024,512]{1,0:T(8,128)(2,1)}, bf16[1024,512]{1,0:T(8,128)(2,1)}, bf16[64...) custom-call(s32[16]{0:T(128)} %bitcast.54, ...), custom_call_target="tpu_custom_call" | custom-call | flops 6979321856 | bytes 20000000 | tf_op jit(solution)/shard_map/update/pallas_call | solution.py:454
  48.0 0.2 collective-permute-start.7
  48.2 0.4 collective-permute-start.9
  48.6 1.4 %collective-permute-done.7 = bf16[336,512]{1,0:T(8,128)(2,1)S(1)} collective-permute-done((bf16[336,512]{1,0:T(8,128)(2,1)}, bf16[336,512]{1,0:T(8,128)(2,1)S(1)}, u32[]{:S(2)}, u32[]{:S(2)}) %collective-permute-start.7) | collective-permute-done | bytes 344096 | tf_op jit(solution)/shard_map/ppermute | solution.py:560
  49.9 1.1 add_convert_fusion.3
  51.1 0.2 collective-permute-start.13
  51.3 0.4 collective-permute-start.11
  51.7 2.9 %collective-permute-start.8 = (bf16[336,512]{1,0:T(8,128)(2,1)S(1)}, bf16[336,512]{1,0:T(8,128)(2,1)S(1)}, u32[]{:S(2)}, u32[]{:S(2)}) collective-permute-start(bf16[336,512]{1,0:T(8,128)(2,1)S(1)} %add_convert_fusion.3), channel_id=1, source_target_pairs={{0,24},{8,16},{16,8},{24,0},{1,25},{9,17},{17,9},{25,1},{2,26},{10... | collective-permute-start | bytes 1032200 | tf_op jit(solution)/shard_map/ppermute | solution.py:560
  54.6 0.1 add_convert_fusion.2
  54.7 1.0 collective-permute-start.10
  55.7 0.1 add_convert_fusion.4
  55.8 0.0 copy-start.3
  55.8 0.9 collective-permute-start.14
  56.7 2.6 %collective-permute-start.16 = (bf16[64,512]{1,0:T(8,128)(2,1)S(1)}, bf16[64,512]{1,0:T(8,128)(2,1)S(1)}, u32[]{:S(2)}, u32[]{:S(2)}) collective-permute-start(bf16[64,512]{1,0:T(8,128)(2,1)S(1)} %get-tuple-element.121), channel_id=1, source_target_pairs={{0,6},{1,7},{2,4},{3,5},{4,2},{5,3},{6,0},{7,1},{8,14},{9,15},{10,... | collective-permute-start | bytes 196616 | tf_op jit(solution)/shard_map/ppermute | solution.py:560
  59.3 0.1 add_convert_fusion.1
  59.4 2.3 %collective-permute-start.12 = (bf16[336,512]{1,0:T(8,128)(2,1)S(1)}, bf16[336,512]{1,0:T(8,128)(2,1)S(1)}, u32[]{:S(2)}, u32[]{:S(2)}) collective-permute-start(bf16[336,512]{1,0:T(8,128)(2,1)S(1)} %add_convert_fusion.1), channel_id=1, source_target_pairs={{0,8},{8,0},{16,24},{24,16},{1,9},{9,1},{17,25},{25,17},{2,10},{10... | collective-permute-start | bytes 1032200 | tf_op jit(solution)/shard_map/ppermute | solution.py:560
  61.7 1.1 collective-permute-done.16
  62.8 1.0 collective-permute-start.15
  63.8 4.5 %collective-permute-done.15 = bf16[64,512]{1,0:T(8,128)(2,1)S(1)} collective-permute-done((bf16[64,512]{1,0:T(8,128)(2,1)S(1)}, bf16[64,512]{1,0:T(8,128)(2,1)S(1)}, u32[]{:S(2)}, u32[]{:S(2)}) %collective-permute-start.15) | collective-permute-done | bytes 65568 | tf_op jit(solution)/shard_map/ppermute | solution.py:560
  68.4 2.3 %collective-permute-done.10 = bf16[336,512]{1,0:T(8,128)(2,1)S(1)} collective-permute-done((bf16[336,512]{1,0:T(8,128)(2,1)S(1)}, bf16[336,512]{1,0:T(8,128)(2,1)S(1)}, u32[]{:S(2)}, u32[]{:S(2)}) %collective-permute-start.10) | collective-permute-done | bytes 344096 | tf_op jit(solution)/shard_map/ppermute | solution.py:560
  70.7 1.8 %collective-permute-done.12 = bf16[336,512]{1,0:T(8,128)(2,1)S(1)} collective-permute-done((bf16[336,512]{1,0:T(8,128)(2,1)S(1)}, bf16[336,512]{1,0:T(8,128)(2,1)S(1)}, u32[]{:S(2)}, u32[]{:S(2)}) %collective-permute-start.12) | collective-permute-done | bytes 344096 | tf_op jit(solution)/shard_map/ppermute | solution.py:560
  72.4 0.2 add_convert_fusion
  72.8 0.6 collective-permute-start.17
  73.4 0.2 copy-done.9
  73.6 2.8 %collective-permute-start.19 = (bf16[88,512]{1,0:T(8,128)(2,1)S(1)}, bf16[88,512]{1,0:T(8,128)(2,1)S(1)}, u32[]{:S(2)}, u32[]{:S(2)}) collective-permute-start(bf16[88,512]{1,0:T(8,128)(2,1)S(1)} %get-tuple-element.125), channel_id=1, source_target_pairs={{0,6},{1,7},{2,4},{3,5},{4,2},{5,3},{6,0},{7,1},{8,14},{9,15},{10,... | collective-permute-start | bytes 270344 | tf_op jit(solution)/shard_map/ppermute | solution.py:560
  76.4 0.0 collective-permute-start.18
  76.5 0.9 collective-permute-done.17
  77.5 1.3 %collective-permute-start.20 = (bf16[64,512]{1,0:T(8,128)(2,1)S(1)}, bf16[64,512]{1,0:T(8,128)(2,1)S(1)}, u32[]{:S(2)}, u32[]{:S(2)}) collective-permute-start(bf16[64,512]{1,0:T(8,128)(2,1)S(1)} %pad_maximum_fusion.6), channel_id=1, source_target_pairs={{8,0},{16,8},{24,16},{9,1},{17,9},{25,17},{10,2},{18,10},{26,18},{... | collective-permute-start | bytes 196616 | tf_op jit(solution)/shard_map/ppermute | solution.py:725
  78.8 4.5 %collective-permute-start.21 = (bf16[64,512]{1,0:T(8,128)(2,1)S(1)}, bf16[64,512]{1,0:T(8,128)(2,1)S(1)}, u32[]{:S(2)}, u32[]{:S(2)}) collective-permute-start(bf16[64,512]{1,0:T(8,128)(2,1)S(1)} %pad_maximum_fusion.7), channel_id=1, source_target_pairs={{0,8},{8,16},{16,24},{1,9},{9,17},{17,25},{2,10},{10,18},{18,26},{... | collective-permute-start | bytes 196616 | tf_op jit(solution)/shard_map/ppermute | solution.py:725
  83.4 0.9 collective-permute-done.18
  84.3 1.0 collective-permute-done.21.refs_5_
  85.2 0.6 copy-done.11
  85.8 0.1 convert_add_fusion.refs_10_
  85.9 0.8 collective-permute-start.22
  86.7 2.3 %collective-permute-start.23 = (bf16[80,512]{1,0:T(8,128)(2,1)S(1)}, bf16[80,512]{1,0:T(8,128)(2,1)S(1)}, u32[]{:S(2)}, u32[]{:S(2)}) collective-permute-start(bf16[80,512]{1,0:T(8,128)(2,1)S(1)} %slice.114), channel_id=1, source_target_pairs={{0,4},{1,5},{2,6},{3,7},{4,0},{5,1},{6,2},{7,3},{8,12},{9,13},{10,... | collective-permute-start | bytes 245768 | tf_op jit(solution)/shard_map/ppermute | solution.py:560
  89.0 1.4 %collective-permute-start.24 = (bf16[80,512]{1,0:T(8,128)(2,1)S(1)}, bf16[80,512]{1,0:T(8,128)(2,1)S(1)}, u32[]{:S(2)}, u32[]{:S(2)}) collective-permute-start(bf16[80,512]{1,0:T(8,128)(2,1)S(1)} %slice.114), channel_id=1, source_target_pairs={{0,6},{1,7},{2,4},{3,5},{4,2},{5,3},{6,0},{7,1},{8,14},{9,15},{10,... | collective-permute-start | bytes 245768 | tf_op jit(solution)/shard_map/ppermute | solution.py:560
  90.4 0.0 collective-permute-done.22
  90.5 2.1 %collective-permute-done.23 = bf16[80,512]{1,0:T(8,128)(2,1)S(1)} collective-permute-done((bf16[80,512]{1,0:T(8,128)(2,1)S(1)}, bf16[80,512]{1,0:T(8,128)(2,1)S(1)}, u32[]{:S(2)}, u32[]{:S(2)}) %collective-permute-start.23) | collective-permute-done | bytes 81952 | tf_op jit(solution)/shard_map/ppermute | solution.py:560
  92.5 2.8 %collective-permute-done.24 = bf16[80,512]{1,0:T(8,128)(2,1)S(1)} collective-permute-done((bf16[80,512]{1,0:T(8,128)(2,1)S(1)}, bf16[80,512]{1,0:T(8,128)(2,1)S(1)}, u32[]{:S(2)}, u32[]{:S(2)}) %collective-permute-start.24) | collective-permute-done | bytes 81952 | tf_op jit(solution)/shard_map/ppermute | solution.py:560
  95.4 0.6 gather_fusion
  96.0 2.6 %collective-permute-start.27 = (bf16[320,512]{1,0:T(8,128)(2,1)S(1)}, bf16[320,512]{1,0:T(8,128)(2,1)S(1)}, u32[]{:S(2)}, u32[]{:S(2)}) collective-permute-start(bf16[320,512]{1,0:T(8,128)(2,1)S(1)} %bitcast.34), channel_id=1, source_target_pairs={{0,24},{8,16},{16,8},{24,0},{1,25},{9,17},{17,9},{25,1},{2,26},{10... | collective-permute-start | bytes 983048 | tf_op jit(solution)/shard_map/ppermute | solution.py:560
  98.6 1.3 %collective-permute-start.26 = (bf16[320,512]{1,0:T(8,128)(2,1)S(1)}, bf16[320,512]{1,0:T(8,128)(2,1)S(1)}, u32[]{:S(2)}, u32[]{:S(2)}) collective-permute-start(bf16[320,512]{1,0:T(8,128)(2,1)S(1)} %bitcast.35), channel_id=1, source_target_pairs={{0,16},{8,24},{16,0},{24,8},{1,17},{9,25},{17,1},{25,9},{2,18},{10... | collective-permute-start | bytes 983048 | tf_op jit(solution)/shard_map/ppermute | solution.py:560
  99.9 0.5 collective-permute-start.25
  100.4 5.6 %finish.1 = (bf16[1024,512]{1,0:T(8,128)(2,1)}, f32[1,512]{1,0:T(1,128)}, f32[1,512]{1,0:T(1,128)}, f32[1,512]{1,0:T(1,128)}) custom-call(s32[16]{0:T(128)} %bitcast.55, bf16[1024,512]{1,0:T(8,128)(2,1)} %bitcast.44, bf16[1024,512]{1,0:T(8,128)(2,1)} %get-tuple-element.86.refs_1_, bf16[1024,512]{1,0:T(8,128)(2,1)} %get-tuple-element.87.refs_2_, ...), custom_call_target="tpu_custom_call" | custom-call | flops 1610612736 | bytes 8000000 | tf_op jit(solution)/shard_map/finish/pallas_call | solution.py:543
  106.0 1.0 unpack_1.1
  107.0 2.7 %collective-permute-done.26.refs_3_ = bf16[320,512]{1,0:T(8,128)(2,1)S(1)} collective-permute-done((bf16[320,512]{1,0:T(8,128)(2,1)S(1)}, bf16[320,512]{1,0:T(8,128)(2,1)S(1)}, u32[]{:S(2)}, u32[]{:S(2)}) %collective-permute-start.26) | collective-permute-done | bytes 327712 | tf_op jit(solution)/shard_map/ppermute | solution.py:560
  109.7 1.5 %collective-permute-done.25.refs_1_ = bf16[320,512]{1,0:T(8,128)(2,1)} collective-permute-done((bf16[320,512]{1,0:T(8,128)(2,1)S(1)}, bf16[320,512]{1,0:T(8,128)(2,1)}, u32[]{:S(2)}, u32[]{:S(2)}) %collective-permute-start.25) | collective-permute-done | bytes 327712 | tf_op jit(solution)/shard_map/ppermute | solution.py:560
  111.2 0.5 collective-permute-start.30
  111.7 1.8 %collective-permute-done.29.refs_2_ = bf16[320,512]{1,0:T(8,128)(2,1)S(1)} collective-permute-done((bf16[320,512]{1,0:T(8,128)(2,1)}, bf16[320,512]{1,0:T(8,128)(2,1)S(1)}, u32[]{:S(2)}, u32[]{:S(2)}) %collective-permute-start.29) | collective-permute-done | bytes 327712 | tf_op jit(solution)/shard_map/ppermute | solution.py:560
  113.5 0.3 collective-permute-done.31.refs_6_
  113.8 3.4 %unpack_7.1 = (f32[512,512]{1,0:T(8,128)}, f32[512,512]{1,0:T(8,128)}, f32[512,512]{1,0:T(8,128)}, f32[512,512]{1,0:T(8,128)}, f32[512,512]{1,0:T(8,128)}) custom-call(bf16[320,512]{1,0:T(8,128)(2,1)S(1)} %collective-permute-done.28.refs_0_, ...), custom_call_target="tpu_custom_call", output_to_operand_aliasing={{0}: (7, {}), {1}: (8, {}), {2}: (9, {}), {3}: (10, {}), {4... | custom-call | bytes 8000000 | tf_op jit(solution)/shard_map/unpack_7/pallas_call | solution.py:638
  (69 shorter events, 0.4 us)
Async XLA Ops:
  1.5 8.9 %collective-permute-start.1 = (bf16[64,512]{1,0:T(8,128)(2,1)S(1)}, bf16[64,512]{1,0:T(8,128)(2,1)S(1)}, u32[]{:S(2)}, u32[]{:S(2)}) collective-permute-start(bf16[64,512]{1,0:T(8,128)(2,1)S(1)} %get-tuple-element.114), channel_id=1, source_target_pairs={{8,0},{16,8},{24,16},{9,1},{17,9},{25,17},{10,2},{18,10},{26,18},{... | collective-permute-start | bytes 196616 | tf_op jit(solution)/shard_map/ppermute | solution.py:687
  2.8 7.6 %collective-permute-start = (bf16[64,512]{1,0:T(8,128)(2,1)S(1)}, bf16[64,512]{1,0:T(8,128)(2,1)S(1)}, u32[]{:S(2)}, u32[]{:S(2)}) collective-permute-start(bf16[64,512]{1,0:T(8,128)(2,1)S(1)} %get-tuple-element.115), channel_id=1, source_target_pairs={{0,8},{8,16},{16,24},{1,9},{9,17},{17,25},{2,10},{10,18},{18,26},{... | collective-permute-start | bytes 196616 | tf_op jit(solution)/shard_map/ppermute | solution.py:686
  10.5 0.9 copy-start.12
  10.5 0.9 copy-start.13
  10.5 10.4 %copy-start.2 = (bf16[48,512]{1,0:T(8,128)(2,1)S(1)}, bf16[48,512]{1,0:T(8,128)(2,1)}, u32[]{:S(2)}) copy-start(bf16[48,512]{1,0:T(8,128)(2,1)} %pack_nodes.1) | copy-start | bytes 147460
  11.4 7.2 %collective-permute-start.4 = (bf16[64,512]{1,0:T(8,128)(2,1)S(1)}, bf16[64,512]{1,0:T(8,128)(2,1)S(1)}, u32[]{:S(2)}, u32[]{:S(2)}) collective-permute-start(bf16[64,512]{1,0:T(8,128)(2,1)S(1)} %pad_maximum_fusion.5), channel_id=1, source_target_pairs={{0,6},{1,7},{2,4},{3,5},{4,2},{5,3},{6,0},{7,1},{8,14},{9,15},{10,... | collective-permute-start | bytes 196616 | tf_op jit(solution)/shard_map/ppermute | solution.py:560
  15.6 5.2 %collective-permute-start.3 = (bf16[64,512]{1,0:T(8,128)(2,1)S(1)}, bf16[64,512]{1,0:T(8,128)(2,1)S(1)}, u32[]{:S(2)}, u32[]{:S(2)}) collective-permute-start(bf16[64,512]{1,0:T(8,128)(2,1)S(1)} %pad_maximum_fusion.5), channel_id=1, source_target_pairs={{0,4},{1,5},{2,6},{3,7},{4,0},{5,1},{6,2},{7,3},{8,12},{9,13},{10,... | collective-permute-start | bytes 196616 | tf_op jit(solution)/shard_map/ppermute | solution.py:560
  15.6 5.2 %collective-permute-start.2 = (bf16[64,512]{1,0:T(8,128)(2,1)S(1)}, bf16[64,512]{1,0:T(8,128)(2,1)S(1)}, u32[]{:S(2)}, u32[]{:S(2)}) collective-permute-start(bf16[64,512]{1,0:T(8,128)(2,1)S(1)} %pad_maximum_fusion.5), channel_id=1, source_target_pairs={{0,2},{1,3},{2,0},{3,1},{4,6},{5,7},{6,4},{7,5},{8,10},{9,11},{10,... | collective-permute-start | bytes 196616 | tf_op jit(solution)/shard_map/ppermute | solution.py:560
  21.0 1.6 %copy-start.7 = (bf16[256,512]{1,0:T(8,128)(2,1)}, bf16[256,512]{1,0:T(8,128)(2,1)S(1)}, u32[]{:S(2)}) copy-start(bf16[256,512]{1,0:T(8,128)(2,1)S(1)} %concatenate.26.refs_2_) | copy-start | bytes 786436
  21.0 1.6 %collective-permute-start.5 = (bf16[256,512]{1,0:T(8,128)(2,1)S(1)}, bf16[256,512]{1,0:T(8,128)(2,1)S(1)}, u32[]{:S(2)}, u32[]{:S(2)}) collective-permute-start(bf16[256,512]{1,0:T(8,128)(2,1)S(1)} %concatenate.26.refs_2_), channel_id=1, source_target_pairs={{0,1},{1,0},{2,3},{3,2},{4,5},{5,4},{6,7},{7,6},{8,9},{9,8},{10,11... | collective-permute-start | bytes 786440 | tf_op jit(solution)/shard_map/ppermute | solution.py:560
  22.6 0.7 copy-start.16
  48.0 1.9 %collective-permute-start.7 = (bf16[336,512]{1,0:T(8,128)(2,1)}, bf16[336,512]{1,0:T(8,128)(2,1)S(1)}, u32[]{:S(2)}, u32[]{:S(2)}) collective-permute-start(bf16[336,512]{1,0:T(8,128)(2,1)} %get-tuple-element.66), channel_id=1, source_target_pairs={{0,1},{1,0},{2,3},{3,2},{4,5},{5,4},{6,7},{7,6},{8,9},{9,8},{10,11... | collective-permute-start | bytes 1032200 | tf_op jit(solution)/shard_map/ppermute | solution.py:560
  48.2 6.4 %collective-permute-start.9 = (bf16[336,512]{1,0:T(8,128)(2,1)}, bf16[336,512]{1,0:T(8,128)(2,1)S(1)}, u32[]{:S(2)}, u32[]{:S(2)}) collective-permute-start(bf16[336,512]{1,0:T(8,128)(2,1)} %get-tuple-element.70), channel_id=1, source_target_pairs={{0,1},{1,0},{2,3},{3,2},{4,5},{5,4},{6,7},{7,6},{8,9},{9,8},{10,11... | collective-permute-start | bytes 1032200 | tf_op jit(solution)/shard_map/ppermute | solution.py:560
  49.9 1.2 copy-start.15
  49.9 1.4 %copy-start.14 = (bf16[336,512]{1,0:T(8,128)(2,1)S(1)}, bf16[336,512]{1,0:T(8,128)(2,1)}, u32[]{:S(2)}) copy-start(bf16[336,512]{1,0:T(8,128)(2,1)} %get-tuple-element.72) | copy-start | bytes 1032196
  49.9 4.7 %copy-start.4 = (bf16[336,512]{1,0:T(8,128)(2,1)S(1)}, bf16[336,512]{1,0:T(8,128)(2,1)}, u32[]{:S(2)}) copy-start(bf16[336,512]{1,0:T(8,128)(2,1)} %get-tuple-element.69) | copy-start | bytes 1032196
  51.1 4.6 %collective-permute-start.13 = (bf16[256,512]{1,0:T(8,128)(2,1)S(1)}, bf16[256,512]{1,0:T(8,128)(2,1)S(1)}, u32[]{:S(2)}, u32[]{:S(2)}) collective-permute-start(bf16[256,512]{1,0:T(8,128)(2,1)S(1)} %copy-done.15), channel_id=1, source_target_pairs={{0,1},{1,0},{2,3},{3,2},{4,5},{5,4},{6,7},{7,6},{8,9},{9,8},{10,11... | collective-permute-start | bytes 786440 | tf_op jit(solution)/shard_map/ppermute | solution.py:560
  51.3 8.0 %collective-permute-start.11 = (bf16[336,512]{1,0:T(8,128)(2,1)S(1)}, bf16[336,512]{1,0:T(8,128)(2,1)S(1)}, u32[]{:S(2)}, u32[]{:S(2)}) collective-permute-start(bf16[336,512]{1,0:T(8,128)(2,1)S(1)} %copy-done.14), channel_id=1, source_target_pairs={{0,1},{1,0},{2,3},{3,2},{4,5},{5,4},{6,7},{7,6},{8,9},{9,8},{10,11... | collective-permute-start | bytes 1032200 | tf_op jit(solution)/shard_map/ppermute | solution.py:560
  51.7 16.7 %collective-permute-start.8 = (bf16[336,512]{1,0:T(8,128)(2,1)S(1)}, bf16[336,512]{1,0:T(8,128)(2,1)S(1)}, u32[]{:S(2)}, u32[]{:S(2)}) collective-permute-start(bf16[336,512]{1,0:T(8,128)(2,1)S(1)} %add_convert_fusion.3), channel_id=1, source_target_pairs={{0,24},{8,16},{16,8},{24,0},{1,25},{9,17},{17,9},{25,1},{2,26},{10... | collective-permute-start | bytes 1032200 | tf_op jit(solution)/shard_map/ppermute | solution.py:560
  54.6 1.1 copy-start.6
  54.7 15.9 %collective-permute-start.10 = (bf16[336,512]{1,0:T(8,128)(2,1)S(1)}, bf16[336,512]{1,0:T(8,128)(2,1)S(1)}, u32[]{:S(2)}, u32[]{:S(2)}) collective-permute-start(bf16[336,512]{1,0:T(8,128)(2,1)S(1)} %add_convert_fusion.2), channel_id=1, source_target_pairs={{0,16},{8,24},{16,0},{24,8},{1,17},{9,25},{17,1},{25,9},{2,18},{10... | collective-permute-start | bytes 1032200 | tf_op jit(solution)/shard_map/ppermute | solution.py:560
  55.8 3.5 %copy-start.3 = (bf16[336,512]{1,0:T(8,128)(2,1)S(1)}, bf16[336,512]{1,0:T(8,128)(2,1)}, u32[]{:S(2)}) copy-start(bf16[336,512]{1,0:T(8,128)(2,1)} %get-tuple-element.71) | copy-start | bytes 1032196
  55.8 5.9 %collective-permute-start.14 = (bf16[64,512]{1,0:T(8,128)(2,1)S(1)}, bf16[64,512]{1,0:T(8,128)(2,1)S(1)}, u32[]{:S(2)}, u32[]{:S(2)}) collective-permute-start(bf16[64,512]{1,0:T(8,128)(2,1)S(1)} %get-tuple-element.120), channel_id=1, source_target_pairs={{0,2},{1,3},{2,0},{3,1},{4,6},{5,7},{6,4},{7,5},{8,10},{9,11},{10,... | collective-permute-start | bytes 196616 | tf_op jit(solution)/shard_map/ppermute | solution.py:560
  56.7 6.1 %collective-permute-start.16 = (bf16[64,512]{1,0:T(8,128)(2,1)S(1)}, bf16[64,512]{1,0:T(8,128)(2,1)S(1)}, u32[]{:S(2)}, u32[]{:S(2)}) collective-permute-start(bf16[64,512]{1,0:T(8,128)(2,1)S(1)} %get-tuple-element.121), channel_id=1, source_target_pairs={{0,6},{1,7},{2,4},{3,5},{4,2},{5,3},{6,0},{7,1},{8,14},{9,15},{10,... | collective-permute-start | bytes 196616 | tf_op jit(solution)/shard_map/ppermute | solution.py:560
  59.4 13.0 %copy-start.5 = (bf16[336,512]{1,0:T(8,128)(2,1)S(1)}, bf16[336,512]{1,0:T(8,128)(2,1)}, u32[]{:S(2)}) copy-start(bf16[336,512]{1,0:T(8,128)(2,1)} %get-tuple-element.63) | copy-start | bytes 1032196
  59.4 13.0 %collective-permute-start.12 = (bf16[336,512]{1,0:T(8,128)(2,1)S(1)}, bf16[336,512]{1,0:T(8,128)(2,1)S(1)}, u32[]{:S(2)}, u32[]{:S(2)}) collective-permute-start(bf16[336,512]{1,0:T(8,128)(2,1)S(1)} %add_convert_fusion.1), channel_id=1, source_target_pairs={{0,8},{8,0},{16,24},{24,16},{1,9},{9,1},{17,25},{25,17},{2,10},{10... | collective-permute-start | bytes 1032200 | tf_op jit(solution)/shard_map/ppermute | solution.py:560
  61.7 10.7 %collective-permute-start.6 = (bf16[336,512]{1,0:T(8,128)(2,1)}, bf16[336,512]{1,0:T(8,128)(2,1)S(1)}, u32[]{:S(2)}, u32[]{:S(2)}) collective-permute-start(bf16[336,512]{1,0:T(8,128)(2,1)} %get-tuple-element.64), channel_id=1, source_target_pairs={{0,1},{1,0},{2,3},{3,2},{4,5},{5,4},{6,7},{7,6},{8,9},{9,8},{10,11... | collective-permute-start | bytes 1032200 | tf_op jit(solution)/shard_map/ppermute | solution.py:560
  62.8 5.5 %collective-permute-start.15 = (bf16[64,512]{1,0:T(8,128)(2,1)S(1)}, bf16[64,512]{1,0:T(8,128)(2,1)S(1)}, u32[]{:S(2)}, u32[]{:S(2)}) collective-permute-start(bf16[64,512]{1,0:T(8,128)(2,1)S(1)} %get-tuple-element.122), channel_id=1, source_target_pairs={{0,4},{1,5},{2,6},{3,7},{4,0},{5,1},{6,2},{7,3},{8,12},{9,13},{10,... | collective-permute-start | bytes 196616 | tf_op jit(solution)/shard_map/ppermute | solution.py:560
  68.4 9.0 %copy-start.1 = (f32[64,512]{1,0:T(8,128)}, f32[64,512]{1,0:T(8,128)S(1)}, u32[]{:S(2)}) copy-start(f32[64,512]{1,0:T(8,128)S(1)} %convert_add_fusion.1.refs_6_) | copy-start | bytes 393220
  72.8 0.8 copy-start.9
  72.8 4.6 %collective-permute-start.17 = (bf16[88,512]{1,0:T(8,128)(2,1)S(1)}, bf16[88,512]{1,0:T(8,128)(2,1)S(1)}, u32[]{:S(2)}, u32[]{:S(2)}) collective-permute-start(bf16[88,512]{1,0:T(8,128)(2,1)S(1)} %get-tuple-element.126), channel_id=1, source_target_pairs={{0,2},{1,3},{2,0},{3,1},{4,6},{5,7},{6,4},{7,5},{8,10},{9,11},{10,... | collective-permute-start | bytes 270344 | tf_op jit(solution)/shard_map/ppermute | solution.py:560
  73.6 9.7 %collective-permute-start.19 = (bf16[88,512]{1,0:T(8,128)(2,1)S(1)}, bf16[88,512]{1,0:T(8,128)(2,1)S(1)}, u32[]{:S(2)}, u32[]{:S(2)}) collective-permute-start(bf16[88,512]{1,0:T(8,128)(2,1)S(1)} %get-tuple-element.125), channel_id=1, source_target_pairs={{0,6},{1,7},{2,4},{3,5},{4,2},{5,3},{6,0},{7,1},{8,14},{9,15},{10,... | collective-permute-start | bytes 270344 | tf_op jit(solution)/shard_map/ppermute | solution.py:560
  76.4 1.0 copy-start.8
  76.4 7.8 %collective-permute-start.18 = (bf16[88,512]{1,0:T(8,128)(2,1)S(1)}, bf16[88,512]{1,0:T(8,128)(2,1)S(1)}, u32[]{:S(2)}, u32[]{:S(2)}) collective-permute-start(bf16[88,512]{1,0:T(8,128)(2,1)S(1)} %get-tuple-element.127), channel_id=1, source_target_pairs={{0,4},{1,5},{2,6},{3,7},{4,0},{5,1},{6,2},{7,3},{8,12},{9,13},{10,... | collective-permute-start | bytes 270344 | tf_op jit(solution)/shard_map/ppermute | solution.py:560
  77.5 6.8 %collective-permute-start.20 = (bf16[64,512]{1,0:T(8,128)(2,1)S(1)}, bf16[64,512]{1,0:T(8,128)(2,1)S(1)}, u32[]{:S(2)}, u32[]{:S(2)}) collective-permute-start(bf16[64,512]{1,0:T(8,128)(2,1)S(1)} %pad_maximum_fusion.6), channel_id=1, source_target_pairs={{8,0},{16,8},{24,16},{9,1},{17,9},{25,17},{10,2},{18,10},{26,18},{... | collective-permute-start | bytes 196616 | tf_op jit(solution)/shard_map/ppermute | solution.py:725
  78.8 6.4 %collective-permute-start.21 = (bf16[64,512]{1,0:T(8,128)(2,1)S(1)}, bf16[64,512]{1,0:T(8,128)(2,1)S(1)}, u32[]{:S(2)}, u32[]{:S(2)}) collective-permute-start(bf16[64,512]{1,0:T(8,128)(2,1)S(1)} %pad_maximum_fusion.7), channel_id=1, source_target_pairs={{0,8},{8,16},{16,24},{1,9},{9,17},{17,25},{2,10},{10,18},{18,26},{... | collective-permute-start | bytes 196616 | tf_op jit(solution)/shard_map/ppermute | solution.py:725
  84.3 1.7 %copy-start.10 = (bf16[64,512]{1,0:T(8,128)(2,1)}, bf16[64,512]{1,0:T(8,128)(2,1)S(1)}, u32[]{:S(2)}) copy-start(bf16[64,512]{1,0:T(8,128)(2,1)S(1)} %collective-permute-done.20.refs_4_) | copy-start | bytes 196612
  85.2 0.6 copy-start.11
  85.9 4.5 %copy-start = (f32[88,512]{1,0:T(8,128)}, f32[88,512]{1,0:T(8,128)S(1)}, u32[]{:S(2)}) copy-start(f32[88,512]{1,0:T(8,128)S(1)} %convert_add_fusion.refs_10_) | copy-start | bytes 540676
  85.9 4.5 %collective-permute-start.22 = (bf16[80,512]{1,0:T(8,128)(2,1)S(1)}, bf16[80,512]{1,0:T(8,128)(2,1)S(1)}, u32[]{:S(2)}, u32[]{:S(2)}) collective-permute-start(bf16[80,512]{1,0:T(8,128)(2,1)S(1)} %slice.114), channel_id=1, source_target_pairs={{0,2},{1,3},{2,0},{3,1},{4,6},{5,7},{6,4},{7,5},{8,10},{9,11},{10,... | collective-permute-start | bytes 245768 | tf_op jit(solution)/shard_map/ppermute | solution.py:560
  86.7 5.8 %collective-permute-start.23 = (bf16[80,512]{1,0:T(8,128)(2,1)S(1)}, bf16[80,512]{1,0:T(8,128)(2,1)S(1)}, u32[]{:S(2)}, u32[]{:S(2)}) collective-permute-start(bf16[80,512]{1,0:T(8,128)(2,1)S(1)} %slice.114), channel_id=1, source_target_pairs={{0,4},{1,5},{2,6},{3,7},{4,0},{5,1},{6,2},{7,3},{8,12},{9,13},{10,... | collective-permute-start | bytes 245768 | tf_op jit(solution)/shard_map/ppermute | solution.py:560
  89.0 6.3 %collective-permute-start.24 = (bf16[80,512]{1,0:T(8,128)(2,1)S(1)}, bf16[80,512]{1,0:T(8,128)(2,1)S(1)}, u32[]{:S(2)}, u32[]{:S(2)}) collective-permute-start(bf16[80,512]{1,0:T(8,128)(2,1)S(1)} %slice.114), channel_id=1, source_target_pairs={{0,6},{1,7},{2,4},{3,5},{4,2},{5,3},{6,0},{7,1},{8,14},{9,15},{10,... | collective-permute-start | bytes 245768 | tf_op jit(solution)/shard_map/ppermute | solution.py:560
  96.0 11.0 %collective-permute-start.27 = (bf16[320,512]{1,0:T(8,128)(2,1)S(1)}, bf16[320,512]{1,0:T(8,128)(2,1)S(1)}, u32[]{:S(2)}, u32[]{:S(2)}) collective-permute-start(bf16[320,512]{1,0:T(8,128)(2,1)S(1)} %bitcast.34), channel_id=1, source_target_pairs={{0,24},{8,16},{16,8},{24,0},{1,25},{9,17},{17,9},{25,1},{2,26},{10... | collective-permute-start | bytes 983048 | tf_op jit(solution)/shard_map/ppermute | solution.py:560
  98.6 11.2 %collective-permute-start.26 = (bf16[320,512]{1,0:T(8,128)(2,1)S(1)}, bf16[320,512]{1,0:T(8,128)(2,1)S(1)}, u32[]{:S(2)}, u32[]{:S(2)}) collective-permute-start(bf16[320,512]{1,0:T(8,128)(2,1)S(1)} %bitcast.35), channel_id=1, source_target_pairs={{0,16},{8,24},{16,0},{24,8},{1,17},{9,25},{17,1},{25,9},{2,18},{10... | collective-permute-start | bytes 983048 | tf_op jit(solution)/shard_map/ppermute | solution.py:560
  99.9 11.3 %collective-permute-start.25 = (bf16[320,512]{1,0:T(8,128)(2,1)S(1)}, bf16[320,512]{1,0:T(8,128)(2,1)}, u32[]{:S(2)}, u32[]{:S(2)}) collective-permute-start(bf16[320,512]{1,0:T(8,128)(2,1)S(1)} %bitcast.36), channel_id=1, source_target_pairs={{0,8},{8,0},{16,24},{24,16},{1,9},{9,1},{17,25},{25,17},{2,10},{10... | collective-permute-start | bytes 983048 | tf_op jit(solution)/shard_map/ppermute | solution.py:560
  106.0 5.8 %collective-permute-start.28 = (bf16[320,512]{1,0:T(8,128)(2,1)S(1)}, bf16[320,512]{1,0:T(8,128)(2,1)S(1)}, u32[]{:S(2)}, u32[]{:S(2)}) collective-permute-start(bf16[320,512]{1,0:T(8,128)(2,1)S(1)} %bitcast.37), channel_id=1, source_target_pairs={{0,1},{1,0},{2,3},{3,2},{4,5},{5,4},{6,7},{7,6},{8,9},{9,8},{10,11... | collective-permute-start | bytes 983048 | tf_op jit(solution)/shard_map/ppermute | solution.py:560
  111.2 2.3 %collective-permute-start.29 = (bf16[320,512]{1,0:T(8,128)(2,1)}, bf16[320,512]{1,0:T(8,128)(2,1)S(1)}, u32[]{:S(2)}, u32[]{:S(2)}) collective-permute-start(bf16[320,512]{1,0:T(8,128)(2,1)} %collective-permute-done.25.refs_1_), channel_id=1, source_target_pairs={{0,1},{1,0},{2,3},{3,2},{4,5},{5,4},{6,7},{7,6},{8,9},{9,8},{10,11... | collective-permute-start | bytes 983048 | tf_op jit(solution)/shard_map/ppermute | solution.py:560
  111.2 2.3 %collective-permute-start.30 = (bf16[320,512]{1,0:T(8,128)(2,1)S(1)}, bf16[320,512]{1,0:T(8,128)(2,1)S(1)}, u32[]{:S(2)}, u32[]{:S(2)}) collective-permute-start(bf16[320,512]{1,0:T(8,128)(2,1)S(1)} %collective-permute-done.26.refs_3_), channel_id=1, source_target_pairs={{0,1},{1,0},{2,3},{3,2},{4,5},{5,4},{6,7},{7,6},{8,9},{9,8},{10,11... | collective-permute-start | bytes 983048 | tf_op jit(solution)/shard_map/ppermute | solution.py:560
  111.7 2.1 %collective-permute-start.31 = (bf16[320,512]{1,0:T(8,128)(2,1)S(1)}, bf16[320,512]{1,0:T(8,128)(2,1)S(1)}, u32[]{:S(2)}, u32[]{:S(2)}) collective-permute-start(bf16[320,512]{1,0:T(8,128)(2,1)S(1)} %collective-permute-done.27.refs_5_), channel_id=1, source_target_pairs={{0,1},{1,0},{2,3},{3,2},{4,5},{5,4},{6,7},{7,6},{8,9},{9,8},{10,11... | collective-permute-start | bytes 983048 | tf_op jit(solution)/shard_map/ppermute | solution.py:560

commit v6 on v5

--- a/solution.py
+++ b/solution.py
@@ -62,10 +62,12 @@
     count, patch_rows = slots.shape[0], rows // cols
     size = count + 2 * patch_rows
     place = lax.broadcasted_iota(jnp.int32, (size, 1), 0)
+    core = lax.axis_index("lon") % 2
+    outer = jnp.where(core == 0, 0, cols - 1)
     wanted = jnp.where(
         place < count + patch_rows,
-        (place - count) * cols,
-        (place - count - patch_rows) * cols + cols - 1,
+        (place - count) * cols + outer,
+        (place - count - patch_rows) * cols + cols - 1 - outer,
     )
     for k in range(count):
         wanted = jnp.where(place == k, slots[k], wanted)
@@ -132,24 +134,31 @@
     ) = take(24)
     rows = patch_rows * cols
     depth = nodes.shape[-1]
-    pack = coarse_count + 2 * patch_rows + 16
+    pack = coarse_count + patch_rows + 8
     chip_count = lon_count // 2
+    half_far = chip_count * pack + patch_rows + 16
     lat, lon = lax.axis_index("lat"), lax.axis_index("lon")
-    core = lon % 2
+    core, chip = lon % 2, lon // 2
     top_valid, bottom_valid = lat > 0, lat < lat_count - 1
+    even_lat = 1 - lat % 2
 
     def place_of(other):
         apart = other ^ lon
         return (apart % 2) * chip_count + apart // 2
 
-    right_at = place_of((lon + 1) % lon_count) * pack
-    left_at = place_of((lon + lon_count - 1) % lon_count) * pack
+    outer_chip = (chip + chip_count - 1 + 2 * core) % chip_count
+    outer_at = half_far + (chip ^ outer_chip) * pack + coarse_count
+    inner_at = half_far + chip_count * pack
+    right_at = jnp.where(core == 0, inner_at, outer_at)
+    left_at = jnp.where(core == 0, outer_at, inner_at)
     tile = 16
 
     upper, lower = pl.ds(0, cols), pl.ds(cols, cols)
     arriving = [
-        pltpu.make_async_copy(source, near_nodes.at[place], near_sems.at[k])
-        for k, (source, place) in enumerate(zip(sources[:2], (upper, lower)))
+        pltpu.make_async_copy(
+            source, near_nodes.at[pl.ds(aligned(start, cols), cols)], near_sems.at[k]
+        )
+        for k, (source, start) in enumerate(zip(sources[:2], (even_lat * cols, cols - even_lat * cols)))
     ]
     loads = {}
     for k, (source, target) in enumerate(zip(sources[2:], held[1:])):
@@ -172,7 +181,6 @@
     for copy in (*arriving, loads[0], loads[1]):
         copy.wait()
     near_half = 0.5 * to_f32(to_bf16(dot(near_nodes[...], w_send[...])))
-    half_far = chip_count * pack
     same, cross = pl.ds(0, half_far), pl.ds(half_far, half_far)
     far[same, :] = 0.5 * to_f32(to_bf16(dot(gathered[...], w_send[...])))
     far[cross, :] = 0.5 * to_f32(to_bf16(dot(crossed[...], w_send[...])))
@@ -181,18 +189,18 @@
     last = lax.broadcasted_iota(jnp.int32, (cols, 1), 0) == cols - 1
     top = jnp.where(top_valid, near_half[:cols], ABSENT)
     bottom = jnp.where(bottom_valid, near_half[cols : 2 * cols], ABSENT)
-    corner_at = pack - 16
-    right_corners = far[pl.ds(aligned(right_at + corner_at, 16), 16), :]
-    left_corners = far[pl.ds(aligned(left_at + corner_at, 16), 16), :]
-    top_corner = jnp.where(top_valid, right_corners[0:1], ABSENT)
-    bottom_corner = jnp.where(bottom_valid, left_corners[15:16], ABSENT)
+    right_corner = pl.ds(aligned(right_at + patch_rows, 8), 8)
+    left_corner = pl.ds(aligned(left_at + patch_rows, 8), 8)
+    top_corner = jnp.where(top_valid, far[right_corner, :][0:1], ABSENT)
+    bottom_corner = jnp.where(bottom_valid, far[left_corner, :][0:1], ABSENT)
     mid[pl.ds(0, cols), :] = top
     mid[pl.ds(rows + cols, cols), :] = bottom
     right[pl.ds(0, cols), :] = jnp.where(last, top_corner, pltpu.roll(top, cols - 1, 0))
     left[pl.ds(rows + cols, cols), :] = jnp.where(first, bottom_corner, pltpu.roll(bottom, 1, 0))
 
-    right_edge = far[pl.ds(aligned(right_at + coarse_count, 16), patch_rows), :]
-    left_edge = far[pl.ds(aligned(left_at + coarse_count + patch_rows, 16), patch_rows), :]
+    right_place = pl.ds(aligned(right_at, 8), patch_rows)
+    left_place = pl.ds(aligned(left_at, 8), patch_rows)
+    right_edge, left_edge = far[right_place, :], far[left_place, :]
     for row in range(patch_rows):
         there = pl.ds((row + 1) * cols, cols)
         for lane in range(0, depth, 128):
@@ -233,9 +241,8 @@
             send_hot[row, :] = to_f32(coarse_lane == first_id + long_senders[source, edge])
             recv_hot[row, :] = to_f32(slot_lane == long_receivers[source, edge])
     for source in range(lon_count):
-        coarse[pl.ds(source * coarse_count, coarse_count), :] = far[
-            pl.ds(source * pack, coarse_count), :
-        ]
+        start = source // chip_count * half_far + source % chip_count * pack
+        coarse[pl.ds(source * coarse_count, coarse_count), :] = far[pl.ds(start, coarse_count), :]
     coarse_recv = 0.5 * (dot(gathered[pl.ds(0, coarse_count), :], w_recv[...]) + edge_bias[...])
     long_half = dot_exact(send_hot[...], coarse[...]) + dot_exact(
         recv_hot[...], coarse_recv
@@ -365,10 +372,10 @@
             )
             right_edge = jnp.where(edge_place == row, to_right[cols - 1 : cols], right_edge)
             left_edge = jnp.where(edge_place == row, to_left[0:1], left_edge)
-        far[pl.ds(aligned(right_at + coarse_count, 16), patch_rows), lanes] = right_edge
-        far[pl.ds(aligned(left_at + coarse_count + patch_rows, 16), patch_rows), lanes] = left_edge
+        far[right_place, lanes] = right_edge
+        far[left_place, lanes] = left_edge
     row_first, row_last = pl.ds(cols, cols), pl.ds(rows, cols)
-    sixteen = lax.broadcasted_iota(jnp.int32, (16, 1), 0)
+    eight = lax.broadcasted_iota(jnp.int32, (8, 1), 0)
     for lane in range(0, depth, 128):
         lanes = pl.ds(lane, 128)
         to_right = slope_times(5, row_first, lanes)
@@ -379,10 +386,8 @@
         )
         near_d[upper, lanes] = to_bf16(up)
         near_d[lower, lanes] = to_bf16(down)
-        corner = jnp.where(sixteen == 0, to_right[cols - 1 : cols], 0.0)
-        far[pl.ds(aligned(right_at + corner_at, 16), 16), lanes] = corner
-        corner = jnp.where(sixteen == 15, to_left[0:1], 0.0)
-        far[pl.ds(aligned(left_at + corner_at, 16), 16), lanes] = corner
+        far[right_corner, lanes] = jnp.where(eight == 0, to_right[cols - 1 : cols], 0.0)
+        far[left_corner, lanes] = jnp.where(eight == 0, to_left[0:1], 0.0)
     d_up[...] = near_d[upper, :]
     d_down[...] = near_d[lower, :]
     leave(d_up, results[4], out_sems.at[4])
@@ -398,9 +403,8 @@
         total[spot, :] = total[spot, :] + coarse_d[pl.ds(k, 1), :]
     coarse[...] = dot_exact_tn(send_hot[...], long_d)
     for source in range(lon_count):
-        far[pl.ds(source * pack, coarse_count), :] = coarse[
-            pl.ds(source * coarse_count, coarse_count), :
-        ]
+        start = source // chip_count * half_far + source % chip_count * pack
+        far[pl.ds(start, coarse_count), :] = coarse[pl.ds(source * coarse_count, coarse_count), :]
     d_gathered[...] = to_bf16(far[same, :])
     d_crossed[...] = to_bf16(far[cross, :])
     leave(d_gathered, results[6], out_sems.at[6])
@@ -442,7 +446,7 @@
     share = depth // (2 * lat_count)
     edge_count = ints[1].shape[0] * ints[1].shape[1]
     coarse_ids = lon_count * coarse_count
-    far_rows = lon_count * (coarse_count + 2 * patch_rows + 16)
+    far_rows = lon_count * (coarse_count + patch_rows + 8) + 2 * (patch_rows + 16)
     near_rows = 2 * cols
     long_rows = rows + 2 * cols
     out = lambda *size: jax.ShapeDtypeStruct(size, jnp.bfloat16)
@@ -501,8 +505,8 @@
         d_pre_b,
         d_recv_b,
         d_send,
-        from_below,
-        from_above,
+        one,
+        two,
         back,
         w_self,
         w_recv,
@@ -516,15 +520,17 @@
     for start in range(0, rows, step_rows):
         block = pl.ds(start, step_rows)
         total[block, :] = to_f32(d_send[block, :])
-    for start, part in ((rows - cols, from_below), (0, from_above)):
-        total[pl.ds(start, cols), :] += to_f32(part[...])
+    start = (1 - lax.axis_index("lat") % 2) * (rows - cols)
+    for start, part in ((start, one), (rows - cols - start, two)):
+        total[pl.ds(aligned(start, cols), cols), :] += to_f32(part[...])
     for which, vector in enumerate(vectors):
         vector[...] = scale * summed[pl.ds(summed.shape[0] - 8 + which, 1), :]
     returned = back[...]
+    outer = jnp.where(lax.axis_index("lon") % 2 == 0, 0, cols - 1)
     for row in range(patch_rows):
-        for spot, at in ((row * cols, 0), (row * cols + cols - 1, patch_rows)):
+        for spot, at in ((outer, 0), (cols - 1 - outer, patch_rows)):
             one = coarse_count + at + row
-            total[pl.ds(spot, 1), :] += returned[one : one + 1]
+            total[pl.ds(row * cols + spot, 1), :] += returned[one : one + 1]
     for k in range(coarse_count):
         total[pl.ds(slots[k], 1), :] += returned[k : k + 1]
     for start in range(0, rows, step_rows):
@@ -680,24 +686,32 @@
     flat = nodes.reshape(rows, depth)
     cot = cotangent.reshape(rows, depth)
 
-    down = [(i, i + 1) for i in range(lat_count - 1)]
-    up = [(i + 1, i) for i in range(lat_count - 1)]
-
-    above = lax.ppermute(flat[-cols:], "lat", down)
-    below = lax.ppermute(flat[:cols], "lat", up)
+    odd = lax.axis_index("lat") % 2 == 1
+    firsts = [(i, i ^ 1) for i in range(lat_count)]
+    seconds = [pair for i in range(1, lat_count - 1, 2) for pair in ((i, i + 1), (i + 1, i))]
+
+    def paired(to_above, to_below):
+        one = lax.ppermute(jnp.where(odd, to_above, to_below), "lat", firsts)
+        return one, lax.ppermute(jnp.where(odd, to_below, to_above), "lat", seconds)
+
+    one, two = paired(flat[:cols], flat[-cols:])
     packed = pack_nodes(cols, slots, flat)
-    filler = jnp.zeros((14, depth), jnp.bfloat16)
-    packed = jnp.concatenate([packed, above[:1], filler, below[-1:]])
-    chips = [swapped(packed, "lon", 2 * k) for k in range(1, chip_count)]
-    gathered = jnp.concatenate([packed, *chips])
+    outer_is_left = lon % 2 == 0
+    corners = jnp.where(odd, one[:1], two[:1]), jnp.where(odd, two[-1:], one[-1:])
+    outer_corner = jnp.where(outer_is_left, corners[0], corners[1])
+    inner_corner = jnp.where(outer_is_left, corners[1], corners[0])
+    outer_end, filler = coarse_count + patch_rows, jnp.zeros((15, depth), jnp.bfloat16)
+    message = jnp.concatenate([packed[:outer_end], outer_corner, filler[:7]])
+    chips = [swapped(message, "lon", 2 * k) for k in range(1, chip_count)]
+    gathered = jnp.concatenate([message, *chips, packed[outer_end:], inner_corner, filler])
     crossed = swapped(gathered, "lon", 1)
     outs = update(
         dims,
         (slots, long_senders.reshape(lon_count, -1), long_receivers.reshape(lon_count, -1)),
         (edge_bias[None], node_bias[None], gain[None]),
         (
-            above,
-            below,
+            one,
+            two,
             gathered,
             crossed,
             w_send,
@@ -714,17 +728,21 @@
 
     def returning(d_crossed):
         chips = to_bf16(to_f32(d_gathered) + to_f32(swapped(d_crossed, "lon", 1)))
-        parts = chips.reshape(chip_count, -1, depth)
+        inner = to_f32(chips[-patch_rows - 16 :])
+        parts = chips[: -patch_rows - 16].reshape(chip_count, -1, depth)
         received = [swapped(parts[step], "lon", 2 * step) for step in range(1, chip_count)]
-        return sum([to_f32(one) for one in received], to_f32(parts[0]))
-
-    def borders(back):
-        corners = to_bf16(back[-16:])
-        ups = jnp.concatenate([to_bf16(to_f32(d_up[:1]) + to_f32(corners[:1])), d_up[1:]])
-        downs = jnp.concatenate([d_down[:-1], to_bf16(to_f32(d_down[-1:]) + to_f32(corners[-1:]))])
-        return lax.ppermute(ups, "lat", up), lax.ppermute(downs, "lat", down)
-
-    total, back, bordered = summed_part(mine, other, d_crossed, returning, borders)
+        return sum([to_f32(one) for one in received], to_f32(parts[0])), inner
+
+    def borders(returned):
+        outer_corner, inner_corner = returned[0][outer_end :][:1], returned[1][patch_rows:][:1]
+        up_corner = jnp.where(outer_is_left, outer_corner, inner_corner)
+        down_corner = jnp.where(outer_is_left, inner_corner, outer_corner)
+        ups = jnp.concatenate([to_bf16(to_f32(d_up[:1]) + up_corner), d_up[1:]])
+        downs = jnp.concatenate([d_down[:-1], to_bf16(to_f32(d_down[-1:]) + down_corner)])
+        return paired(ups, downs)
+
+    total, (back, inner), bordered = summed_part(mine, other, d_crossed, returning, borders)
+    back = jnp.concatenate([back[:outer_end], inner[:patch_rows]])
     grad_nodes, *vectors = finish(
         dims,
         scale,

time: 118 us -> 114 us (0.966)
  starting transfers between devices: 42.1 us -> 36.4 us
    ppermute x28, starting transfers between devices: 29.5 us -> 25.4 us  [swapped(): return lax.ppermute(values, axis, [(i, i ^ bit) for i in range(count)])]
    ppermute x4, starting transfers between devices: 12.6 us -> 11 us  [the longest x2 9.64 us: paired(): one = lax.ppermute(jnp.where(odd, to_above, to_below), 'lat', firsts)]
    ppermute x28, waiting for transfers between devices: 30.1 us -> 31.4 us  [swapped(): return lax.ppermute(values, axis, [(i, i ^ bit) for i in range(count)])]
  transfers between devices with their start and end apart: 32 -> 32, of which waited for: 17 -> 17; matrix products, arithmetic and copies ran while one was open for 1% -> 3% of each run, Pallas kernels for 7% -> 8%
where the time goes in v6:
time: 114 us
  Pallas kernels  36.7 us (32%)
  starting transfers between devices  36.4 us (32%)
  waiting for transfers between devices  31.8 us (28%)
  local copies, waits for them, and re-layouts  4.41 us (4%)
  other arithmetic  3.34 us (3%)
    ppermute x28, waiting for transfers between devices, swapped(): return lax.ppermute(values, axis, [(i, i ^ bit) for i in range(count)])  31.4 us
    ppermute x28, starting transfers between devices, swapped(): return lax.ppermute(values, axis, [(i, i ^ bit) for i in range(count)])  25.4 us
    pallas_call x1, Pallas kernels, update(): pl.pallas_call(functools.partial(update_kernel, dims), in_specs=[smem] *...  24.5 us
    ppermute x2, starting transfers between devices, paired(): one = lax.ppermute(jnp.where(odd, to_above, to_below), 'lat', firsts)  9.64 us
    pallas_call x1, Pallas kernels, finish(): pl.pallas_call(functools.partial(finish_kernel, dims, scale), in_specs=[s...  5.68 us
    pallas_call x2, Pallas kernels, unpack(): pl.pallas_call(functools.partial(unpack_kernel, pieces, scale), in_specs=...  4.36 us
  transfers between devices with their start and end apart: 32, of which 17 were waited for; matrix products, arithmetic and copies ran while one was open for 3% of the time, Pallas kernels for 8%

profile of v6, /device:TPU:0, one launch (start us, length us, event | category | flops | bytes accessed | tf_op | source)
XLA Modules:
  0.0 113.8 jit_solution(1616890917336362338)
XLA Ops:
  0.7 0.9 select_bitcast_fusion
  1.5 0.7 collective-permute-start.1
  2.2 5.7 %collective-permute-start = (bf16[64,512]{1,0:T(8,128)(2,1)S(1)}, bf16[64,512]{1,0:T(8,128)(2,1)S(1)}, u32[]{:S(2)}, u32[]{:S(2)}) collective-permute-start(bf16[64,512]{1,0:T(8,128)(2,1)S(1)} %get-tuple-element.119), channel_id=1, source_target_pairs={{0,8},{8,0},{16,24},{24,16},{1,9},{9,1},{17,25},{25,17},{2,10},{10... | collective-permute-start | bytes 196616 | tf_op jit(solution)/shard_map/ppermute | solution.py:694
  8.0 2.1 %pack_nodes.1 = bf16[48,512]{1,0:T(8,128)(2,1)} custom-call(s32[16]{0:T(128)} %bitcast.53, bf16[1024,512]{1,0:T(8,128)(2,1)} %bitcast.39), custom_call_target="tpu_custom_call" | custom-call | tf_op jit(solution)/shard_map/pack_nodes/pallas_call | solution.py:82
  10.1 0.8 slice.118
  10.9 0.2 collective-permute-done.refs_0_
  11.1 3.7 %collective-permute-start.4 = (bf16[40,512]{1,0:T(8,128)(2,1)S(1)}, bf16[40,512]{1,0:T(8,128)(2,1)S(1)}, u32[]{:S(2)}, u32[]{:S(2)}) collective-permute-start(bf16[40,512]{1,0:T(8,128)(2,1)S(1)} %pad_maximum_fusion.8), channel_id=1, source_target_pairs={{0,6},{1,7},{2,4},{3,5},{4,2},{5,3},{6,0},{7,1},{8,14},{9,15},{10,... | collective-permute-start | bytes 122888 | tf_op jit(solution)/shard_map/ppermute | solution.py:566
  14.8 0.8 collective-permute-start.2
  15.6 1.5 %collective-permute-done.4 = bf16[40,512]{1,0:T(8,128)(2,1)S(1)} collective-permute-done((bf16[40,512]{1,0:T(8,128)(2,1)S(1)}, bf16[40,512]{1,0:T(8,128)(2,1)S(1)}, u32[]{:S(2)}, u32[]{:S(2)}) %collective-permute-start.4) | collective-permute-done | bytes 40992 | tf_op jit(solution)/shard_map/ppermute | solution.py:566
  17.1 2.6 %collective-permute-done.3 = bf16[40,512]{1,0:T(8,128)(2,1)S(1)} collective-permute-done((bf16[40,512]{1,0:T(8,128)(2,1)S(1)}, bf16[40,512]{1,0:T(8,128)(2,1)S(1)}, u32[]{:S(2)}, u32[]{:S(2)}) %collective-permute-start.3) | collective-permute-done | bytes 40992 | tf_op jit(solution)/shard_map/ppermute | solution.py:566
  19.7 0.2 concatenate.29.refs_2_
  19.9 0.1 collective-permute-start.5
  20.0 1.4 %collective-permute-done.5.refs_3_ = bf16[192,512]{1,0:T(8,128)(2,1)S(1)} collective-permute-done((bf16[192,512]{1,0:T(8,128)(2,1)S(1)}, bf16[192,512]{1,0:T(8,128)(2,1)S(1)}, u32[]{:S(2)}, u32[]{:S(2)}) %collective-permute-start.5) | collective-permute-done | bytes 196640 | tf_op jit(solution)/shard_map/ppermute | solution.py:566
  21.4 0.7 copy-done.14
  22.1 24.5 %update.1 = (bf16[1024,512]{1,0:T(8,128)(2,1)}, bf16[1024,512]{1,0:T(8,128)(2,1)}, bf16[1024,512]{1,0:T(8,128)(2,1)}, bf16[1024,512]{1,0:T(8,128)(2,1)}, bf16[64...) custom-call(s32[16]{0:T(128)} %bitcast.54, ...), custom_call_target="tpu_custom_call" | custom-call | flops 6979321856 | bytes 20000000 | tf_op jit(solution)/shard_map/update/pallas_call | solution.py:458
  46.6 0.2 collective-permute-start.7
  46.9 0.4 collective-permute-start.9
  47.2 0.1 collective-permute-start.6
  47.4 0.4 collective-permute-start.11
  47.7 0.8 collective-permute-done.7
  48.6 1.1 add_convert_fusion.3
  49.7 0.2 collective-permute-start.13
  49.9 1.4 %collective-permute-start.8 = (bf16[336,512]{1,0:T(8,128)(2,1)S(1)}, bf16[336,512]{1,0:T(8,128)(2,1)S(1)}, u32[]{:S(2)}, u32[]{:S(2)}) collective-permute-start(bf16[336,512]{1,0:T(8,128)(2,1)S(1)} %add_convert_fusion.3), channel_id=1, source_target_pairs={{0,24},{8,16},{16,8},{24,0},{1,25},{9,17},{17,9},{25,1},{2,26},{10... | collective-permute-start | bytes 1032200 | tf_op jit(solution)/shard_map/ppermute | solution.py:566
  51.4 0.1 add_convert_fusion.2
  51.5 1.2 %collective-permute-start.10 = (bf16[336,512]{1,0:T(8,128)(2,1)S(1)}, bf16[336,512]{1,0:T(8,128)(2,1)S(1)}, u32[]{:S(2)}, u32[]{:S(2)}) collective-permute-start(bf16[336,512]{1,0:T(8,128)(2,1)S(1)} %add_convert_fusion.2), channel_id=1, source_target_pairs={{0,16},{8,24},{16,0},{24,8},{1,17},{9,25},{17,1},{25,9},{2,18},{10... | collective-permute-start | bytes 1032200 | tf_op jit(solution)/shard_map/ppermute | solution.py:566
  52.7 0.1 add_convert_fusion.4
  52.8 0.1 collective-permute-start.14
  52.9 3.5 %collective-permute-start.16 = (bf16[40,512]{1,0:T(8,128)(2,1)S(1)}, bf16[40,512]{1,0:T(8,128)(2,1)S(1)}, u32[]{:S(2)}, u32[]{:S(2)}) collective-permute-start(bf16[40,512]{1,0:T(8,128)(2,1)S(1)} %get-tuple-element.125), channel_id=1, source_target_pairs={{0,6},{1,7},{2,4},{3,5},{4,2},{5,3},{6,0},{7,1},{8,14},{9,15},{10,... | collective-permute-start | bytes 122888 | tf_op jit(solution)/shard_map/ppermute | solution.py:566
  56.4 0.1 add_convert_fusion.1
  56.5 0.4 collective-permute-done.14
  56.9 0.9 collective-permute-start.12
  57.7 1.0 collective-permute-done.16
  58.8 1.0 collective-permute-start.15
  59.8 3.9 %collective-permute-done.15 = bf16[40,512]{1,0:T(8,128)(2,1)S(1)} collective-permute-done((bf16[40,512]{1,0:T(8,128)(2,1)S(1)}, bf16[40,512]{1,0:T(8,128)(2,1)S(1)}, u32[]{:S(2)}, u32[]{:S(2)}) %collective-permute-start.15) | collective-permute-done | bytes 40992 | tf_op jit(solution)/shard_map/ppermute | solution.py:566
  63.7 4.8 %collective-permute-done.10 = bf16[336,512]{1,0:T(8,128)(2,1)S(1)} collective-permute-done((bf16[336,512]{1,0:T(8,128)(2,1)S(1)}, bf16[336,512]{1,0:T(8,128)(2,1)S(1)}, u32[]{:S(2)}, u32[]{:S(2)}) %collective-permute-start.10) | collective-permute-done | bytes 344096 | tf_op jit(solution)/shard_map/ppermute | solution.py:566
  68.5 0.2 add_convert_fusion
  68.9 0.1 collective-permute-start.17
  69.0 0.7 copy-done.7
  69.7 2.8 %collective-permute-start.19 = (bf16[88,512]{1,0:T(8,128)(2,1)S(1)}, bf16[88,512]{1,0:T(8,128)(2,1)S(1)}, u32[]{:S(2)}, u32[]{:S(2)}) collective-permute-start(bf16[88,512]{1,0:T(8,128)(2,1)S(1)} %get-tuple-element.133), channel_id=1, source_target_pairs={{0,6},{1,7},{2,4},{3,5},{4,2},{5,3},{6,0},{7,1},{8,14},{9,15},{10,... | collective-permute-start | bytes 270344 | tf_op jit(solution)/shard_map/ppermute | solution.py:566
  72.6 0.9 collective-permute-done.17
  73.6 0.7 collective-permute-start.21
  74.2 3.9 %collective-permute-start.20 = (bf16[64,512]{1,0:T(8,128)(2,1)S(1)}, bf16[64,512]{1,0:T(8,128)(2,1)S(1)}, u32[]{:S(2)}, u32[]{:S(2)}) collective-permute-start(bf16[64,512]{1,0:T(8,128)(2,1)S(1)} %get-tuple-element.130), channel_id=1, source_target_pairs={{0,8},{8,0},{16,24},{24,16},{1,9},{9,1},{17,25},{25,17},{2,10},{10... | collective-permute-start | bytes 196616 | tf_op jit(solution)/shard_map/ppermute | solution.py:694
  78.2 2.7 %collective-permute-done.18 = bf16[88,512]{1,0:T(8,128)(2,1)S(1)} collective-permute-done((bf16[88,512]{1,0:T(8,128)(2,1)S(1)}, bf16[88,512]{1,0:T(8,128)(2,1)S(1)}, u32[]{:S(2)}, u32[]{:S(2)}) %collective-permute-start.18) | collective-permute-done | bytes 90144 | tf_op jit(solution)/shard_map/ppermute | solution.py:566
  80.8 0.2 collective-permute-done.20.refs_4_
  81.1 0.4 copy-done.9
  81.5 0.2 copy-done.10
  81.6 0.7 collective-permute-start.22
  82.4 2.2 %collective-permute-start.23 = (bf16[80,512]{1,0:T(8,128)(2,1)S(1)}, bf16[80,512]{1,0:T(8,128)(2,1)S(1)}, u32[]{:S(2)}, u32[]{:S(2)}) collective-permute-start(bf16[80,512]{1,0:T(8,128)(2,1)S(1)} %slice.165), channel_id=1, source_target_pairs={{0,4},{1,5},{2,6},{3,7},{4,0},{5,1},{6,2},{7,3},{8,12},{9,13},{10,... | collective-permute-start | bytes 245768 | tf_op jit(solution)/shard_map/ppermute | solution.py:566
  84.6 1.5 %collective-permute-start.24 = (bf16[80,512]{1,0:T(8,128)(2,1)S(1)}, bf16[80,512]{1,0:T(8,128)(2,1)S(1)}, u32[]{:S(2)}, u32[]{:S(2)}) collective-permute-start(bf16[80,512]{1,0:T(8,128)(2,1)S(1)} %slice.165), channel_id=1, source_target_pairs={{0,6},{1,7},{2,4},{3,5},{4,2},{5,3},{6,0},{7,1},{8,14},{9,15},{10,... | collective-permute-start | bytes 245768 | tf_op jit(solution)/shard_map/ppermute | solution.py:566
  86.1 0.8 collective-permute-done.22
  86.9 4.4 %collective-permute-done.23 = bf16[80,512]{1,0:T(8,128)(2,1)S(1)} collective-permute-done((bf16[80,512]{1,0:T(8,128)(2,1)S(1)}, bf16[80,512]{1,0:T(8,128)(2,1)S(1)}, u32[]{:S(2)}, u32[]{:S(2)}) %collective-permute-start.23) | collective-permute-done | bytes 81952 | tf_op jit(solution)/shard_map/ppermute | solution.py:566
  91.3 0.6 gather_fusion
  91.9 1.5 %collective-permute-start.27 = (bf16[320,512]{1,0:T(8,128)(2,1)S(1)}, bf16[320,512]{1,0:T(8,128)(2,1)S(1)}, u32[]{:S(2)}, u32[]{:S(2)}) collective-permute-start(bf16[320,512]{1,0:T(8,128)(2,1)S(1)} %bitcast.34), channel_id=1, source_target_pairs={{0,24},{8,16},{16,8},{24,0},{1,25},{9,17},{17,9},{25,1},{2,26},{10... | collective-permute-start | bytes 983048 | tf_op jit(solution)/shard_map/ppermute | solution.py:566
  93.4 1.3 %collective-permute-start.26 = (bf16[320,512]{1,0:T(8,128)(2,1)S(1)}, bf16[320,512]{1,0:T(8,128)(2,1)S(1)}, u32[]{:S(2)}, u32[]{:S(2)}) collective-permute-start(bf16[320,512]{1,0:T(8,128)(2,1)S(1)} %bitcast.35), channel_id=1, source_target_pairs={{0,16},{8,24},{16,0},{24,8},{1,17},{9,25},{17,1},{25,9},{2,18},{10... | collective-permute-start | bytes 983048 | tf_op jit(solution)/shard_map/ppermute | solution.py:566
  94.7 0.8 collective-permute-start.25
  95.5 0.7 slice-done.1
  96.3 0.6 pad_maximum_fusion.5.refs_6_
  96.9 5.7 %finish.1 = (bf16[1024,512]{1,0:T(8,128)(2,1)}, f32[1,512]{1,0:T(1,128)}, f32[1,512]{1,0:T(1,128)}, f32[1,512]{1,0:T(1,128)}) custom-call(s32[16]{0:T(128)} %bitcast.55, bf16[1024,512]{1,0:T(8,128)(2,1)} %bitcast.44, bf16[1024,512]{1,0:T(8,128)(2,1)} %get-tuple-element.90.refs_1_, bf16[1024,512]{1,0:T(8,128)(2,1)} %get-tuple-element.91.refs_2_, ...), custom_call_target="tpu_custom_call" | custom-call | flops 1610612736 | bytes 8000000 | tf_op jit(solution)/shard_map/finish/pallas_call | solution.py:549
  102.6 1.0 unpack_1.1
  103.6 4.1 %collective-permute-done.26.refs_3_ = bf16[320,512]{1,0:T(8,128)(2,1)S(1)} collective-permute-done((bf16[320,512]{1,0:T(8,128)(2,1)S(1)}, bf16[320,512]{1,0:T(8,128)(2,1)S(1)}, u32[]{:S(2)}, u32[]{:S(2)}) %collective-permute-start.26) | collective-permute-done | bytes 327712 | tf_op jit(solution)/shard_map/ppermute | solution.py:566
  107.7 0.5 collective-permute-start.30
  108.2 1.6 %collective-permute-done.29.refs_2_ = bf16[320,512]{1,0:T(8,128)(2,1)S(1)} collective-permute-done((bf16[320,512]{1,0:T(8,128)(2,1)}, bf16[320,512]{1,0:T(8,128)(2,1)S(1)}, u32[]{:S(2)}, u32[]{:S(2)}) %collective-permute-start.29) | collective-permute-done | bytes 327712 | tf_op jit(solution)/shard_map/ppermute | solution.py:566
  109.9 0.4 collective-permute-done.31.refs_6_
  110.3 3.4 %unpack_7.1 = (f32[512,512]{1,0:T(8,128)}, f32[512,512]{1,0:T(8,128)}, f32[512,512]{1,0:T(8,128)}, f32[512,512]{1,0:T(8,128)}, f32[512,512]{1,0:T(8,128)}) custom-call(bf16[320,512]{1,0:T(8,128)(2,1)S(1)} %collective-permute-done.28.refs_0_, ...), custom_call_target="tpu_custom_call", output_to_operand_aliasing={{0}: (7, {}), {1}: (8, {}), {2}: (9, {}), {3}: (10, {}), {4... | custom-call | bytes 8000000 | tf_op jit(solution)/shard_map/unpack_7/pallas_call | solution.py:644
  (71 shorter events, 0.5 us)
Async XLA Ops:
  1.5 9.3 %collective-permute-start.1 = (bf16[64,512]{1,0:T(8,128)(2,1)S(1)}, bf16[64,512]{1,0:T(8,128)(2,1)S(1)}, u32[]{:S(2)}, u32[]{:S(2)}) collective-permute-start(bf16[64,512]{1,0:T(8,128)(2,1)S(1)} %get-tuple-element.118), channel_id=1, source_target_pairs={{8,16},{16,8},{9,17},{17,9},{10,18},{18,10},{11,19},{19,11},{12,20... | collective-permute-start | bytes 196616 | tf_op jit(solution)/shard_map/ppermute | solution.py:695
  2.2 8.9 %collective-permute-start = (bf16[64,512]{1,0:T(8,128)(2,1)S(1)}, bf16[64,512]{1,0:T(8,128)(2,1)S(1)}, u32[]{:S(2)}, u32[]{:S(2)}) collective-permute-start(bf16[64,512]{1,0:T(8,128)(2,1)S(1)} %get-tuple-element.119), channel_id=1, source_target_pairs={{0,8},{8,0},{16,24},{24,16},{1,9},{9,1},{17,25},{25,17},{2,10},{10... | collective-permute-start | bytes 196616 | tf_op jit(solution)/shard_map/ppermute | solution.py:694
  10.9 4.7 %copy-start.11 = (bf16[64,512]{1,0:T(8,128)(2,1)}, bf16[64,512]{1,0:T(8,128)(2,1)S(1)}, u32[]{:S(2)}) copy-start(bf16[64,512]{1,0:T(8,128)(2,1)S(1)} %collective-permute-done.1.refs_1_) | copy-start | bytes 196612
  11.1 4.5 %copy-start.12 = (bf16[64,512]{1,0:T(8,128)(2,1)}, bf16[64,512]{1,0:T(8,128)(2,1)S(1)}, u32[]{:S(2)}) copy-start(bf16[64,512]{1,0:T(8,128)(2,1)S(1)} %collective-permute-done.refs_0_) | copy-start | bytes 196612
  11.1 5.9 %collective-permute-start.4 = (bf16[40,512]{1,0:T(8,128)(2,1)S(1)}, bf16[40,512]{1,0:T(8,128)(2,1)S(1)}, u32[]{:S(2)}, u32[]{:S(2)}) collective-permute-start(bf16[40,512]{1,0:T(8,128)(2,1)S(1)} %pad_maximum_fusion.8), channel_id=1, source_target_pairs={{0,6},{1,7},{2,4},{3,5},{4,2},{5,3},{6,0},{7,1},{8,14},{9,15},{10,... | collective-permute-start | bytes 122888 | tf_op jit(solution)/shard_map/ppermute | solution.py:566
  14.8 4.9 %collective-permute-start.3 = (bf16[40,512]{1,0:T(8,128)(2,1)S(1)}, bf16[40,512]{1,0:T(8,128)(2,1)S(1)}, u32[]{:S(2)}, u32[]{:S(2)}) collective-permute-start(bf16[40,512]{1,0:T(8,128)(2,1)S(1)} %pad_maximum_fusion.8), channel_id=1, source_target_pairs={{0,4},{1,5},{2,6},{3,7},{4,0},{5,1},{6,2},{7,3},{8,12},{9,13},{10,... | collective-permute-start | bytes 122888 | tf_op jit(solution)/shard_map/ppermute | solution.py:566
  14.8 4.9 %collective-permute-start.2 = (bf16[40,512]{1,0:T(8,128)(2,1)S(1)}, bf16[40,512]{1,0:T(8,128)(2,1)S(1)}, u32[]{:S(2)}, u32[]{:S(2)}) collective-permute-start(bf16[40,512]{1,0:T(8,128)(2,1)S(1)} %pad_maximum_fusion.8), channel_id=1, source_target_pairs={{0,2},{1,3},{2,0},{3,1},{4,6},{5,7},{6,4},{7,5},{8,10},{9,11},{10,... | collective-permute-start | bytes 122888 | tf_op jit(solution)/shard_map/ppermute | solution.py:566
  15.6 4.1 %slice-start = ((bf16[48,512]{1,0:T(8,128)(2,1)}), bf16[16,512]{1,0:T(8,128)(2,1)S(1)}, s32[]{:S(2)}) async-start(bf16[48,512]{1,0:T(8,128)(2,1)} %pack_nodes.1), calls=%async_computation | async-start | bytes 32768 | tf_op jit(solution)/shard_map/slice | solution.py:706
  19.9 1.5 %copy-start.4 = (bf16[192,512]{1,0:T(8,128)(2,1)}, bf16[192,512]{1,0:T(8,128)(2,1)S(1)}, u32[]{:S(2)}) copy-start(bf16[192,512]{1,0:T(8,128)(2,1)S(1)} %concatenate.29.refs_2_) | copy-start | bytes 589828
  19.9 1.5 %collective-permute-start.5 = (bf16[192,512]{1,0:T(8,128)(2,1)S(1)}, bf16[192,512]{1,0:T(8,128)(2,1)S(1)}, u32[]{:S(2)}, u32[]{:S(2)}) collective-permute-start(bf16[192,512]{1,0:T(8,128)(2,1)S(1)} %concatenate.29.refs_2_), channel_id=1, source_target_pairs={{0,1},{1,0},{2,3},{3,2},{4,5},{5,4},{6,7},{7,6},{8,9},{9,8},{10,11... | collective-permute-start | bytes 589832 | tf_op jit(solution)/shard_map/ppermute | solution.py:566
  21.4 0.7 copy-start.14
  46.6 1.9 %collective-permute-start.7 = (bf16[336,512]{1,0:T(8,128)(2,1)}, bf16[336,512]{1,0:T(8,128)(2,1)S(1)}, u32[]{:S(2)}, u32[]{:S(2)}) collective-permute-start(bf16[336,512]{1,0:T(8,128)(2,1)} %get-tuple-element.68), channel_id=1, source_target_pairs={{0,1},{1,0},{2,3},{3,2},{4,5},{5,4},{6,7},{7,6},{8,9},{9,8},{10,11... | collective-permute-start | bytes 1032200 | tf_op jit(solution)/shard_map/ppermute | solution.py:566
  46.9 4.5 %collective-permute-start.9 = (bf16[336,512]{1,0:T(8,128)(2,1)}, bf16[336,512]{1,0:T(8,128)(2,1)S(1)}, u32[]{:S(2)}, u32[]{:S(2)}) collective-permute-start(bf16[336,512]{1,0:T(8,128)(2,1)} %get-tuple-element.72), channel_id=1, source_target_pairs={{0,1},{1,0},{2,3},{3,2},{4,5},{5,4},{6,7},{7,6},{8,9},{9,8},{10,11... | collective-permute-start | bytes 1032200 | tf_op jit(solution)/shard_map/ppermute | solution.py:566
  47.2 21.3 %collective-permute-start.6 = (bf16[336,512]{1,0:T(8,128)(2,1)}, bf16[336,512]{1,0:T(8,128)(2,1)S(1)}, u32[]{:S(2)}, u32[]{:S(2)}) collective-permute-start(bf16[336,512]{1,0:T(8,128)(2,1)} %get-tuple-element.66), channel_id=1, source_target_pairs={{0,1},{1,0},{2,3},{3,2},{4,5},{5,4},{6,7},{7,6},{8,9},{9,8},{10,11... | collective-permute-start | bytes 1032200 | tf_op jit(solution)/shard_map/ppermute | solution.py:566
  47.4 5.5 %collective-permute-start.11 = (bf16[336,512]{1,0:T(8,128)(2,1)}, bf16[336,512]{1,0:T(8,128)(2,1)S(1)}, u32[]{:S(2)}, u32[]{:S(2)}) collective-permute-start(bf16[336,512]{1,0:T(8,128)(2,1)} %get-tuple-element.74), channel_id=1, source_target_pairs={{0,1},{1,0},{2,3},{3,2},{4,5},{5,4},{6,7},{7,6},{8,9},{9,8},{10,11... | collective-permute-start | bytes 1032200 | tf_op jit(solution)/shard_map/ppermute | solution.py:566
  48.6 1.1 copy-start.13
  48.6 2.8 %copy-start.2 = (bf16[336,512]{1,0:T(8,128)(2,1)S(1)}, bf16[336,512]{1,0:T(8,128)(2,1)}, u32[]{:S(2)}) copy-start(bf16[336,512]{1,0:T(8,128)(2,1)} %get-tuple-element.71) | copy-start | bytes 1032196
  49.7 3.0 %collective-permute-start.13 = (bf16[192,512]{1,0:T(8,128)(2,1)S(1)}, bf16[192,512]{1,0:T(8,128)(2,1)S(1)}, u32[]{:S(2)}, u32[]{:S(2)}) collective-permute-start(bf16[192,512]{1,0:T(8,128)(2,1)S(1)} %copy-done.13), channel_id=1, source_target_pairs={{0,1},{1,0},{2,3},{3,2},{4,5},{5,4},{6,7},{7,6},{8,9},{9,8},{10,11... | collective-permute-start | bytes 589832 | tf_op jit(solution)/shard_map/ppermute | solution.py:566
  49.9 13.8 %collective-permute-start.8 = (bf16[336,512]{1,0:T(8,128)(2,1)S(1)}, bf16[336,512]{1,0:T(8,128)(2,1)S(1)}, u32[]{:S(2)}, u32[]{:S(2)}) collective-permute-start(bf16[336,512]{1,0:T(8,128)(2,1)S(1)} %add_convert_fusion.3), channel_id=1, source_target_pairs={{0,24},{8,16},{16,8},{24,0},{1,25},{9,17},{17,9},{25,1},{2,26},{10... | collective-permute-start | bytes 1032200 | tf_op jit(solution)/shard_map/ppermute | solution.py:566
  51.4 1.3 %copy-start.5 = (bf16[192,512]{1,0:T(8,128)(2,1)S(1)}, bf16[192,512]{1,0:T(8,128)(2,1)}, u32[]{:S(2)}) copy-start(bf16[192,512]{1,0:T(8,128)(2,1)} %get-tuple-element.75) | copy-start | bytes 589828
  51.5 17.1 %collective-permute-start.10 = (bf16[336,512]{1,0:T(8,128)(2,1)S(1)}, bf16[336,512]{1,0:T(8,128)(2,1)S(1)}, u32[]{:S(2)}, u32[]{:S(2)}) collective-permute-start(bf16[336,512]{1,0:T(8,128)(2,1)S(1)} %add_convert_fusion.2), channel_id=1, source_target_pairs={{0,16},{8,24},{16,0},{24,8},{1,17},{9,25},{17,1},{25,9},{2,18},{10... | collective-permute-start | bytes 1032200 | tf_op jit(solution)/shard_map/ppermute | solution.py:566
  52.7 3.6 %copy-start.1 = (bf16[336,512]{1,0:T(8,128)(2,1)S(1)}, bf16[336,512]{1,0:T(8,128)(2,1)}, u32[]{:S(2)}) copy-start(bf16[336,512]{1,0:T(8,128)(2,1)} %get-tuple-element.73) | copy-start | bytes 1032196
  52.8 4.1 %collective-permute-start.14 = (bf16[40,512]{1,0:T(8,128)(2,1)S(1)}, bf16[40,512]{1,0:T(8,128)(2,1)S(1)}, u32[]{:S(2)}, u32[]{:S(2)}) collective-permute-start(bf16[40,512]{1,0:T(8,128)(2,1)S(1)} %get-tuple-element.124), channel_id=1, source_target_pairs={{0,2},{1,3},{2,0},{3,1},{4,6},{5,7},{6,4},{7,5},{8,10},{9,11},{10,... | collective-permute-start | bytes 122888 | tf_op jit(solution)/shard_map/ppermute | solution.py:566
  52.9 5.9 %collective-permute-start.16 = (bf16[40,512]{1,0:T(8,128)(2,1)S(1)}, bf16[40,512]{1,0:T(8,128)(2,1)S(1)}, u32[]{:S(2)}, u32[]{:S(2)}) collective-permute-start(bf16[40,512]{1,0:T(8,128)(2,1)S(1)} %get-tuple-element.125), channel_id=1, source_target_pairs={{0,6},{1,7},{2,4},{3,5},{4,2},{5,3},{6,0},{7,1},{8,14},{9,15},{10,... | collective-permute-start | bytes 122888 | tf_op jit(solution)/shard_map/ppermute | solution.py:566
  56.4 12.1 %copy-start.3 = (bf16[336,512]{1,0:T(8,128)(2,1)S(1)}, bf16[336,512]{1,0:T(8,128)(2,1)}, u32[]{:S(2)}) copy-start(bf16[336,512]{1,0:T(8,128)(2,1)} %get-tuple-element.65) | copy-start | bytes 1032196
  56.9 11.7 %collective-permute-start.12 = (bf16[336,512]{1,0:T(8,128)(2,1)S(1)}, bf16[336,512]{1,0:T(8,128)(2,1)S(1)}, u32[]{:S(2)}, u32[]{:S(2)}) collective-permute-start(bf16[336,512]{1,0:T(8,128)(2,1)S(1)} %add_convert_fusion.1), channel_id=1, source_target_pairs={{0,8},{8,0},{16,24},{24,16},{1,9},{9,1},{17,25},{25,17},{2,10},{10... | collective-permute-start | bytes 1032200 | tf_op jit(solution)/shard_map/ppermute | solution.py:566
  58.8 4.9 %collective-permute-start.15 = (bf16[40,512]{1,0:T(8,128)(2,1)S(1)}, bf16[40,512]{1,0:T(8,128)(2,1)S(1)}, u32[]{:S(2)}, u32[]{:S(2)}) collective-permute-start(bf16[40,512]{1,0:T(8,128)(2,1)S(1)} %get-tuple-element.126), channel_id=1, source_target_pairs={{0,4},{1,5},{2,6},{3,7},{4,0},{5,1},{6,2},{7,3},{8,12},{9,13},{10,... | collective-permute-start | bytes 122888 | tf_op jit(solution)/shard_map/ppermute | solution.py:566
  59.8 35.7 %copy-start.6 = (f32[32,512]{1,0:T(8,128)}, f32[32,512]{1,0:T(8,128)S(1)}, u32[]{:S(2)}) copy-start(f32[32,512]{1,0:T(8,128)S(1)} %slice_convert_fusion.1) | copy-start | bytes 196612
  68.9 0.8 copy-start.7
  68.9 4.6 %collective-permute-start.17 = (bf16[88,512]{1,0:T(8,128)(2,1)S(1)}, bf16[88,512]{1,0:T(8,128)(2,1)S(1)}, u32[]{:S(2)}, u32[]{:S(2)}) collective-permute-start(bf16[88,512]{1,0:T(8,128)(2,1)S(1)} %get-tuple-element.134), channel_id=1, source_target_pairs={{0,2},{1,3},{2,0},{3,1},{4,6},{5,7},{6,4},{7,5},{8,10},{9,11},{10,... | collective-permute-start | bytes 270344 | tf_op jit(solution)/shard_map/ppermute | solution.py:566
  69.7 3.8 %copy-start.8 = (bf16[64,512]{1,0:T(8,128)(2,1)S(1)}, bf16[64,512]{1,0:T(8,128)(2,1)}, u32[]{:S(2)}) copy-start(bf16[64,512]{1,0:T(8,128)(2,1)} %get-tuple-element.86) | copy-start | bytes 196612
  69.7 8.4 %collective-permute-start.19 = (bf16[88,512]{1,0:T(8,128)(2,1)S(1)}, bf16[88,512]{1,0:T(8,128)(2,1)S(1)}, u32[]{:S(2)}, u32[]{:S(2)}) collective-permute-start(bf16[88,512]{1,0:T(8,128)(2,1)S(1)} %get-tuple-element.133), channel_id=1, source_target_pairs={{0,6},{1,7},{2,4},{3,5},{4,2},{5,3},{6,0},{7,1},{8,14},{9,15},{10,... | collective-permute-start | bytes 270344 | tf_op jit(solution)/shard_map/ppermute | solution.py:566
  72.6 8.3 %collective-permute-start.18 = (bf16[88,512]{1,0:T(8,128)(2,1)S(1)}, bf16[88,512]{1,0:T(8,128)(2,1)S(1)}, u32[]{:S(2)}, u32[]{:S(2)}) collective-permute-start(bf16[88,512]{1,0:T(8,128)(2,1)S(1)} %get-tuple-element.135), channel_id=1, source_target_pairs={{0,4},{1,5},{2,6},{3,7},{4,0},{5,1},{6,2},{7,3},{8,12},{9,13},{10,... | collective-permute-start | bytes 270344 | tf_op jit(solution)/shard_map/ppermute | solution.py:566
  73.6 7.3 %collective-permute-start.21 = (bf16[64,512]{1,0:T(8,128)(2,1)S(1)}, bf16[64,512]{1,0:T(8,128)(2,1)S(1)}, u32[]{:S(2)}, u32[]{:S(2)}) collective-permute-start(bf16[64,512]{1,0:T(8,128)(2,1)S(1)} %get-tuple-element.129), channel_id=1, source_target_pairs={{8,16},{16,8},{9,17},{17,9},{10,18},{18,10},{11,19},{19,11},{12,20... | collective-permute-start | bytes 196616 | tf_op jit(solution)/shard_map/ppermute | solution.py:695
  74.2 6.8 %collective-permute-start.20 = (bf16[64,512]{1,0:T(8,128)(2,1)S(1)}, bf16[64,512]{1,0:T(8,128)(2,1)S(1)}, u32[]{:S(2)}, u32[]{:S(2)}) collective-permute-start(bf16[64,512]{1,0:T(8,128)(2,1)S(1)} %get-tuple-element.130), channel_id=1, source_target_pairs={{0,8},{8,0},{16,24},{24,16},{1,9},{9,1},{17,25},{25,17},{2,10},{10... | collective-permute-start | bytes 196616 | tf_op jit(solution)/shard_map/ppermute | solution.py:694
  80.8 0.6 copy-start.9
  81.0 0.6 copy-start.10
  81.6 4.5 %copy-start = (f32[88,512]{1,0:T(8,128)}, f32[88,512]{1,0:T(8,128)S(1)}, u32[]{:S(2)}) copy-start(f32[88,512]{1,0:T(8,128)S(1)} %convert_add_fusion.refs_10_) | copy-start | bytes 540676
  81.6 5.3 %collective-permute-start.22 = (bf16[80,512]{1,0:T(8,128)(2,1)S(1)}, bf16[80,512]{1,0:T(8,128)(2,1)S(1)}, u32[]{:S(2)}, u32[]{:S(2)}) collective-permute-start(bf16[80,512]{1,0:T(8,128)(2,1)S(1)} %slice.165), channel_id=1, source_target_pairs={{0,2},{1,3},{2,0},{3,1},{4,6},{5,7},{6,4},{7,5},{8,10},{9,11},{10,... | collective-permute-start | bytes 245768 | tf_op jit(solution)/shard_map/ppermute | solution.py:566
  82.4 8.9 %collective-permute-start.23 = (bf16[80,512]{1,0:T(8,128)(2,1)S(1)}, bf16[80,512]{1,0:T(8,128)(2,1)S(1)}, u32[]{:S(2)}, u32[]{:S(2)}) collective-permute-start(bf16[80,512]{1,0:T(8,128)(2,1)S(1)} %slice.165), channel_id=1, source_target_pairs={{0,4},{1,5},{2,6},{3,7},{4,0},{5,1},{6,2},{7,3},{8,12},{9,13},{10,... | collective-permute-start | bytes 245768 | tf_op jit(solution)/shard_map/ppermute | solution.py:566
  84.6 6.7 %collective-permute-start.24 = (bf16[80,512]{1,0:T(8,128)(2,1)S(1)}, bf16[80,512]{1,0:T(8,128)(2,1)S(1)}, u32[]{:S(2)}, u32[]{:S(2)}) collective-permute-start(bf16[80,512]{1,0:T(8,128)(2,1)S(1)} %slice.165), channel_id=1, source_target_pairs={{0,6},{1,7},{2,4},{3,5},{4,2},{5,3},{6,0},{7,1},{8,14},{9,15},{10,... | collective-permute-start | bytes 245768 | tf_op jit(solution)/shard_map/ppermute | solution.py:566
  91.9 11.7 %collective-permute-start.27 = (bf16[320,512]{1,0:T(8,128)(2,1)S(1)}, bf16[320,512]{1,0:T(8,128)(2,1)S(1)}, u32[]{:S(2)}, u32[]{:S(2)}) collective-permute-start(bf16[320,512]{1,0:T(8,128)(2,1)S(1)} %bitcast.34), channel_id=1, source_target_pairs={{0,24},{8,16},{16,8},{24,0},{1,25},{9,17},{17,9},{25,1},{2,26},{10... | collective-permute-start | bytes 983048 | tf_op jit(solution)/shard_map/ppermute | solution.py:566
  93.4 14.3 %collective-permute-start.26 = (bf16[320,512]{1,0:T(8,128)(2,1)S(1)}, bf16[320,512]{1,0:T(8,128)(2,1)S(1)}, u32[]{:S(2)}, u32[]{:S(2)}) collective-permute-start(bf16[320,512]{1,0:T(8,128)(2,1)S(1)} %bitcast.35), channel_id=1, source_target_pairs={{0,16},{8,24},{16,0},{24,8},{1,17},{9,25},{17,1},{25,9},{2,18},{10... | collective-permute-start | bytes 983048 | tf_op jit(solution)/shard_map/ppermute | solution.py:566
  94.7 13.0 %collective-permute-start.25 = (bf16[320,512]{1,0:T(8,128)(2,1)S(1)}, bf16[320,512]{1,0:T(8,128)(2,1)}, u32[]{:S(2)}, u32[]{:S(2)}) collective-permute-start(bf16[320,512]{1,0:T(8,128)(2,1)S(1)} %bitcast.36), channel_id=1, source_target_pairs={{0,8},{8,0},{16,24},{24,16},{1,9},{9,1},{17,25},{25,17},{2,10},{10... | collective-permute-start | bytes 983048 | tf_op jit(solution)/shard_map/ppermute | solution.py:566
  95.5 0.8 slice-start.1
  102.6 5.7 %collective-permute-start.28 = (bf16[320,512]{1,0:T(8,128)(2,1)S(1)}, bf16[320,512]{1,0:T(8,128)(2,1)S(1)}, u32[]{:S(2)}, u32[]{:S(2)}) collective-permute-start(bf16[320,512]{1,0:T(8,128)(2,1)S(1)} %bitcast.37), channel_id=1, source_target_pairs={{0,1},{1,0},{2,3},{3,2},{4,5},{5,4},{6,7},{7,6},{8,9},{9,8},{10,11... | collective-permute-start | bytes 983048 | tf_op jit(solution)/shard_map/ppermute | solution.py:566
  107.7 2.1 %collective-permute-start.29 = (bf16[320,512]{1,0:T(8,128)(2,1)}, bf16[320,512]{1,0:T(8,128)(2,1)S(1)}, u32[]{:S(2)}, u32[]{:S(2)}) collective-permute-start(bf16[320,512]{1,0:T(8,128)(2,1)} %collective-permute-done.25.refs_1_), channel_id=1, source_target_pairs={{0,1},{1,0},{2,3},{3,2},{4,5},{5,4},{6,7},{7,6},{8,9},{9,8},{10,11... | collective-permute-start | bytes 983048 | tf_op jit(solution)/shard_map/ppermute | solution.py:566
  107.7 2.1 %collective-permute-start.30 = (bf16[320,512]{1,0:T(8,128)(2,1)S(1)}, bf16[320,512]{1,0:T(8,128)(2,1)S(1)}, u32[]{:S(2)}, u32[]{:S(2)}) collective-permute-start(bf16[320,512]{1,0:T(8,128)(2,1)S(1)} %collective-permute-done.26.refs_3_), channel_id=1, source_target_pairs={{0,1},{1,0},{2,3},{3,2},{4,5},{5,4},{6,7},{7,6},{8,9},{9,8},{10,11... | collective-permute-start | bytes 983048 | tf_op jit(solution)/shard_map/ppermute | solution.py:566
  108.2 2.1 %collective-permute-start.31 = (bf16[320,512]{1,0:T(8,128)(2,1)S(1)}, bf16[320,512]{1,0:T(8,128)(2,1)S(1)}, u32[]{:S(2)}, u32[]{:S(2)}) collective-permute-start(bf16[320,512]{1,0:T(8,128)(2,1)S(1)} %collective-permute-done.27.refs_5_), channel_id=1, source_target_pairs={{0,1},{1,0},{2,3},{3,2},{4,5},{5,4},{6,7},{7,6},{8,9},{9,8},{10,11... | collective-permute-start | bytes 983048 | tf_op jit(solution)/shard_map/ppermute | solution.py:566

commit v7 on v6

--- a/solution.py
+++ b/solution.py
@@ -575,7 +575,7 @@
     crossed = {step: swapped(other[step], "lon", 1) for step in order}
     messages = [to_bf16(to_f32(mine[step]) + to_f32(crossed[step])) for step in order[:-1]]
     messages[0], d_crossed = lax.optimization_barrier((messages[0], d_crossed))
-    received = [swapped(part, "lat", step) for part, step in zip(messages, order)]
+    received = [swapped(messages[lat_count - 1 - step], "lat", step) for step in order[-2::-1]]
     received, returned = lax.optimization_barrier((received, returning(d_crossed)))
     total = to_f32(mine[0]) + to_f32(crossed[0])
     for part in received:
@@ -588,7 +588,8 @@
         part = lax.dynamic_index_in_dim(parts, chip ^ step, axis=1, keepdims=False)
         return jnp.concatenate([part.reshape(-1, depth), vectors])
 
-    received = [swapped(message_for(step), "lon", 2 * step) for step in range(1, chip_count)]
+    steps = [1, *range(chip_count - 1, 1, -1)]
+    received = [swapped(message_for(step), "lon", 2 * step) for step in steps]
     received[0], returned = lax.optimization_barrier((received[0], returned))
     received, bordered = lax.optimization_barrier((received, borders(returned)))
     total = to_f32(message_for(0))
@@ -691,8 +692,8 @@
     seconds = [pair for i in range(1, lat_count - 1, 2) for pair in ((i, i + 1), (i + 1, i))]
 
     def paired(to_above, to_below):
-        one = lax.ppermute(jnp.where(odd, to_above, to_below), "lat", firsts)
-        return one, lax.ppermute(jnp.where(odd, to_below, to_above), "lat", seconds)
+        two = lax.ppermute(jnp.where(odd, to_below, to_above), "lat", seconds)
+        return lax.ppermute(jnp.where(odd, to_above, to_below), "lat", firsts), two
 
     one, two = paired(flat[:cols], flat[-cols:])
     packed = pack_nodes(cols, slots, flat)
@@ -702,7 +703,7 @@
     inner_corner = jnp.where(outer_is_left, corners[1], corners[0])
     outer_end, filler = coarse_count + patch_rows, jnp.zeros((15, depth), jnp.bfloat16)
     message = jnp.concatenate([packed[:outer_end], outer_corner, filler[:7]])
-    chips = [swapped(message, "lon", 2 * k) for k in range(1, chip_count)]
+    chips = [swapped(message, "lon", 2 * k) for k in range(chip_count - 1, 0, -1)][::-1]
     gathered = jnp.concatenate([message, *chips, packed[outer_end:], inner_corner, filler])
     crossed = swapped(gathered, "lon", 1)
     outs = update(
@@ -730,7 +731,8 @@
         chips = to_bf16(to_f32(d_gathered) + to_f32(swapped(d_crossed, "lon", 1)))
         inner = to_f32(chips[-patch_rows - 16 :])
         parts = chips[: -patch_rows - 16].reshape(chip_count, -1, depth)
-        received = [swapped(parts[step], "lon", 2 * step) for step in range(1, chip_count)]
+        steps = [1, *range(chip_count - 1, 1, -1)]
+        received = [swapped(parts[step], "lon", 2 * step) for step in steps]
         return sum([to_f32(one) for one in received], to_f32(parts[0])), inner
 
     def borders(returned):
@@ -762,13 +764,12 @@
     )
 
     ready = gathered_share(total, lat_count)
-    shares = [swapped(ready, "lat", step) for step in range(1, lat_count)]
+    shares = [swapped(ready, "lat", step) for step in range(lat_count - 1, 0, -1)][::-1]
     outs = unpack([(0, 0)], scale, [ready])
     shares, grad_nodes, outs = lax.optimization_barrier((shares, grad_nodes, outs))
     crossed = [swapped(part, "lon", 1) for part in (ready, *shares)]
-    pieces = [(1, 0)] + [(flip, step) for step in range(1, lat_count) for flip in range(2)]
-    parts = [crossed[step] if flip else shares[step - 1] for flip, step in pieces]
-    outs = unpack(pieces, scale, parts, outs)
+    outs = unpack([(0, step) for step in range(1, lat_count)], scale, shares, outs)
+    outs = unpack([(1, step) for step in range(lat_count)], scale, crossed, outs)
     return (
         new_nodes.reshape(patch_rows, cols, depth),
         grad_nodes.reshape(patch_rows, cols, depth),

time: 114 us -> 114 us (level)
  starting transfers between devices: 36.4 us -> 30.9 us
  waiting for transfers between devices: 31.8 us -> 35 us
    ppermute x4, starting transfers between devices: 11 us -> 4.39 us  [the longest x2 3.07 us: paired(): lax.ppermute(jnp.where(odd, to_above, to_below), 'lat', firsts)]
    ppermute x28, waiting for transfers between devices: 31.4 us -> 35 us  [swapped(): return lax.ppermute(values, axis, [(i, i ^ bit) for i in range(count)])]
    ppermute x28, starting transfers between devices: 25.4 us -> 26.5 us  [swapped(): return lax.ppermute(values, axis, [(i, i ^ bit) for i in range(count)])]
    pallas_call x2 -> x3, Pallas kernels: 4.36 us -> 5.44 us  [unpack(): pl.pallas_call(functools.partial(unpack_kernel, pieces, scale), in_specs=...]
  transfers between devices with their start and end apart: 32 -> 32, of which waited for: 17 -> 14; matrix products, arithmetic and copies ran while one was open for 3% -> 3% of each run, Pallas kernels for 8% -> 10%
where the time goes in v7:
time: 114 us; the launch traced here: 113 us
  Pallas kernels  37.8 us (33%)
  waiting for transfers between devices  35 us (31%)
  starting transfers between devices  30.9 us (27%)
  local copies, waits for them, and re-layouts  4.84 us (4%)
  other arithmetic  3.34 us (3%)
  between operations  1.26 us (1%)
    ppermute x28, waiting for transfers between devices, swapped(): return lax.ppermute(values, axis, [(i, i ^ bit) for i in range(count)])  35 us
    ppermute x28, starting transfers between devices, swapped(): return lax.ppermute(values, axis, [(i, i ^ bit) for i in range(count)])  26.5 us
    pallas_call x1, Pallas kernels, update(): pl.pallas_call(functools.partial(update_kernel, dims), in_specs=[smem] *...  24.5 us
    pallas_call x1, Pallas kernels, finish(): pl.pallas_call(functools.partial(finish_kernel, dims, scale), in_specs=[s...  5.69 us
    pallas_call x3, Pallas kernels, unpack(): pl.pallas_call(functools.partial(unpack_kernel, pieces, scale), in_specs=...  5.44 us
    ppermute x2, starting transfers between devices, paired(): lax.ppermute(jnp.where(odd, to_above, to_below), 'lat', firsts)  3.07 us
    unnamed x30, local copies, waits for them, and re-layouts  2.35 us
  transfers between devices with their start and end apart: 32, of which 14 were waited for; matrix products, arithmetic and copies ran while one was open for 3% of the time, Pallas kernels for 10%

profile of v7, /device:TPU:0, one launch (start us, length us, event | category | flops | bytes accessed | tf_op | source)
XLA Modules:
  0.0 113.2 jit_solution(16044066510225935302)
XLA Ops:
  0.7 0.9 select_bitcast_fusion
  1.5 3.0 %collective-permute-start = (bf16[64,512]{1,0:T(8,128)(2,1)S(1)}, bf16[64,512]{1,0:T(8,128)(2,1)S(1)}, u32[]{:S(2)}, u32[]{:S(2)}) collective-permute-start(bf16[64,512]{1,0:T(8,128)(2,1)S(1)} %get-tuple-element.129), channel_id=1, source_target_pairs={{0,8},{8,0},{16,24},{24,16},{1,9},{9,1},{17,25},{25,17},{2,10},{10... | collective-permute-start | bytes 196616 | tf_op jit(solution)/shard_map/ppermute | solution.py:696
  4.5 0.7 collective-permute-start.1
  5.2 2.1 %pack_nodes.1 = bf16[48,512]{1,0:T(8,128)(2,1)} custom-call(s32[16]{0:T(128)} %bitcast.53, bf16[1024,512]{1,0:T(8,128)(2,1)} %bitcast.39), custom_call_target="tpu_custom_call" | custom-call | tf_op jit(solution)/shard_map/pack_nodes/pallas_call | solution.py:82
  7.4 0.8 slice.118
  8.2 1.6 %collective-permute-start.2 = (bf16[40,512]{1,0:T(8,128)(2,1)S(1)}, bf16[40,512]{1,0:T(8,128)(2,1)S(1)}, u32[]{:S(2)}, u32[]{:S(2)}) collective-permute-start(bf16[40,512]{1,0:T(8,128)(2,1)S(1)} %pad_maximum_fusion.8), channel_id=1, source_target_pairs={{0,2},{1,3},{2,0},{3,1},{4,6},{5,7},{6,4},{7,5},{8,10},{9,11},{10,... | collective-permute-start | bytes 122888 | tf_op jit(solution)/shard_map/ppermute | solution.py:566
  9.9 2.6 %collective-permute-start.3 = (bf16[40,512]{1,0:T(8,128)(2,1)S(1)}, bf16[40,512]{1,0:T(8,128)(2,1)S(1)}, u32[]{:S(2)}, u32[]{:S(2)}) collective-permute-start(bf16[40,512]{1,0:T(8,128)(2,1)S(1)} %pad_maximum_fusion.8), channel_id=1, source_target_pairs={{0,4},{1,5},{2,6},{3,7},{4,0},{5,1},{6,2},{7,3},{8,12},{9,13},{10,... | collective-permute-start | bytes 122888 | tf_op jit(solution)/shard_map/ppermute | solution.py:566
  12.4 0.2 collective-permute-start.4
  12.7 2.6 %collective-permute-done.3 = bf16[40,512]{1,0:T(8,128)(2,1)S(1)} collective-permute-done((bf16[40,512]{1,0:T(8,128)(2,1)S(1)}, bf16[40,512]{1,0:T(8,128)(2,1)S(1)}, u32[]{:S(2)}, u32[]{:S(2)}) %collective-permute-start.3) | collective-permute-done | bytes 40992 | tf_op jit(solution)/shard_map/ppermute | solution.py:566
  15.2 3.0 %collective-permute-done.4 = bf16[40,512]{1,0:T(8,128)(2,1)S(1)} collective-permute-done((bf16[40,512]{1,0:T(8,128)(2,1)S(1)}, bf16[40,512]{1,0:T(8,128)(2,1)S(1)}, u32[]{:S(2)}, u32[]{:S(2)}) %collective-permute-start.4) | collective-permute-done | bytes 40992 | tf_op jit(solution)/shard_map/ppermute | solution.py:566
  18.2 0.2 concatenate.29.refs_2_
  18.4 0.1 collective-permute-start.5
  18.5 1.4 %collective-permute-done.5.refs_3_ = bf16[192,512]{1,0:T(8,128)(2,1)S(1)} collective-permute-done((bf16[192,512]{1,0:T(8,128)(2,1)S(1)}, bf16[192,512]{1,0:T(8,128)(2,1)S(1)}, u32[]{:S(2)}, u32[]{:S(2)}) %collective-permute-start.5) | collective-permute-done | bytes 196640 | tf_op jit(solution)/shard_map/ppermute | solution.py:566
  19.9 0.7 copy-done.14
  20.6 24.5 %update.1 = (bf16[1024,512]{1,0:T(8,128)(2,1)}, bf16[1024,512]{1,0:T(8,128)(2,1)}, bf16[1024,512]{1,0:T(8,128)(2,1)}, bf16[1024,512]{1,0:T(8,128)(2,1)}, bf16[64...) custom-call(s32[16]{0:T(128)} %bitcast.54, ...), custom_call_target="tpu_custom_call" | custom-call | flops 6979321856 | bytes 20000000 | tf_op jit(solution)/shard_map/update/pallas_call | solution.py:458
  45.2 0.2 collective-permute-start.11
  45.4 0.4 collective-permute-start.9
  45.8 0.1 collective-permute-start.7
  45.9 0.4 collective-permute-start.6
  46.3 0.8 collective-permute-done.11
  47.1 1.1 add_convert_fusion.1
  48.3 0.2 collective-permute-start.13
  48.5 1.6 %collective-permute-start.12 = (bf16[336,512]{1,0:T(8,128)(2,1)S(1)}, bf16[336,512]{1,0:T(8,128)(2,1)S(1)}, u32[]{:S(2)}, u32[]{:S(2)}) collective-permute-start(bf16[336,512]{1,0:T(8,128)(2,1)S(1)} %add_convert_fusion.1), channel_id=1, source_target_pairs={{0,24},{8,16},{16,8},{24,0},{1,25},{9,17},{17,9},{25,1},{2,26},{10... | collective-permute-start | bytes 1032200 | tf_op jit(solution)/shard_map/ppermute | solution.py:566
  50.1 0.1 add_convert_fusion.2
  50.2 4.1 %collective-permute-start.10 = (bf16[336,512]{1,0:T(8,128)(2,1)S(1)}, bf16[336,512]{1,0:T(8,128)(2,1)S(1)}, u32[]{:S(2)}, u32[]{:S(2)}) collective-permute-start(bf16[336,512]{1,0:T(8,128)(2,1)S(1)} %add_convert_fusion.2), channel_id=1, source_target_pairs={{0,16},{8,24},{16,0},{24,8},{1,17},{9,25},{17,1},{25,9},{2,18},{10... | collective-permute-start | bytes 1032200 | tf_op jit(solution)/shard_map/ppermute | solution.py:566
  54.3 0.1 add_convert_fusion.4
  54.4 0.1 collective-permute-start.14
  54.5 0.6 collective-permute-start.15
  55.1 0.3 copy-done.1
  55.3 0.1 add_convert_fusion.3
  55.4 3.1 %collective-permute-done.14 = bf16[40,512]{1,0:T(8,128)(2,1)S(1)} collective-permute-done((bf16[40,512]{1,0:T(8,128)(2,1)S(1)}, bf16[40,512]{1,0:T(8,128)(2,1)S(1)}, u32[]{:S(2)}, u32[]{:S(2)}) %collective-permute-start.14) | collective-permute-done | bytes 40992 | tf_op jit(solution)/shard_map/ppermute | solution.py:566
  58.5 1.5 %collective-permute-start.8 = (bf16[336,512]{1,0:T(8,128)(2,1)S(1)}, bf16[336,512]{1,0:T(8,128)(2,1)S(1)}, u32[]{:S(2)}, u32[]{:S(2)}) collective-permute-start(bf16[336,512]{1,0:T(8,128)(2,1)S(1)} %add_convert_fusion.3), channel_id=1, source_target_pairs={{0,8},{8,0},{16,24},{24,16},{1,9},{9,1},{17,25},{25,17},{2,10},{10... | collective-permute-start | bytes 1032200 | tf_op jit(solution)/shard_map/ppermute | solution.py:566
  60.0 0.4 collective-permute-done.15
  60.4 4.9 %collective-permute-done.16 = bf16[40,512]{1,0:T(8,128)(2,1)S(1)} collective-permute-done((bf16[40,512]{1,0:T(8,128)(2,1)S(1)}, bf16[40,512]{1,0:T(8,128)(2,1)S(1)}, u32[]{:S(2)}, u32[]{:S(2)}) %collective-permute-start.16) | collective-permute-done | bytes 40992 | tf_op jit(solution)/shard_map/ppermute | solution.py:566
  65.3 3.9 %collective-permute-done.10 = bf16[336,512]{1,0:T(8,128)(2,1)S(1)} collective-permute-done((bf16[336,512]{1,0:T(8,128)(2,1)S(1)}, bf16[336,512]{1,0:T(8,128)(2,1)S(1)}, u32[]{:S(2)}, u32[]{:S(2)}) %collective-permute-start.10) | collective-permute-done | bytes 344096 | tf_op jit(solution)/shard_map/ppermute | solution.py:566
  69.3 1.4 %collective-permute-done.8 = bf16[336,512]{1,0:T(8,128)(2,1)S(1)} collective-permute-done((bf16[336,512]{1,0:T(8,128)(2,1)S(1)}, bf16[336,512]{1,0:T(8,128)(2,1)S(1)}, u32[]{:S(2)}, u32[]{:S(2)}) %collective-permute-start.8) | collective-permute-done | bytes 344096 | tf_op jit(solution)/shard_map/ppermute | solution.py:566
  70.6 0.2 add_convert_fusion
  71.0 0.1 collective-permute-start.17
  71.1 0.7 copy-done.7
  71.8 0.5 collective-permute-start.18
  72.3 2.3 %collective-permute-start.19 = (bf16[88,512]{1,0:T(8,128)(2,1)S(1)}, bf16[88,512]{1,0:T(8,128)(2,1)S(1)}, u32[]{:S(2)}, u32[]{:S(2)}) collective-permute-start(bf16[88,512]{1,0:T(8,128)(2,1)S(1)} %get-tuple-element.143), channel_id=1, source_target_pairs={{0,4},{1,5},{2,6},{3,7},{4,0},{5,1},{6,2},{7,3},{8,12},{9,13},{10,... | collective-permute-start | bytes 270344 | tf_op jit(solution)/shard_map/ppermute | solution.py:566
  74.6 2.4 %collective-permute-done.17 = bf16[88,512]{1,0:T(8,128)(2,1)S(1)} collective-permute-done((bf16[88,512]{1,0:T(8,128)(2,1)S(1)}, bf16[88,512]{1,0:T(8,128)(2,1)S(1)}, u32[]{:S(2)}, u32[]{:S(2)}) %collective-permute-start.17) | collective-permute-done | bytes 90144 | tf_op jit(solution)/shard_map/ppermute | solution.py:566
  77.1 0.1 collective-permute-start.20
  77.2 0.7 collective-permute-start.21
  77.9 1.0 collective-permute-done.18
  78.9 3.4 %collective-permute-done.19 = bf16[88,512]{1,0:T(8,128)(2,1)S(1)} collective-permute-done((bf16[88,512]{1,0:T(8,128)(2,1)S(1)}, bf16[88,512]{1,0:T(8,128)(2,1)S(1)}, u32[]{:S(2)}, u32[]{:S(2)}) %collective-permute-start.19) | collective-permute-done | bytes 90144 | tf_op jit(solution)/shard_map/ppermute | solution.py:566
  82.3 0.6 copy-done.10
  82.9 0.1 convert_add_fusion.refs_10_
  83.0 0.1 collective-permute-start.22
  83.1 1.7 %collective-permute-start.23 = (bf16[80,512]{1,0:T(8,128)(2,1)S(1)}, bf16[80,512]{1,0:T(8,128)(2,1)S(1)}, u32[]{:S(2)}, u32[]{:S(2)}) collective-permute-start(bf16[80,512]{1,0:T(8,128)(2,1)S(1)} %slice.165), channel_id=1, source_target_pairs={{0,4},{1,5},{2,6},{3,7},{4,0},{5,1},{6,2},{7,3},{8,12},{9,13},{10,... | collective-permute-start | bytes 245768 | tf_op jit(solution)/shard_map/ppermute | solution.py:566
  84.8 2.7 %collective-permute-start.24 = (bf16[80,512]{1,0:T(8,128)(2,1)S(1)}, bf16[80,512]{1,0:T(8,128)(2,1)S(1)}, u32[]{:S(2)}, u32[]{:S(2)}) collective-permute-start(bf16[80,512]{1,0:T(8,128)(2,1)S(1)} %slice.165), channel_id=1, source_target_pairs={{0,6},{1,7},{2,4},{3,5},{4,2},{5,3},{6,0},{7,1},{8,14},{9,15},{10,... | collective-permute-start | bytes 245768 | tf_op jit(solution)/shard_map/ppermute | solution.py:566
  87.5 4.0 %collective-permute-done.23 = bf16[80,512]{1,0:T(8,128)(2,1)S(1)} collective-permute-done((bf16[80,512]{1,0:T(8,128)(2,1)S(1)}, bf16[80,512]{1,0:T(8,128)(2,1)S(1)}, u32[]{:S(2)}, u32[]{:S(2)}) %collective-permute-start.23) | collective-permute-done | bytes 81952 | tf_op jit(solution)/shard_map/ppermute | solution.py:566
  91.6 0.6 gather_fusion
  92.2 3.3 %collective-permute-start.25 = (bf16[320,512]{1,0:T(8,128)(2,1)S(1)}, bf16[320,512]{1,0:T(8,128)(2,1)S(1)}, u32[]{:S(2)}, u32[]{:S(2)}) collective-permute-start(bf16[320,512]{1,0:T(8,128)(2,1)S(1)} %bitcast.34), channel_id=1, source_target_pairs={{0,8},{8,0},{16,24},{24,16},{1,9},{9,1},{17,25},{25,17},{2,10},{10... | collective-permute-start | bytes 983048 | tf_op jit(solution)/shard_map/ppermute | solution.py:566
  95.5 1.5 %collective-permute-start.27 = (bf16[320,512]{1,0:T(8,128)(2,1)S(1)}, bf16[320,512]{1,0:T(8,128)(2,1)}, u32[]{:S(2)}, u32[]{:S(2)}) collective-permute-start(bf16[320,512]{1,0:T(8,128)(2,1)S(1)} %bitcast.36), channel_id=1, source_target_pairs={{0,24},{8,16},{16,8},{24,0},{1,25},{9,17},{17,9},{25,1},{2,26},{10... | collective-permute-start | bytes 983048 | tf_op jit(solution)/shard_map/ppermute | solution.py:566
  97.1 0.8 slice-done
  97.9 0.6 pad_maximum_fusion.5.refs_6_
  98.6 5.7 %finish.1 = (bf16[1024,512]{1,0:T(8,128)(2,1)}, f32[1,512]{1,0:T(1,128)}, f32[1,512]{1,0:T(1,128)}, f32[1,512]{1,0:T(1,128)}) custom-call(s32[16]{0:T(128)} %bitcast.55, bf16[1024,512]{1,0:T(8,128)(2,1)} %bitcast.44, bf16[1024,512]{1,0:T(8,128)(2,1)} %get-tuple-element.95.refs_1_, bf16[1024,512]{1,0:T(8,128)(2,1)} %get-tuple-element.96.refs_2_, ...), custom_call_target="tpu_custom_call" | custom-call | flops 1610612736 | bytes 8000000 | tf_op jit(solution)/shard_map/finish/pallas_call | solution.py:549
  104.2 1.0 unpack_1.1
  105.2 0.1 collective-permute-start.28
  105.3 2.7 %collective-permute-done.26.refs_1_ = bf16[320,512]{1,0:T(8,128)(2,1)S(1)} collective-permute-done((bf16[320,512]{1,0:T(8,128)(2,1)S(1)}, bf16[320,512]{1,0:T(8,128)(2,1)S(1)}, u32[]{:S(2)}, u32[]{:S(2)}) %collective-permute-start.26) | collective-permute-done | bytes 327712 | tf_op jit(solution)/shard_map/ppermute | solution.py:566
  108.1 0.5 collective-permute-start.30
  108.6 2.3 %unpack_3.1 = (f32[512,512]{1,0:T(8,128)}, f32[512,512]{1,0:T(8,128)}, f32[512,512]{1,0:T(8,128)}, f32[512,512]{1,0:T(8,128)}, f32[512,512]{1,0:T(8,128)}) custom-call(bf16[320,512]{1,0:T(8,128)(2,1)S(1)} %collective-permute-done.25.refs_0_, ...), custom_call_target="tpu_custom_call", output_to_operand_aliasing={{0}: (3, {}), {1}: (4, {}), {2}: (5, {}), {3}: (6, {}), {4}... | custom-call | bytes 8000000 | tf_op jit(solution)/shard_map/unpack_3/pallas_call | solution.py:645
  111.0 2.1 %unpack_4.1 = (f32[512,512]{1,0:T(8,128)}, f32[512,512]{1,0:T(8,128)}, f32[512,512]{1,0:T(8,128)}, f32[512,512]{1,0:T(8,128)}, f32[512,512]{1,0:T(8,128)}) custom-call(bf16[320,512]{1,0:T(8,128)(2,1)S(1)} %collective-permute-done.28.refs_0_, ...), custom_call_target="tpu_custom_call", output_to_operand_aliasing={{0}: (4, {}), {1}: (5, {}), {2}: (6, {}), {3}: (7, {}), {4}... | custom-call | bytes 8000000 | tf_op jit(solution)/shard_map/unpack_4/pallas_call | solution.py:645
  (72 shorter events, 0.5 us)
Async XLA Ops:
  1.5 6.6 %collective-permute-start = (bf16[64,512]{1,0:T(8,128)(2,1)S(1)}, bf16[64,512]{1,0:T(8,128)(2,1)S(1)}, u32[]{:S(2)}, u32[]{:S(2)}) collective-permute-start(bf16[64,512]{1,0:T(8,128)(2,1)S(1)} %get-tuple-element.129), channel_id=1, source_target_pairs={{0,8},{8,0},{16,24},{24,16},{1,9},{9,1},{17,25},{25,17},{2,10},{10... | collective-permute-start | bytes 196616 | tf_op jit(solution)/shard_map/ppermute | solution.py:696
  4.5 3.6 %collective-permute-start.1 = (bf16[64,512]{1,0:T(8,128)(2,1)S(1)}, bf16[64,512]{1,0:T(8,128)(2,1)S(1)}, u32[]{:S(2)}, u32[]{:S(2)}) collective-permute-start(bf16[64,512]{1,0:T(8,128)(2,1)S(1)} %get-tuple-element.128), channel_id=1, source_target_pairs={{8,16},{16,8},{9,17},{17,9},{10,18},{18,10},{11,19},{19,11},{12,20... | collective-permute-start | bytes 196616 | tf_op jit(solution)/shard_map/ppermute | solution.py:695
  8.1 4.5 %copy-start.11 = (bf16[64,512]{1,0:T(8,128)(2,1)}, bf16[64,512]{1,0:T(8,128)(2,1)S(1)}, u32[]{:S(2)}) copy-start(bf16[64,512]{1,0:T(8,128)(2,1)S(1)} %collective-permute-done.refs_0_) | copy-start | bytes 196612
  8.1 4.5 %copy-start.12 = (bf16[64,512]{1,0:T(8,128)(2,1)}, bf16[64,512]{1,0:T(8,128)(2,1)S(1)}, u32[]{:S(2)}) copy-start(bf16[64,512]{1,0:T(8,128)(2,1)S(1)} %collective-permute-done.1.refs_1_) | copy-start | bytes 196612
  8.2 4.5 %collective-permute-start.2 = (bf16[40,512]{1,0:T(8,128)(2,1)S(1)}, bf16[40,512]{1,0:T(8,128)(2,1)S(1)}, u32[]{:S(2)}, u32[]{:S(2)}) collective-permute-start(bf16[40,512]{1,0:T(8,128)(2,1)S(1)} %pad_maximum_fusion.8), channel_id=1, source_target_pairs={{0,2},{1,3},{2,0},{3,1},{4,6},{5,7},{6,4},{7,5},{8,10},{9,11},{10,... | collective-permute-start | bytes 122888 | tf_op jit(solution)/shard_map/ppermute | solution.py:566
  9.9 5.4 %collective-permute-start.3 = (bf16[40,512]{1,0:T(8,128)(2,1)S(1)}, bf16[40,512]{1,0:T(8,128)(2,1)S(1)}, u32[]{:S(2)}, u32[]{:S(2)}) collective-permute-start(bf16[40,512]{1,0:T(8,128)(2,1)S(1)} %pad_maximum_fusion.8), channel_id=1, source_target_pairs={{0,4},{1,5},{2,6},{3,7},{4,0},{5,1},{6,2},{7,3},{8,12},{9,13},{10,... | collective-permute-start | bytes 122888 | tf_op jit(solution)/shard_map/ppermute | solution.py:566
  12.4 5.8 %collective-permute-start.4 = (bf16[40,512]{1,0:T(8,128)(2,1)S(1)}, bf16[40,512]{1,0:T(8,128)(2,1)S(1)}, u32[]{:S(2)}, u32[]{:S(2)}) collective-permute-start(bf16[40,512]{1,0:T(8,128)(2,1)S(1)} %pad_maximum_fusion.8), channel_id=1, source_target_pairs={{0,6},{1,7},{2,4},{3,5},{4,2},{5,3},{6,0},{7,1},{8,14},{9,15},{10,... | collective-permute-start | bytes 122888 | tf_op jit(solution)/shard_map/ppermute | solution.py:566
  12.7 5.6 %slice-start.1 = ((bf16[48,512]{1,0:T(8,128)(2,1)}), bf16[16,512]{1,0:T(8,128)(2,1)S(1)}, s32[]{:S(2)}) async-start(bf16[48,512]{1,0:T(8,128)(2,1)} %pack_nodes.1), calls=%async_computation.1 | async-start | bytes 32768 | tf_op jit(solution)/shard_map/slice | solution.py:707
  18.4 1.5 %copy-start.5 = (bf16[192,512]{1,0:T(8,128)(2,1)}, bf16[192,512]{1,0:T(8,128)(2,1)S(1)}, u32[]{:S(2)}) copy-start(bf16[192,512]{1,0:T(8,128)(2,1)S(1)} %concatenate.29.refs_2_) | copy-start | bytes 589828
  18.4 1.5 %collective-permute-start.5 = (bf16[192,512]{1,0:T(8,128)(2,1)S(1)}, bf16[192,512]{1,0:T(8,128)(2,1)S(1)}, u32[]{:S(2)}, u32[]{:S(2)}) collective-permute-start(bf16[192,512]{1,0:T(8,128)(2,1)S(1)} %concatenate.29.refs_2_), channel_id=1, source_target_pairs={{0,1},{1,0},{2,3},{3,2},{4,5},{5,4},{6,7},{7,6},{8,9},{9,8},{10,11... | collective-permute-start | bytes 589832 | tf_op jit(solution)/shard_map/ppermute | solution.py:566
  19.9 0.7 copy-start.14
  45.2 1.9 %collective-permute-start.11 = (bf16[336,512]{1,0:T(8,128)(2,1)}, bf16[336,512]{1,0:T(8,128)(2,1)S(1)}, u32[]{:S(2)}, u32[]{:S(2)}) collective-permute-start(bf16[336,512]{1,0:T(8,128)(2,1)} %get-tuple-element.77), channel_id=1, source_target_pairs={{0,1},{1,0},{2,3},{3,2},{4,5},{5,4},{6,7},{7,6},{8,9},{9,8},{10,11... | collective-permute-start | bytes 1032200 | tf_op jit(solution)/shard_map/ppermute | solution.py:566
  45.4 4.7 %collective-permute-start.9 = (bf16[336,512]{1,0:T(8,128)(2,1)}, bf16[336,512]{1,0:T(8,128)(2,1)S(1)}, u32[]{:S(2)}, u32[]{:S(2)}) collective-permute-start(bf16[336,512]{1,0:T(8,128)(2,1)} %get-tuple-element.75), channel_id=1, source_target_pairs={{0,1},{1,0},{2,3},{3,2},{4,5},{5,4},{6,7},{7,6},{8,9},{9,8},{10,11... | collective-permute-start | bytes 1032200 | tf_op jit(solution)/shard_map/ppermute | solution.py:566
  45.8 8.7 %collective-permute-start.7 = (bf16[336,512]{1,0:T(8,128)(2,1)}, bf16[336,512]{1,0:T(8,128)(2,1)S(1)}, u32[]{:S(2)}, u32[]{:S(2)}) collective-permute-start(bf16[336,512]{1,0:T(8,128)(2,1)} %get-tuple-element.73), channel_id=1, source_target_pairs={{0,1},{1,0},{2,3},{3,2},{4,5},{5,4},{6,7},{7,6},{8,9},{9,8},{10,11... | collective-permute-start | bytes 1032200 | tf_op jit(solution)/shard_map/ppermute | solution.py:566
  45.9 24.7 %collective-permute-start.6 = (bf16[336,512]{1,0:T(8,128)(2,1)}, bf16[336,512]{1,0:T(8,128)(2,1)S(1)}, u32[]{:S(2)}, u32[]{:S(2)}) collective-permute-start(bf16[336,512]{1,0:T(8,128)(2,1)} %get-tuple-element.71), channel_id=1, source_target_pairs={{0,1},{1,0},{2,3},{3,2},{4,5},{5,4},{6,7},{7,6},{8,9},{9,8},{10,11... | collective-permute-start | bytes 1032200 | tf_op jit(solution)/shard_map/ppermute | solution.py:566
  47.1 1.1 copy-start.13
  47.1 3.0 %copy-start.2 = (bf16[336,512]{1,0:T(8,128)(2,1)S(1)}, bf16[336,512]{1,0:T(8,128)(2,1)}, u32[]{:S(2)}) copy-start(bf16[336,512]{1,0:T(8,128)(2,1)} %get-tuple-element.74) | copy-start | bytes 1032196
  48.3 6.1 %collective-permute-start.13 = (bf16[192,512]{1,0:T(8,128)(2,1)S(1)}, bf16[192,512]{1,0:T(8,128)(2,1)S(1)}, u32[]{:S(2)}, u32[]{:S(2)}) collective-permute-start(bf16[192,512]{1,0:T(8,128)(2,1)S(1)} %copy-done.13), channel_id=1, source_target_pairs={{0,1},{1,0},{2,3},{3,2},{4,5},{5,4},{6,7},{7,6},{8,9},{9,8},{10,11... | collective-permute-start | bytes 589832 | tf_op jit(solution)/shard_map/ppermute | solution.py:566
  48.5 16.9 %collective-permute-start.12 = (bf16[336,512]{1,0:T(8,128)(2,1)S(1)}, bf16[336,512]{1,0:T(8,128)(2,1)S(1)}, u32[]{:S(2)}, u32[]{:S(2)}) collective-permute-start(bf16[336,512]{1,0:T(8,128)(2,1)S(1)} %add_convert_fusion.1), channel_id=1, source_target_pairs={{0,24},{8,16},{16,8},{24,0},{1,25},{9,17},{17,9},{25,1},{2,26},{10... | collective-permute-start | bytes 1032200 | tf_op jit(solution)/shard_map/ppermute | solution.py:566
  50.1 4.2 %copy-start.6 = (bf16[192,512]{1,0:T(8,128)(2,1)S(1)}, bf16[192,512]{1,0:T(8,128)(2,1)}, u32[]{:S(2)}) copy-start(bf16[192,512]{1,0:T(8,128)(2,1)} %get-tuple-element.80) | copy-start | bytes 589828
  50.2 19.1 %collective-permute-start.10 = (bf16[336,512]{1,0:T(8,128)(2,1)S(1)}, bf16[336,512]{1,0:T(8,128)(2,1)S(1)}, u32[]{:S(2)}, u32[]{:S(2)}) collective-permute-start(bf16[336,512]{1,0:T(8,128)(2,1)S(1)} %add_convert_fusion.2), channel_id=1, source_target_pairs={{0,16},{8,24},{16,0},{24,8},{1,17},{9,25},{17,1},{25,9},{2,18},{10... | collective-permute-start | bytes 1032200 | tf_op jit(solution)/shard_map/ppermute | solution.py:566
  54.3 1.0 copy-start.1
  54.4 4.1 %collective-permute-start.14 = (bf16[40,512]{1,0:T(8,128)(2,1)S(1)}, bf16[40,512]{1,0:T(8,128)(2,1)S(1)}, u32[]{:S(2)}, u32[]{:S(2)}) collective-permute-start(bf16[40,512]{1,0:T(8,128)(2,1)S(1)} %get-tuple-element.134), channel_id=1, source_target_pairs={{0,2},{1,3},{2,0},{3,1},{4,6},{5,7},{6,4},{7,5},{8,10},{9,11},{10,... | collective-permute-start | bytes 122888 | tf_op jit(solution)/shard_map/ppermute | solution.py:566
  54.5 5.9 %collective-permute-start.15 = (bf16[40,512]{1,0:T(8,128)(2,1)S(1)}, bf16[40,512]{1,0:T(8,128)(2,1)S(1)}, u32[]{:S(2)}, u32[]{:S(2)}) collective-permute-start(bf16[40,512]{1,0:T(8,128)(2,1)S(1)} %get-tuple-element.136), channel_id=1, source_target_pairs={{0,6},{1,7},{2,4},{3,5},{4,2},{5,3},{6,0},{7,1},{8,14},{9,15},{10,... | collective-permute-start | bytes 122888 | tf_op jit(solution)/shard_map/ppermute | solution.py:566
  55.4 15.2 %copy-start.3 = (bf16[336,512]{1,0:T(8,128)(2,1)S(1)}, bf16[336,512]{1,0:T(8,128)(2,1)}, u32[]{:S(2)}) copy-start(bf16[336,512]{1,0:T(8,128)(2,1)} %get-tuple-element.70) | copy-start | bytes 1032196
  58.5 12.2 %collective-permute-start.8 = (bf16[336,512]{1,0:T(8,128)(2,1)S(1)}, bf16[336,512]{1,0:T(8,128)(2,1)S(1)}, u32[]{:S(2)}, u32[]{:S(2)}) collective-permute-start(bf16[336,512]{1,0:T(8,128)(2,1)S(1)} %add_convert_fusion.3), channel_id=1, source_target_pairs={{0,8},{8,0},{16,24},{24,16},{1,9},{9,1},{17,25},{25,17},{2,10},{10... | collective-permute-start | bytes 1032200 | tf_op jit(solution)/shard_map/ppermute | solution.py:566
  60.4 4.9 %collective-permute-start.16 = (bf16[40,512]{1,0:T(8,128)(2,1)S(1)}, bf16[40,512]{1,0:T(8,128)(2,1)S(1)}, u32[]{:S(2)}, u32[]{:S(2)}) collective-permute-start(bf16[40,512]{1,0:T(8,128)(2,1)S(1)} %get-tuple-element.135), channel_id=1, source_target_pairs={{0,4},{1,5},{2,6},{3,7},{4,0},{5,1},{6,2},{7,3},{8,12},{9,13},{10,... | collective-permute-start | bytes 122888 | tf_op jit(solution)/shard_map/ppermute | solution.py:566
  65.3 31.7 %copy-start.4 = (f32[40,512]{1,0:T(8,128)}, f32[40,512]{1,0:T(8,128)S(1)}, u32[]{:S(2)}) copy-start(f32[40,512]{1,0:T(8,128)S(1)} %convert_add_fusion.1) | copy-start | bytes 245764
  70.9 0.8 copy-start.7
  71.0 6.0 %collective-permute-start.17 = (bf16[88,512]{1,0:T(8,128)(2,1)S(1)}, bf16[88,512]{1,0:T(8,128)(2,1)S(1)}, u32[]{:S(2)}, u32[]{:S(2)}) collective-permute-start(bf16[88,512]{1,0:T(8,128)(2,1)S(1)} %get-tuple-element.144), channel_id=1, source_target_pairs={{0,2},{1,3},{2,0},{3,1},{4,6},{5,7},{6,4},{7,5},{8,10},{9,11},{10,... | collective-permute-start | bytes 270344 | tf_op jit(solution)/shard_map/ppermute | solution.py:566
  71.8 5.2 %copy-start.8 = (bf16[64,512]{1,0:T(8,128)(2,1)S(1)}, bf16[64,512]{1,0:T(8,128)(2,1)}, u32[]{:S(2)}) copy-start(bf16[64,512]{1,0:T(8,128)(2,1)} %get-tuple-element.91) | copy-start | bytes 196612
  71.8 7.1 %collective-permute-start.18 = (bf16[88,512]{1,0:T(8,128)(2,1)S(1)}, bf16[88,512]{1,0:T(8,128)(2,1)S(1)}, u32[]{:S(2)}, u32[]{:S(2)}) collective-permute-start(bf16[88,512]{1,0:T(8,128)(2,1)S(1)} %get-tuple-element.145), channel_id=1, source_target_pairs={{0,6},{1,7},{2,4},{3,5},{4,2},{5,3},{6,0},{7,1},{8,14},{9,15},{10,... | collective-permute-start | bytes 270344 | tf_op jit(solution)/shard_map/ppermute | solution.py:566
  72.3 9.9 %collective-permute-start.19 = (bf16[88,512]{1,0:T(8,128)(2,1)S(1)}, bf16[88,512]{1,0:T(8,128)(2,1)S(1)}, u32[]{:S(2)}, u32[]{:S(2)}) collective-permute-start(bf16[88,512]{1,0:T(8,128)(2,1)S(1)} %get-tuple-element.143), channel_id=1, source_target_pairs={{0,4},{1,5},{2,6},{3,7},{4,0},{5,1},{6,2},{7,3},{8,12},{9,13},{10,... | collective-permute-start | bytes 270344 | tf_op jit(solution)/shard_map/ppermute | solution.py:566
  77.1 5.2 %collective-permute-start.20 = (bf16[64,512]{1,0:T(8,128)(2,1)S(1)}, bf16[64,512]{1,0:T(8,128)(2,1)S(1)}, u32[]{:S(2)}, u32[]{:S(2)}) collective-permute-start(bf16[64,512]{1,0:T(8,128)(2,1)S(1)} %get-tuple-element.140), channel_id=1, source_target_pairs={{0,8},{8,0},{16,24},{24,16},{1,9},{9,1},{17,25},{25,17},{2,10},{10... | collective-permute-start | bytes 196616 | tf_op jit(solution)/shard_map/ppermute | solution.py:696
  77.2 5.1 %collective-permute-start.21 = (bf16[64,512]{1,0:T(8,128)(2,1)S(1)}, bf16[64,512]{1,0:T(8,128)(2,1)S(1)}, u32[]{:S(2)}, u32[]{:S(2)}) collective-permute-start(bf16[64,512]{1,0:T(8,128)(2,1)S(1)} %get-tuple-element.139), channel_id=1, source_target_pairs={{8,16},{16,8},{9,17},{17,9},{10,18},{18,10},{11,19},{19,11},{12,20... | collective-permute-start | bytes 196616 | tf_op jit(solution)/shard_map/ppermute | solution.py:695
  82.3 0.7 copy-start.9
  82.3 0.7 copy-start.10
  83.0 4.5 %copy-start = (f32[88,512]{1,0:T(8,128)}, f32[88,512]{1,0:T(8,128)S(1)}, u32[]{:S(2)}) copy-start(f32[88,512]{1,0:T(8,128)S(1)} %convert_add_fusion.refs_10_) | copy-start | bytes 540676
  83.0 4.5 %collective-permute-start.22 = (bf16[80,512]{1,0:T(8,128)(2,1)S(1)}, bf16[80,512]{1,0:T(8,128)(2,1)S(1)}, u32[]{:S(2)}, u32[]{:S(2)}) collective-permute-start(bf16[80,512]{1,0:T(8,128)(2,1)S(1)} %slice.165), channel_id=1, source_target_pairs={{0,2},{1,3},{2,0},{3,1},{4,6},{5,7},{6,4},{7,5},{8,10},{9,11},{10,... | collective-permute-start | bytes 245768 | tf_op jit(solution)/shard_map/ppermute | solution.py:566
  83.1 8.4 %collective-permute-start.23 = (bf16[80,512]{1,0:T(8,128)(2,1)S(1)}, bf16[80,512]{1,0:T(8,128)(2,1)S(1)}, u32[]{:S(2)}, u32[]{:S(2)}) collective-permute-start(bf16[80,512]{1,0:T(8,128)(2,1)S(1)} %slice.165), channel_id=1, source_target_pairs={{0,4},{1,5},{2,6},{3,7},{4,0},{5,1},{6,2},{7,3},{8,12},{9,13},{10,... | collective-permute-start | bytes 245768 | tf_op jit(solution)/shard_map/ppermute | solution.py:566
  84.8 6.7 %collective-permute-start.24 = (bf16[80,512]{1,0:T(8,128)(2,1)S(1)}, bf16[80,512]{1,0:T(8,128)(2,1)S(1)}, u32[]{:S(2)}, u32[]{:S(2)}) collective-permute-start(bf16[80,512]{1,0:T(8,128)(2,1)S(1)} %slice.165), channel_id=1, source_target_pairs={{0,6},{1,7},{2,4},{3,5},{4,2},{5,3},{6,0},{7,1},{8,14},{9,15},{10,... | collective-permute-start | bytes 245768 | tf_op jit(solution)/shard_map/ppermute | solution.py:566
  92.2 13.1 %collective-permute-start.25 = (bf16[320,512]{1,0:T(8,128)(2,1)S(1)}, bf16[320,512]{1,0:T(8,128)(2,1)S(1)}, u32[]{:S(2)}, u32[]{:S(2)}) collective-permute-start(bf16[320,512]{1,0:T(8,128)(2,1)S(1)} %bitcast.34), channel_id=1, source_target_pairs={{0,8},{8,0},{16,24},{24,16},{1,9},{9,1},{17,25},{25,17},{2,10},{10... | collective-permute-start | bytes 983048 | tf_op jit(solution)/shard_map/ppermute | solution.py:566
  95.5 12.5 %collective-permute-start.26 = (bf16[320,512]{1,0:T(8,128)(2,1)S(1)}, bf16[320,512]{1,0:T(8,128)(2,1)S(1)}, u32[]{:S(2)}, u32[]{:S(2)}) collective-permute-start(bf16[320,512]{1,0:T(8,128)(2,1)S(1)} %bitcast.35), channel_id=1, source_target_pairs={{0,16},{8,24},{16,0},{24,8},{1,17},{9,25},{17,1},{25,9},{2,18},{10... | collective-permute-start | bytes 983048 | tf_op jit(solution)/shard_map/ppermute | solution.py:566
  95.5 12.5 %collective-permute-start.27 = (bf16[320,512]{1,0:T(8,128)(2,1)S(1)}, bf16[320,512]{1,0:T(8,128)(2,1)}, u32[]{:S(2)}, u32[]{:S(2)}) collective-permute-start(bf16[320,512]{1,0:T(8,128)(2,1)S(1)} %bitcast.36), channel_id=1, source_target_pairs={{0,24},{8,16},{16,8},{24,0},{1,25},{9,17},{17,9},{25,1},{2,26},{10... | collective-permute-start | bytes 983048 | tf_op jit(solution)/shard_map/ppermute | solution.py:566
  97.1 0.8 slice-start
  105.2 5.7 %collective-permute-start.28 = (bf16[320,512]{1,0:T(8,128)(2,1)S(1)}, bf16[320,512]{1,0:T(8,128)(2,1)S(1)}, u32[]{:S(2)}, u32[]{:S(2)}) collective-permute-start(bf16[320,512]{1,0:T(8,128)(2,1)S(1)} %bitcast.38), channel_id=1, source_target_pairs={{0,1},{1,0},{2,3},{3,2},{4,5},{5,4},{6,7},{7,6},{8,9},{9,8},{10,11... | collective-permute-start | bytes 983048 | tf_op jit(solution)/shard_map/ppermute | solution.py:566
  108.1 2.9 %collective-permute-start.29 = (bf16[320,512]{1,0:T(8,128)(2,1)S(1)}, bf16[320,512]{1,0:T(8,128)(2,1)S(1)}, u32[]{:S(2)}, u32[]{:S(2)}) collective-permute-start(bf16[320,512]{1,0:T(8,128)(2,1)S(1)} %collective-permute-done.25.refs_0_), channel_id=1, source_target_pairs={{0,1},{1,0},{2,3},{3,2},{4,5},{5,4},{6,7},{7,6},{8,9},{9,8},{10,11... | collective-permute-start | bytes 983048 | tf_op jit(solution)/shard_map/ppermute | solution.py:566
  108.1 2.9 %collective-permute-start.30 = (bf16[320,512]{1,0:T(8,128)(2,1)S(1)}, bf16[320,512]{1,0:T(8,128)(2,1)S(1)}, u32[]{:S(2)}, u32[]{:S(2)}) collective-permute-start(bf16[320,512]{1,0:T(8,128)(2,1)S(1)} %collective-permute-done.26.refs_1_), channel_id=1, source_target_pairs={{0,1},{1,0},{2,3},{3,2},{4,5},{5,4},{6,7},{7,6},{8,9},{9,8},{10,11... | collective-permute-start | bytes 983048 | tf_op jit(solution)/shard_map/ppermute | solution.py:566
  108.6 2.4 %collective-permute-start.31 = (bf16[320,512]{1,0:T(8,128)(2,1)}, bf16[320,512]{1,0:T(8,128)(2,1)S(1)}, u32[]{:S(2)}, u32[]{:S(2)}) collective-permute-start(bf16[320,512]{1,0:T(8,128)(2,1)} %collective-permute-done.27.refs_2_), channel_id=1, source_target_pairs={{0,1},{1,0},{2,3},{3,2},{4,5},{5,4},{6,7},{7,6},{8,9},{9,8},{10,11... | collective-permute-start | bytes 983048 | tf_op jit(solution)/shard_map/ppermute | solution.py:566
